TPU v7x, 256 devices: a whole 4x4x8 slice. The times are simulated.
256 devices in a mesh: row: 8 (over z_lo, core), col: 16 (over x, y), wf: 2 (over z_hi).
Axes of the slice: x: 4, y: 4, z: 8 (z_hi: 2, z_lo: 4; z = z_hi * 4 + z_lo), core: 2. Of those that a mesh axis runs over, the one named last changes fastest.
Arguments:
- wave_blocks: bfloat16 [2, 32, 128, 128], P(None, None, 'wf'), may hold values from -0.5 to 0.5
- left_operators: bfloat16 [96, 32, 2, 128, 128], P('row', 'col'), may hold values from -0.375 to 0.375
- right_operators: bfloat16 [32, 128, 2, 128, 128], P(None, 'col', None, 'wf'), may hold values from -0.01171875 to 0.01171875
- left_table: int32 [96, 32], P('row'), may hold values from 0 to 31, as said below
- right_table: int32 [128, 32], replicated, may hold values from 0 to 31, as said below
- assignment: int32 [96], replicated, may hold values from 0 to 95, each once
- kramers_map: int32 [96], replicated, may hold values from 0 to 95, each once
Outputs:
- rdm: float32 [2, 2, 96, 128], P(None, None, 'row', ('col', 'wf'))
Inputs may be any that keep to these rules, and one draw needn't show every extreme that they name: left_table[s, q] is q, q + 1 or q + 2 modulo 32. right_table[j, q] is q, q + 1 or q + 2 modulo 32. `assignment`: a permutation. `kramers_map`: a permutation.
All inputs are finite; a program needn't handle non-finite values.
Results may differ from a plain program's by a relative error of at most 0.0041.
Values may be sent and summed in bfloat16 or wider, within the bound.
No kernel may reach another device: no remote copies, remote signals or barrier semaphores. Data moves between devices by JAX's collectives and lax.ppermute only.
A program may use at most 128 MiB of HBM per device.

v0:
```python
import jax
import jax.numpy as jnp
from jax import lax
from jax.sharding import PartitionSpec as P


def finish_slot(totals):
    real_part = jnp.stack(
        [totals[0, ..., 0] - totals[1, ..., 1], totals[2, ..., 0] - totals[3, ..., 1]]
    )
    imag_part = jnp.stack(
        [totals[0, ..., 1] + totals[1, ..., 0], totals[2, ..., 1] + totals[3, ..., 0]]
    )
    return jnp.stack([real_part, imag_part])


def local(
    wave_blocks, left_operators, right_operators, left_table, right_table, assignment, kramers_map
):
    local_left = left_operators.shape[0]
    block_count = left_operators.shape[1]
    local_right = right_operators.shape[1]
    panel_width = wave_blocks.shape[2]
    full_width = wave_blocks.shape[3]
    flat_width = panel_width * full_width
    block_start = lax.axis_index("col") * block_count
    own_table = lax.dynamic_slice_in_dim(left_table, block_start, block_count, 1)
    gathered = lax.all_gather(wave_blocks, "wf", axis=2, tiled=True)
    sources = gathered[:, own_table]
    own_wave = lax.dynamic_slice_in_dim(gathered, block_start, block_count, 1)
    product = jnp.einsum(
        "iqcab,diqbe->iqcdae", left_operators, sources, preferred_element_type=jnp.float32
    )
    real_real = product[:, :, 0, 0]
    real_imag = product[:, :, 0, 1]
    imag_real = product[:, :, 1, 0]
    imag_imag = product[:, :, 1, 1]
    turned = jnp.stack(
        [
            real_real - imag_imag,
            real_imag + imag_real,
            real_real + imag_imag,
            real_imag - imag_real,
        ],
        axis=2,
    ).astype(jnp.bfloat16)
    own_wave = lax.dynamic_slice_in_dim(
        own_wave, lax.axis_index("wf") * panel_width, panel_width, 3
    )
    bracket = jnp.einsum("dqar,iqkae->qdkire", own_wave, turned, preferred_element_type=jnp.float32)
    tiles = jnp.stack(
        [
            bracket[:, 0, 0] + bracket[:, 1, 1],
            bracket[:, 0, 1] - bracket[:, 1, 0],
            bracket[:, 0, 2] + bracket[:, 1, 3],
            bracket[:, 0, 3] - bracket[:, 1, 2],
        ],
        axis=1,
    ).astype(jnp.bfloat16)
    tiles = tiles.reshape(block_count, 4 * local_left, flat_width)
    right_flat = right_operators.reshape(right_operators.shape[0], 2 * local_right, flat_width)
    own_right = lax.dynamic_slice_in_dim(
        right_table, lax.axis_index("col") * local_right, local_right, 0
    )
    section = lax.all_gather(tiles, "col", axis=0, tiled=True)
    count = section.shape[0]
    paired = lax.dot_general(
        section, right_flat, (((2,), (2,)), ((0,), (0,))), preferred_element_type=jnp.float32
    )
    paired = paired.reshape(count, 4, local_left, local_right, 2)
    matching = (left_table.T[:, :, None] == own_right.T[:, None, :]).astype(jnp.float32)
    totals = jnp.sum(paired * matching[:, None, :, :, None], axis=0)
    shares = lax.psum_scatter(finish_slot(totals), "wf", scatter_dimension=3, tiled=True)
    all_slots = lax.all_gather(shares, "row", axis=2, tiled=True)
    row_offset = lax.axis_index("row") * local_left
    targets = row_offset + jnp.arange(local_left, dtype=jnp.int32)
    pick_direct = (assignment[None, :] == targets[:, None]).astype(jnp.float32)
    partners = lax.dynamic_slice_in_dim(kramers_map, row_offset, local_left, 0)
    pick_barred = (assignment[None, :] == partners[:, None]).astype(jnp.float32)
    direct = jnp.einsum(
        "ls,cst->clt", pick_direct, all_slots[:, 0], precision=lax.Precision.HIGHEST
    )
    barred = jnp.einsum(
        "ls,cst->clt", pick_barred, all_slots[:, 1], precision=lax.Precision.HIGHEST
    )
    return jnp.stack([direct, barred], axis=1)


def solution(mesh):
    return jax.shard_map(
        local,
        mesh=mesh,
        in_specs=(
            P(None, None, "wf", None),
            P("row", "col", None, None, None),
            P(None, "col", None, "wf", None),
            P("row", None),
            P(),
            P(),
            P(),
        ),
        out_specs=P(None, None, "row", ("col", "wf")),
        check_vma=False,
    )
```

profile of v0, /device:TPU:1, one launch (start us, length us, event | category | flops | bytes accessed | tf_op | source)
XLA Modules:
  0.0 305.7 jit_solution(8293304461741637223)
XLA Ops:
  6.5 0.0 copy-start
  6.5 0.0 all-gather.3.cloned.1.call-start
  6.5 3.0 copy.60
  9.5 0.0 all-gather.3.cloned.1.call-update
  9.6 0.0 all-gather.5.cloned.1.call-start
  9.6 0.0 copy-done.2
  9.6 0.1 compare_select_fusion
  9.7 0.1 reshape.248
  9.8 68.9 %all-gather.3.cloned.1.call-done = bf16[2,32,128,128]{3,1,0,2:T(8,128)(2,1)} async-done(((bf16[2,32,64,128]{3,1,0,2:T(8,128)(2,1)}), bf16[2,32,128,128]{3,1,0,2:T(8,128)(2,1)}) %all-gather.3.cloned.1.call-update) | async-done | bytes 2097168 | tf_op jit(solution)/shard_map/all_gather | solution.py:28
  78.7 4.3 %copy.61 = bf16[2,32,128,128]{3,2,1,0:T(8,128)(2,1)} copy(bf16[2,32,128,128]{3,1,0,2:T(8,128)(2,1)} %all-gather.3.cloned.1.call-done) | data formatting | bytes 4194304 | tf_op jit(solution)/shard_map/all_gather | solution.py:28
  82.9 2.4 gather_fusion
  85.4 1.6 copy.62
  87.0 0.0 copy-done
  87.0 2.4 convolution_bitcast_fusion
  89.4 0.7 fusion.9
  90.1 0.2 fusion.11
  90.3 1.5 constant_dynamic-slice_fusion
  91.8 0.1 copy.94
  91.9 1.5 fusion.2
  93.5 0.5 fusion.20
  94.0 0.1 fusion.23
  94.1 0.2 pad_maximum_fusion
  94.3 0.2 copy.76
  94.5 2.1 convert_element_type.15
  96.6 0.0 all-gather.5.cloned.1.call-update
  96.7 0.7 copy-done.3
  97.4 0.1 dynamic-slice_bitcast_fusion
  97.4 0.1 copy.77
  97.5 0.1 mul.26
  97.6 0.2 copy.78
  97.9 0.0 copy-start.6
  97.9 0.0 copy-start.4
  97.9 13.6 %reshape.245 = bf16[32,16,8192]{2,1,0:T(8,128)(2,1)} reshape(bf16[32,8,2,64,128]{4,3,2,1,0:T(8,128)(2,1)} %param.9) | data formatting | bytes 16777216 | tf_op jit(solution)/shard_map/reshape | solution.py:61
  111.5 0.0 copy-done.6
  111.6 0.6 dynamic-slice
  112.8 0.1 dynamic_slice.17
  112.9 139.3 %all-gather.5.cloned.1.call-done = bf16[32,48,8192]{2,1,0:T(8,128)(2,1)} async-done(((bf16[2,48,8192]{2,1,0:T(8,128)(2,1)}), bf16[32,48,8192]{2,1,0:T(8,128)(2,1)}) %all-gather.5.cloned.1.call-update) | async-done | bytes 25165840 | tf_op jit(solution)/shard_map/all_gather | solution.py:65
  252.1 14.1 %fusion.8 = f32[48,16]{0,1:T(8,128)S(1)} fusion(f32[32,48,16]{1,2,0:T(8,128)S(1)} %copy.78, bf16[32,48,8192]{2,1,0:T(8,128)(2,1)} %all-gather.5.cloned.1.call-done, bf16[32,16,8192]{2,1,0:T(8,128)(2,1)} %reshape.245), kind=kOutput, calls=%fused_computation.17 | convolution fusion | flops 402701568 | bytes 33655808 | tf_op jit(solution)/shard_map/dot_general | solution.py:67
  266.2 0.1 reduce_sum.12
  266.4 14.3 %all-reduce = f32[2,2,12,8]{2,3,0,1:T(8,128)S(1)} all-reduce(f32[2,2,12,8]{2,3,0,1:T(8,128)S(1)} %copy.79), channel_id=2, replica_groups=mesh['row'=8,'col'=16,'wf'=2] {'wf'}, use_global_device_ids=true, to_apply=%region_1.0.clone | all-reduce | flops 384 | bytes 3072
  280.7 0.1 copy.80
  280.8 16.6 %all_gather.11 = f32[2,2,96,4]{3,1,0,2:T(2,128)S(1)} all-gather(f32[2,2,12,4]{3,1,0,2:T(2,128)S(1)} %copy.80), channel_id=1, replica_groups=mesh['row'=8,'col'=16,'wf'=2] {'row'}, dimensions={2}, use_global_device_ids=true | all-gather | bytes 6912 | tf_op jit(solution)/shard_map/all_gather | solution.py:74
  297.4 0.2 fusion.35
  297.6 0.1 copy.102
  297.7 0.1 copy.101
  297.8 0.2 convolution_bitcast_fusion.1
  298.0 0.2 convolution_bitcast_fusion.2
  298.2 0.6 pad_maximum_fusion.2
  (15 shorter events, 0.1 us)
Async XLA Ops:
  6.5 80.5 %copy-start = (bf16[12,2,2,128,128]{4,3,2,1,0:T(8,128)(2,1)S(1)}, bf16[12,2,2,128,128]{4,3,2,1,0:T(8,128)(2,1)}, u32[]{:S(2)}) copy-start(bf16[12,2,2,128,128]{4,3,2,1,0:T(8,128)(2,1)} %param.8) | copy-start | bytes 4718596
  6.5 3.1 %copy-start.2 = (s32[12,32]{1,0:T(8,128)S(1)}, s32[12,32]{1,0:T(8,128)}, u32[]{:S(2)}) copy-start(s32[12,32]{1,0:T(8,128)} %param.10) | copy-start | bytes 4612
  6.5 72.2 %all-gather.3.cloned.1.call-start = ((), (), s32[]{:S(2)}) async-start(), calls=%async_computation | async-start | bytes 3145728 | tf_op jit(solution)/shard_map/all_gather | solution.py:28
  9.6 242.6 %all-gather.5.cloned.1.call-start = ((), (), s32[]{:S(2)}) async-start(), calls=%async_computation.1 | async-start | bytes 26738688 | tf_op jit(solution)/shard_map/all_gather | solution.py:65
  96.6 0.7 copy-start.3
  97.9 13.7 %copy-start.6 = (u32[256]{0:T(256)S(1)}, u32[256]{0:T(256)}, u32[]{:S(2)}) copy-start(u32[256]{0:T(256)} %constant.59) | copy-start | bytes 3076
  97.9 14.9 %copy-start.4 = (s32[96]{0:T(128)S(1)}, s32[96]{0:T(128)}, u32[]{:S(2)}) copy-start(s32[96]{0:T(128)} %param.13) | copy-start | bytes 1156
  112.9 184.9 %copy-start.5 = (s32[96]{0:T(128)S(1)}, s32[96]{0:T(128)}, u32[]{:S(2)}) copy-start(s32[96]{0:T(128)} %param.12) | copy-start | bytes 1156
  252.1 46.7 %copy-start.1 = (bf16[12,2,2,128,128]{4,3,2,1,0:T(8,128)(2,1)S(1)}, bf16[12,2,2,128,128]{4,3,2,1,0:T(8,128)(2,1)}, u32[]{:S(2)}) copy-start(bf16[12,2,2,128,128]{4,3,2,1,0:T(8,128)(2,1)} %param.8) | copy-start | bytes 4718596
Sparse Core Ops, SparseCore 0:
  9.7 68.9 all-gather.2
  96.8 155.3 all-gather.4
where the time goes:
time: 306 us
  waiting for transfers between devices  208 us (68%)
  local copies, waits for them, and re-layouts  31.3 us (10%)
  blocking collectives  30.9 us (10%)
  matrix products  18.4 us (6%)
  between operations  14.3 us (5%)
    all_gather x1, waiting for transfers between devices, local(): section = lax.all_gather(tiles, 'col', axis=0, tiled=True)  139 us
    all_gather x1, waiting for transfers between devices, local(): gathered = lax.all_gather(wave_blocks, 'wf', axis=2, tiled=True)  68.9 us
    all_gather x1, blocking collectives, local(): all_slots = lax.all_gather(shares, 'row', axis=2, tiled=True)  16.6 us
    unnamed x1, blocking collectives  14.3 us
    dot_general x1, matrix products, local(): lax.dot_general(section, right_flat, (((2,), (2,)), ((0,), (0,))), prefer...  14.1 us
    reshape x1, local copies, waits for them, and re-layouts, local(): right_operators.reshape(right_operators.shape[0], 2 * local_right, flat_w...  13.6 us
  transfers between devices with their start and end apart: 2, of which 2 were waited for; matrix products, arithmetic and copies ran while one was open for 5% of the time, Pallas kernels for 0%

commit v1 on v0

v1 whole, which is shorter than its diff:
```python
import functools

import jax
import jax.numpy as jnp
from jax import lax
from jax.experimental import pallas as pl
from jax.experimental.pallas import tpu as pltpu
from jax.sharding import PartitionSpec as P

BF = jnp.bfloat16
F32 = jnp.float32
VMEM = 48 * 1024 * 1024


def iota(shape, axis):
    return lax.broadcasted_iota(jnp.int32, shape, axis)


def params():
    return pltpu.CompilerParams(vmem_limit_bytes=VMEM)


def pick_right_kernel(place_ref, right_ref, out_ref):
    to, of = iota((256, 256), 0), iota((256, 256), 1)
    a, c, j = to // 16, (to % 16) // 8, to % 8
    order = (of == (j * 2 + c) * 16 + a).astype(BF)
    for block in range(out_ref.shape[0]):
        rows = right_ref[block].reshape(256, 128)
        turned = jnp.dot(order, rows, preferred_element_type=F32).astype(BF)
        out_ref[block] = turned.reshape(16, 16, 128)


def pick_right(place, right_operators):
    view = right_operators.reshape(16, 2, 8, 2, 4, 16, 128)
    return pl.pallas_call(
        pick_right_kernel,
        grid_spec=pltpu.PrefetchScalarGridSpec(
            num_scalar_prefetch=1,
            grid=(4,),
            in_specs=[
                pl.BlockSpec(
                    (4, None, 8, 2, None, 16, 128),
                    lambda i, place: (i, place[0], 0, 0, place[1], 0, 0),
                )
            ],
            out_specs=pl.BlockSpec((4, 16, 16, 128), lambda i, place: (i, 0, 0, 0)),
        ),
        out_shape=jax.ShapeDtypeStruct((16, 16, 16, 128), BF),
        compiler_params=params(),
        name="pick_right",
    )(place, view)


def tiles_kernel(
    place_ref, own_wave, far_wave, own_left, far_left,
    home, up1, down1, up2, down2, sides, bras, stage,
):
    z = place_ref[2]
    low = z < 4

    def wave(c, o):
        mine, other = own_wave[c, o], far_wave[c, o]
        return jnp.concatenate(
            [jnp.where(low, mine, other), jnp.where(low, other, mine)], axis=0
        )

    for o in range(3):
        re, im = wave(0, o), wave(1, o)
        top = jnp.concatenate([re, im, re, im], axis=1)
        bottom = jnp.concatenate([-im, re, im, -re], axis=1)
        sides[o] = jnp.concatenate([top, bottom], axis=0)
        if o == 0:
            re_t, im_t = re.T, im.T
            bras[0] = jnp.concatenate([re_t, im_t], axis=1)
            bras[1] = jnp.concatenate([-im_t, re_t], axis=1)
    spots = [z, lax.rem(z + 1, 8), lax.rem(z + 7, 8), lax.rem(z + 2, 8), lax.rem(z + 6, 8)]
    bra = jnp.concatenate(
        [bras[c, pl.ds(pl.multiple_of(spot * 16, 16), 16), :] for c in range(2) for spot in spots],
        axis=0,
    )
    to, of = iota((256, 256), 0), iota((256, 256), 1)
    order = ((to // 16 == of % 16) & (to % 16 == of // 16)).astype(BF)
    outs = [home, up1, down1, up2, down2]
    for group in range(6):
        for member in range(4):
            s = group * 4 + member
            source = own_left if s < 12 else far_left
            operator = jnp.concatenate([source[s % 12, 0], source[s % 12, 1]], axis=1)
            side = sides[place_ref[3 + s]]
            turned = jnp.dot(operator, side, preferred_element_type=F32).astype(BF)
            ket = jnp.concatenate(
                [
                    jnp.concatenate([turned[:, 0:128], turned[:, 256:384]], axis=1),
                    jnp.concatenate([turned[:, 128:256], turned[:, 384:512]], axis=1),
                ],
                axis=0,
            )
            stage[member] = jnp.dot(bra, ket, preferred_element_type=F32).astype(BF)
        for spot, out in enumerate(outs):
            if spot == 3 and group >= 3 or spot == 4 and group < 3:
                continue
            rows = jnp.concatenate(
                [
                    stage[member, c * 80 + spot * 16 : c * 80 + spot * 16 + 16, kind * 128 : kind * 128 + 128]
                    for member in range(4)
                    for kind in range(2)
                    for c in range(2)
                ],
                axis=0,
            )
            turned = jnp.dot(order, rows, preferred_element_type=F32).astype(BF)
            out[group - 3 if spot == 4 else group] = turned.reshape(16, 16, 128)


def make_tiles(place, own_wave, far_wave, left_operators, far_left):
    full = lambda shape: pl.BlockSpec(shape, lambda i, place: (0,) * len(shape))
    sizes = [6, 6, 6, 3, 3]
    return pl.pallas_call(
        tiles_kernel,
        grid_spec=pltpu.PrefetchScalarGridSpec(
            num_scalar_prefetch=1,
            grid=(1,),
            in_specs=[
                full((2, 3, 64, 128)),
                full((2, 3, 64, 128)),
                pl.BlockSpec(
                    (12, None, 2, 128, 128), lambda i, place: (0, place[0], 0, 0, 0)
                ),
                full((12, 2, 128, 128)),
            ],
            out_specs=[full((n, 16, 16, 128)) for n in sizes],
            scratch_shapes=[
                pltpu.VMEM((3, 256, 512), BF),
                pltpu.VMEM((2, 128, 256), BF),
                pltpu.VMEM((4, 160, 256), BF),
            ],
        ),
        out_shape=[jax.ShapeDtypeStruct((n, 16, 16, 128), BF) for n in sizes],
        compiler_params=params(),
        name="make_tiles",
    )(place, own_wave, far_wave, left_operators, far_left)


def contract_kernel(
    home, up1, down1, up2, down2, right, slot_label, right_label, slot_key, real_key, imag_key, sign, out
):
    paired = jnp.zeros((256, 384), F32)
    for step in range(8):
        lefts = []
        rights = []
        for a in (2 * step, 2 * step + 1):
            lefts.append(
                jnp.concatenate(
                    [ref[:, a].reshape(-1, 128) for ref in (home, up1, down1, up2, down2)], axis=0
                )
            )
            rights.append(right[:, a].reshape(256, 128))
        paired += lax.dot_general(
            jnp.concatenate(rights, axis=1),
            jnp.concatenate(lefts, axis=1),
            (((1,), (1,)), ((), ())),
            preferred_element_type=F32,
        )
    paired = paired.reshape(16, 2, 8, 384)
    match = right_label[...] == slot_label[...]
    total = jnp.zeros((128, 384), F32)
    for c in range(2):
        part = jnp.where(match, paired[:, c].reshape(128, 384), 0.0)
        if c == 0:
            pick = (slot_key[...] == real_key[...]).astype(F32).astype(BF)
        else:
            pick = jnp.where(slot_key[...] == imag_key[...], sign[...], 0.0).astype(BF)
        for _ in range(3):
            piece = part.astype(BF)
            total += jnp.dot(piece, pick, preferred_element_type=F32)
            part = part - piece.astype(F32)
    out[...] = total.reshape(16, 8, 384)


def contract(tiles, right, labels):
    return pl.pallas_call(
        contract_kernel,
        out_shape=jax.ShapeDtypeStruct((16, 8, 384), F32),
        compiler_params=params(),
        name="contract",
    )(*tiles, right, *labels)


def ring(step):
    pairs = []
    for z in range(8):
        for core in range(2):
            place = lambda z: ((z % 4) * 2 + core) * 2 + z // 4
            pairs.append((place(z), place(step(z))))
    return pairs


def local(
    wave_blocks, left_operators, right_operators, left_table, right_table, assignment, kramers_map
):
    line = ("row", "wf")
    row, col, wf = lax.axis_index("row"), lax.axis_index("col"), lax.axis_index("wf")
    core, z_lo = row % 2, row // 2
    z = wf * 4 + z_lo
    q = 2 * col + core

    own_wave = jnp.concatenate(
        [lax.dynamic_slice_in_dim(wave_blocks, (q + o) % 32, 1, 1) for o in range(3)], axis=1
    )
    far_wave = lax.ppermute(
        own_wave, line, ring(lambda z: (z + 2) % 8 if z in (2, 3, 6, 7) else (z - 2) % 8)
    )
    swap = [(i, i ^ 1) for i in range(8)]
    give = lax.dynamic_index_in_dim(left_operators, 1 - core, 1, keepdims=False)
    far_left = lax.ppermute(give, "row", swap)
    columns = lax.dynamic_slice_in_dim(left_table, 2 * col, 2, 1)
    own_label = lax.dynamic_index_in_dim(columns, core, 1, keepdims=False)
    far_label = lax.ppermute(
        lax.dynamic_index_in_dim(columns, 1 - core, 1, keepdims=False), "row", swap
    )
    shift = jnp.mod(jnp.concatenate([own_label, far_label]) - q, 32)
    place = jnp.stack([core, z_lo, z]).astype(jnp.int32)
    right = pick_right(place, right_operators)
    home, up1, down1, up2, down2 = make_tiles(
        jnp.concatenate([place, shift]), own_wave, far_wave, left_operators, far_left
    )
    right, home = lax.optimization_barrier((right, home))
    tiles = [
        home,
        lax.ppermute(up1, line, ring(lambda z: (z + 1) % 8)),
        lax.ppermute(down1, line, ring(lambda z: (z + 7) % 8)),
        lax.ppermute(up2, line, ring(lambda z: (z + 2) % 8)),
        lax.ppermute(down2, line, ring(lambda z: (z + 6) % 8)),
    ]
    right = lax.all_to_all(right, "col", 0, 0, tiled=True)

    all_table = lax.all_gather(left_table, "row", axis=0, tiled=True)
    q_label = lax.dynamic_index_in_dim(all_table, q, 1, keepdims=False)
    both = jnp.stack([q_label, assignment], axis=0).reshape(2, 4, 2, 12)
    both = jnp.where(core == 0, both, both[:, :, ::-1])
    both = jnp.concatenate([both, both], axis=1)
    both = lax.dynamic_slice_in_dim(both, z_lo, 4, 1)
    both = both[:, jnp.array([0, 3, 1, 2])].reshape(2, 96)
    kind_c = jnp.arange(4, dtype=jnp.int32)
    slot_label = jnp.repeat(both[0], 4)[None, :]
    slot_key = (both[1][:, None] * 4 + kind_c[None, :]).reshape(384, 1)
    right_label = lax.dynamic_index_in_dim(right_table, q, 1, keepdims=True)
    target = jnp.stack([jnp.arange(96, dtype=jnp.int32), kramers_map]).reshape(1, 2, 8, 12)
    target = target.transpose(2, 0, 1, 3)
    kind = jnp.arange(2, dtype=jnp.int32)[None, None, :, None]
    part = jnp.arange(2, dtype=jnp.int32)[None, :, None, None]
    real_key = (target * 4 + kind * 2 + part).reshape(1, 384)
    imag_key = (target * 4 + kind * 2 + 1 - part).reshape(1, 384)
    sign = jnp.broadcast_to((2 * part - 1).astype(F32), (8, 2, 2, 12)).reshape(1, 384)

    shares = contract(
        tiles, right, [slot_label, right_label, slot_key, real_key, imag_key, sign]
    )
    shares = jnp.sum(lax.all_to_all(shares, "col", 0, 0, tiled=True), axis=0)
    shares = shares.reshape(2, 4, 8, 48).transpose(2, 0, 1, 3).reshape(16, 192)
    total = jnp.sum(lax.all_to_all(shares, line, 0, 0, tiled=True), axis=0)
    return total.reshape(4, 2, 2, 12).transpose(1, 2, 3, 0)


def solution(mesh):
    return jax.shard_map(
        local,
        mesh=mesh,
        in_specs=(
            P(None, None, "wf", None),
            P("row", "col", None, None, None),
            P(None, "col", None, "wf", None),
            P("row", None),
            P(),
            P(),
            P(),
        ),
        out_specs=P(None, None, "row", ("col", "wf")),
        check_vma=False,
    )
```

time: 306 us -> 98.1 us (0.32)
  waiting for transfers between devices: 208 us -> 12 us
  local copies, waits for them, and re-layouts: 31.3 us -> 6.81 us
  starting transfers between devices: 0.04 us -> 21.1 us
  matrix products: 18.4 us -> 0 us
  between operations: 14.3 us -> 0.25 us
  Pallas kernels: 0 us -> 13.9 us
  blocking collectives: 30.9 us -> 43 us
    all_gather x2 -> x0, waiting for transfers between devices: 208 us -> none  [the longest x1 139 us: local(): section = lax.all_gather(tiles, 'col', axis=0, tiled=True)]
    all_to_all x0 -> x2, blocking collectives: none -> 29.1 us  [the longest x1 15.9 us: local(): total = jnp.sum(lax.all_to_all(shares, line, 0, 0, tiled=True), axis=0)]
    dot_general x5 -> x0, matrix products: 18.4 us -> none  [the longest x1 14.1 us: local(): lax.dot_general(section, right_flat, (((2,), (2,)), ((0,), (0,))), prefer...]
    ppermute x0 -> x7, starting transfers between devices: none -> 14.4 us  [the longest x1 4.39 us: local(): lax.ppermute(own_wave, line, ring(lambda z: (z + 2) % 8 if z in (2, 3, 6,...]
    unnamed x1 -> x0, blocking collectives: 14.3 us -> none
    pallas_call x0 -> x3, Pallas kernels: none -> 13.9 us  [the longest x1 8.13 us: make_tiles(): pl.pallas_call(tiles_kernel, grid_spec=pltpu.PrefetchScalarGridSpec(num_s...]
    reshape x1 -> x3, local copies, waits for them, and re-layouts: 13.6 us -> 0.28 us  [the longest x1 0.11 us: local(): jnp.broadcast_to((2 * part - 1).astype(F32), (8, 2, 2, 12)).reshape(1, 384)]
    ppermute x0 -> x7, waiting for transfers between devices: none -> 12 us  [the longest x1 9.75 us: local(): lax.ppermute(up2, line, ring(lambda z: (z + 2) % 8))]
  transfers between devices with their start and end apart: 2 -> 8, of which waited for: 2 -> 2; matrix products, arithmetic and copies ran while one was open for 5% -> 6% of each run, Pallas kernels for 0% -> 5%
where the time goes in v1:
time: 98.1 us; the launch traced here: 97.7 us
  blocking collectives  43 us (44%)
  starting transfers between devices  21.1 us (22%)
  Pallas kernels  13.9 us (14%)
  waiting for transfers between devices  12 us (12%)
  local copies, waits for them, and re-layouts  6.81 us (7%)
    all_to_all x1, blocking collectives, local(): total = jnp.sum(lax.all_to_all(shares, line, 0, 0, tiled=True), axis=0)  15.9 us
    all_gather x1, blocking collectives, local(): all_table = lax.all_gather(left_table, 'row', axis=0, tiled=True)  13.9 us
    all_to_all x1, blocking collectives, local(): shares = jnp.sum(lax.all_to_all(shares, 'col', 0, 0, tiled=True), axis=0)  13.2 us
    ppermute x1, waiting for transfers between devices, local(): lax.ppermute(up2, line, ring(lambda z: (z + 2) % 8))  9.75 us
    pallas_call x1, Pallas kernels, make_tiles(): pl.pallas_call(tiles_kernel, grid_spec=pltpu.PrefetchScalarGridSpec(num_s...  8.13 us
    all_to_all x1, starting transfers between devices, local(): right = lax.all_to_all(right, 'col', 0, 0, tiled=True)  6.75 us
    pallas_call x1, Pallas kernels, pick_right(): pl.pallas_call(pick_right_kernel, grid_spec=pltpu.PrefetchScalarGridSpec(...  4.47 us
    ppermute x1, starting transfers between devices, local(): lax.ppermute(own_wave, line, ring(lambda z: (z + 2) % 8 if z in (2, 3, 6,...  4.39 us
  transfers between devices with their start and end apart: 8, of which 2 were waited for; matrix products, arithmetic and copies ran while one was open for 6% of the time, Pallas kernels for 5%

profile of v1, /device:TPU:1, one launch (start us, length us, event | category | flops | bytes accessed | tf_op | source)
XLA Modules:
  0.0 97.7 jit_solution(4735074501440296444)
XLA Ops:
  0.1 0.9 dynamic-slice_reduce_fusion.2
  1.0 3.3 %collective-permute-start = (s32[12]{0:T(128)S(1)}, s32[12]{0:T(128)S(1)}, u32[]{:S(2)}, u32[]{:S(2)}) collective-permute-start(s32[12]{0:T(128)S(1)} %get-tuple-element.20), channel_id=1, source_target_pairs={{0,32},{32,0},{64,96},{96,64},{128,160},{160,128},{192,224},{224,1... | collective-permute-start | bytes 152 | tf_op jit(solution)/shard_map/ppermute | solution.py:218
  4.3 0.8 constant_dynamic-slice_fusion.3
  5.1 4.4 %collective-permute-start.1 = (bf16[2,3,64,128]{3,2,1,0:T(8,128)(2,1)S(1)}, bf16[2,3,64,128]{3,2,1,0:T(8,128)(2,1)S(1)}, u32[]{:S(2)}, u32[]{:S(2)}) collective-permute-start(bf16[2,3,64,128]{3,2,1,0:T(8,128)(2,1)S(1)} %pad_maximum_fusion.own_wave), channel_id=1, source_target_pairs={{0,129},{32,161},{64,193},{96,225},{128,1},{160,33},{192,65},{224,... | collective-permute-start | bytes 294920 | tf_op jit(solution)/shard_map/ppermute | solution.py:210
  9.5 2.1 %dynamic-slice_bitcast_fusion = bf16[12,2,128,128]{3,2,1,0:T(8,128)(2,1)} fusion(bf16[12,2,2,128,128]{4,3,2,1,0:T(8,128)(2,1)} %own_left.1, s32[]{:T(128)S(6)} %select_n.82), kind=kLoop, calls=%fused_computation.1 | loop fusion | bytes 1572868 | tf_op jit(solution)/shard_map/jit(dynamic_index_in_dim)/squeeze | solution.py:214
  11.6 0.3 collective-permute-start.2
  12.0 13.9 %all-gather = s32[8,12,32]{2,1,0:T(8,128)S(1)} all-gather(s32[1,12,32]{2,1,0:T(8,128)S(1)} %bitcast.28), channel_id=1, replica_groups=mesh['row'=8,'col'=16,'wf'=2] {'row'}, dimensions={0}, use_global_device_ids=true | all-gather | bytes 13824 | tf_op jit(solution)/shard_map/all_gather | solution.py:237
  25.9 0.2 dynamic-slice_reduce_fusion
  26.1 0.1 stack.38
  26.2 0.0 copy-done.3
  26.2 0.1 stack.39
  26.4 0.1 pad_add_fusion.place_ref
  26.5 0.1 stack.44
  26.6 4.5 %pick_right.1 = bf16[16,16,16,128]{3,2,1,0:T(8,128)(2,1)} custom-call(s32[3]{0:T(128)S(1)} %pad_add_fusion.place_ref, bf16[16,2,8,2,4,16,128]{6,5,4,3,2,1,0:T(8,128)(2,1)} %bitcast.26), custom_call_target="tpu_custom_call" | custom-call | tf_op jit(solution)/shard_map/pick_right/pallas_call | solution.py:35
  31.1 0.6 gather_fusion
  31.7 0.1 fusion.3
  31.7 0.0 collective-permute-done
  31.7 0.1 and_select_fusion
  31.8 0.1 pad_add_fusion.1.place_ref
  31.9 0.0 collective-permute-done.1.far_wave
  31.9 8.1 %make_tiles.1 = (bf16[6,16,16,128]{3,2,1,0:T(8,128)(2,1)S(1)}, bf16[6,16,16,128]{3,2,1,0:T(8,128)(2,1)}, bf16[6,16,16,128]{3,2,1,0:T(8,128)(2,1)S(1)}, bf16[3,16...) custom-call(s32[27]{0:T(128)S(1)} %pad_add_fusion.1.place_ref, bf16[2,3,64,128]{3,2,1,0:T(8,128)(2,1)S(1)} %pad_maximum_fusion.own_wave, ...), custom_call_target="tpu_custom_call" | custom-call | tf_op jit(solution)/shard_map/make_tiles/pallas_call | solution.py:118
  40.0 6.8 %all-to-all-start = ((bf16[16,16,16,128]{3,2,1,0:T(8,128)(2,1)}), bf16[16,16,16,128]{3,2,1,0:T(8,128)(2,1)S(1)}, u32[]{:S(2)}, u32[]{:S(2)}) async-start(bf16[16,16,16,128]{3,2,1,0:T(8,128)(2,1)} %pick_right.1), calls=%async_computation | async-start | bytes 2097152 | tf_op jit(solution)/shard_map/all_to_all | solution.py:235
  46.8 0.1 fusion.2
  46.9 0.1 squeeze.19
  47.0 0.1 broadcast_in_dim.7
  47.0 0.1 broadcast_in_dim_reshape.3.slot_label
  47.2 0.1 mul.49
  47.3 0.1 iota_add_fusion
  47.4 0.1 collective-permute-start.3
  47.4 2.7 %collective-permute-start.4 = (bf16[6,16,16,128]{3,2,1,0:T(8,128)(2,1)S(1)}, bf16[6,16,16,128]{3,2,1,0:T(8,128)(2,1)S(1)}, u32[]{:S(2)}, u32[]{:S(2)}) collective-permute-start(bf16[6,16,16,128]{3,2,1,0:T(8,128)(2,1)S(1)} %get-tuple-element.15), channel_id=1, source_target_pairs={{0,193},{32,225},{64,0},{96,32},{128,64},{160,96},{192,128},{224,1... | collective-permute-start | bytes 1179656 | tf_op jit(solution)/shard_map/ppermute | solution.py:231
  50.1 0.0 collective-permute-start.5
  50.1 3.6 %collective-permute-start.6 = (bf16[3,16,16,128]{3,2,1,0:T(8,128)(2,1)}, bf16[3,16,16,128]{3,2,1,0:T(8,128)(2,1)S(1)}, u32[]{:S(2)}, u32[]{:S(2)}) collective-permute-start(bf16[3,16,16,128]{3,2,1,0:T(8,128)(2,1)} %get-tuple-element.17), channel_id=1, source_target_pairs={{0,129},{32,161},{64,193},{96,225},{128,0},{160,32},{192,64},{224,... | collective-permute-start | bytes 589832 | tf_op jit(solution)/shard_map/ppermute | solution.py:233
  53.7 0.1 copy.31.right_label
  53.8 0.1 add.191.slot_key
  53.9 0.1 add.186.real_key
  54.0 0.1 sub.47.imag_key
  54.2 0.1 broadcast_in_dim.16
  54.2 0.1 reshape.138.sign
  54.4 9.8 %collective-permute-done.5.up2 = bf16[3,16,16,128]{3,2,1,0:T(8,128)(2,1)S(1)} collective-permute-done((bf16[3,16,16,128]{3,2,1,0:T(8,128)(2,1)}, bf16[3,16,16,128]{3,2,1,0:T(8,128)(2,1)S(1)}, u32[]{:S(2)}, u32[]{:S(2)}) %collective-permute-start.5) | collective-permute-done | bytes 196640 | tf_op jit(solution)/shard_map/ppermute | solution.py:232
  64.1 2.3 %collective-permute-done.6.down2 = bf16[3,16,16,128]{3,2,1,0:T(8,128)(2,1)S(1)} collective-permute-done((bf16[3,16,16,128]{3,2,1,0:T(8,128)(2,1)}, bf16[3,16,16,128]{3,2,1,0:T(8,128)(2,1)S(1)}, u32[]{:S(2)}, u32[]{:S(2)}) %collective-permute-start.6) | collective-permute-done | bytes 196640 | tf_op jit(solution)/shard_map/ppermute | solution.py:233
  66.4 0.0 all-to-all-done.right
  66.4 1.3 %contract.1 = f32[16,8,384]{2,1,0:T(8,128)S(1)} custom-call(bf16[6,16,16,128]{3,2,1,0:T(8,128)(2,1)S(1)} %get-tuple-element.13.home, bf16[6,16,16,128]{3,2,1,0:T(8,128)(2,1)S(1)} %collective-permute-done.3.up1, bf16[6,16,16,128]{3,2,1,0:T(8,128)(2,1)S(1)} %collective-permute-done.4.down1, bf16[3,16,16,128]{3,2,1,0:T(8,128)(2,1)S(1)} %collective-permute-done.5.up2, ...), custom_call_target="tpu_custom_call" | custom-call | tf_op jit(solution)/shard_map/contract/pallas_call | solution.py:181
  67.6 13.2 %all_to_all.20 = f32[16,8,384]{2,1,0:T(8,128)S(1)} all-to-all(f32[16,8,384]{2,1,0:T(8,128)S(1)} %contract.1), channel_id=1, replica_groups=mesh['row'=8,'col'=16,'wf'=2] {'col'}, dimensions={0} | all-to-all | bytes 393216 | tf_op jit(solution)/shard_map/all_to_all | solution.py:259
  80.9 0.1 reshape.139
  81.0 0.1 all_to_all.16
  81.1 15.9 %all_to_all.21 = f32[16,1,192]{2,1,0:T(1,128)S(1)} all-to-all(f32[16,1,192]{2,1,0:T(1,128)S(1)} %all_to_all.16), channel_id=1, replica_groups=mesh['row'=8,'col'=16,'wf'=2] {'row','wf'}, dimensions={0} | all-to-all | bytes 24576 | tf_op jit(solution)/shard_map/all_to_all | solution.py:261
  97.0 0.1 reshape.140
  97.1 0.6 copy.30
  (34 shorter events, 0.3 us)
Async XLA Ops:
  0.0 53.7 %copy-start = (s32[128,32]{0,1:T(8,128)S(1)}, s32[128,32]{0,1:T(8,128)}, u32[]{:S(2)}) copy-start(s32[128,32]{0,1:T(8,128)} %param.12) | copy-start | bytes 49156
  0.0 26.4 %copy-start.5 = (s32[4]{0:T(128)S(1)}, s32[4]{0:T(128)}, u32[]{:S(2)}) copy-start(s32[4]{0:T(128)} %constant.132) | copy-start | bytes 52
  0.0 12.0 %copy-start.2 = (s32[12,32]{1,0:T(8,128)S(1)}, s32[12,32]{1,0:T(8,128)}, u32[]{:S(2)}) copy-start(s32[12,32]{1,0:T(8,128)} %param.11) | copy-start | bytes 4612
  0.0 26.2 %copy-start.3 = (s32[96]{0:T(128)S(1)}, s32[96]{0:T(128)}, u32[]{:S(2)}) copy-start(s32[96]{0:T(128)} %param.13) | copy-start | bytes 1156
  0.0 26.5 %copy-start.4 = (s32[96]{0:T(128)S(1)}, s32[96]{0:T(128)}, u32[]{:S(2)}) copy-start(s32[96]{0:T(128)} %param.14) | copy-start | bytes 1156
  1.0 30.7 %collective-permute-start = (s32[12]{0:T(128)S(1)}, s32[12]{0:T(128)S(1)}, u32[]{:S(2)}, u32[]{:S(2)}) collective-permute-start(s32[12]{0:T(128)S(1)} %get-tuple-element.20), channel_id=1, source_target_pairs={{0,32},{32,0},{64,96},{96,64},{128,160},{160,128},{192,224},{224,1... | collective-permute-start | bytes 152 | tf_op jit(solution)/shard_map/ppermute | solution.py:218
  5.1 26.8 %collective-permute-start.1 = (bf16[2,3,64,128]{3,2,1,0:T(8,128)(2,1)S(1)}, bf16[2,3,64,128]{3,2,1,0:T(8,128)(2,1)S(1)}, u32[]{:S(2)}, u32[]{:S(2)}) collective-permute-start(bf16[2,3,64,128]{3,2,1,0:T(8,128)(2,1)S(1)} %pad_maximum_fusion.own_wave), channel_id=1, source_target_pairs={{0,129},{32,161},{64,193},{96,225},{128,1},{160,33},{192,65},{224,... | collective-permute-start | bytes 294920 | tf_op jit(solution)/shard_map/ppermute | solution.py:210
  11.6 20.3 %collective-permute-start.2 = (bf16[12,2,128,128]{3,2,1,0:T(8,128)(2,1)}, bf16[12,2,128,128]{3,2,1,0:T(8,128)(2,1)S(1)}, u32[]{:S(2)}, u32[]{:S(2)}) collective-permute-start(bf16[12,2,128,128]{3,2,1,0:T(8,128)(2,1)} %dynamic-slice_bitcast_fusion), channel_id=1, source_target_pairs={{0,32},{32,0},{64,96},{96,64},{128,160},{160,128},{192,224},{224,1... | collective-permute-start | bytes 2359304 | tf_op jit(solution)/shard_map/ppermute | solution.py:215
  26.6 5.3 %copy-start.1 = (bf16[12,2,2,128,128]{4,3,2,1,0:T(8,128)(2,1)S(1)}, bf16[12,2,2,128,128]{4,3,2,1,0:T(8,128)(2,1)}, u32[]{:S(2)}) copy-start(bf16[12,2,2,128,128]{4,3,2,1,0:T(8,128)(2,1)} %own_left.1) | copy-start | bytes 4718596
  40.0 26.3 %all-to-all-start = ((bf16[16,16,16,128]{3,2,1,0:T(8,128)(2,1)}), bf16[16,16,16,128]{3,2,1,0:T(8,128)(2,1)S(1)}, u32[]{:S(2)}, u32[]{:S(2)}) async-start(bf16[16,16,16,128]{3,2,1,0:T(8,128)(2,1)} %pick_right.1), calls=%async_computation | async-start | bytes 2097152 | tf_op jit(solution)/shard_map/all_to_all | solution.py:235
  47.4 19.0 %collective-permute-start.3 = (bf16[6,16,16,128]{3,2,1,0:T(8,128)(2,1)}, bf16[6,16,16,128]{3,2,1,0:T(8,128)(2,1)S(1)}, u32[]{:S(2)}, u32[]{:S(2)}) collective-permute-start(bf16[6,16,16,128]{3,2,1,0:T(8,128)(2,1)} %get-tuple-element.14), channel_id=1, source_target_pairs={{0,64},{32,96},{64,128},{96,160},{128,192},{160,224},{192,1},{224,... | collective-permute-start | bytes 1179656 | tf_op jit(solution)/shard_map/ppermute | solution.py:230
  47.4 18.9 %collective-permute-start.4 = (bf16[6,16,16,128]{3,2,1,0:T(8,128)(2,1)S(1)}, bf16[6,16,16,128]{3,2,1,0:T(8,128)(2,1)S(1)}, u32[]{:S(2)}, u32[]{:S(2)}) collective-permute-start(bf16[6,16,16,128]{3,2,1,0:T(8,128)(2,1)S(1)} %get-tuple-element.15), channel_id=1, source_target_pairs={{0,193},{32,225},{64,0},{96,32},{128,64},{160,96},{192,128},{224,1... | collective-permute-start | bytes 1179656 | tf_op jit(solution)/shard_map/ppermute | solution.py:231
  50.1 14.0 %collective-permute-start.5 = (bf16[3,16,16,128]{3,2,1,0:T(8,128)(2,1)}, bf16[3,16,16,128]{3,2,1,0:T(8,128)(2,1)S(1)}, u32[]{:S(2)}, u32[]{:S(2)}) collective-permute-start(bf16[3,16,16,128]{3,2,1,0:T(8,128)(2,1)} %get-tuple-element.16), channel_id=1, source_target_pairs={{0,128},{32,160},{64,192},{96,224},{128,1},{160,33},{192,65},{224,... | collective-permute-start | bytes 589832 | tf_op jit(solution)/shard_map/ppermute | solution.py:232
  50.1 16.2 %collective-permute-start.6 = (bf16[3,16,16,128]{3,2,1,0:T(8,128)(2,1)}, bf16[3,16,16,128]{3,2,1,0:T(8,128)(2,1)S(1)}, u32[]{:S(2)}, u32[]{:S(2)}) collective-permute-start(bf16[3,16,16,128]{3,2,1,0:T(8,128)(2,1)} %get-tuple-element.17), channel_id=1, source_target_pairs={{0,129},{32,161},{64,193},{96,225},{128,0},{160,32},{192,64},{224,... | collective-permute-start | bytes 589832 | tf_op jit(solution)/shard_map/ppermute | solution.py:233

commit v2 on v1

v2 whole, which is shorter than its diff:
```python
import functools

import jax
import jax.numpy as jnp
from jax import lax
from jax.experimental import pallas as pl
from jax.experimental.pallas import tpu as pltpu
from jax.sharding import PartitionSpec as P

BF = jnp.bfloat16
F32 = jnp.float32
VMEM = 48 * 1024 * 1024


def iota(shape, axis):
    return lax.broadcasted_iota(jnp.int32, shape, axis)


def params():
    return pltpu.CompilerParams(vmem_limit_bytes=VMEM)


def pick_right_kernel(place_ref, right_ref, out_ref):
    for block in range(out_ref.shape[0]):
        rows = jnp.concatenate(
            [right_ref[block, j, c][None] for c in range(2) for j in range(8)], axis=0
        )
        out_ref[block] = jnp.swapaxes(rows, 0, 1)


def pick_right(place, right_operators):
    view = right_operators.reshape(16, 2, 8, 2, 4, 16, 128)
    return pl.pallas_call(
        pick_right_kernel,
        grid_spec=pltpu.PrefetchScalarGridSpec(
            num_scalar_prefetch=1,
            grid=(4,),
            in_specs=[
                pl.BlockSpec(
                    (4, None, 8, 2, None, 16, 128),
                    lambda i, place: (i, place[0], 0, 0, place[1], 0, 0),
                )
            ],
            out_specs=pl.BlockSpec((4, 16, 16, 128), lambda i, place: (i, 0, 0, 0)),
        ),
        out_shape=jax.ShapeDtypeStruct((16, 16, 16, 128), BF),
        compiler_params=params(),
        name="pick_right",
    )(place, view)


GROUPS = (6, 6, 6, 3, 3)
STARTS = (0, 96, 192, 288, 336)


def tiles_kernel(
    place_ref, own_table, far_table, own_wave, far_wave, own_left, far_left,
    home, up1, down1, up2, down2, sides, bras, kets,
):
    z, q = place_ref[2], place_ref[3]
    outs = (home, up1, down1, up2, down2)
    low = z < 4

    def wave(c, o):
        mine, other = own_wave[c, o], far_wave[c, o]
        return jnp.concatenate(
            [jnp.where(low, mine, other), jnp.where(low, other, mine)], axis=0
        )

    for o in range(3):
        re, im = wave(0, o), wave(1, o)
        top = jnp.concatenate([re, im, re, im], axis=1)
        bottom = jnp.concatenate([-im, re, im, -re], axis=1)
        sides[o] = jnp.concatenate([top, bottom], axis=0)
        if o == 0:
            re_t, im_t = re.T, im.T
            bras[0] = jnp.concatenate([re_t, im_t], axis=1)
            bras[1] = jnp.concatenate([-im_t, re_t], axis=1)
    spots = [z, lax.rem(z + 1, 8), lax.rem(z + 7, 8), lax.rem(z + 2, 8), lax.rem(z + 6, 8)]

    def bra(picked):
        return jnp.concatenate(
            [
                bras[c, pl.ds(pl.multiple_of(spots[i] * 16, 16), 16), :]
                for c in range(2)
                for i in picked
            ],
            axis=0,
        )

    labels = [own_table[s, q] for s in range(12)] + [far_table[s, q] for s in range(12)]
    shifts = [lax.rem(label - q + 32, 32) for label in labels]
    for half in range(2):
        picked = (0, 1, 2, 3 + half)
        left = bra(picked)
        source = far_left if half else own_left
        for s in range(12):
            operator = jnp.concatenate([source[s, 0], source[s, 1]], axis=1)
            turned = jnp.dot(
                operator, sides[shifts[half * 12 + s]], preferred_element_type=F32
            ).astype(BF)
            kets[s] = jnp.concatenate(
                [
                    jnp.concatenate([turned[:, 0:128], turned[:, 256:384]], axis=1),
                    jnp.concatenate([turned[:, 128:256], turned[:, 384:512]], axis=1),
                ],
                axis=0,
            )
        for group in range(3):
            brackets = [
                jnp.dot(left, kets[group * 4 + s], preferred_element_type=F32).astype(BF)
                for s in range(4)
            ]
            for i, spot in enumerate(picked):
                rows = jnp.concatenate(
                    [
                        brackets[s][
                            c * 64 + i * 16 : c * 64 + i * 16 + 16,
                            kind * 128 : kind * 128 + 128,
                        ][None]
                        for s in range(4)
                        for kind in range(2)
                        for c in range(2)
                    ],
                    axis=0,
                )
                first = (group if spot > 2 else half * 3 + group) * 16
                outs[spot][first : first + 16] = jnp.swapaxes(rows, 0, 1)
    for spot, out in enumerate(outs):
        count = GROUPS[spot] * 4
        offset = 12 if spot == 4 else 0
        for tile in range(3):
            place = (iota((16, 128), 1) + tile * 128 - STARTS[spot]) // 4
            row = jnp.zeros((16, 128), F32)
            low_s, high_s = (tile * 128 - STARTS[spot]) // 4, (tile * 128 + 128 - STARTS[spot]) // 4
            for s in range(max(0, low_s), min(count, high_s)):
                row = jnp.where(place == s, labels[offset + s].astype(F32), row)
            out[GROUPS[spot] * 16 + tile] = row.astype(BF)


def make_tiles(place, own_table, far_table, own_wave, far_wave, left_operators, far_left):
    full = lambda shape: pl.BlockSpec(shape, lambda i, place: (0,) * len(shape))
    table = pl.BlockSpec(memory_space=pltpu.SMEM)
    operators = pl.BlockSpec(
        (12, None, 2, 128, 128), lambda i, place: (0, place[0], 0, 0, 0)
    )
    return pl.pallas_call(
        tiles_kernel,
        grid_spec=pltpu.PrefetchScalarGridSpec(
            num_scalar_prefetch=1,
            grid=(1,),
            in_specs=[
                table, table, full((2, 3, 64, 128)), full((2, 3, 64, 128)), operators, operators
            ],
            out_specs=[full((n * 16 + 3, 16, 128)) for n in GROUPS],
            scratch_shapes=[
                pltpu.VMEM((3, 256, 512), BF),
                pltpu.VMEM((2, 128, 256), BF),
                pltpu.VMEM((12, 256, 256), BF),
            ],
        ),
        out_shape=[jax.ShapeDtypeStruct((n * 16 + 3, 16, 128), BF) for n in GROUPS],
        compiler_params=params(),
        name="make_tiles",
    )(place, own_table, far_table, own_wave, far_wave, left_operators, far_left)


def contract_kernel(
    place_ref, home, up1, down1, up2, down2, right, right_table, slot_key, real_key, imag_key, sign, out
):
    arrays = (home, up1, down1, up2, down2)
    paired = jnp.zeros((256, 384), F32)
    for step in range(8):
        lefts = []
        rights = []
        for a in (2 * step, 2 * step + 1):
            lefts.append(
                jnp.concatenate(
                    [ref[g * 16 + a] for ref, n in zip(arrays, GROUPS) for g in range(n)], axis=0
                )
            )
            rights.append(right[:, a].reshape(256, 128))
        paired += lax.dot_general(
            jnp.concatenate(rights, axis=1),
            jnp.concatenate(lefts, axis=1),
            (((1,), (1,)), ((), ())),
            preferred_element_type=F32,
        )
    paired = paired.reshape(16, 2, 8, 384)
    slot_label = jnp.concatenate(
        [
            sum(ref[n * 16 + tile].astype(F32)[0:1] for ref, n in zip(arrays, GROUPS))
            for tile in range(3)
        ],
        axis=1,
    )
    here = iota((128, 32), 1) == place_ref[3]
    right_label = jnp.sum(
        jnp.where(here, right_table[...].astype(F32), 0.0), axis=1, keepdims=True
    )
    match = right_label == slot_label
    total = jnp.zeros((128, 384), F32)
    for c in range(2):
        part = jnp.where(match, paired[:, c].reshape(128, 384), 0.0)
        if c == 0:
            pick = (slot_key[...] == real_key[...]).astype(F32).astype(BF)
        else:
            pick = jnp.where(slot_key[...] == imag_key[...], sign[...], 0.0).astype(BF)
        for _ in range(3):
            piece = part.astype(BF)
            total += jnp.dot(piece, pick, preferred_element_type=F32)
            part = part - piece.astype(F32)
    out[...] = total.reshape(16, 8, 384)


def contract(place, tiles, right, right_table, keys):
    whole = pl.BlockSpec(memory_space=pltpu.VMEM)
    return pl.pallas_call(
        contract_kernel,
        in_specs=[pl.BlockSpec(memory_space=pltpu.SMEM)] + [whole] * 11,
        out_shape=jax.ShapeDtypeStruct((16, 8, 384), F32),
        compiler_params=params(),
        name="contract",
    )(place, *tiles, right, right_table, *keys)


def ring(step):
    pairs = []
    for z in range(8):
        for core in range(2):
            place = lambda z: ((z % 4) * 2 + core) * 2 + z // 4
            pairs.append((place(z), place(step(z))))
    return pairs


def local(
    wave_blocks, left_operators, right_operators, left_table, right_table, assignment, kramers_map
):
    line = ("row", "wf")
    row, col, wf = lax.axis_index("row"), lax.axis_index("col"), lax.axis_index("wf")
    core, z_lo = row % 2, row // 2
    z = wf * 4 + z_lo
    q = 2 * col + core

    own_wave = jnp.concatenate(
        [lax.dynamic_slice_in_dim(wave_blocks, (q + o) % 32, 1, 1) for o in range(3)], axis=1
    )
    far_wave = lax.ppermute(
        own_wave, line, ring(lambda z: (z + 2) % 8 if z in (2, 3, 6, 7) else (z - 2) % 8)
    )
    swap = [(i, i ^ 1) for i in range(8)]
    far_left = lax.ppermute(left_operators, "row", swap)
    far_table = lax.ppermute(left_table, "row", swap)
    place = jnp.stack([core, z_lo, z, q]).astype(jnp.int32)
    right = pick_right(place, right_operators)
    right = lax.all_to_all(right, "col", 0, 0, tiled=True)
    home, up1, down1, up2, down2 = make_tiles(
        place, left_table, far_table, own_wave, far_wave, left_operators, far_left
    )
    tiles = [
        home,
        lax.ppermute(up1, line, ring(lambda z: (z + 1) % 8)),
        lax.ppermute(down1, line, ring(lambda z: (z + 7) % 8)),
        lax.ppermute(up2, line, ring(lambda z: (z + 2) % 8)),
        lax.ppermute(down2, line, ring(lambda z: (z + 6) % 8)),
    ]

    held = assignment.reshape(4, 2, 12)
    held = jnp.where(core == 0, held, held[:, ::-1])
    held = lax.dynamic_slice_in_dim(jnp.concatenate([held, held], axis=0), z_lo, 4, 0)
    held = jnp.concatenate([held[0:1], held[3:4], held[1:3]], axis=0).reshape(96, 1)
    slot_key = (held * 4 + jnp.arange(4, dtype=jnp.int32)[None, :]).reshape(384, 1)
    target = jnp.stack([jnp.arange(96, dtype=jnp.int32), kramers_map]).reshape(1, 2, 8, 12)
    target = target.transpose(2, 0, 1, 3)
    kind = jnp.arange(2, dtype=jnp.int32)[None, None, :, None]
    part = jnp.arange(2, dtype=jnp.int32)[None, :, None, None]
    real_key = (target * 4 + kind * 2 + part).reshape(1, 384)
    imag_key = (target * 4 + kind * 2 + 1 - part).reshape(1, 384)
    sign = jnp.broadcast_to((2 * part - 1).astype(F32), (8, 2, 2, 12)).reshape(1, 384)

    shares = contract(place, tiles, right, right_table, [slot_key, real_key, imag_key, sign])
    shares = jnp.sum(lax.all_to_all(shares, "col", 0, 0, tiled=True), axis=0)
    shares = shares.reshape(2, 4, 8, 4, 12).transpose(2, 0, 3, 1, 4).reshape(16, 192)
    total = jnp.sum(lax.all_to_all(shares, line, 0, 0, tiled=True), axis=0)
    return total.reshape(2, 2, 4, 12).transpose(0, 1, 3, 2)


def solution(mesh):
    return jax.shard_map(
        local,
        mesh=mesh,
        in_specs=(
            P(None, None, "wf", None),
            P("row", "col", None, None, None),
            P(None, "col", None, "wf", None),
            P("row", None),
            P(),
            P(),
            P(),
        ),
        out_specs=P(None, None, "row", ("col", "wf")),
        check_vma=False,
    )
```

time: 98.1 us -> 77.3 us (0.79)
  blocking collectives: 43 us -> 28.9 us
  local copies, waits for them, and re-layouts: 6.81 us -> 2.85 us
  Pallas kernels: 13.9 us -> 10.3 us
  waiting for transfers between devices: 12 us -> 13.1 us
    all_gather x1 -> x0, blocking collectives: 13.9 us -> none  [local(): all_table = lax.all_gather(left_table, 'row', axis=0, tiled=True)]
    pallas_call x1, Pallas kernels: 8.13 us -> 4.43 us  [make_tiles(): pl.pallas_call(tiles_kernel, grid_spec=pltpu.PrefetchScalarGridSpec(num_s...]
    ppermute x1, waiting for transfers between devices: 9.75 us -> 6.36 us  [local(): lax.ppermute(up2, line, ring(lambda z: (z + 2) % 8))]
    all_to_all x1, waiting for transfers between devices: 0.01 us -> 3.13 us  [local(): right = lax.all_to_all(right, 'col', 0, 0, tiled=True)]
    ppermute x2, starting transfers between devices: 3.67 us -> 0.96 us  [the longest x1 0.96 us: local(): far_left = lax.ppermute(left_operators, 'row', swap)]
    ppermute x1, starting transfers between devices: 4.39 us -> 6.94 us  [local(): lax.ppermute(own_wave, line, ring(lambda z: (z + 2) % 8 if z in (2, 3, 6,...]
    squeeze x2 -> x0, local copies, waits for them, and re-layouts: 2.21 us -> none  [the longest x1 2.13 us: local(): give = lax.dynamic_index_in_dim(left_operators, 1 - core, 1, keepdims=False)]
    ppermute x1, waiting for transfers between devices: 2.26 us -> 3.61 us  [local(): lax.ppermute(down2, line, ring(lambda z: (z + 6) % 8))]
  transfers between devices with their start and end apart: 8 -> 8, of which waited for: 2 -> 3; matrix products, arithmetic and copies ran while one was open for 6% -> 2% of each run, Pallas kernels for 5% -> 11%
where the time goes in v2:
time: 77.3 us; the launch traced here: 76.9 us
  blocking collectives  28.9 us (37%)
  starting transfers between devices  21.1 us (27%)
  waiting for transfers between devices  13.1 us (17%)
  Pallas kernels  10.3 us (13%)
  local copies, waits for them, and re-layouts  2.85 us (4%)
    all_to_all x1, blocking collectives, local(): total = jnp.sum(lax.all_to_all(shares, line, 0, 0, tiled=True), axis=0)  16.4 us
    all_to_all x1, blocking collectives, local(): shares = jnp.sum(lax.all_to_all(shares, 'col', 0, 0, tiled=True), axis=0)  12.4 us
    ppermute x1, starting transfers between devices, local(): lax.ppermute(own_wave, line, ring(lambda z: (z + 2) % 8 if z in (2, 3, 6,...  6.94 us
    all_to_all x1, starting transfers between devices, local(): right = lax.all_to_all(right, 'col', 0, 0, tiled=True)  6.9 us
    ppermute x1, waiting for transfers between devices, local(): lax.ppermute(up2, line, ring(lambda z: (z + 2) % 8))  6.36 us
    pallas_call x1, Pallas kernels, make_tiles(): pl.pallas_call(tiles_kernel, grid_spec=pltpu.PrefetchScalarGridSpec(num_s...  4.43 us
    pallas_call x1, Pallas kernels, pick_right(): pl.pallas_call(pick_right_kernel, grid_spec=pltpu.PrefetchScalarGridSpec(...  4.05 us
    ppermute x1, waiting for transfers between devices, local(): lax.ppermute(down2, line, ring(lambda z: (z + 6) % 8))  3.61 us
  transfers between devices with their start and end apart: 8, of which 3 were waited for; matrix products, arithmetic and copies ran while one was open for 2% of the time, Pallas kernels for 11%

profile of v2, /device:TPU:1, one launch (start us, length us, event | category | flops | bytes accessed | tf_op | source)
XLA Modules:
  0.0 76.9 jit_solution(3771252664991125596)
XLA Ops:
  0.0 0.8 %constant_dynamic-slice_fusion.2 = (bf16[2,1,64,128]{3,2,1,0:T(8,128)(2,1)S(1)}, bf16[2,1,64,128]{3,2,1,0:T(8,128)(2,1)S(1)}, bf16[2,1,64,128]{3,2,1,0:T(8,128)(2,1)S(1)}) fusion(bf16[2,32,64,128]{3,2,1,0:T(8,128)(2,1)} %param.7, s32[]{:T(128)S(6)} %select_n.46, s32[]{:T(128)S(6)} %select_n.50, s32[]{:T(128)S(6)} %select_n.48), kind=kLoop, calls=%fused_computation.17 | loop fusion | bytes 196620 | tf_op jit(solution)/shard_map/dynamic_slice | solution.py:246
  0.8 6.9 %collective-permute-start.1 = (bf16[2,3,64,128]{3,2,1,0:T(8,128)(2,1)S(1)}, bf16[2,3,64,128]{3,2,1,0:T(8,128)(2,1)S(1)}, u32[]{:S(2)}, u32[]{:S(2)}) collective-permute-start(bf16[2,3,64,128]{3,2,1,0:T(8,128)(2,1)S(1)} %pad_maximum_fusion.own_wave), channel_id=1, source_target_pairs={{0,129},{32,161},{64,193},{96,225},{128,1},{160,33},{192,65},{224,... | collective-permute-start | bytes 294920 | tf_op jit(solution)/shard_map/ppermute | solution.py:248
  7.8 1.0 %collective-permute-start.2 = (bf16[12,2,2,128,128]{4,3,2,1,0:T(8,128)(2,1)}, bf16[12,2,2,128,128]{4,3,2,1,0:T(8,128)(2,1)}, u32[]{:S(2)}, u32[]{:S(2)}) collective-permute-start(bf16[12,2,2,128,128]{4,3,2,1,0:T(8,128)(2,1)} %own_left.1), channel_id=1, source_target_pairs={{0,32},{32,0},{64,96},{96,64},{128,160},{160,128},{192,224},{224,1... | collective-permute-start | bytes 4718600 | tf_op jit(solution)/shard_map/ppermute | solution.py:252
  8.7 0.0 collective-permute-start
  8.7 0.1 pad_add_fusion.place_ref
  8.8 4.1 %pick_right.1 = bf16[16,16,16,128]{3,2,1,0:T(8,128)(2,1)} custom-call(s32[4]{0:T(128)S(1)} %pad_add_fusion.place_ref, bf16[16,2,8,2,4,16,128]{6,5,4,3,2,1,0:T(8,128)(2,1)} %bitcast.19), custom_call_target="tpu_custom_call" | custom-call | tf_op jit(solution)/shard_map/pick_right/pallas_call | solution.py:33
  12.8 0.0 copy-start.3
  12.8 0.0 copy-start.4
  12.8 0.0 copy-start
  12.9 6.9 %all-to-all-start = ((bf16[16,16,16,128]{3,2,1,0:T(8,128)(2,1)}), bf16[16,16,16,128]{3,2,1,0:T(8,128)(2,1)S(1)}, u32[]{:S(2)}, u32[]{:S(2)}) async-start(bf16[16,16,16,128]{3,2,1,0:T(8,128)(2,1)} %pick_right.1), calls=%async_computation | async-start | bytes 2097152 | tf_op jit(solution)/shard_map/all_to_all | solution.py:256
  19.8 0.0 copy-done.3
  19.8 0.1 reshape.131
  20.0 0.1 mul.48
  20.1 0.0 copy-done.4
  20.1 0.1 stack.36
  20.2 0.1 fusion.2
  20.2 0.1 iota_add_fusion
  20.3 0.0 copy-start.2
  20.4 0.0 collective-permute-done.far_table
  20.4 0.0 collective-permute-done.1.far_wave
  20.4 0.0 collective-permute-done.2.far_left
  20.4 0.0 copy-done
  20.4 0.0 copy-done.1
  20.4 4.4 %make_tiles.1 = (bf16[99,16,128]{2,1,0:T(8,128)(2,1)S(1)}, bf16[99,16,128]{2,1,0:T(8,128)(2,1)}, bf16[99,16,128]{2,1,0:T(8,128)(2,1)}, bf16[51,16,128]{2,1,0:T(8,128)(2,1)}, bf16[51,16,128]{2,1,0:T(8,128)(2,1)S(1)}) custom-call(s32[4]{0:T(128)S(1)} %pad_add_fusion.place_ref, s32[12,32]{1,0:T(8,128)S(1)} %copy-done.1, ...), custom_call_target="tpu_custom_call" | custom-call | tf_op jit(solution)/shard_map/make_tiles/pallas_call | solution.py:147
  24.8 0.8 collective-permute-start.3
  25.6 1.9 %collective-permute-start.4 = (bf16[99,16,128]{2,1,0:T(8,128)(2,1)}, bf16[99,16,128]{2,1,0:T(8,128)(2,1)S(1)}, u32[]{:S(2)}, u32[]{:S(2)}) collective-permute-start(bf16[99,16,128]{2,1,0:T(8,128)(2,1)} %get-tuple-element.12), channel_id=1, source_target_pairs={{0,193},{32,225},{64,0},{96,32},{128,64},{160,96},{192,128},{224,1... | collective-permute-start | bytes 1216520 | tf_op jit(solution)/shard_map/ppermute | solution.py:263
  27.5 0.1 fusion.1
  27.6 0.1 collective-permute-start.5
  27.7 3.6 %collective-permute-start.6 = (bf16[51,16,128]{2,1,0:T(8,128)(2,1)S(1)}, bf16[51,16,128]{2,1,0:T(8,128)(2,1)S(1)}, u32[]{:S(2)}, u32[]{:S(2)}) collective-permute-start(bf16[51,16,128]{2,1,0:T(8,128)(2,1)S(1)} %get-tuple-element.14), channel_id=1, source_target_pairs={{0,129},{32,161},{64,193},{96,225},{128,0},{160,32},{192,64},{224,... | collective-permute-start | bytes 626696 | tf_op jit(solution)/shard_map/ppermute | solution.py:265
  31.2 0.1 add.152.slot_key
  31.3 0.1 add.148.real_key
  31.5 0.1 sub.34.imag_key
  31.6 0.0 copy-done.2
  31.6 0.1 copy.22.right_table
  31.7 0.1 broadcast_in_dim.2
  31.8 0.1 reshape.132.sign
  31.9 3.1 %all-to-all-done.right = bf16[16,16,16,128]{3,2,1,0:T(8,128)(2,1)S(1)} async-done(((bf16[16,16,16,128]{3,2,1,0:T(8,128)(2,1)}), bf16[16,16,16,128]{3,2,1,0:T(8,128)(2,1)S(1)}, u32[]{:S(2)}, u32[]{:S(2)}) %all-to-all-start) | async-done | bytes 1048608 | tf_op jit(solution)/shard_map/all_to_all | solution.py:256
  35.0 6.4 %collective-permute-done.5.up2 = bf16[51,16,128]{2,1,0:T(8,128)(2,1)S(1)} collective-permute-done((bf16[51,16,128]{2,1,0:T(8,128)(2,1)}, bf16[51,16,128]{2,1,0:T(8,128)(2,1)S(1)}, u32[]{:S(2)}, u32[]{:S(2)}) %collective-permute-start.5) | collective-permute-done | bytes 208928 | tf_op jit(solution)/shard_map/ppermute | solution.py:264
  41.4 3.6 %collective-permute-done.6.down2 = bf16[51,16,128]{2,1,0:T(8,128)(2,1)S(1)} collective-permute-done((bf16[51,16,128]{2,1,0:T(8,128)(2,1)S(1)}, bf16[51,16,128]{2,1,0:T(8,128)(2,1)S(1)}, u32[]{:S(2)}, u32[]{:S(2)}) %collective-permute-start.6) | collective-permute-done | bytes 208928 | tf_op jit(solution)/shard_map/ppermute | solution.py:265
  45.0 0.0 collective-permute-done.3.up1
  45.0 0.0 collective-permute-done.4.down1
  45.0 1.8 %contract.1 = f32[16,8,384]{2,1,0:T(8,128)S(1)} custom-call(s32[4]{0:T(128)S(1)} %pad_add_fusion.place_ref, bf16[99,16,128]{2,1,0:T(8,128)(2,1)S(1)} %get-tuple-element.10.home, bf16[99,16,128]{2,1,0:T(8,128)(2,1)S(1)} %collective-permute-done.3.up1, bf16[99,16,128]{2,1,0:T(8,128)(2,1)S(1)} %collective-permute-done.4.down1, ...), custom_call_target="tpu_custom_call" | custom-call | tf_op jit(solution)/shard_map/contract/pallas_call | solution.py:218
  46.8 12.4 %all_to_all.20 = f32[16,8,384]{2,1,0:T(8,128)S(1)} all-to-all(f32[16,8,384]{2,1,0:T(8,128)S(1)} %contract.1), channel_id=1, replica_groups=mesh['row'=8,'col'=16,'wf'=2] {'col'}, dimensions={0} | all-to-all | bytes 393216 | tf_op jit(solution)/shard_map/all_to_all | solution.py:282
  59.3 0.2 reshape.133
  59.4 0.1 copy.24
  59.5 0.2 all_to_all.16
  59.7 16.4 %all_to_all.21 = f32[16,1,192]{2,1,0:T(1,128)S(1)} all-to-all(f32[16,1,192]{2,1,0:T(1,128)S(1)} %all_to_all.16), channel_id=1, replica_groups=mesh['row'=8,'col'=16,'wf'=2] {'row','wf'}, dimensions={0} | all-to-all | bytes 24576 | tf_op jit(solution)/shard_map/all_to_all | solution.py:284
  76.2 0.7 reshape.134
  (17 shorter events, 0.2 us)
Async XLA Ops:
  0.8 19.5 %collective-permute-start.1 = (bf16[2,3,64,128]{3,2,1,0:T(8,128)(2,1)S(1)}, bf16[2,3,64,128]{3,2,1,0:T(8,128)(2,1)S(1)}, u32[]{:S(2)}, u32[]{:S(2)}) collective-permute-start(bf16[2,3,64,128]{3,2,1,0:T(8,128)(2,1)S(1)} %pad_maximum_fusion.own_wave), channel_id=1, source_target_pairs={{0,129},{32,161},{64,193},{96,225},{128,1},{160,33},{192,65},{224,... | collective-permute-start | bytes 294920 | tf_op jit(solution)/shard_map/ppermute | solution.py:248
  7.8 12.6 %collective-permute-start.2 = (bf16[12,2,2,128,128]{4,3,2,1,0:T(8,128)(2,1)}, bf16[12,2,2,128,128]{4,3,2,1,0:T(8,128)(2,1)}, u32[]{:S(2)}, u32[]{:S(2)}) collective-permute-start(bf16[12,2,2,128,128]{4,3,2,1,0:T(8,128)(2,1)} %own_left.1), channel_id=1, source_target_pairs={{0,32},{32,0},{64,96},{96,64},{128,160},{160,128},{192,224},{224,1... | collective-permute-start | bytes 4718600 | tf_op jit(solution)/shard_map/ppermute | solution.py:252
  8.7 11.6 %collective-permute-start = (s32[12,32]{1,0:T(8,128)}, s32[12,32]{1,0:T(8,128)S(1)}, u32[]{:S(2)}, u32[]{:S(2)}) collective-permute-start(s32[12,32]{1,0:T(8,128)} %own_table.1), channel_id=1, source_target_pairs={{0,32},{32,0},{64,96},{96,64},{128,160},{160,128},{192,224},{224,1... | collective-permute-start | bytes 4616 | tf_op jit(solution)/shard_map/ppermute | solution.py:253
  12.8 6.9 %copy-start.3 = (s32[96]{0:T(128)S(1)}, s32[96]{0:T(128)}, u32[]{:S(2)}) copy-start(s32[96]{0:T(128)} %param.12) | copy-start | bytes 1156
  12.8 7.2 %copy-start.4 = (s32[96]{0:T(128)S(1)}, s32[96]{0:T(128)}, u32[]{:S(2)}) copy-start(s32[96]{0:T(128)} %param.13) | copy-start | bytes 1156
  12.8 7.5 %copy-start = (bf16[12,2,2,128,128]{4,3,2,1,0:T(8,128)(2,1)S(1)}, bf16[12,2,2,128,128]{4,3,2,1,0:T(8,128)(2,1)}, u32[]{:S(2)}) copy-start(bf16[12,2,2,128,128]{4,3,2,1,0:T(8,128)(2,1)} %own_left.1) | copy-start | bytes 4718596
  12.8 7.5 %copy-start.1 = (s32[12,32]{1,0:T(8,128)S(1)}, s32[12,32]{1,0:T(8,128)}, u32[]{:S(2)}) copy-start(s32[12,32]{1,0:T(8,128)} %own_table.1) | copy-start | bytes 4612
  12.9 22.2 %all-to-all-start = ((bf16[16,16,16,128]{3,2,1,0:T(8,128)(2,1)}), bf16[16,16,16,128]{3,2,1,0:T(8,128)(2,1)S(1)}, u32[]{:S(2)}, u32[]{:S(2)}) async-start(bf16[16,16,16,128]{3,2,1,0:T(8,128)(2,1)} %pick_right.1), calls=%async_computation | async-start | bytes 2097152 | tf_op jit(solution)/shard_map/all_to_all | solution.py:256
  20.3 11.2 %copy-start.2 = (s32[128,32]{0,1:T(8,128)S(1)}, s32[128,32]{0,1:T(8,128)}, u32[]{:S(2)}) copy-start(s32[128,32]{0,1:T(8,128)} %param.11) | copy-start | bytes 49156
  24.8 20.1 %collective-permute-start.3 = (bf16[99,16,128]{2,1,0:T(8,128)(2,1)}, bf16[99,16,128]{2,1,0:T(8,128)(2,1)S(1)}, u32[]{:S(2)}, u32[]{:S(2)}) collective-permute-start(bf16[99,16,128]{2,1,0:T(8,128)(2,1)} %get-tuple-element.11), channel_id=1, source_target_pairs={{0,64},{32,96},{64,128},{96,160},{128,192},{160,224},{192,1},{224,... | collective-permute-start | bytes 1216520 | tf_op jit(solution)/shard_map/ppermute | solution.py:262
  25.6 19.4 %collective-permute-start.4 = (bf16[99,16,128]{2,1,0:T(8,128)(2,1)}, bf16[99,16,128]{2,1,0:T(8,128)(2,1)S(1)}, u32[]{:S(2)}, u32[]{:S(2)}) collective-permute-start(bf16[99,16,128]{2,1,0:T(8,128)(2,1)} %get-tuple-element.12), channel_id=1, source_target_pairs={{0,193},{32,225},{64,0},{96,32},{128,64},{160,96},{192,128},{224,1... | collective-permute-start | bytes 1216520 | tf_op jit(solution)/shard_map/ppermute | solution.py:263
  27.6 13.8 %collective-permute-start.5 = (bf16[51,16,128]{2,1,0:T(8,128)(2,1)}, bf16[51,16,128]{2,1,0:T(8,128)(2,1)S(1)}, u32[]{:S(2)}, u32[]{:S(2)}) collective-permute-start(bf16[51,16,128]{2,1,0:T(8,128)(2,1)} %get-tuple-element.13), channel_id=1, source_target_pairs={{0,128},{32,160},{64,192},{96,224},{128,1},{160,33},{192,65},{224,... | collective-permute-start | bytes 626696 | tf_op jit(solution)/shard_map/ppermute | solution.py:264
  27.7 17.3 %collective-permute-start.6 = (bf16[51,16,128]{2,1,0:T(8,128)(2,1)S(1)}, bf16[51,16,128]{2,1,0:T(8,128)(2,1)S(1)}, u32[]{:S(2)}, u32[]{:S(2)}) collective-permute-start(bf16[51,16,128]{2,1,0:T(8,128)(2,1)S(1)} %get-tuple-element.14), channel_id=1, source_target_pairs={{0,129},{32,161},{64,193},{96,225},{128,0},{160,32},{192,64},{224,... | collective-permute-start | bytes 626696 | tf_op jit(solution)/shard_map/ppermute | solution.py:265

commit v3 on v2

--- a/solution.py
+++ b/solution.py
@@ -20,37 +20,43 @@
     return pltpu.CompilerParams(vmem_limit_bytes=VMEM)
 
 
-def pick_right_kernel(place_ref, right_ref, out_ref):
+def pick_right_kernel(place_ref, near_ref, cross_ref, out_ref):
     for block in range(out_ref.shape[0]):
-        rows = jnp.concatenate(
-            [right_ref[block, j, c][None] for c in range(2) for j in range(8)], axis=0
-        )
-        out_ref[block] = jnp.swapaxes(rows, 0, 1)
+        for ref, first in ((near_ref, 0), (cross_ref, 8)):
+            rows = jnp.concatenate(
+                [ref[block, j, c][None] for c in range(2) for j in range(8)], axis=0
+            )
+            rows = jnp.swapaxes(rows, 0, 1)
+            if first:
+                out_ref[block, 16:24] = rows[8:16]
+            else:
+                out_ref[block, 0:16] = rows
 
 
 def pick_right(place, right_operators):
     view = right_operators.reshape(16, 2, 8, 2, 4, 16, 128)
+    rows = lambda flip: pl.BlockSpec(
+        (8, None, 8, 2, None, 16, 128),
+        lambda i, place: (i, place[0], 0, 0, place[1] ^ flip, 0, 0),
+    )
     return pl.pallas_call(
         pick_right_kernel,
         grid_spec=pltpu.PrefetchScalarGridSpec(
             num_scalar_prefetch=1,
-            grid=(4,),
-            in_specs=[
-                pl.BlockSpec(
-                    (4, None, 8, 2, None, 16, 128),
-                    lambda i, place: (i, place[0], 0, 0, place[1], 0, 0),
-                )
-            ],
-            out_specs=pl.BlockSpec((4, 16, 16, 128), lambda i, place: (i, 0, 0, 0)),
+            grid=(2,),
+            in_specs=[rows(0), rows(2)],
+            out_specs=pl.BlockSpec((8, 24, 16, 128), lambda i, place: (i, 0, 0, 0)),
         ),
-        out_shape=jax.ShapeDtypeStruct((16, 16, 16, 128), BF),
+        out_shape=jax.ShapeDtypeStruct((16, 24, 16, 128), BF),
         compiler_params=params(),
         name="pick_right",
-    )(place, view)
+    )(place, view, view)
 
 
 GROUPS = (6, 6, 6, 3, 3)
+ROWS = (24, 16, 16, 8, 8)
 STARTS = (0, 96, 192, 288, 336)
+TILES = tuple(n * rows for n, rows in zip(GROUPS, ROWS))
 
 
 def tiles_kernel(
@@ -78,21 +84,22 @@
             bras[1] = jnp.concatenate([-im_t, re_t], axis=1)
     spots = [z, lax.rem(z + 1, 8), lax.rem(z + 7, 8), lax.rem(z + 2, 8), lax.rem(z + 6, 8)]
 
-    def bra(picked):
-        return jnp.concatenate(
-            [
-                bras[c, pl.ds(pl.multiple_of(spots[i] * 16, 16), 16), :]
-                for c in range(2)
-                for i in picked
-            ],
-            axis=0,
-        )
+    upper = iota((16, 256), 0) < 8
+
+    def bra(far):
+        def block(c, spot):
+            return bras[c, pl.ds(pl.multiple_of(spot * 16, 16), 16), :]
+
+        parts = []
+        for c in range(2):
+            parts += [block(c, spot) for spot in spots[0:3]]
+            parts.append(jnp.where(upper, block(c, spots[far]), block(c, z ^ 2)))
+        return jnp.concatenate(parts, axis=0)
 
     labels = [own_table[s, q] for s in range(12)] + [far_table[s, q] for s in range(12)]
     shifts = [lax.rem(label - q + 32, 32) for label in labels]
     for half in range(2):
-        picked = (0, 1, 2, 3 + half)
-        left = bra(picked)
+        left = bra(3 + half)
         source = far_left if half else own_left
         for s in range(12):
             operator = jnp.concatenate([source[s, 0], source[s, 1]], axis=1)
@@ -111,7 +118,7 @@
                 jnp.dot(left, kets[group * 4 + s], preferred_element_type=F32).astype(BF)
                 for s in range(4)
             ]
-            for i, spot in enumerate(picked):
+            for i in range(4):
                 rows = jnp.concatenate(
                     [
                         brackets[s][
@@ -124,8 +131,13 @@
                     ],
                     axis=0,
                 )
-                first = (group if spot > 2 else half * 3 + group) * 16
-                outs[spot][first : first + 16] = jnp.swapaxes(rows, 0, 1)
+                rows = jnp.swapaxes(rows, 0, 1)
+                whole = half * 3 + group
+                if i < 3:
+                    outs[i][whole * 16 : whole * 16 + 16] = rows
+                else:
+                    outs[3 + half][group * 8 : group * 8 + 8] = rows[0:8]
+                    home[96 + whole * 8 : 96 + whole * 8 + 8] = rows[8:16]
     for spot, out in enumerate(outs):
         count = GROUPS[spot] * 4
         offset = 12 if spot == 4 else 0
@@ -135,7 +147,7 @@
             low_s, high_s = (tile * 128 - STARTS[spot]) // 4, (tile * 128 + 128 - STARTS[spot]) // 4
             for s in range(max(0, low_s), min(count, high_s)):
                 row = jnp.where(place == s, labels[offset + s].astype(F32), row)
-            out[GROUPS[spot] * 16 + tile] = row.astype(BF)
+            out[TILES[spot] + tile] = row.astype(BF)
 
 
 def make_tiles(place, own_table, far_table, own_wave, far_wave, left_operators, far_left):
@@ -152,14 +164,14 @@
             in_specs=[
                 table, table, full((2, 3, 64, 128)), full((2, 3, 64, 128)), operators, operators
             ],
-            out_specs=[full((n * 16 + 3, 16, 128)) for n in GROUPS],
+            out_specs=[full((n + 3, 16, 128)) for n in TILES],
             scratch_shapes=[
                 pltpu.VMEM((3, 256, 512), BF),
                 pltpu.VMEM((2, 128, 256), BF),
                 pltpu.VMEM((12, 256, 256), BF),
             ],
         ),
-        out_shape=[jax.ShapeDtypeStruct((n * 16 + 3, 16, 128), BF) for n in GROUPS],
+        out_shape=[jax.ShapeDtypeStruct((n + 3, 16, 128), BF) for n in TILES],
         compiler_params=params(),
         name="make_tiles",
     )(place, own_table, far_table, own_wave, far_wave, left_operators, far_left)
@@ -169,27 +181,35 @@
     place_ref, home, up1, down1, up2, down2, right, right_table, slot_key, real_key, imag_key, sign, out
 ):
     arrays = (home, up1, down1, up2, down2)
-    paired = jnp.zeros((256, 384), F32)
-    for step in range(8):
-        lefts = []
-        rights = []
-        for a in (2 * step, 2 * step + 1):
-            lefts.append(
+    zero = jnp.zeros((96, 128), BF)
+
+    def lefts(a):
+        if a >= 16:
+            return [home[96 + g * 8 + a - 16] for g in range(6)] + [zero[0:32]]
+        tiles = [ref[g * 16 + a] for ref in arrays[0:3] for g in range(6)]
+        if a >= 8:
+            return tiles + [zero]
+        return tiles + [ref[g * 8 + a] for ref in arrays[3:5] for g in range(3)]
+
+    def product(start):
+        total = 0.0
+        for a in range(start, start + 8, 2):
+            total += lax.dot_general(
+                jnp.concatenate([right[:, a + i].reshape(256, 128) for i in range(2)], axis=1),
                 jnp.concatenate(
-                    [ref[g * 16 + a] for ref, n in zip(arrays, GROUPS) for g in range(n)], axis=0
-                )
+                    [jnp.concatenate(lefts(a + i), axis=0) for i in range(2)], axis=1
+                ),
+                (((1,), (1,)), ((), ())),
+                preferred_element_type=F32,
             )
-            rights.append(right[:, a].reshape(256, 128))
-        paired += lax.dot_general(
-            jnp.concatenate(rights, axis=1),
-            jnp.concatenate(lefts, axis=1),
-            (((1,), (1,)), ((), ())),
-            preferred_element_type=F32,
-        )
+        return total
+
+    paired = product(0) + product(8)
+    paired = jnp.concatenate([paired[:, 0:128] + product(16), paired[:, 128:384]], axis=1)
     paired = paired.reshape(16, 2, 8, 384)
     slot_label = jnp.concatenate(
         [
-            sum(ref[n * 16 + tile].astype(F32)[0:1] for ref, n in zip(arrays, GROUPS))
+            sum(ref[n + tile].astype(F32)[0:1] for ref, n in zip(arrays, TILES))
             for tile in range(3)
         ],
         axis=1,

time: 77.3 us -> 75.4 us (0.975)
  waiting for transfers between devices: 13.1 us -> 6.98 us
  local copies, waits for them, and re-layouts: 2.85 us -> 6.11 us
  blocking collectives: 28.9 us -> 30 us
    ppermute x1, waiting for transfers between devices: 6.36 us -> 0.01 us  [local(): lax.ppermute(up2, line, ring(lambda z: (z + 2) % 8))]
    all_to_all x1, waiting for transfers between devices: 3.13 us -> 6.9 us  [local(): right = lax.all_to_all(right, 'col', 0, 0, tiled=True)]
    ppermute x1, waiting for transfers between devices: 3.61 us -> 0.06 us  [local(): lax.ppermute(down2, line, ring(lambda z: (z + 6) % 8))]
    unnamed x11 -> x15, local copies, waits for them, and re-layouts: 0.12 us -> 3.38 us
    pallas_call x1, Pallas kernels: 4.05 us -> 3.26 us  [pick_right(): pl.pallas_call(pick_right_kernel, grid_spec=pltpu.PrefetchScalarGridSpec(...]
  transfers between devices with their start and end apart: 8 -> 8, of which waited for: 3 -> 2; matrix products, arithmetic and copies ran while one was open for 2% -> 3% of each run, Pallas kernels for 11% -> 10%
where the time goes in v3:
time: 75.4 us; the launch traced here: 75 us
  blocking collectives  30 us (40%)
  starting transfers between devices  21.1 us (28%)
  Pallas kernels  10 us (13%)
  waiting for transfers between devices  6.98 us (9%)
  local copies, waits for them, and re-layouts  6.11 us (8%)
    all_to_all x1, blocking collectives, local(): total = jnp.sum(lax.all_to_all(shares, line, 0, 0, tiled=True), axis=0)  16.9 us
    all_to_all x1, blocking collectives, local(): shares = jnp.sum(lax.all_to_all(shares, 'col', 0, 0, tiled=True), axis=0)  13.1 us
    ppermute x1, starting transfers between devices, local(): lax.ppermute(own_wave, line, ring(lambda z: (z + 2) % 8 if z in (2, 3, 6,...  6.94 us
    all_to_all x1, starting transfers between devices, local(): right = lax.all_to_all(right, 'col', 0, 0, tiled=True)  6.9 us
    all_to_all x1, waiting for transfers between devices, local(): right = lax.all_to_all(right, 'col', 0, 0, tiled=True)  6.9 us
    pallas_call x1, Pallas kernels, make_tiles(): pl.pallas_call(tiles_kernel, grid_spec=pltpu.PrefetchScalarGridSpec(num_s...  4.33 us
    ppermute x1, starting transfers between devices, local(): lax.ppermute(down2, line, ring(lambda z: (z + 6) % 8))  3.56 us
    unnamed x15, local copies, waits for them, and re-layouts  3.38 us
  transfers between devices with their start and end apart: 8, of which 2 were waited for; matrix products, arithmetic and copies ran while one was open for 3% of the time, Pallas kernels for 10%

profile of v3, /device:TPU:1, one launch (start us, length us, event | category | flops | bytes accessed | tf_op | source)
XLA Modules:
  0.0 75.0 jit_solution(8155503307576464413)
XLA Ops:
  0.0 0.8 %constant_dynamic-slice_fusion.2 = (bf16[2,1,64,128]{3,2,1,0:T(8,128)(2,1)S(1)}, bf16[2,1,64,128]{3,2,1,0:T(8,128)(2,1)S(1)}, bf16[2,1,64,128]{3,2,1,0:T(8,128)(2,1)S(1)}) fusion(bf16[2,32,64,128]{3,2,1,0:T(8,128)(2,1)} %param.7, s32[]{:T(128)S(6)} %select_n.46, s32[]{:T(128)S(6)} %select_n.50, s32[]{:T(128)S(6)} %select_n.48), kind=kLoop, calls=%fused_computation.17 | loop fusion | bytes 196620 | tf_op jit(solution)/shard_map/dynamic_slice | solution.py:266
  0.8 6.9 %collective-permute-start.1 = (bf16[2,3,64,128]{3,2,1,0:T(8,128)(2,1)S(1)}, bf16[2,3,64,128]{3,2,1,0:T(8,128)(2,1)S(1)}, u32[]{:S(2)}, u32[]{:S(2)}) collective-permute-start(bf16[2,3,64,128]{3,2,1,0:T(8,128)(2,1)S(1)} %pad_maximum_fusion.own_wave), channel_id=1, source_target_pairs={{0,129},{32,161},{64,193},{96,225},{128,1},{160,33},{192,65},{224,... | collective-permute-start | bytes 294920 | tf_op jit(solution)/shard_map/ppermute | solution.py:268
  7.8 1.0 %collective-permute-start.2 = (bf16[12,2,2,128,128]{4,3,2,1,0:T(8,128)(2,1)}, bf16[12,2,2,128,128]{4,3,2,1,0:T(8,128)(2,1)}, u32[]{:S(2)}, u32[]{:S(2)}) collective-permute-start(bf16[12,2,2,128,128]{4,3,2,1,0:T(8,128)(2,1)} %own_left.1), channel_id=1, source_target_pairs={{0,32},{32,0},{64,96},{96,64},{128,160},{160,128},{192,224},{224,1... | collective-permute-start | bytes 4718600 | tf_op jit(solution)/shard_map/ppermute | solution.py:272
  8.7 0.0 collective-permute-start
  8.7 0.1 pad_add_fusion.place_ref
  8.8 3.3 %pick_right.1 = bf16[16,24,16,128]{3,2,1,0:T(8,128)(2,1)} custom-call(s32[4]{0:T(128)S(1)} %pad_add_fusion.place_ref, bf16[16,2,8,2,4,16,128]{6,5,4,3,2,1,0:T(8,128)(2,1)} %bitcast.19, bf16[16,2,8,2,4,16,128]{6,5,4,3,2,1,0:T(8,128)(2,1)} %bitcast.20), custom_call_target="tpu_custom_call" | custom-call | tf_op jit(solution)/shard_map/pick_right/pallas_call | solution.py:42
  12.0 0.0 copy-start.5
  12.1 0.0 copy-start.3
  12.1 6.9 %all-to-all-start = ((bf16[16,24,16,128]{3,2,1,0:T(8,128)(2,1)}), bf16[16,24,16,128]{3,2,1,0:T(8,128)(2,1)S(1)}, u32[]{:S(2)}, u32[]{:S(2)}) async-start(bf16[16,24,16,128]{3,2,1,0:T(8,128)(2,1)} %pick_right.1), calls=%async_computation | async-start | bytes 3145728 | tf_op jit(solution)/shard_map/all_to_all | solution.py:276
  19.0 0.0 copy-done.5
  19.0 0.1 reshape.131
  19.2 0.1 mul.48
  19.3 0.0 copy-done.6
  19.3 0.1 stack.36
  19.4 0.1 fusion.2
  19.5 0.1 iota_add_fusion
  19.6 0.0 collective-permute-done.far_table
  19.6 0.0 collective-permute-done.1.far_wave
  19.6 0.0 collective-permute-done.2.far_left
  19.6 0.0 copy-done
  19.6 0.0 copy-done.3
  19.6 4.3 %make_tiles.1 = (bf16[147,16,128]{2,1,0:T(8,128)(2,1)S(1)}, bf16[99,16,128]{2,1,0:T(8,128)(2,1)}, bf16[99,16,128]{2,1,0:T(8,128)(2,1)}, bf16[27,16,128]{2,1,0:T(8,128)(2,1)S(1)}, bf16[27,16,128]{2,1,0:T(8,128)(2,1)S(1)}) custom-call(s32[4]{0:T(128)S(1)} %pad_add_fusion.place_ref, s32[12,32]{1,0:T(8,128)S(1)} %copy-done.3, ...), custom_call_target="tpu_custom_call" | custom-call | tf_op jit(solution)/shard_map/make_tiles/pallas_call | solution.py:159
  23.9 0.8 %copy-done.1 = bf16[147,16,128]{2,1,0:T(8,128)(2,1)} copy-done((bf16[147,16,128]{2,1,0:T(8,128)(2,1)}, bf16[147,16,128]{2,1,0:T(8,128)(2,1)S(1)}, u32[]{:S(2)}) %copy-start.1) | copy-done | bytes 602136
  24.8 0.6 copy-done.4
  25.4 0.7 collective-permute-start.3
  26.1 1.9 %collective-permute-start.4 = (bf16[99,16,128]{2,1,0:T(8,128)(2,1)}, bf16[99,16,128]{2,1,0:T(8,128)(2,1)S(1)}, u32[]{:S(2)}, u32[]{:S(2)}) collective-permute-start(bf16[99,16,128]{2,1,0:T(8,128)(2,1)} %get-tuple-element.12), channel_id=1, source_target_pairs={{0,193},{32,225},{64,0},{96,32},{128,64},{160,96},{192,128},{224,1... | collective-permute-start | bytes 1216520 | tf_op jit(solution)/shard_map/ppermute | solution.py:283
  28.1 0.1 fusion.1
  28.2 0.1 add.152.slot_key
  28.3 0.1 add.148.real_key
  28.4 0.1 sub.34.imag_key
  28.5 0.8 %copy.22.right_table = s32[128,32]{1,0:T(8,128)S(1)} copy(s32[128,32]{0,1:T(8,128)} %param.11) | data formatting | bytes 32768 | tf_op args[4]
  29.3 0.1 collective-permute-start.5
  29.4 3.6 %collective-permute-start.6 = (bf16[27,16,128]{2,1,0:T(8,128)(2,1)S(1)}, bf16[27,16,128]{2,1,0:T(8,128)(2,1)S(1)}, u32[]{:S(2)}, u32[]{:S(2)}) collective-permute-start(bf16[27,16,128]{2,1,0:T(8,128)(2,1)S(1)} %get-tuple-element.14), channel_id=1, source_target_pairs={{0,129},{32,161},{64,193},{96,225},{128,0},{160,32},{192,64},{224,... | collective-permute-start | bytes 331784 | tf_op jit(solution)/shard_map/ppermute | solution.py:285
  33.0 0.1 broadcast_in_dim.2
  33.1 0.1 reshape.132.sign
  33.2 6.9 %all-to-all-done.right = bf16[16,24,16,128]{3,2,1,0:T(8,128)(2,1)S(1)} async-done(((bf16[16,24,16,128]{3,2,1,0:T(8,128)(2,1)}), bf16[16,24,16,128]{3,2,1,0:T(8,128)(2,1)S(1)}, u32[]{:S(2)}, u32[]{:S(2)}) %all-to-all-start) | async-done | bytes 1572896 | tf_op jit(solution)/shard_map/all_to_all | solution.py:276
  40.1 0.0 collective-permute-done.5.up2
  40.1 0.1 collective-permute-done.6.down2
  40.2 0.0 collective-permute-done.3.up1
  40.2 0.0 collective-permute-done.4.down1
  40.2 1.1 %copy-done.2 = bf16[147,16,128]{2,1,0:T(8,128)(2,1)S(1)} copy-done((bf16[147,16,128]{2,1,0:T(8,128)(2,1)S(1)}, bf16[147,16,128]{2,1,0:T(8,128)(2,1)}, u32[]{:S(2)}) %copy-start.2) | copy-done | bytes 602136
  41.2 2.5 %contract.1 = f32[16,8,384]{2,1,0:T(8,128)S(1)} custom-call(s32[4]{0:T(128)S(1)} %pad_add_fusion.place_ref, bf16[147,16,128]{2,1,0:T(8,128)(2,1)S(1)} %copy-done.2, bf16[99,16,128]{2,1,0:T(8,128)(2,1)S(1)} %collective-permute-done.3.up1, bf16[99,16,128]{2,1,0:T(8,128)(2,1)S(1)} %collective-permute-done.4.down1, ...), custom_call_target="tpu_custom_call" | custom-call | tf_op jit(solution)/shard_map/contract/pallas_call | solution.py:238
  43.7 13.1 %all_to_all.20 = f32[16,8,384]{2,1,0:T(8,128)S(1)} all-to-all(f32[16,8,384]{2,1,0:T(8,128)S(1)} %contract.1), channel_id=1, replica_groups=mesh['row'=8,'col'=16,'wf'=2] {'col'}, dimensions={0} | all-to-all | bytes 393216 | tf_op jit(solution)/shard_map/all_to_all | solution.py:302
  56.8 0.2 reshape.133
  57.0 0.1 copy.24
  57.1 0.2 all_to_all.16
  57.3 16.9 %all_to_all.21 = f32[16,1,192]{2,1,0:T(1,128)S(1)} all-to-all(f32[16,1,192]{2,1,0:T(1,128)S(1)} %all_to_all.16), channel_id=1, replica_groups=mesh['row'=8,'col'=16,'wf'=2] {'row','wf'}, dimensions={0} | all-to-all | bytes 24576 | tf_op jit(solution)/shard_map/all_to_all | solution.py:304
  74.3 0.7 reshape.134
  (21 shorter events, 0.2 us)
Async XLA Ops:
  0.8 18.8 %collective-permute-start.1 = (bf16[2,3,64,128]{3,2,1,0:T(8,128)(2,1)S(1)}, bf16[2,3,64,128]{3,2,1,0:T(8,128)(2,1)S(1)}, u32[]{:S(2)}, u32[]{:S(2)}) collective-permute-start(bf16[2,3,64,128]{3,2,1,0:T(8,128)(2,1)S(1)} %pad_maximum_fusion.own_wave), channel_id=1, source_target_pairs={{0,129},{32,161},{64,193},{96,225},{128,1},{160,33},{192,65},{224,... | collective-permute-start | bytes 294920 | tf_op jit(solution)/shard_map/ppermute | solution.py:268
  7.8 11.8 %collective-permute-start.2 = (bf16[12,2,2,128,128]{4,3,2,1,0:T(8,128)(2,1)}, bf16[12,2,2,128,128]{4,3,2,1,0:T(8,128)(2,1)}, u32[]{:S(2)}, u32[]{:S(2)}) collective-permute-start(bf16[12,2,2,128,128]{4,3,2,1,0:T(8,128)(2,1)} %own_left.1), channel_id=1, source_target_pairs={{0,32},{32,0},{64,96},{96,64},{128,160},{160,128},{192,224},{224,1... | collective-permute-start | bytes 4718600 | tf_op jit(solution)/shard_map/ppermute | solution.py:272
  8.7 10.8 %collective-permute-start = (s32[12,32]{1,0:T(8,128)}, s32[12,32]{1,0:T(8,128)S(1)}, u32[]{:S(2)}, u32[]{:S(2)}) collective-permute-start(s32[12,32]{1,0:T(8,128)} %own_table.1), channel_id=1, source_target_pairs={{0,32},{32,0},{64,96},{96,64},{128,160},{160,128},{192,224},{224,1... | collective-permute-start | bytes 4616 | tf_op jit(solution)/shard_map/ppermute | solution.py:273
  12.0 6.9 %copy-start.5 = (s32[96]{0:T(128)S(1)}, s32[96]{0:T(128)}, u32[]{:S(2)}) copy-start(s32[96]{0:T(128)} %param.12) | copy-start | bytes 1156
  12.0 7.2 %copy-start.6 = (s32[96]{0:T(128)S(1)}, s32[96]{0:T(128)}, u32[]{:S(2)}) copy-start(s32[96]{0:T(128)} %param.13) | copy-start | bytes 1156
  12.1 7.5 %copy-start = (bf16[12,2,2,128,128]{4,3,2,1,0:T(8,128)(2,1)S(1)}, bf16[12,2,2,128,128]{4,3,2,1,0:T(8,128)(2,1)}, u32[]{:S(2)}) copy-start(bf16[12,2,2,128,128]{4,3,2,1,0:T(8,128)(2,1)} %own_left.1) | copy-start | bytes 4718596
  12.1 7.5 %copy-start.3 = (s32[12,32]{1,0:T(8,128)S(1)}, s32[12,32]{1,0:T(8,128)}, u32[]{:S(2)}) copy-start(s32[12,32]{1,0:T(8,128)} %own_table.1) | copy-start | bytes 4612
  12.1 28.0 %all-to-all-start = ((bf16[16,24,16,128]{3,2,1,0:T(8,128)(2,1)}), bf16[16,24,16,128]{3,2,1,0:T(8,128)(2,1)S(1)}, u32[]{:S(2)}, u32[]{:S(2)}) async-start(bf16[16,24,16,128]{3,2,1,0:T(8,128)(2,1)} %pick_right.1), calls=%async_computation | async-start | bytes 3145728 | tf_op jit(solution)/shard_map/all_to_all | solution.py:276
  23.9 0.8 %copy-start.1 = (bf16[147,16,128]{2,1,0:T(8,128)(2,1)}, bf16[147,16,128]{2,1,0:T(8,128)(2,1)S(1)}, u32[]{:S(2)}) copy-start(bf16[147,16,128]{2,1,0:T(8,128)(2,1)S(1)} %get-tuple-element.10.home) | copy-start | bytes 1806340
  24.8 0.6 copy-start.4
  25.4 14.7 %collective-permute-start.3 = (bf16[99,16,128]{2,1,0:T(8,128)(2,1)}, bf16[99,16,128]{2,1,0:T(8,128)(2,1)S(1)}, u32[]{:S(2)}, u32[]{:S(2)}) collective-permute-start(bf16[99,16,128]{2,1,0:T(8,128)(2,1)} %get-tuple-element.11), channel_id=1, source_target_pairs={{0,64},{32,96},{64,128},{96,160},{128,192},{160,224},{192,1},{224,... | collective-permute-start | bytes 1216520 | tf_op jit(solution)/shard_map/ppermute | solution.py:282
  26.1 14.0 %collective-permute-start.4 = (bf16[99,16,128]{2,1,0:T(8,128)(2,1)}, bf16[99,16,128]{2,1,0:T(8,128)(2,1)S(1)}, u32[]{:S(2)}, u32[]{:S(2)}) collective-permute-start(bf16[99,16,128]{2,1,0:T(8,128)(2,1)} %get-tuple-element.12), channel_id=1, source_target_pairs={{0,193},{32,225},{64,0},{96,32},{128,64},{160,96},{192,128},{224,1... | collective-permute-start | bytes 1216520 | tf_op jit(solution)/shard_map/ppermute | solution.py:283
  29.3 10.8 %collective-permute-start.5 = (bf16[27,16,128]{2,1,0:T(8,128)(2,1)}, bf16[27,16,128]{2,1,0:T(8,128)(2,1)S(1)}, u32[]{:S(2)}, u32[]{:S(2)}) collective-permute-start(bf16[27,16,128]{2,1,0:T(8,128)(2,1)} %copy-done.4), channel_id=1, source_target_pairs={{0,128},{32,160},{64,192},{96,224},{128,1},{160,33},{192,65},{224,... | collective-permute-start | bytes 331784 | tf_op jit(solution)/shard_map/ppermute | solution.py:284
  29.4 10.7 %collective-permute-start.6 = (bf16[27,16,128]{2,1,0:T(8,128)(2,1)S(1)}, bf16[27,16,128]{2,1,0:T(8,128)(2,1)S(1)}, u32[]{:S(2)}, u32[]{:S(2)}) collective-permute-start(bf16[27,16,128]{2,1,0:T(8,128)(2,1)S(1)} %get-tuple-element.14), channel_id=1, source_target_pairs={{0,129},{32,161},{64,193},{96,225},{128,0},{160,32},{192,64},{224,... | collective-permute-start | bytes 331784 | tf_op jit(solution)/shard_map/ppermute | solution.py:285
  40.2 1.1 %copy-start.2 = (bf16[147,16,128]{2,1,0:T(8,128)(2,1)S(1)}, bf16[147,16,128]{2,1,0:T(8,128)(2,1)}, u32[]{:S(2)}) copy-start(bf16[147,16,128]{2,1,0:T(8,128)(2,1)} %copy-done.1) | copy-start | bytes 1806340

commit v4 on v3

--- a/solution.py
+++ b/solution.py
@@ -9,15 +9,14 @@
 
 BF = jnp.bfloat16
 F32 = jnp.float32
-VMEM = 48 * 1024 * 1024
 
 
 def iota(shape, axis):
     return lax.broadcasted_iota(jnp.int32, shape, axis)
 
 
-def params():
-    return pltpu.CompilerParams(vmem_limit_bytes=VMEM)
+def params(mebibytes):
+    return pltpu.CompilerParams(vmem_limit_bytes=mebibytes * 1024 * 1024)
 
 
 def pick_right_kernel(place_ref, near_ref, cross_ref, out_ref):
@@ -48,7 +47,7 @@
             out_specs=pl.BlockSpec((8, 24, 16, 128), lambda i, place: (i, 0, 0, 0)),
         ),
         out_shape=jax.ShapeDtypeStruct((16, 24, 16, 128), BF),
-        compiler_params=params(),
+        compiler_params=params(12),
         name="pick_right",
     )(place, view, view)
 
@@ -172,13 +171,27 @@
             ],
         ),
         out_shape=[jax.ShapeDtypeStruct((n + 3, 16, 128), BF) for n in TILES],
-        compiler_params=params(),
+        compiler_params=params(20),
         name="make_tiles",
     )(place, own_table, far_table, own_wave, far_wave, left_operators, far_left)
 
 
+def picks_kernel(slot_key, real_key, imag_key, sign, out):
+    out[0:384] = (slot_key[...] == real_key[...]).astype(F32).astype(BF)
+    out[384:768] = jnp.where(slot_key[...] == imag_key[...], sign[...], 0.0).astype(BF)
+
+
+def make_picks(keys):
+    return pl.pallas_call(
+        picks_kernel,
+        out_shape=jax.ShapeDtypeStruct((768, 384), BF),
+        compiler_params=params(8),
+        name="make_picks",
+    )(*keys)
+
+
 def contract_kernel(
-    place_ref, home, up1, down1, up2, down2, right, right_table, slot_key, real_key, imag_key, sign, out
+    place_ref, home, up1, down1, up2, down2, right, right_table, picks, out, paired_ref
 ):
     arrays = (home, up1, down1, up2, down2)
     zero = jnp.zeros((96, 128), BF)
@@ -205,8 +218,11 @@
         return total
 
     paired = product(0) + product(8)
-    paired = jnp.concatenate([paired[:, 0:128] + product(16), paired[:, 128:384]], axis=1)
-    paired = paired.reshape(16, 2, 8, 384)
+    cross = product(16)
+    for third in range(3):
+        lanes = slice(third * 128, third * 128 + 128)
+        paired_ref[third] = paired[:, lanes] + cross if third == 0 else paired[:, lanes]
+
     slot_label = jnp.concatenate(
         [
             sum(ref[n + tile].astype(F32)[0:1] for ref, n in zip(arrays, TILES))
@@ -214,34 +230,45 @@
         ],
         axis=1,
     )
-    here = iota((128, 32), 1) == place_ref[3]
-    right_label = jnp.sum(
-        jnp.where(here, right_table[...].astype(F32), 0.0), axis=1, keepdims=True
-    )
+    row = iota((128, 128), 0)
+    j = (row % 16) * 8 + (row // 16 % 2) * 4 + row // 32
+    labels = right_table[pl.ds(place_ref[3], 1), :].astype(F32)
+    right_label = jnp.sum(jnp.where(iota((128, 128), 1) == j, labels, 0.0), axis=1, keepdims=True)
     match = right_label == slot_label
+
+    def part(c):
+        rows = [
+            jnp.concatenate(
+                [paired_ref[third, pl.ds(c * 8 + w * 4 + j, 16, 16), :] for third in range(3)],
+                axis=1,
+            )
+            for j in range(4)
+            for w in range(2)
+        ]
+        return jnp.where(match, jnp.concatenate(rows, axis=0), 0.0)
+
+    rest = jnp.concatenate([part(0), part(1)], axis=1)
     total = jnp.zeros((128, 384), F32)
-    for c in range(2):
-        part = jnp.where(match, paired[:, c].reshape(128, 384), 0.0)
-        if c == 0:
-            pick = (slot_key[...] == real_key[...]).astype(F32).astype(BF)
-        else:
-            pick = jnp.where(slot_key[...] == imag_key[...], sign[...], 0.0).astype(BF)
-        for _ in range(3):
-            piece = part.astype(BF)
-            total += jnp.dot(piece, pick, preferred_element_type=F32)
-            part = part - piece.astype(F32)
-    out[...] = total.reshape(16, 8, 384)
-
-
-def contract(place, tiles, right, right_table, keys):
+    for _ in range(3):
+        piece = rest.astype(BF)
+        total += jnp.dot(piece, picks[...], preferred_element_type=F32)
+        rest = rest - piece.astype(F32)
+    for j in range(4):
+        for row in range(8):
+            out[row, :, j * 48 : j * 48 + 48] = total[j * 32 : j * 32 + 32, row * 48 : row * 48 + 48]
+
+
+def contract(place, tiles, right, right_table, picks):
     whole = pl.BlockSpec(memory_space=pltpu.VMEM)
     return pl.pallas_call(
         contract_kernel,
-        in_specs=[pl.BlockSpec(memory_space=pltpu.SMEM)] + [whole] * 11,
-        out_shape=jax.ShapeDtypeStruct((16, 8, 384), F32),
-        compiler_params=params(),
+        in_specs=[pl.BlockSpec(memory_space=pltpu.SMEM)] + [whole] * 8,
+        out_specs=whole,
+        out_shape=jax.ShapeDtypeStruct((8, 32, 192), F32),
+        scratch_shapes=[pltpu.VMEM((3, 256, 128), F32)],
+        compiler_params=params(16),
         name="contract",
-    )(place, *tiles, right, right_table, *keys)
+    )(place, *tiles, right, right_table, picks)
 
 
 def ring(step):
@@ -277,6 +304,7 @@
     home, up1, down1, up2, down2 = make_tiles(
         place, left_table, far_table, own_wave, far_wave, left_operators, far_left
     )
+    assignment, kramers_map, home = lax.optimization_barrier((assignment, kramers_map, home))
     tiles = [
         home,
         lax.ppermute(up1, line, ring(lambda z: (z + 1) % 8)),
@@ -298,11 +326,12 @@
     imag_key = (target * 4 + kind * 2 + 1 - part).reshape(1, 384)
     sign = jnp.broadcast_to((2 * part - 1).astype(F32), (8, 2, 2, 12)).reshape(1, 384)
 
-    shares = contract(place, tiles, right, right_table, [slot_key, real_key, imag_key, sign])
-    shares = jnp.sum(lax.all_to_all(shares, "col", 0, 0, tiled=True), axis=0)
-    shares = shares.reshape(2, 4, 8, 4, 12).transpose(2, 0, 3, 1, 4).reshape(16, 192)
-    total = jnp.sum(lax.all_to_all(shares, line, 0, 0, tiled=True), axis=0)
-    return total.reshape(2, 2, 4, 12).transpose(0, 1, 3, 2)
+    picks = make_picks([slot_key, real_key, imag_key, sign])
+    shares = contract(place, tiles, right, right_table.T, picks)
+    shares = lax.all_to_all(
+        shares.reshape(256, 192), ("row", "wf", "col"), 0, 0, tiled=True
+    )
+    return jnp.sum(shares, axis=0).reshape(4, 2, 2, 12).transpose(1, 2, 3, 0)
 
 
 def solution(mesh):

time: 75.4 us -> 75.3 us (level)
    ppermute x1, starting transfers between devices: 6.94 us -> 4.37 us  [local(): lax.ppermute(own_wave, line, ring(lambda z: (z + 2) % 8 if z in (2, 3, 6,...]
    ppermute x1, starting transfers between devices: 0.96 us -> 3.24 us  [local(): far_left = lax.ppermute(left_operators, 'row', swap)]
    pallas_call x1, Pallas kernels: 3.26 us -> 2.25 us  [pick_right(): pl.pallas_call(pick_right_kernel, grid_spec=pltpu.PrefetchScalarGridSpec(...]
    unnamed x15 -> x16, local copies, waits for them, and re-layouts: 3.38 us -> 4.24 us
    reshape x2 -> x1, local copies, waits for them, and re-layouts: 0.88 us -> 0.09 us  [local(): return jnp.sum(shares, axis=0).reshape(4, 2, 2, 12).transpose(1, 2, 3, 0)]
    all_to_all x2 -> x1, blocking collectives: 30 us -> 29.3 us  [local(): lax.all_to_all(shares.reshape(256, 192), ('row', 'wf', 'col'), 0, 0, tile...]
  transfers between devices with their start and end apart: 8 -> 8, of which waited for: 2 -> 1; matrix products, arithmetic and copies ran while one was open for 3% -> 3% of each run, Pallas kernels for 10% -> 9%
where the time goes in v4:
time: 75.3 us; the launch traced here: 75 us
  blocking collectives  29.3 us (39%)
  starting transfers between devices  20.8 us (28%)
  Pallas kernels  9.59 us (13%)
  waiting for transfers between devices  7.57 us (10%)
  local copies, waits for them, and re-layouts  6.81 us (9%)
    all_to_all x1, blocking collectives, local(): lax.all_to_all(shares.reshape(256, 192), ('row', 'wf', 'col'), 0, 0, tile...  29.3 us
    all_to_all x1, waiting for transfers between devices, local(): right = lax.all_to_all(right, 'col', 0, 0, tiled=True)  7.55 us
    all_to_all x1, starting transfers between devices, local(): right = lax.all_to_all(right, 'col', 0, 0, tiled=True)  6.89 us
    pallas_call x1, Pallas kernels, make_tiles(): pl.pallas_call(tiles_kernel, grid_spec=pltpu.PrefetchScalarGridSpec(num_s...  4.4 us
    ppermute x1, starting transfers between devices, local(): lax.ppermute(own_wave, line, ring(lambda z: (z + 2) % 8 if z in (2, 3, 6,...  4.37 us
    unnamed x16, local copies, waits for them, and re-layouts  4.24 us
    ppermute x1, starting transfers between devices, local(): lax.ppermute(down2, line, ring(lambda z: (z + 6) % 8))  3.57 us
    ppermute x1, starting transfers between devices, local(): far_left = lax.ppermute(left_operators, 'row', swap)  3.24 us
  transfers between devices with their start and end apart: 8, of which 1 were waited for; matrix products, arithmetic and copies ran while one was open for 3% of the time, Pallas kernels for 9%

profile of v4, /device:TPU:1, one launch (start us, length us, event | category | flops | bytes accessed | tf_op | source)
XLA Modules:
  0.0 75.0 jit_solution(13771629364962811564)
XLA Ops:
  0.0 3.2 %collective-permute-start.2 = (bf16[12,2,2,128,128]{4,3,2,1,0:T(8,128)(2,1)}, bf16[12,2,2,128,128]{4,3,2,1,0:T(8,128)(2,1)}, u32[]{:S(2)}, u32[]{:S(2)}) collective-permute-start(bf16[12,2,2,128,128]{4,3,2,1,0:T(8,128)(2,1)} %own_left.1), channel_id=1, source_target_pairs={{0,32},{32,0},{64,96},{96,64},{128,160},{160,128},{192,224},{224,1... | collective-permute-start | bytes 4718600 | tf_op jit(solution)/shard_map/ppermute | solution.py:299
  3.2 0.0 collective-permute-start
  3.2 0.8 %constant_dynamic-slice_fusion.2 = (bf16[2,1,64,128]{3,2,1,0:T(8,128)(2,1)S(1)}, bf16[2,1,64,128]{3,2,1,0:T(8,128)(2,1)S(1)}, bf16[2,1,64,128]{3,2,1,0:T(8,128)(2,1)S(1)}) fusion(bf16[2,32,64,128]{3,2,1,0:T(8,128)(2,1)} %param.7, s32[]{:T(128)S(6)} %select_n.46, s32[]{:T(128)S(6)} %select_n.50, s32[]{:T(128)S(6)} %select_n.48), kind=kLoop, calls=%fused_computation.17 | loop fusion | bytes 196620 | tf_op jit(solution)/shard_map/dynamic_slice | solution.py:293
  4.1 4.4 %collective-permute-start.1 = (bf16[2,3,64,128]{3,2,1,0:T(8,128)(2,1)S(1)}, bf16[2,3,64,128]{3,2,1,0:T(8,128)(2,1)S(1)}, u32[]{:S(2)}, u32[]{:S(2)}) collective-permute-start(bf16[2,3,64,128]{3,2,1,0:T(8,128)(2,1)S(1)} %pad_maximum_fusion.own_wave), channel_id=1, source_target_pairs={{0,129},{32,161},{64,193},{96,225},{128,1},{160,33},{192,65},{224,... | collective-permute-start | bytes 294920 | tf_op jit(solution)/shard_map/ppermute | solution.py:295
  8.4 0.1 pad_add_fusion.place_ref
  8.5 3.4 %copy-done = bf16[32,8,2,64,128]{4,3,2,1,0:T(8,128)(2,1)S(1)} copy-done((bf16[32,8,2,64,128]{4,3,2,1,0:T(8,128)(2,1)S(1)}, bf16[32,8,2,64,128]{4,3,2,1,0:T(8,128)(2,1)}, u32[]{:S(2)}) %copy-start) | copy-done | bytes 8388632
  11.9 2.3 %pick_right.1 = bf16[16,24,16,128]{3,2,1,0:T(8,128)(2,1)} custom-call(s32[4]{0:T(128)S(1)} %pad_add_fusion.place_ref, bf16[16,2,8,2,4,16,128]{6,5,4,3,2,1,0:T(8,128)(2,1)S(1)} %bitcast.20, bf16[16,2,8,2,4,16,128]{6,5,4,3,2,1,0:T(8,128)(2,1)S(1)} %bitcast.21), custom_call_target="tpu_custom_call" | custom-call | tf_op jit(solution)/shard_map/pick_right/pallas_call | solution.py:41
  14.1 6.9 %all-to-all-start = ((bf16[16,24,16,128]{3,2,1,0:T(8,128)(2,1)}), bf16[16,24,16,128]{3,2,1,0:T(8,128)(2,1)S(1)}, u32[]{:S(2)}, u32[]{:S(2)}) async-start(bf16[16,24,16,128]{3,2,1,0:T(8,128)(2,1)} %pick_right.1), calls=%async_computation | async-start | bytes 3145728 | tf_op jit(solution)/shard_map/all_to_all | solution.py:303
  21.1 0.1 broadcast_in_dim.2
  21.2 0.1 reshape.129.sign
  21.3 0.0 copy-start.6
  21.3 0.0 copy-start.7
  21.3 0.0 copy-start.4
  21.3 0.0 collective-permute-done.far_table
  21.3 0.0 collective-permute-done.1.far_wave
  21.3 0.0 collective-permute-done.2.far_left
  21.3 0.0 copy-done.1
  21.4 0.0 copy-done.5
  21.4 4.4 %make_tiles.1 = (bf16[147,16,128]{2,1,0:T(8,128)(2,1)S(1)}, bf16[99,16,128]{2,1,0:T(8,128)(2,1)}, bf16[99,16,128]{2,1,0:T(8,128)(2,1)}, bf16[27,16,128]{2,1,0:T(8,128)(2,1)}, bf16[27,16,128]{2,1,0:T(8,128)(2,1)}) custom-call(s32[4]{0:T(128)S(1)} %pad_add_fusion.place_ref, s32[12,32]{1,0:T(8,128)S(1)} %copy-done.5, ...), custom_call_target="tpu_custom_call" | custom-call | tf_op jit(solution)/shard_map/make_tiles/pallas_call | solution.py:158
  25.8 0.8 %copy-done.2 = bf16[147,16,128]{2,1,0:T(8,128)(2,1)} copy-done((bf16[147,16,128]{2,1,0:T(8,128)(2,1)}, bf16[147,16,128]{2,1,0:T(8,128)(2,1)S(1)}, u32[]{:S(2)}) %copy-start.2) | copy-done | bytes 602136
  26.6 0.7 collective-permute-start.3
  27.3 1.9 %collective-permute-start.4 = (bf16[99,16,128]{2,1,0:T(8,128)(2,1)}, bf16[99,16,128]{2,1,0:T(8,128)(2,1)}, u32[]{:S(2)}, u32[]{:S(2)}) collective-permute-start(bf16[99,16,128]{2,1,0:T(8,128)(2,1)} %get-tuple-element.16), channel_id=1, source_target_pairs={{0,193},{32,225},{64,0},{96,32},{128,64},{160,96},{192,128},{224,1... | collective-permute-start | bytes 1216520 | tf_op jit(solution)/shard_map/ppermute | solution.py:311
  29.3 0.0 collective-permute-start.5
  29.3 3.6 %collective-permute-start.6 = (bf16[27,16,128]{2,1,0:T(8,128)(2,1)}, bf16[27,16,128]{2,1,0:T(8,128)(2,1)}, u32[]{:S(2)}, u32[]{:S(2)}) collective-permute-start(bf16[27,16,128]{2,1,0:T(8,128)(2,1)} %get-tuple-element.18), channel_id=1, source_target_pairs={{0,129},{32,161},{64,193},{96,225},{128,0},{160,32},{192,64},{224,... | collective-permute-start | bytes 331784 | tf_op jit(solution)/shard_map/ppermute | solution.py:313
  32.9 0.0 copy-done.6
  32.9 0.1 reshape.128
  33.1 0.1 mul.48
  33.1 0.0 copy-done.7
  33.1 0.1 stack.36
  33.2 0.1 fusion.2
  33.3 0.1 fusion.1
  33.4 0.1 iota_add_fusion
  33.5 0.1 add.152.slot_key
  33.6 0.1 add.148.real_key
  33.7 0.1 sub.34.imag_key
  33.8 0.2 make_picks.1.picks
  34.0 7.5 %all-to-all-done.right = bf16[16,24,16,128]{3,2,1,0:T(8,128)(2,1)S(1)} async-done(((bf16[16,24,16,128]{3,2,1,0:T(8,128)(2,1)}), bf16[16,24,16,128]{3,2,1,0:T(8,128)(2,1)S(1)}, u32[]{:S(2)}, u32[]{:S(2)}) %all-to-all-start) | async-done | bytes 1572896 | tf_op jit(solution)/shard_map/all_to_all | solution.py:303
  41.6 0.0 collective-permute-done.5.up2
  41.6 0.0 collective-permute-done.6.down2
  41.6 0.0 collective-permute-done.3.up1
  41.6 0.0 collective-permute-done.4.down1
  41.6 0.0 copy-done.4
  41.6 2.8 %contract.1 = f32[8,32,192]{2,1,0:T(8,128)S(1)} custom-call(s32[4]{0:T(128)S(1)} %pad_add_fusion.place_ref, bf16[147,16,128]{2,1,0:T(8,128)(2,1)S(1)} %copy-done.3, bf16[99,16,128]{2,1,0:T(8,128)(2,1)S(1)} %collective-permute-done.3.up1, bf16[99,16,128]{2,1,0:T(8,128)(2,1)} %collective-permute-done.4.down1, ...), custom_call_target="tpu_custom_call" | custom-call | tf_op jit(solution)/shard_map/contract/pallas_call | solution.py:263
  44.4 0.3 copy.17
  44.7 29.3 %all_to_all.14 = f32[256,1,192]{2,1,0:T(1,128)S(1)} all-to-all(f32[256,1,192]{2,1,0:T(1,128)S(1)} %copy.17), channel_id=1, replica_groups=mesh['row'=8,'col'=16,'wf'=2] {'row','wf','col'}, dimensions={0} | all-to-all | bytes 393216 | tf_op jit(solution)/shard_map/all_to_all | solution.py:331
  74.0 0.3 reduce_sum.9
  74.3 0.1 reshape.130
  74.4 0.6 copy.18
  (20 shorter events, 0.1 us)
Async XLA Ops:
  0.0 21.3 %collective-permute-start.2 = (bf16[12,2,2,128,128]{4,3,2,1,0:T(8,128)(2,1)}, bf16[12,2,2,128,128]{4,3,2,1,0:T(8,128)(2,1)}, u32[]{:S(2)}, u32[]{:S(2)}) collective-permute-start(bf16[12,2,2,128,128]{4,3,2,1,0:T(8,128)(2,1)} %own_left.1), channel_id=1, source_target_pairs={{0,32},{32,0},{64,96},{96,64},{128,160},{160,128},{192,224},{224,1... | collective-permute-start | bytes 4718600 | tf_op jit(solution)/shard_map/ppermute | solution.py:299
  3.2 18.1 %collective-permute-start = (s32[12,32]{1,0:T(8,128)}, s32[12,32]{1,0:T(8,128)S(1)}, u32[]{:S(2)}, u32[]{:S(2)}) collective-permute-start(s32[12,32]{1,0:T(8,128)} %own_table.1), channel_id=1, source_target_pairs={{0,32},{32,0},{64,96},{96,64},{128,160},{160,128},{192,224},{224,1... | collective-permute-start | bytes 4616 | tf_op jit(solution)/shard_map/ppermute | solution.py:300
  4.1 17.3 %collective-permute-start.1 = (bf16[2,3,64,128]{3,2,1,0:T(8,128)(2,1)S(1)}, bf16[2,3,64,128]{3,2,1,0:T(8,128)(2,1)S(1)}, u32[]{:S(2)}, u32[]{:S(2)}) collective-permute-start(bf16[2,3,64,128]{3,2,1,0:T(8,128)(2,1)S(1)} %pad_maximum_fusion.own_wave), channel_id=1, source_target_pairs={{0,129},{32,161},{64,193},{96,225},{128,1},{160,33},{192,65},{224,... | collective-permute-start | bytes 294920 | tf_op jit(solution)/shard_map/ppermute | solution.py:295
  8.5 3.4 %copy-start = (bf16[32,8,2,64,128]{4,3,2,1,0:T(8,128)(2,1)S(1)}, bf16[32,8,2,64,128]{4,3,2,1,0:T(8,128)(2,1)}, u32[]{:S(2)}) copy-start(bf16[32,8,2,64,128]{4,3,2,1,0:T(8,128)(2,1)} %param.9) | copy-start | bytes 25165828
  14.1 7.2 %copy-start.1 = (bf16[12,2,2,128,128]{4,3,2,1,0:T(8,128)(2,1)S(1)}, bf16[12,2,2,128,128]{4,3,2,1,0:T(8,128)(2,1)}, u32[]{:S(2)}) copy-start(bf16[12,2,2,128,128]{4,3,2,1,0:T(8,128)(2,1)} %own_left.1) | copy-start | bytes 4718596
  14.1 7.2 %copy-start.5 = (s32[12,32]{1,0:T(8,128)S(1)}, s32[12,32]{1,0:T(8,128)}, u32[]{:S(2)}) copy-start(s32[12,32]{1,0:T(8,128)} %own_table.1) | copy-start | bytes 4612
  14.1 27.4 %all-to-all-start = ((bf16[16,24,16,128]{3,2,1,0:T(8,128)(2,1)}), bf16[16,24,16,128]{3,2,1,0:T(8,128)(2,1)S(1)}, u32[]{:S(2)}, u32[]{:S(2)}) async-start(bf16[16,24,16,128]{3,2,1,0:T(8,128)(2,1)} %pick_right.1), calls=%async_computation | async-start | bytes 3145728 | tf_op jit(solution)/shard_map/all_to_all | solution.py:303
  21.3 11.6 %copy-start.6 = (s32[96]{0:T(128)S(1)}, s32[96]{0:T(128)}, u32[]{:S(2)}) copy-start(s32[96]{0:T(128)} %param.12) | copy-start | bytes 1156
  21.3 11.9 %copy-start.7 = (s32[96]{0:T(128)S(1)}, s32[96]{0:T(128)}, u32[]{:S(2)}) copy-start(s32[96]{0:T(128)} %param.13) | copy-start | bytes 1156
  21.3 20.3 %copy-start.4 = (s32[128,32]{0,1:T(8,128)S(1)}, s32[128,32]{0,1:T(8,128)}, u32[]{:S(2)}) copy-start(s32[128,32]{0,1:T(8,128)} %param.11) | copy-start | bytes 49156
  25.8 0.8 %copy-start.2 = (bf16[147,16,128]{2,1,0:T(8,128)(2,1)}, bf16[147,16,128]{2,1,0:T(8,128)(2,1)S(1)}, u32[]{:S(2)}) copy-start(bf16[147,16,128]{2,1,0:T(8,128)(2,1)S(1)} %get-tuple-element.14.home) | copy-start | bytes 1806340
  26.6 15.0 %copy-start.3 = (bf16[147,16,128]{2,1,0:T(8,128)(2,1)S(1)}, bf16[147,16,128]{2,1,0:T(8,128)(2,1)}, u32[]{:S(2)}) copy-start(bf16[147,16,128]{2,1,0:T(8,128)(2,1)} %copy-done.2) | copy-start | bytes 1806340
  26.6 15.0 %collective-permute-start.3 = (bf16[99,16,128]{2,1,0:T(8,128)(2,1)}, bf16[99,16,128]{2,1,0:T(8,128)(2,1)S(1)}, u32[]{:S(2)}, u32[]{:S(2)}) collective-permute-start(bf16[99,16,128]{2,1,0:T(8,128)(2,1)} %get-tuple-element.15), channel_id=1, source_target_pairs={{0,64},{32,96},{64,128},{96,160},{128,192},{160,224},{192,1},{224,... | collective-permute-start | bytes 1216520 | tf_op jit(solution)/shard_map/ppermute | solution.py:310
  27.3 14.2 %collective-permute-start.4 = (bf16[99,16,128]{2,1,0:T(8,128)(2,1)}, bf16[99,16,128]{2,1,0:T(8,128)(2,1)}, u32[]{:S(2)}, u32[]{:S(2)}) collective-permute-start(bf16[99,16,128]{2,1,0:T(8,128)(2,1)} %get-tuple-element.16), channel_id=1, source_target_pairs={{0,193},{32,225},{64,0},{96,32},{128,64},{160,96},{192,128},{224,1... | collective-permute-start | bytes 1216520 | tf_op jit(solution)/shard_map/ppermute | solution.py:311
  29.3 12.3 %collective-permute-start.5 = (bf16[27,16,128]{2,1,0:T(8,128)(2,1)}, bf16[27,16,128]{2,1,0:T(8,128)(2,1)S(1)}, u32[]{:S(2)}, u32[]{:S(2)}) collective-permute-start(bf16[27,16,128]{2,1,0:T(8,128)(2,1)} %get-tuple-element.17), channel_id=1, source_target_pairs={{0,128},{32,160},{64,192},{96,224},{128,1},{160,33},{192,65},{224,... | collective-permute-start | bytes 331784 | tf_op jit(solution)/shard_map/ppermute | solution.py:312
  29.3 12.3 %collective-permute-start.6 = (bf16[27,16,128]{2,1,0:T(8,128)(2,1)}, bf16[27,16,128]{2,1,0:T(8,128)(2,1)}, u32[]{:S(2)}, u32[]{:S(2)}) collective-permute-start(bf16[27,16,128]{2,1,0:T(8,128)(2,1)} %get-tuple-element.18), channel_id=1, source_target_pairs={{0,129},{32,161},{64,193},{96,225},{128,0},{160,32},{192,64},{224,... | collective-permute-start | bytes 331784 | tf_op jit(solution)/shard_map/ppermute | solution.py:313

commit v5 on v4

--- a/solution.py
+++ b/solution.py
@@ -19,37 +19,48 @@
     return pltpu.CompilerParams(vmem_limit_bytes=mebibytes * 1024 * 1024)
 
 
-def pick_right_kernel(place_ref, near_ref, cross_ref, out_ref):
-    for block in range(out_ref.shape[0]):
-        for ref, first in ((near_ref, 0), (cross_ref, 8)):
-            rows = jnp.concatenate(
-                [ref[block, j, c][None] for c in range(2) for j in range(8)], axis=0
+def pick_right_kernel(place_ref, right_ref, out_ref, rows_ref, sem):
+    copies = []
+    for part in range(4):
+        for second in range(2):
+            copy = pltpu.make_async_copy(
+                right_ref.at[pl.ds(part * 4, 4), place_ref[0], :, :, place_ref[1] ^ (2 * second)],
+                rows_ref.at[second, pl.ds(part * 4, 4)],
+                sem.at[part, second],
             )
-            rows = jnp.swapaxes(rows, 0, 1)
-            if first:
-                out_ref[block, 16:24] = rows[8:16]
-            else:
-                out_ref[block, 0:16] = rows
+            copy.start()
+            copies.append(copy)
+    for part in range(4):
+        for second in range(2):
+            copies[part * 2 + second].wait()
+        for target in range(part * 4, part * 4 + 4):
+            for second in range(2):
+                rows = jnp.concatenate(
+                    [rows_ref[second, target, j, c][None] for c in range(2) for j in range(8)],
+                    axis=0,
+                )
+                rows = jnp.swapaxes(rows, 0, 1)
+                if second:
+                    out_ref[target, 16:24] = rows[8:16]
+                else:
+                    out_ref[target, 0:16] = rows
 
 
 def pick_right(place, right_operators):
-    view = right_operators.reshape(16, 2, 8, 2, 4, 16, 128)
-    rows = lambda flip: pl.BlockSpec(
-        (8, None, 8, 2, None, 16, 128),
-        lambda i, place: (i, place[0], 0, 0, place[1] ^ flip, 0, 0),
-    )
     return pl.pallas_call(
         pick_right_kernel,
-        grid_spec=pltpu.PrefetchScalarGridSpec(
-            num_scalar_prefetch=1,
-            grid=(2,),
-            in_specs=[rows(0), rows(2)],
-            out_specs=pl.BlockSpec((8, 24, 16, 128), lambda i, place: (i, 0, 0, 0)),
-        ),
+        in_specs=[
+            pl.BlockSpec(memory_space=pltpu.SMEM), pl.BlockSpec(memory_space=pltpu.HBM)
+        ],
+        out_specs=pl.BlockSpec(memory_space=pltpu.VMEM),
         out_shape=jax.ShapeDtypeStruct((16, 24, 16, 128), BF),
-        compiler_params=params(12),
+        scratch_shapes=[
+            pltpu.VMEM((2, 16, 8, 2, 16, 128), BF),
+            pltpu.SemaphoreType.DMA((4, 2)),
+        ],
+        compiler_params=params(54),
         name="pick_right",
-    )(place, view, view)
+    )(place, right_operators.reshape(16, 2, 8, 2, 4, 16, 128))
 
 
 GROUPS = (6, 6, 6, 3, 3)
@@ -59,11 +70,10 @@
 
 
 def tiles_kernel(
-    place_ref, own_table, far_table, own_wave, far_wave, own_left, far_left,
-    home, up1, down1, up2, down2, sides, bras, kets,
+    sent, place_ref, own_table, far_table, own_wave, far_wave, own_left, far_left, *refs
 ):
+    outs, (sides, bras, kets) = refs[:-3], refs[-3:]
     z, q = place_ref[2], place_ref[3]
-    outs = (home, up1, down1, up2, down2)
     low = z < 4
 
     def wave(c, o):
@@ -81,24 +91,23 @@
             re_t, im_t = re.T, im.T
             bras[0] = jnp.concatenate([re_t, im_t], axis=1)
             bras[1] = jnp.concatenate([-im_t, re_t], axis=1)
-    spots = [z, lax.rem(z + 1, 8), lax.rem(z + 7, 8), lax.rem(z + 2, 8), lax.rem(z + 6, 8)]
-
-    upper = iota((16, 256), 0) < 8
-
-    def bra(far):
-        def block(c, spot):
-            return bras[c, pl.ds(pl.multiple_of(spot * 16, 16), 16), :]
-
-        parts = []
-        for c in range(2):
-            parts += [block(c, spot) for spot in spots[0:3]]
-            parts.append(jnp.where(upper, block(c, spots[far]), block(c, z ^ 2)))
-        return jnp.concatenate(parts, axis=0)
 
     labels = [own_table[s, q] for s in range(12)] + [far_table[s, q] for s in range(12)]
     shifts = [lax.rem(label - q + 32, 32) for label in labels]
     for half in range(2):
-        left = bra(3 + half)
+        if sent:
+            spots = [lax.rem(z + 1, 8), lax.rem(z + 7, 8), lax.rem(z + (6 if half else 2), 8)]
+        else:
+            spots = [z, z ^ 2]
+        width = 16 * len(spots)
+        left = jnp.concatenate(
+            [
+                bras[c, pl.ds(pl.multiple_of(spot * 16, 16), 16), :]
+                for c in range(2)
+                for spot in spots
+            ],
+            axis=0,
+        )
         source = far_left if half else own_left
         for s in range(12):
             operator = jnp.concatenate([source[s, 0], source[s, 1]], axis=1)
@@ -113,15 +122,16 @@
                 axis=0,
             )
         for group in range(3):
+            whole = half * 3 + group
             brackets = [
                 jnp.dot(left, kets[group * 4 + s], preferred_element_type=F32).astype(BF)
                 for s in range(4)
             ]
-            for i in range(4):
+            for i in range(len(spots)):
                 rows = jnp.concatenate(
                     [
                         brackets[s][
-                            c * 64 + i * 16 : c * 64 + i * 16 + 16,
+                            c * width + i * 16 : c * width + i * 16 + 16,
                             kind * 128 : kind * 128 + 128,
                         ][None]
                         for s in range(4)
@@ -131,13 +141,13 @@
                     axis=0,
                 )
                 rows = jnp.swapaxes(rows, 0, 1)
-                whole = half * 3 + group
-                if i < 3:
+                if sent and i == 2:
+                    outs[2 + half][group * 8 : group * 8 + 8] = rows[0:8]
+                elif i == 1 and not sent:
+                    outs[0][96 + whole * 8 : 96 + whole * 8 + 8] = rows[8:16]
+                else:
                     outs[i][whole * 16 : whole * 16 + 16] = rows
-                else:
-                    outs[3 + half][group * 8 : group * 8 + 8] = rows[0:8]
-                    home[96 + whole * 8 : 96 + whole * 8 + 8] = rows[8:16]
-    for spot, out in enumerate(outs):
+    for out, spot in zip(outs, range(1, 5) if sent else range(1)):
         count = GROUPS[spot] * 4
         offset = 12 if spot == 4 else 0
         for tile in range(3):
@@ -149,30 +159,34 @@
             out[TILES[spot] + tile] = row.astype(BF)
 
 
-def make_tiles(place, own_table, far_table, own_wave, far_wave, left_operators, far_left):
+def make_tiles(sent, place, own_table, far_table, own_wave, far_wave, left_operators, far_left):
     full = lambda shape: pl.BlockSpec(shape, lambda i, place: (0,) * len(shape))
     table = pl.BlockSpec(memory_space=pltpu.SMEM)
     operators = pl.BlockSpec(
         (12, None, 2, 128, 128), lambda i, place: (0, place[0], 0, 0, 0)
     )
+    shapes = [(n + 3, 16, 128) for n in (TILES[1:] if sent else TILES[:1])]
     return pl.pallas_call(
-        tiles_kernel,
+        functools.partial(tiles_kernel, sent),
         grid_spec=pltpu.PrefetchScalarGridSpec(
             num_scalar_prefetch=1,
             grid=(1,),
             in_specs=[
                 table, table, full((2, 3, 64, 128)), full((2, 3, 64, 128)), operators, operators
             ],
-            out_specs=[full((n + 3, 16, 128)) for n in TILES],
+            out_specs=[full(shape) for shape in shapes],
             scratch_shapes=[
                 pltpu.VMEM((3, 256, 512), BF),
                 pltpu.VMEM((2, 128, 256), BF),
                 pltpu.VMEM((12, 256, 256), BF),
             ],
         ),
-        out_shape=[jax.ShapeDtypeStruct((n + 3, 16, 128), BF) for n in TILES],
+        out_shape=[jax.ShapeDtypeStruct(shape, BF) for shape in shapes],
+        cost_estimate=pl.CostEstimate(
+            flops=1000000000, bytes_accessed=4000000, transcendentals=0
+        ),
         compiler_params=params(20),
-        name="make_tiles",
+        name="make_tiles" if sent else "make_home",
     )(place, own_table, far_table, own_wave, far_wave, left_operators, far_left)
 
 
@@ -248,11 +262,12 @@
         return jnp.where(match, jnp.concatenate(rows, axis=0), 0.0)
 
     rest = jnp.concatenate([part(0), part(1)], axis=1)
-    total = jnp.zeros((128, 384), F32)
+    pieces = []
     for _ in range(3):
-        piece = rest.astype(BF)
-        total += jnp.dot(piece, picks[...], preferred_element_type=F32)
-        rest = rest - piece.astype(F32)
+        pieces.append(rest.astype(BF))
+        rest = rest - pieces[-1].astype(F32)
+    total = jnp.dot(jnp.concatenate(pieces, axis=0), picks[...], preferred_element_type=F32)
+    total = total[0:128] + total[128:256] + total[256:384]
     for j in range(4):
         for row in range(8):
             out[row, :, j * 48 : j * 48 + 48] = total[j * 32 : j * 32 + 32, row * 48 : row * 48 + 48]
@@ -301,17 +316,22 @@
     place = jnp.stack([core, z_lo, z, q]).astype(jnp.int32)
     right = pick_right(place, right_operators)
     right = lax.all_to_all(right, "col", 0, 0, tiled=True)
-    home, up1, down1, up2, down2 = make_tiles(
-        place, left_table, far_table, own_wave, far_wave, left_operators, far_left
-    )
-    assignment, kramers_map, home = lax.optimization_barrier((assignment, kramers_map, home))
-    tiles = [
-        home,
+    up1, down1, up2, down2 = make_tiles(
+        True, place, left_table, far_table, own_wave, far_wave, left_operators, far_left
+    )
+    far_wave, assignment, kramers_map, up1 = lax.optimization_barrier(
+        (far_wave, assignment, kramers_map, up1)
+    )
+    arrived = [
         lax.ppermute(up1, line, ring(lambda z: (z + 1) % 8)),
         lax.ppermute(down1, line, ring(lambda z: (z + 7) % 8)),
         lax.ppermute(up2, line, ring(lambda z: (z + 2) % 8)),
         lax.ppermute(down2, line, ring(lambda z: (z + 6) % 8)),
     ]
+    (home,) = make_tiles(
+        False, place, left_table, far_table, own_wave, far_wave, left_operators, far_left
+    )
+    tiles = [home] + arrived
 
     held = assignment.reshape(4, 2, 12)
     held = jnp.where(core == 0, held, held[:, ::-1])

time: 75.3 us -> 72.8 us (0.967)
  waiting for transfers between devices: 7.57 us -> 2.77 us
  Pallas kernels: 9.59 us -> 14.1 us
  local copies, waits for them, and re-layouts: 6.81 us -> 4.9 us
  blocking collectives: 29.3 us -> 28.3 us
    all_to_all x1, waiting for transfers between devices: 7.55 us -> 2.75 us  [local(): right = lax.all_to_all(right, 'col', 0, 0, tiled=True)]
    pallas_call x2 -> x3, Pallas kernels: 6.65 us -> 11.3 us  [the longest x2 7.72 us: make_tiles(): pl.pallas_call(functools.partial(tiles_kernel, sent), grid_spec=pltpu.Pre...]
    unnamed x16 -> x18, local copies, waits for them, and re-layouts: 4.24 us -> 2.33 us
    all_to_all x1, blocking collectives: 29.3 us -> 28.3 us  [local(): lax.all_to_all(shares.reshape(256, 192), ('row', 'wf', 'col'), 0, 0, tile...]
  transfers between devices with their start and end apart: 8 -> 8, of which waited for: 1 -> 1; matrix products, arithmetic and copies ran while one was open for 3% -> 3% of each run, Pallas kernels for 9% -> 16%
where the time goes in v5:
time: 72.8 us; the launch traced here: 72.4 us
  blocking collectives  28.3 us (39%)
  starting transfers between devices  20.8 us (29%)
  Pallas kernels  14.1 us (19%)
  local copies, waits for them, and re-layouts  4.9 us (7%)
  waiting for transfers between devices  2.77 us (4%)
  other arithmetic  1.19 us (2%)
    all_to_all x1, blocking collectives, local(): lax.all_to_all(shares.reshape(256, 192), ('row', 'wf', 'col'), 0, 0, tile...  28.3 us
    pallas_call x2, Pallas kernels, make_tiles(): pl.pallas_call(functools.partial(tiles_kernel, sent), grid_spec=pltpu.Pre...  7.72 us
    all_to_all x1, starting transfers between devices, local(): right = lax.all_to_all(right, 'col', 0, 0, tiled=True)  6.9 us
    ppermute x1, starting transfers between devices, local(): lax.ppermute(own_wave, line, ring(lambda z: (z + 2) % 8 if z in (2, 3, 6,...  4.37 us
    ppermute x1, starting transfers between devices, local(): lax.ppermute(down2, line, ring(lambda z: (z + 6) % 8))  3.57 us
    pallas_call x1, Pallas kernels, pick_right(): pl.pallas_call(pick_right_kernel, in_specs=[pl.BlockSpec(memory_space=plt...  3.54 us
    ppermute x1, starting transfers between devices, local(): far_left = lax.ppermute(left_operators, 'row', swap)  3.24 us
    all_to_all x1, waiting for transfers between devices, local(): right = lax.all_to_all(right, 'col', 0, 0, tiled=True)  2.75 us
  transfers between devices with their start and end apart: 8, of which 1 were waited for; matrix products, arithmetic and copies ran while one was open for 3% of the time, Pallas kernels for 16%

profile of v5, /device:TPU:1, one launch (start us, length us, event | category | flops | bytes accessed | tf_op | source)
XLA Modules:
  0.0 72.4 jit_solution(12146446073644896610)
XLA Ops:
  0.0 3.2 %collective-permute-start.2 = (bf16[12,2,2,128,128]{4,3,2,1,0:T(8,128)(2,1)}, bf16[12,2,2,128,128]{4,3,2,1,0:T(8,128)(2,1)}, u32[]{:S(2)}, u32[]{:S(2)}) collective-permute-start(bf16[12,2,2,128,128]{4,3,2,1,0:T(8,128)(2,1)} %own_left.3), channel_id=1, source_target_pairs={{0,32},{32,0},{64,96},{96,64},{128,160},{160,128},{192,224},{224,1... | collective-permute-start | bytes 4718600 | tf_op jit(solution)/shard_map/ppermute | solution.py:314
  3.2 0.0 collective-permute-start
  3.2 0.8 %constant_dynamic-slice_fusion.2 = (bf16[2,1,64,128]{3,2,1,0:T(8,128)(2,1)S(1)}, bf16[2,1,64,128]{3,2,1,0:T(8,128)(2,1)S(1)}, bf16[2,1,64,128]{3,2,1,0:T(8,128)(2,1)S(1)}) fusion(bf16[2,32,64,128]{3,2,1,0:T(8,128)(2,1)} %param.7, s32[]{:T(128)S(6)} %select_n.46, s32[]{:T(128)S(6)} %select_n.50, s32[]{:T(128)S(6)} %select_n.48), kind=kLoop, calls=%fused_computation.17 | loop fusion | bytes 196620 | tf_op jit(solution)/shard_map/dynamic_slice | solution.py:308
  4.1 4.4 %collective-permute-start.1 = (bf16[2,3,64,128]{3,2,1,0:T(8,128)(2,1)S(1)}, bf16[2,3,64,128]{3,2,1,0:T(8,128)(2,1)S(1)}, u32[]{:S(2)}, u32[]{:S(2)}) collective-permute-start(bf16[2,3,64,128]{3,2,1,0:T(8,128)(2,1)S(1)} %pad_maximum_fusion.own_wave), channel_id=1, source_target_pairs={{0,129},{32,161},{64,193},{96,225},{128,1},{160,33},{192,65},{224,... | collective-permute-start | bytes 294920 | tf_op jit(solution)/shard_map/ppermute | solution.py:310
  8.4 0.6 pad_add_fusion.place_ref
  9.0 3.5 %pick_right.1 = bf16[16,24,16,128]{3,2,1,0:T(8,128)(2,1)} custom-call(s32[4]{0:T(128)} %pad_add_fusion.place_ref, bf16[16,2,8,2,4,16,128]{6,5,4,3,2,1,0:T(8,128)(2,1)} %bitcast.22), custom_call_target="tpu_custom_call" | custom-call | tf_op jit(solution)/shard_map/pick_right/pallas_call | solution.py:50
  12.6 0.0 copy-start
  12.6 0.0 copy-start.5
  12.6 0.0 copy-start.6
  12.6 6.9 %all-to-all-start = ((bf16[16,24,16,128]{3,2,1,0:T(8,128)(2,1)}), bf16[16,24,16,128]{3,2,1,0:T(8,128)(2,1)S(1)}, u32[]{:S(2)}, u32[]{:S(2)}) async-start(bf16[16,24,16,128]{3,2,1,0:T(8,128)(2,1)} %pick_right.1), calls=%async_computation | async-start | bytes 3145728 | tf_op jit(solution)/shard_map/all_to_all | solution.py:318
  19.6 0.1 broadcast_in_dim.2
  19.6 0.1 reshape.129.sign
  19.8 0.0 copy-start.7
  19.8 0.0 copy-start.8
  19.8 0.0 collective-permute-done.far_table
  19.8 0.0 collective-permute-done.1.far_wave
  19.8 0.0 copy-start.2
  19.8 0.0 collective-permute-done.2.far_left
  19.8 4.3 %make_tiles.1 = (bf16[99,16,128]{2,1,0:T(8,128)(2,1)}, bf16[99,16,128]{2,1,0:T(8,128)(2,1)}, bf16[27,16,128]{2,1,0:T(8,128)(2,1)}, bf16[27,16,128]{2,1,0:T(8,128)(2,1)}) custom-call(s32[4]{0:T(128)S(1)} %copy-done.6, s32[12,32]{1,0:T(8,128)S(1)} %copy-done.5, s32[12,32]{1,0:T(8,128)S(1)} %collective-permute-done.far_table, ...), custom_call_target="tpu_custom_call" | custom-call | flops 1000000000 | bytes 4000000 | tf_op jit(solution)/shard_map/make_tiles/pallas_call | solution.py:169
  24.2 0.7 %collective-permute-start.3 = (bf16[99,16,128]{2,1,0:T(8,128)(2,1)}, bf16[99,16,128]{2,1,0:T(8,128)(2,1)S(1)}, u32[]{:S(2)}, u32[]{:S(2)}) collective-permute-start(bf16[99,16,128]{2,1,0:T(8,128)(2,1)} %get-tuple-element.15), channel_id=1, source_target_pairs={{0,64},{32,96},{64,128},{96,160},{128,192},{160,224},{192,1},{224,... | collective-permute-start | bytes 1216520 | tf_op jit(solution)/shard_map/ppermute | solution.py:326
  24.9 1.9 %collective-permute-start.4 = (bf16[99,16,128]{2,1,0:T(8,128)(2,1)}, bf16[99,16,128]{2,1,0:T(8,128)(2,1)}, u32[]{:S(2)}, u32[]{:S(2)}) collective-permute-start(bf16[99,16,128]{2,1,0:T(8,128)(2,1)} %get-tuple-element.16), channel_id=1, source_target_pairs={{0,193},{32,225},{64,0},{96,32},{128,64},{160,96},{192,128},{224,1... | collective-permute-start | bytes 1216520 | tf_op jit(solution)/shard_map/ppermute | solution.py:327
  26.9 0.0 collective-permute-start.5
  26.9 3.6 %collective-permute-start.6 = (bf16[27,16,128]{2,1,0:T(8,128)(2,1)}, bf16[27,16,128]{2,1,0:T(8,128)(2,1)S(1)}, u32[]{:S(2)}, u32[]{:S(2)}) collective-permute-start(bf16[27,16,128]{2,1,0:T(8,128)(2,1)} %get-tuple-element.18), channel_id=1, source_target_pairs={{0,129},{32,161},{64,193},{96,225},{128,0},{160,32},{192,64},{224,... | collective-permute-start | bytes 331784 | tf_op jit(solution)/shard_map/ppermute | solution.py:329
  30.4 0.1 reshape.128
  30.6 0.1 mul.48
  30.7 0.1 stack.36
  30.8 0.1 fusion.2
  30.9 0.1 iota_add_fusion
  31.0 0.1 fusion.1
  31.1 0.1 add.152.slot_key
  31.2 0.1 add.148.real_key
  31.3 0.1 sub.34.imag_key
  31.4 0.2 make_picks.1.picks
  31.6 0.0 copy-start.1
  31.6 1.4 %copy-done.1 = bf16[12,2,2,128,128]{4,3,2,1,0:T(8,128)(2,1)S(1)} copy-done((bf16[12,2,2,128,128]{4,3,2,1,0:T(8,128)(2,1)S(1)}, bf16[12,2,2,128,128]{4,3,2,1,0:T(8,128)(2,1)}, u32[]{:S(2)}) %copy-start.1) | copy-done | bytes 1572888
  33.0 0.9 %copy-done.3 = bf16[2,3,64,128]{3,2,1,0:T(8,128)(2,1)S(1)} copy-done((bf16[2,3,64,128]{3,2,1,0:T(8,128)(2,1)S(1)}, bf16[2,3,64,128]{3,2,1,0:T(8,128)(2,1)}, u32[]{:S(2)}) %copy-start.3) | copy-done | bytes 98328
  33.9 3.4 %make_home.1.home = bf16[147,16,128]{2,1,0:T(8,128)(2,1)S(1)} custom-call(s32[4]{0:T(128)S(1)} %copy-done.6, s32[12,32]{1,0:T(8,128)S(1)} %copy-done.5, s32[12,32]{1,0:T(8,128)S(1)} %collective-permute-done.far_table, bf16[2,3,64,128]{3,2,1,0:T(8,128)(2,1)S(1)} %pad_maximum_fusion.own_wave, bf16[2,3,64,128]{3,2,1,0:T(8,128)(2,1)S(1)} %copy-done.3, ...), custom_call_target="tpu_custom_call" | custom-call | flops 1000000000 | bytes 4000000 | tf_op jit(solution)/shard_map/make_home/pallas_call | solution.py:169
  37.3 2.7 %all-to-all-done.right = bf16[16,24,16,128]{3,2,1,0:T(8,128)(2,1)S(1)} async-done(((bf16[16,24,16,128]{3,2,1,0:T(8,128)(2,1)}), bf16[16,24,16,128]{3,2,1,0:T(8,128)(2,1)S(1)}, u32[]{:S(2)}, u32[]{:S(2)}) %all-to-all-start) | async-done | bytes 1572896 | tf_op jit(solution)/shard_map/all_to_all | solution.py:318
  40.0 0.0 collective-permute-done.5.up2
  40.0 0.0 collective-permute-done.6.down2
  40.0 0.0 collective-permute-done.3.up1
  40.0 0.0 collective-permute-done.4.down1
  40.1 2.7 %contract.1 = f32[8,32,192]{2,1,0:T(8,128)S(1)} custom-call(s32[4]{0:T(128)S(1)} %copy-done.6, bf16[147,16,128]{2,1,0:T(8,128)(2,1)S(1)} %make_home.1.home, bf16[99,16,128]{2,1,0:T(8,128)(2,1)S(1)} %collective-permute-done.3.up1, bf16[99,16,128]{2,1,0:T(8,128)(2,1)} %collective-permute-done.4.down1, bf16[27,16,128]{2,1,0:T(8,128)(2,1)S(1)} %collective-permute-done.5.up2, ...), custom_call_target="tpu_custom_call" | custom-call | tf_op jit(solution)/shard_map/contract/pallas_call | solution.py:278
  42.8 0.3 copy.17
  43.1 28.3 %all_to_all.14 = f32[256,1,192]{2,1,0:T(1,128)S(1)} all-to-all(f32[256,1,192]{2,1,0:T(1,128)S(1)} %copy.17), channel_id=1, replica_groups=mesh['row'=8,'col'=16,'wf'=2] {'row','wf','col'}, dimensions={0} | all-to-all | bytes 393216 | tf_op jit(solution)/shard_map/all_to_all | solution.py:351
  71.4 0.3 reduce_sum.9
  71.7 0.1 reshape.130
  71.8 0.6 copy.18
  (23 shorter events, 0.2 us)
Async XLA Ops:
  0.0 19.8 %collective-permute-start.2 = (bf16[12,2,2,128,128]{4,3,2,1,0:T(8,128)(2,1)}, bf16[12,2,2,128,128]{4,3,2,1,0:T(8,128)(2,1)}, u32[]{:S(2)}, u32[]{:S(2)}) collective-permute-start(bf16[12,2,2,128,128]{4,3,2,1,0:T(8,128)(2,1)} %own_left.3), channel_id=1, source_target_pairs={{0,32},{32,0},{64,96},{96,64},{128,160},{160,128},{192,224},{224,1... | collective-permute-start | bytes 4718600 | tf_op jit(solution)/shard_map/ppermute | solution.py:314
  3.2 16.5 %collective-permute-start = (s32[12,32]{1,0:T(8,128)}, s32[12,32]{1,0:T(8,128)S(1)}, u32[]{:S(2)}, u32[]{:S(2)}) collective-permute-start(s32[12,32]{1,0:T(8,128)} %own_table.3), channel_id=1, source_target_pairs={{0,32},{32,0},{64,96},{96,64},{128,160},{160,128},{192,224},{224,1... | collective-permute-start | bytes 4616 | tf_op jit(solution)/shard_map/ppermute | solution.py:315
  4.1 15.7 %collective-permute-start.1 = (bf16[2,3,64,128]{3,2,1,0:T(8,128)(2,1)S(1)}, bf16[2,3,64,128]{3,2,1,0:T(8,128)(2,1)S(1)}, u32[]{:S(2)}, u32[]{:S(2)}) collective-permute-start(bf16[2,3,64,128]{3,2,1,0:T(8,128)(2,1)S(1)} %pad_maximum_fusion.own_wave), channel_id=1, source_target_pairs={{0,129},{32,161},{64,193},{96,225},{128,1},{160,33},{192,65},{224,... | collective-permute-start | bytes 294920 | tf_op jit(solution)/shard_map/ppermute | solution.py:310
  12.6 7.2 %copy-start = (bf16[12,2,2,128,128]{4,3,2,1,0:T(8,128)(2,1)S(1)}, bf16[12,2,2,128,128]{4,3,2,1,0:T(8,128)(2,1)}, u32[]{:S(2)}) copy-start(bf16[12,2,2,128,128]{4,3,2,1,0:T(8,128)(2,1)} %own_left.3) | copy-start | bytes 4718596
  12.6 7.2 %copy-start.5 = (s32[12,32]{1,0:T(8,128)S(1)}, s32[12,32]{1,0:T(8,128)}, u32[]{:S(2)}) copy-start(s32[12,32]{1,0:T(8,128)} %own_table.3) | copy-start | bytes 4612
  12.6 7.2 %copy-start.6 = (s32[4]{0:T(128)S(1)}, s32[4]{0:T(128)}, u32[]{:S(2)}) copy-start(s32[4]{0:T(128)} %pad_add_fusion.place_ref) | copy-start | bytes 52
  12.6 27.4 %all-to-all-start = ((bf16[16,24,16,128]{3,2,1,0:T(8,128)(2,1)}), bf16[16,24,16,128]{3,2,1,0:T(8,128)(2,1)S(1)}, u32[]{:S(2)}, u32[]{:S(2)}) async-start(bf16[16,24,16,128]{3,2,1,0:T(8,128)(2,1)} %pick_right.1), calls=%async_computation | async-start | bytes 3145728 | tf_op jit(solution)/shard_map/all_to_all | solution.py:318
  19.8 10.7 %copy-start.7 = (s32[96]{0:T(128)S(1)}, s32[96]{0:T(128)}, u32[]{:S(2)}) copy-start(s32[96]{0:T(128)} %param.12) | copy-start | bytes 1156
  19.8 11.0 %copy-start.8 = (s32[96]{0:T(128)S(1)}, s32[96]{0:T(128)}, u32[]{:S(2)}) copy-start(s32[96]{0:T(128)} %param.13) | copy-start | bytes 1156
  19.8 4.4 %copy-start.2 = (bf16[2,3,64,128]{3,2,1,0:T(8,128)(2,1)}, bf16[2,3,64,128]{3,2,1,0:T(8,128)(2,1)S(1)}, u32[]{:S(2)}) copy-start(bf16[2,3,64,128]{3,2,1,0:T(8,128)(2,1)S(1)} %collective-permute-done.1.far_wave) | copy-start | bytes 294916
  24.2 15.9 %collective-permute-start.3 = (bf16[99,16,128]{2,1,0:T(8,128)(2,1)}, bf16[99,16,128]{2,1,0:T(8,128)(2,1)S(1)}, u32[]{:S(2)}, u32[]{:S(2)}) collective-permute-start(bf16[99,16,128]{2,1,0:T(8,128)(2,1)} %get-tuple-element.15), channel_id=1, source_target_pairs={{0,64},{32,96},{64,128},{96,160},{128,192},{160,224},{192,1},{224,... | collective-permute-start | bytes 1216520 | tf_op jit(solution)/shard_map/ppermute | solution.py:326
  24.9 15.1 %collective-permute-start.4 = (bf16[99,16,128]{2,1,0:T(8,128)(2,1)}, bf16[99,16,128]{2,1,0:T(8,128)(2,1)}, u32[]{:S(2)}, u32[]{:S(2)}) collective-permute-start(bf16[99,16,128]{2,1,0:T(8,128)(2,1)} %get-tuple-element.16), channel_id=1, source_target_pairs={{0,193},{32,225},{64,0},{96,32},{128,64},{160,96},{192,128},{224,1... | collective-permute-start | bytes 1216520 | tf_op jit(solution)/shard_map/ppermute | solution.py:327
  26.9 13.2 %collective-permute-start.5 = (bf16[27,16,128]{2,1,0:T(8,128)(2,1)}, bf16[27,16,128]{2,1,0:T(8,128)(2,1)S(1)}, u32[]{:S(2)}, u32[]{:S(2)}) collective-permute-start(bf16[27,16,128]{2,1,0:T(8,128)(2,1)} %get-tuple-element.17), channel_id=1, source_target_pairs={{0,128},{32,160},{64,192},{96,224},{128,1},{160,33},{192,65},{224,... | collective-permute-start | bytes 331784 | tf_op jit(solution)/shard_map/ppermute | solution.py:328
  26.9 13.2 %collective-permute-start.6 = (bf16[27,16,128]{2,1,0:T(8,128)(2,1)}, bf16[27,16,128]{2,1,0:T(8,128)(2,1)S(1)}, u32[]{:S(2)}, u32[]{:S(2)}) collective-permute-start(bf16[27,16,128]{2,1,0:T(8,128)(2,1)} %get-tuple-element.18), channel_id=1, source_target_pairs={{0,129},{32,161},{64,193},{96,225},{128,0},{160,32},{192,64},{224,... | collective-permute-start | bytes 331784 | tf_op jit(solution)/shard_map/ppermute | solution.py:329
  31.6 1.4 %copy-start.1 = (bf16[12,2,2,128,128]{4,3,2,1,0:T(8,128)(2,1)S(1)}, bf16[12,2,2,128,128]{4,3,2,1,0:T(8,128)(2,1)}, u32[]{:S(2)}) copy-start(bf16[12,2,2,128,128]{4,3,2,1,0:T(8,128)(2,1)} %own_left.3) | copy-start | bytes 4718596
  33.0 0.9 %copy-start.3 = (bf16[2,3,64,128]{3,2,1,0:T(8,128)(2,1)S(1)}, bf16[2,3,64,128]{3,2,1,0:T(8,128)(2,1)}, u32[]{:S(2)}) copy-start(bf16[2,3,64,128]{3,2,1,0:T(8,128)(2,1)} %copy-done.2) | copy-start | bytes 294916
  33.9 6.2 %copy-start.4 = (s32[128,32]{0,1:T(8,128)S(1)}, s32[128,32]{0,1:T(8,128)}, u32[]{:S(2)}) copy-start(s32[128,32]{0,1:T(8,128)} %param.11) | copy-start | bytes 49156

commit v6 on v5

--- a/solution.py
+++ b/solution.py
@@ -15,16 +15,22 @@
     return lax.broadcasted_iota(jnp.int32, shape, axis)
 
 
+def where():
+    row, col, wf = lax.axis_index("row"), lax.axis_index("col"), lax.axis_index("wf")
+    return row & 1, row >> 1, wf * 4 + (row >> 1), 2 * col + (row & 1)
+
+
 def params(mebibytes):
     return pltpu.CompilerParams(vmem_limit_bytes=mebibytes * 1024 * 1024)
 
 
-def pick_right_kernel(place_ref, right_ref, out_ref, rows_ref, sem):
+def pick_right_kernel(right_ref, out_ref, rows_ref, sem):
+    core, z_lo, _, _ = where()
     copies = []
     for part in range(4):
         for second in range(2):
             copy = pltpu.make_async_copy(
-                right_ref.at[pl.ds(part * 4, 4), place_ref[0], :, :, place_ref[1] ^ (2 * second)],
+                right_ref.at[pl.ds(part * 4, 4), core, :, :, z_lo ^ (2 * second)],
                 rows_ref.at[second, pl.ds(part * 4, 4)],
                 sem.at[part, second],
             )
@@ -46,12 +52,10 @@
                     out_ref[target, 0:16] = rows
 
 
-def pick_right(place, right_operators):
+def pick_right(right_operators):
     return pl.pallas_call(
         pick_right_kernel,
-        in_specs=[
-            pl.BlockSpec(memory_space=pltpu.SMEM), pl.BlockSpec(memory_space=pltpu.HBM)
-        ],
+        in_specs=[pl.BlockSpec(memory_space=pltpu.HBM)],
         out_specs=pl.BlockSpec(memory_space=pltpu.VMEM),
         out_shape=jax.ShapeDtypeStruct((16, 24, 16, 128), BF),
         scratch_shapes=[
@@ -60,7 +64,7 @@
         ],
         compiler_params=params(54),
         name="pick_right",
-    )(place, right_operators.reshape(16, 2, 8, 2, 4, 16, 128))
+    )(right_operators.reshape(16, 2, 8, 2, 4, 16, 128))
 
 
 GROUPS = (6, 6, 6, 3, 3)
@@ -70,11 +74,17 @@
 
 
 def tiles_kernel(
-    sent, place_ref, own_table, far_table, own_wave, far_wave, own_left, far_left, *refs
+    sent, own_table_ref, far_table_ref, own_wave, far_wave, own_left, far_left, *refs
 ):
-    outs, (sides, bras, kets) = refs[:-3], refs[-3:]
-    z, q = place_ref[2], place_ref[3]
+    outs, (sides, bras, kets, own_table, far_table, sem) = refs[:-6], refs[-6:]
+    core, _, z, q = where()
     low = z < 4
+    tables = [
+        pltpu.make_async_copy(own_table_ref, own_table, sem.at[0]),
+        pltpu.make_async_copy(far_table_ref, far_table, sem.at[1]),
+    ]
+    for table in tables:
+        table.start()
 
     def wave(c, o):
         mine, other = own_wave[c, o], far_wave[c, o]
@@ -92,6 +102,8 @@
             bras[0] = jnp.concatenate([re_t, im_t], axis=1)
             bras[1] = jnp.concatenate([-im_t, re_t], axis=1)
 
+    for table in tables:
+        table.wait()
     labels = [own_table[s, q] for s in range(12)] + [far_table[s, q] for s in range(12)]
     shifts = [lax.rem(label - q + 32, 32) for label in labels]
     for half in range(2):
@@ -110,7 +122,7 @@
         )
         source = far_left if half else own_left
         for s in range(12):
-            operator = jnp.concatenate([source[s, 0], source[s, 1]], axis=1)
+            operator = jnp.concatenate([source[s, core, 0], source[s, core, 1]], axis=1)
             turned = jnp.dot(
                 operator, sides[shifts[half * 12 + s]], preferred_element_type=F32
             ).astype(BF)
@@ -159,35 +171,28 @@
             out[TILES[spot] + tile] = row.astype(BF)
 
 
-def make_tiles(sent, place, own_table, far_table, own_wave, far_wave, left_operators, far_left):
-    full = lambda shape: pl.BlockSpec(shape, lambda i, place: (0,) * len(shape))
-    table = pl.BlockSpec(memory_space=pltpu.SMEM)
-    operators = pl.BlockSpec(
-        (12, None, 2, 128, 128), lambda i, place: (0, place[0], 0, 0, 0)
-    )
+def make_tiles(sent, own_table, far_table, own_wave, far_wave, left_operators, far_left):
+    anywhere, whole = pl.BlockSpec(memory_space=pl.ANY), pl.BlockSpec(memory_space=pltpu.VMEM)
     shapes = [(n + 3, 16, 128) for n in (TILES[1:] if sent else TILES[:1])]
     return pl.pallas_call(
         functools.partial(tiles_kernel, sent),
-        grid_spec=pltpu.PrefetchScalarGridSpec(
-            num_scalar_prefetch=1,
-            grid=(1,),
-            in_specs=[
-                table, table, full((2, 3, 64, 128)), full((2, 3, 64, 128)), operators, operators
-            ],
-            out_specs=[full(shape) for shape in shapes],
-            scratch_shapes=[
-                pltpu.VMEM((3, 256, 512), BF),
-                pltpu.VMEM((2, 128, 256), BF),
-                pltpu.VMEM((12, 256, 256), BF),
-            ],
-        ),
+        in_specs=[anywhere] * 2 + [whole] * 4,
+        out_specs=[whole] * len(shapes),
         out_shape=[jax.ShapeDtypeStruct(shape, BF) for shape in shapes],
+        scratch_shapes=[
+            pltpu.VMEM((3, 256, 512), BF),
+            pltpu.VMEM((2, 128, 256), BF),
+            pltpu.VMEM((12, 256, 256), BF),
+            pltpu.SMEM((12, 32), jnp.int32),
+            pltpu.SMEM((12, 32), jnp.int32),
+            pltpu.SemaphoreType.DMA((2,)),
+        ],
         cost_estimate=pl.CostEstimate(
             flops=1000000000, bytes_accessed=4000000, transcendentals=0
         ),
         compiler_params=params(20),
         name="make_tiles" if sent else "make_home",
-    )(place, own_table, far_table, own_wave, far_wave, left_operators, far_left)
+    )(own_table, far_table, own_wave, far_wave, left_operators, far_left)
 
 
 def picks_kernel(slot_key, real_key, imag_key, sign, out):
@@ -205,7 +210,7 @@
 
 
 def contract_kernel(
-    place_ref, home, up1, down1, up2, down2, right, right_table, picks, out, paired_ref
+    home, up1, down1, up2, down2, right, right_table, picks, out, paired_ref
 ):
     arrays = (home, up1, down1, up2, down2)
     zero = jnp.zeros((96, 128), BF)
@@ -246,7 +251,7 @@
     )
     row = iota((128, 128), 0)
     j = (row % 16) * 8 + (row // 16 % 2) * 4 + row // 32
-    labels = right_table[pl.ds(place_ref[3], 1), :].astype(F32)
+    labels = right_table[pl.ds(where()[3], 1), :].astype(F32)
     right_label = jnp.sum(jnp.where(iota((128, 128), 1) == j, labels, 0.0), axis=1, keepdims=True)
     match = right_label == slot_label
 
@@ -273,17 +278,17 @@
             out[row, :, j * 48 : j * 48 + 48] = total[j * 32 : j * 32 + 32, row * 48 : row * 48 + 48]
 
 
-def contract(place, tiles, right, right_table, picks):
+def contract(tiles, right, right_table, picks):
     whole = pl.BlockSpec(memory_space=pltpu.VMEM)
     return pl.pallas_call(
         contract_kernel,
-        in_specs=[pl.BlockSpec(memory_space=pltpu.SMEM)] + [whole] * 8,
+        in_specs=[whole] * 8,
         out_specs=whole,
         out_shape=jax.ShapeDtypeStruct((8, 32, 192), F32),
         scratch_shapes=[pltpu.VMEM((3, 256, 128), F32)],
         compiler_params=params(16),
         name="contract",
-    )(place, *tiles, right, right_table, picks)
+    )(*tiles, right, right_table, picks)
 
 
 def ring(step):
@@ -299,11 +304,7 @@
     wave_blocks, left_operators, right_operators, left_table, right_table, assignment, kramers_map
 ):
     line = ("row", "wf")
-    row, col, wf = lax.axis_index("row"), lax.axis_index("col"), lax.axis_index("wf")
-    core, z_lo = row % 2, row // 2
-    z = wf * 4 + z_lo
-    q = 2 * col + core
-
+    core, z_lo, _, q = where()
     own_wave = jnp.concatenate(
         [lax.dynamic_slice_in_dim(wave_blocks, (q + o) % 32, 1, 1) for o in range(3)], axis=1
     )
@@ -313,11 +314,10 @@
     swap = [(i, i ^ 1) for i in range(8)]
     far_left = lax.ppermute(left_operators, "row", swap)
     far_table = lax.ppermute(left_table, "row", swap)
-    place = jnp.stack([core, z_lo, z, q]).astype(jnp.int32)
-    right = pick_right(place, right_operators)
+    right = pick_right(right_operators)
     right = lax.all_to_all(right, "col", 0, 0, tiled=True)
     up1, down1, up2, down2 = make_tiles(
-        True, place, left_table, far_table, own_wave, far_wave, left_operators, far_left
+        True, left_table, far_table, own_wave, far_wave, left_operators, far_left
     )
     far_wave, assignment, kramers_map, up1 = lax.optimization_barrier(
         (far_wave, assignment, kramers_map, up1)
@@ -329,7 +329,7 @@
         lax.ppermute(down2, line, ring(lambda z: (z + 6) % 8)),
     ]
     (home,) = make_tiles(
-        False, place, left_table, far_table, own_wave, far_wave, left_operators, far_left
+        False, left_table, far_table, own_wave, far_wave, left_operators, far_left
     )
     tiles = [home] + arrived
 
@@ -347,7 +347,7 @@
     sign = jnp.broadcast_to((2 * part - 1).astype(F32), (8, 2, 2, 12)).reshape(1, 384)
 
     picks = make_picks([slot_key, real_key, imag_key, sign])
-    shares = contract(place, tiles, right, right_table.T, picks)
+    shares = contract(tiles, right, right_table.T, picks)
     shares = lax.all_to_all(
         shares.reshape(256, 192), ("row", "wf", "col"), 0, 0, tiled=True
     )

time: 72.8 us -> 72 us (0.989)
  waiting for transfers between devices: 2.77 us -> 1.97 us
    all_to_all x1, waiting for transfers between devices: 2.75 us -> 1.96 us  [local(): right = lax.all_to_all(right, 'col', 0, 0, tiled=True)]
    unnamed x18 -> x16, local copies, waits for them, and re-layouts: 2.33 us -> 2.33 us
where the time goes in v6:
time: 72 us; the launch traced here: 71.5 us
  blocking collectives  28.8 us (40%)
  starting transfers between devices  20.8 us (29%)
  Pallas kernels  14.2 us (20%)
  local copies, waits for them, and re-layouts  4.9 us (7%)
  waiting for transfers between devices  1.97 us (3%)
    all_to_all x1, blocking collectives, local(): lax.all_to_all(shares.reshape(256, 192), ('row', 'wf', 'col'), 0, 0, tile...  28.8 us
    pallas_call x2, Pallas kernels, make_tiles(): pl.pallas_call(functools.partial(tiles_kernel, sent), in_specs=[anywhere]...  8.43 us
    all_to_all x1, starting transfers between devices, local(): right = lax.all_to_all(right, 'col', 0, 0, tiled=True)  6.9 us
    ppermute x1, starting transfers between devices, local(): lax.ppermute(own_wave, line, ring(lambda z: (z + 2) % 8 if z in (2, 3, 6,...  4.37 us
    ppermute x1, starting transfers between devices, local(): lax.ppermute(down2, line, ring(lambda z: (z + 6) % 8))  3.57 us
    ppermute x1, starting transfers between devices, local(): far_left = lax.ppermute(left_operators, 'row', swap)  3.24 us
    pallas_call x1, Pallas kernels, pick_right(): pl.pallas_call(pick_right_kernel, in_specs=[pl.BlockSpec(memory_space=plt...  2.87 us
    pallas_call x1, Pallas kernels, contract(): pl.pallas_call(contract_kernel, in_specs=[whole] * 8, out_specs=whole, ou...  2.7 us
  transfers between devices with their start and end apart: 8, of which 1 were waited for; matrix products, arithmetic and copies ran while one was open for 3% of the time, Pallas kernels for 16%

profile of v6, /device:TPU:1, one launch (start us, length us, event | category | flops | bytes accessed | tf_op | source)
XLA Modules:
  0.0 71.5 jit_solution(2133347833873398674)
XLA Ops:
  0.0 3.2 %collective-permute-start.2 = (bf16[12,2,2,128,128]{4,3,2,1,0:T(8,128)(2,1)}, bf16[12,2,2,128,128]{4,3,2,1,0:T(8,128)(2,1)}, u32[]{:S(2)}, u32[]{:S(2)}) collective-permute-start(bf16[12,2,2,128,128]{4,3,2,1,0:T(8,128)(2,1)} %own_left.3), channel_id=1, source_target_pairs={{0,32},{32,0},{64,96},{96,64},{128,160},{160,128},{192,224},{224,1... | collective-permute-start | bytes 4718600 | tf_op jit(solution)/shard_map/ppermute | solution.py:315
  3.2 0.0 collective-permute-start
  3.2 0.8 %constant_dynamic-slice_fusion.2 = (bf16[2,1,64,128]{3,2,1,0:T(8,128)(2,1)S(1)}, bf16[2,1,64,128]{3,2,1,0:T(8,128)(2,1)S(1)}, bf16[2,1,64,128]{3,2,1,0:T(8,128)(2,1)S(1)}) fusion(bf16[2,32,64,128]{3,2,1,0:T(8,128)(2,1)} %param.7, s32[]{:T(128)S(6)} %select_n.36, s32[]{:T(128)S(6)} %select_n.40, s32[]{:T(128)S(6)} %select_n.38), kind=kLoop, calls=%fused_computation.17 | loop fusion | bytes 196620 | tf_op jit(solution)/shard_map/dynamic_slice | solution.py:309
  4.1 4.4 %collective-permute-start.1 = (bf16[2,3,64,128]{3,2,1,0:T(8,128)(2,1)S(1)}, bf16[2,3,64,128]{3,2,1,0:T(8,128)(2,1)S(1)}, u32[]{:S(2)}, u32[]{:S(2)}) collective-permute-start(bf16[2,3,64,128]{3,2,1,0:T(8,128)(2,1)S(1)} %pad_maximum_fusion.own_wave), channel_id=1, source_target_pairs={{0,129},{32,161},{64,193},{96,225},{128,1},{160,33},{192,65},{224,... | collective-permute-start | bytes 294920 | tf_op jit(solution)/shard_map/ppermute | solution.py:311
  8.4 2.9 %pick_right.1 = bf16[16,24,16,128]{3,2,1,0:T(8,128)(2,1)} custom-call(bf16[16,2,8,2,4,16,128]{6,5,4,3,2,1,0:T(8,128)(2,1)} %bitcast.18), custom_call_target="tpu_custom_call" | custom-call | tf_op jit(solution)/shard_map/pick_right/pallas_call | solution.py:56
  11.3 0.0 copy-start
  11.3 0.0 copy-start.5
  11.3 6.9 %all-to-all-start = ((bf16[16,24,16,128]{3,2,1,0:T(8,128)(2,1)}), bf16[16,24,16,128]{3,2,1,0:T(8,128)(2,1)S(1)}, u32[]{:S(2)}, u32[]{:S(2)}) async-start(bf16[16,24,16,128]{3,2,1,0:T(8,128)(2,1)} %pick_right.1), calls=%async_computation | async-start | bytes 3145728 | tf_op jit(solution)/shard_map/all_to_all | solution.py:318
  18.3 0.1 broadcast_in_dim.2
  18.4 0.1 reshape.129.sign
  18.5 0.0 copy-start.6
  18.5 0.0 copy-start.7
  18.5 0.0 collective-permute-done.far_table_ref
  18.5 0.0 collective-permute-done.1.far_wave
  18.5 0.0 collective-permute-done.2.far_left
  18.6 4.7 %make_tiles.1 = (bf16[99,16,128]{2,1,0:T(8,128)(2,1)}, bf16[99,16,128]{2,1,0:T(8,128)(2,1)}, bf16[27,16,128]{2,1,0:T(8,128)(2,1)}, bf16[27,16,128]{2,1,0:T(8,128)(2,1)}) custom-call(s32[12,32]{1,0:T(8,128)S(1)} %copy-done.5, s32[12,32]{1,0:T(8,128)S(1)} %collective-permute-done.far_table_ref, bf16[2,3,64,128]{3,2,1,0:T(8,128)(2,1)S(1)} %pad_maximum_fusion.own_wave, ...), custom_call_target="tpu_custom_call" | custom-call | flops 1000000000 | bytes 4000000 | tf_op jit(solution)/shard_map/make_tiles/pallas_call | solution.py:177
  23.3 0.0 copy-done.2
  23.3 0.8 %collective-permute-start.3 = (bf16[99,16,128]{2,1,0:T(8,128)(2,1)}, bf16[99,16,128]{2,1,0:T(8,128)(2,1)S(1)}, u32[]{:S(2)}, u32[]{:S(2)}) collective-permute-start(bf16[99,16,128]{2,1,0:T(8,128)(2,1)} %get-tuple-element.15), channel_id=1, source_target_pairs={{0,64},{32,96},{64,128},{96,160},{128,192},{160,224},{192,1},{224,... | collective-permute-start | bytes 1216520 | tf_op jit(solution)/shard_map/ppermute | solution.py:326
  24.1 1.9 %collective-permute-start.4 = (bf16[99,16,128]{2,1,0:T(8,128)(2,1)}, bf16[99,16,128]{2,1,0:T(8,128)(2,1)}, u32[]{:S(2)}, u32[]{:S(2)}) collective-permute-start(bf16[99,16,128]{2,1,0:T(8,128)(2,1)} %get-tuple-element.16), channel_id=1, source_target_pairs={{0,193},{32,225},{64,0},{96,32},{128,64},{160,96},{192,128},{224,1... | collective-permute-start | bytes 1216520 | tf_op jit(solution)/shard_map/ppermute | solution.py:327
  26.0 0.0 collective-permute-start.5
  26.0 3.6 %collective-permute-start.6 = (bf16[27,16,128]{2,1,0:T(8,128)(2,1)}, bf16[27,16,128]{2,1,0:T(8,128)(2,1)S(1)}, u32[]{:S(2)}, u32[]{:S(2)}) collective-permute-start(bf16[27,16,128]{2,1,0:T(8,128)(2,1)} %get-tuple-element.18), channel_id=1, source_target_pairs={{0,129},{32,161},{64,193},{96,225},{128,0},{160,32},{192,64},{224,... | collective-permute-start | bytes 331784 | tf_op jit(solution)/shard_map/ppermute | solution.py:329
  29.6 0.0 copy-done.6
  29.6 0.1 reshape.128
  29.8 0.1 mul.44
  29.9 0.0 copy-done.7
  29.9 0.1 stack.16
  30.0 0.1 fusion.2
  30.1 0.1 iota_add_fusion
  30.2 0.1 fusion.1
  30.3 0.1 add.143.slot_key
  30.4 0.1 add.139.real_key
  30.5 0.1 sub.29.imag_key
  30.6 0.2 make_picks.1.picks
  30.8 0.0 copy-start.1
  30.8 1.4 %copy-done.1 = bf16[12,2,2,128,128]{4,3,2,1,0:T(8,128)(2,1)S(1)} copy-done((bf16[12,2,2,128,128]{4,3,2,1,0:T(8,128)(2,1)S(1)}, bf16[12,2,2,128,128]{4,3,2,1,0:T(8,128)(2,1)}, u32[]{:S(2)}) %copy-start.1) | copy-done | bytes 1572888
  32.2 0.9 %copy-done.3 = bf16[2,3,64,128]{3,2,1,0:T(8,128)(2,1)S(1)} copy-done((bf16[2,3,64,128]{3,2,1,0:T(8,128)(2,1)S(1)}, bf16[2,3,64,128]{3,2,1,0:T(8,128)(2,1)}, u32[]{:S(2)}) %copy-start.3) | copy-done | bytes 98328
  33.1 3.7 %make_home.1.home = bf16[147,16,128]{2,1,0:T(8,128)(2,1)S(1)} custom-call(s32[12,32]{1,0:T(8,128)S(1)} %copy-done.5, s32[12,32]{1,0:T(8,128)S(1)} %collective-permute-done.far_table_ref, bf16[2,3,64,128]{3,2,1,0:T(8,128)(2,1)S(1)} %pad_maximum_fusion.own_wave, bf16[2,3,64,128]{3,2,1,0:T(8,128)(2,1)S(1)} %copy-done.3, ...), custom_call_target="tpu_custom_call" | custom-call | flops 1000000000 | bytes 4000000 | tf_op jit(solution)/shard_map/make_home/pallas_call | solution.py:177
  36.8 2.0 %all-to-all-done.right = bf16[16,24,16,128]{3,2,1,0:T(8,128)(2,1)S(1)} async-done(((bf16[16,24,16,128]{3,2,1,0:T(8,128)(2,1)}), bf16[16,24,16,128]{3,2,1,0:T(8,128)(2,1)S(1)}, u32[]{:S(2)}, u32[]{:S(2)}) %all-to-all-start) | async-done | bytes 1572896 | tf_op jit(solution)/shard_map/all_to_all | solution.py:318
  38.8 0.0 collective-permute-done.5.up2
  38.8 0.0 collective-permute-done.6.down2
  38.8 0.0 collective-permute-done.3.up1
  38.8 0.0 collective-permute-done.4.down1
  38.8 2.7 %contract.1 = f32[8,32,192]{2,1,0:T(8,128)S(1)} custom-call(bf16[147,16,128]{2,1,0:T(8,128)(2,1)S(1)} %make_home.1.home, bf16[99,16,128]{2,1,0:T(8,128)(2,1)S(1)} %collective-permute-done.3.up1, bf16[99,16,128]{2,1,0:T(8,128)(2,1)} %collective-permute-done.4.down1, bf16[27,16,128]{2,1,0:T(8,128)(2,1)S(1)} %collective-permute-done.5.up2, ...), custom_call_target="tpu_custom_call" | custom-call | tf_op jit(solution)/shard_map/contract/pallas_call | solution.py:283
  41.5 0.3 copy.17
  41.8 28.8 %all_to_all.14 = f32[256,1,192]{2,1,0:T(1,128)S(1)} all-to-all(f32[256,1,192]{2,1,0:T(1,128)S(1)} %copy.17), channel_id=1, replica_groups=mesh['row'=8,'col'=16,'wf'=2] {'row','wf','col'}, dimensions={0} | all-to-all | bytes 393216 | tf_op jit(solution)/shard_map/all_to_all | solution.py:351
  70.5 0.3 reduce_sum.9
  70.8 0.1 reshape.130
  70.9 0.6 copy.18
  (20 shorter events, 0.2 us)
Async XLA Ops:
  0.0 18.5 %collective-permute-start.2 = (bf16[12,2,2,128,128]{4,3,2,1,0:T(8,128)(2,1)}, bf16[12,2,2,128,128]{4,3,2,1,0:T(8,128)(2,1)}, u32[]{:S(2)}, u32[]{:S(2)}) collective-permute-start(bf16[12,2,2,128,128]{4,3,2,1,0:T(8,128)(2,1)} %own_left.3), channel_id=1, source_target_pairs={{0,32},{32,0},{64,96},{96,64},{128,160},{160,128},{192,224},{224,1... | collective-permute-start | bytes 4718600 | tf_op jit(solution)/shard_map/ppermute | solution.py:315
  3.2 15.3 %collective-permute-start = (s32[12,32]{1,0:T(8,128)}, s32[12,32]{1,0:T(8,128)S(1)}, u32[]{:S(2)}, u32[]{:S(2)}) collective-permute-start(s32[12,32]{1,0:T(8,128)} %own_table_ref.3), channel_id=1, source_target_pairs={{0,32},{32,0},{64,96},{96,64},{128,160},{160,128},{192,224},{224,1... | collective-permute-start | bytes 4616 | tf_op jit(solution)/shard_map/ppermute | solution.py:316
  4.1 14.4 %collective-permute-start.1 = (bf16[2,3,64,128]{3,2,1,0:T(8,128)(2,1)S(1)}, bf16[2,3,64,128]{3,2,1,0:T(8,128)(2,1)S(1)}, u32[]{:S(2)}, u32[]{:S(2)}) collective-permute-start(bf16[2,3,64,128]{3,2,1,0:T(8,128)(2,1)S(1)} %pad_maximum_fusion.own_wave), channel_id=1, source_target_pairs={{0,129},{32,161},{64,193},{96,225},{128,1},{160,33},{192,65},{224,... | collective-permute-start | bytes 294920 | tf_op jit(solution)/shard_map/ppermute | solution.py:311
  11.3 7.2 %copy-start = (bf16[12,2,2,128,128]{4,3,2,1,0:T(8,128)(2,1)S(1)}, bf16[12,2,2,128,128]{4,3,2,1,0:T(8,128)(2,1)}, u32[]{:S(2)}) copy-start(bf16[12,2,2,128,128]{4,3,2,1,0:T(8,128)(2,1)} %own_left.3) | copy-start | bytes 4718596
  11.3 7.2 %copy-start.5 = (s32[12,32]{1,0:T(8,128)S(1)}, s32[12,32]{1,0:T(8,128)}, u32[]{:S(2)}) copy-start(s32[12,32]{1,0:T(8,128)} %own_table_ref.3) | copy-start | bytes 4612
  11.3 27.4 %all-to-all-start = ((bf16[16,24,16,128]{3,2,1,0:T(8,128)(2,1)}), bf16[16,24,16,128]{3,2,1,0:T(8,128)(2,1)S(1)}, u32[]{:S(2)}, u32[]{:S(2)}) async-start(bf16[16,24,16,128]{3,2,1,0:T(8,128)(2,1)} %pick_right.1), calls=%async_computation | async-start | bytes 3145728 | tf_op jit(solution)/shard_map/all_to_all | solution.py:318
  18.5 11.1 %copy-start.6 = (s32[96]{0:T(128)S(1)}, s32[96]{0:T(128)}, u32[]{:S(2)}) copy-start(s32[96]{0:T(128)} %param.12) | copy-start | bytes 1156
  18.5 11.4 %copy-start.7 = (s32[96]{0:T(128)S(1)}, s32[96]{0:T(128)}, u32[]{:S(2)}) copy-start(s32[96]{0:T(128)} %param.13) | copy-start | bytes 1156
  18.5 4.8 %copy-start.2 = (bf16[2,3,64,128]{3,2,1,0:T(8,128)(2,1)}, bf16[2,3,64,128]{3,2,1,0:T(8,128)(2,1)S(1)}, u32[]{:S(2)}) copy-start(bf16[2,3,64,128]{3,2,1,0:T(8,128)(2,1)S(1)} %collective-permute-done.1.far_wave) | copy-start | bytes 294916
  23.3 15.5 %collective-permute-start.3 = (bf16[99,16,128]{2,1,0:T(8,128)(2,1)}, bf16[99,16,128]{2,1,0:T(8,128)(2,1)S(1)}, u32[]{:S(2)}, u32[]{:S(2)}) collective-permute-start(bf16[99,16,128]{2,1,0:T(8,128)(2,1)} %get-tuple-element.15), channel_id=1, source_target_pairs={{0,64},{32,96},{64,128},{96,160},{128,192},{160,224},{192,1},{224,... | collective-permute-start | bytes 1216520 | tf_op jit(solution)/shard_map/ppermute | solution.py:326
  24.1 14.7 %collective-permute-start.4 = (bf16[99,16,128]{2,1,0:T(8,128)(2,1)}, bf16[99,16,128]{2,1,0:T(8,128)(2,1)}, u32[]{:S(2)}, u32[]{:S(2)}) collective-permute-start(bf16[99,16,128]{2,1,0:T(8,128)(2,1)} %get-tuple-element.16), channel_id=1, source_target_pairs={{0,193},{32,225},{64,0},{96,32},{128,64},{160,96},{192,128},{224,1... | collective-permute-start | bytes 1216520 | tf_op jit(solution)/shard_map/ppermute | solution.py:327
  26.0 12.7 %collective-permute-start.5 = (bf16[27,16,128]{2,1,0:T(8,128)(2,1)}, bf16[27,16,128]{2,1,0:T(8,128)(2,1)S(1)}, u32[]{:S(2)}, u32[]{:S(2)}) collective-permute-start(bf16[27,16,128]{2,1,0:T(8,128)(2,1)} %get-tuple-element.17), channel_id=1, source_target_pairs={{0,128},{32,160},{64,192},{96,224},{128,1},{160,33},{192,65},{224,... | collective-permute-start | bytes 331784 | tf_op jit(solution)/shard_map/ppermute | solution.py:328
  26.0 12.7 %collective-permute-start.6 = (bf16[27,16,128]{2,1,0:T(8,128)(2,1)}, bf16[27,16,128]{2,1,0:T(8,128)(2,1)S(1)}, u32[]{:S(2)}, u32[]{:S(2)}) collective-permute-start(bf16[27,16,128]{2,1,0:T(8,128)(2,1)} %get-tuple-element.18), channel_id=1, source_target_pairs={{0,129},{32,161},{64,193},{96,225},{128,0},{160,32},{192,64},{224,... | collective-permute-start | bytes 331784 | tf_op jit(solution)/shard_map/ppermute | solution.py:329
  30.8 1.4 %copy-start.1 = (bf16[12,2,2,128,128]{4,3,2,1,0:T(8,128)(2,1)S(1)}, bf16[12,2,2,128,128]{4,3,2,1,0:T(8,128)(2,1)}, u32[]{:S(2)}) copy-start(bf16[12,2,2,128,128]{4,3,2,1,0:T(8,128)(2,1)} %own_left.3) | copy-start | bytes 4718596
  32.2 0.9 %copy-start.3 = (bf16[2,3,64,128]{3,2,1,0:T(8,128)(2,1)S(1)}, bf16[2,3,64,128]{3,2,1,0:T(8,128)(2,1)}, u32[]{:S(2)}) copy-start(bf16[2,3,64,128]{3,2,1,0:T(8,128)(2,1)} %copy-done.2) | copy-start | bytes 294916
  33.1 5.7 %copy-start.4 = (s32[128,32]{0,1:T(8,128)S(1)}, s32[128,32]{0,1:T(8,128)}, u32[]{:S(2)}) copy-start(s32[128,32]{0,1:T(8,128)} %param.11) | copy-start | bytes 49156

commit v7 on v6

--- a/solution.py
+++ b/solution.py
@@ -76,15 +76,19 @@
 def tiles_kernel(
     sent, own_table_ref, far_table_ref, own_wave, far_wave, own_left, far_left, *refs
 ):
-    outs, (sides, bras, kets, own_table, far_table, sem) = refs[:-6], refs[-6:]
+    count = 4 if sent else 1
+    results, outs = refs[:count], refs[count : 2 * count] if sent else refs[:count]
+    sides, bras, kets, operators, own_table, far_table, sem, out_sem = refs[-8:]
     core, _, z, q = where()
     low = z < 4
-    tables = [
+    copies = [
         pltpu.make_async_copy(own_table_ref, own_table, sem.at[0]),
         pltpu.make_async_copy(far_table_ref, far_table, sem.at[1]),
+        pltpu.make_async_copy(own_left.at[:, core], operators.at[0], sem.at[2]),
+        pltpu.make_async_copy(far_left.at[:, core], operators.at[1], sem.at[3]),
     ]
-    for table in tables:
-        table.start()
+    for copy in copies:
+        copy.start()
 
     def wave(c, o):
         mine, other = own_wave[c, o], far_wave[c, o]
@@ -102,10 +106,22 @@
             bras[0] = jnp.concatenate([re_t, im_t], axis=1)
             bras[1] = jnp.concatenate([-im_t, re_t], axis=1)
 
-    for table in tables:
-        table.wait()
+    copies[0].wait()
+    copies[1].wait()
     labels = [own_table[s, q] for s in range(12)] + [far_table[s, q] for s in range(12)]
     shifts = [lax.rem(label - q + 32, 32) for label in labels]
+    for out, spot in zip(outs, range(1, 5) if sent else range(1)):
+        members = GROUPS[spot] * 4
+        offset = 12 if spot == 4 else 0
+        for tile in range(3):
+            place = (iota((16, 128), 1) + tile * 128 - STARTS[spot]) // 4
+            row = jnp.zeros((16, 128), F32)
+            low_s, high_s = (tile * 128 - STARTS[spot]) // 4, (tile * 128 + 128 - STARTS[spot]) // 4
+            for s in range(max(0, low_s), min(members, high_s)):
+                row = jnp.where(place == s, labels[offset + s].astype(F32), row)
+            out[TILES[spot] + tile] = row.astype(BF)
+
+    leaving = []
     for half in range(2):
         if sent:
             spots = [lax.rem(z + 1, 8), lax.rem(z + 7, 8), lax.rem(z + (6 if half else 2), 8)]
@@ -120,9 +136,11 @@
             ],
             axis=0,
         )
-        source = far_left if half else own_left
+        copies[2 + half].wait()
         for s in range(12):
-            operator = jnp.concatenate([source[s, core, 0], source[s, core, 1]], axis=1)
+            operator = jnp.concatenate(
+                [operators[half, s, 0], operators[half, s, 1]], axis=1
+            )
             turned = jnp.dot(
                 operator, sides[shifts[half * 12 + s]], preferred_element_type=F32
             ).astype(BF)
@@ -159,16 +177,19 @@
                     outs[0][96 + whole * 8 : 96 + whole * 8 + 8] = rows[8:16]
                 else:
                     outs[i][whole * 16 : whole * 16 + 16] = rows
-    for out, spot in zip(outs, range(1, 5) if sent else range(1)):
-        count = GROUPS[spot] * 4
-        offset = 12 if spot == 4 else 0
-        for tile in range(3):
-            place = (iota((16, 128), 1) + tile * 128 - STARTS[spot]) // 4
-            row = jnp.zeros((16, 128), F32)
-            low_s, high_s = (tile * 128 - STARTS[spot]) // 4, (tile * 128 + 128 - STARTS[spot]) // 4
-            for s in range(max(0, low_s), min(count, high_s)):
-                row = jnp.where(place == s, labels[offset + s].astype(F32), row)
-            out[TILES[spot] + tile] = row.astype(BF)
+        if sent:
+            part = slice(48, TILES[1] + 3) if half else slice(0, 48)
+            for i, tiles in ((0, part), (1, part), (2 + half, slice(0, TILES[3] + 3))):
+                size = tiles.stop - tiles.start
+                copy = pltpu.make_async_copy(
+                    outs[i].at[pl.ds(tiles.start, size)],
+                    results[i].at[pl.ds(tiles.start, size)],
+                    out_sem.at[half, min(i, 2)],
+                )
+                copy.start()
+                leaving.append(copy)
+    for copy in leaving:
+        copy.wait()
 
 
 def make_tiles(sent, own_table, far_table, own_wave, far_wave, left_operators, far_left):
@@ -176,16 +197,19 @@
     shapes = [(n + 3, 16, 128) for n in (TILES[1:] if sent else TILES[:1])]
     return pl.pallas_call(
         functools.partial(tiles_kernel, sent),
-        in_specs=[anywhere] * 2 + [whole] * 4,
-        out_specs=[whole] * len(shapes),
+        in_specs=[anywhere] * 2 + [whole] * 2 + [anywhere] * 2,
+        out_specs=[anywhere if sent else whole] * len(shapes),
         out_shape=[jax.ShapeDtypeStruct(shape, BF) for shape in shapes],
-        scratch_shapes=[
+        scratch_shapes=[pltpu.VMEM(shape, BF) for shape in shapes if sent]
+        + [
             pltpu.VMEM((3, 256, 512), BF),
             pltpu.VMEM((2, 128, 256), BF),
             pltpu.VMEM((12, 256, 256), BF),
+            pltpu.VMEM((2, 12, 2, 128, 128), BF),
             pltpu.SMEM((12, 32), jnp.int32),
             pltpu.SMEM((12, 32), jnp.int32),
-            pltpu.SemaphoreType.DMA((2,)),
+            pltpu.SemaphoreType.DMA((4,)),
+            pltpu.SemaphoreType.DMA((2, 3)),
         ],
         cost_estimate=pl.CostEstimate(
             flops=1000000000, bytes_accessed=4000000, transcendentals=0

time: 72 us -> 70.6 us (0.981)
  waiting for transfers between devices: 1.97 us -> 4.38 us
  Pallas kernels: 14.2 us -> 11.8 us
  blocking collectives: 28.8 us -> 27.5 us
    pallas_call x2, Pallas kernels: 8.43 us -> 6.03 us  [make_tiles(): pl.pallas_call(functools.partial(tiles_kernel, sent), in_specs=[anywhere]...]
    all_to_all x1, waiting for transfers between devices: 1.96 us -> 4.36 us  [local(): right = lax.all_to_all(right, 'col', 0, 0, tiled=True)]
    all_to_all x1, blocking collectives: 28.8 us -> 27.5 us  [local(): lax.all_to_all(shares.reshape(256, 192), ('row', 'wf', 'col'), 0, 0, tile...]
  transfers between devices with their start and end apart: 8 -> 8, of which waited for: 1 -> 1; matrix products, arithmetic and copies ran while one was open for 3% -> 3% of each run, Pallas kernels for 16% -> 13%
where the time goes in v7:
time: 70.6 us; the launch traced here: 70.3 us
  blocking collectives  27.5 us (39%)
  starting transfers between devices  20.8 us (29%)
  Pallas kernels  11.8 us (17%)
  local copies, waits for them, and re-layouts  4.9 us (7%)
  waiting for transfers between devices  4.38 us (6%)
    all_to_all x1, blocking collectives, local(): lax.all_to_all(shares.reshape(256, 192), ('row', 'wf', 'col'), 0, 0, tile...  27.5 us
    all_to_all x1, starting transfers between devices, local(): right = lax.all_to_all(right, 'col', 0, 0, tiled=True)  6.9 us
    pallas_call x2, Pallas kernels, make_tiles(): pl.pallas_call(functools.partial(tiles_kernel, sent), in_specs=[anywhere]...  6.03 us
    ppermute x1, starting transfers between devices, local(): lax.ppermute(own_wave, line, ring(lambda z: (z + 2) % 8 if z in (2, 3, 6,...  4.37 us
    all_to_all x1, waiting for transfers between devices, local(): right = lax.all_to_all(right, 'col', 0, 0, tiled=True)  4.36 us
    ppermute x1, starting transfers between devices, local(): lax.ppermute(down2, line, ring(lambda z: (z + 6) % 8))  3.57 us
    ppermute x1, starting transfers between devices, local(): far_left = lax.ppermute(left_operators, 'row', swap)  3.24 us
    pallas_call x1, Pallas kernels, pick_right(): pl.pallas_call(pick_right_kernel, in_specs=[pl.BlockSpec(memory_space=plt...  2.87 us
  transfers between devices with their start and end apart: 8, of which 1 were waited for; matrix products, arithmetic and copies ran while one was open for 3% of the time, Pallas kernels for 13%

profile of v7, /device:TPU:1, one launch (start us, length us, event | category | flops | bytes accessed | tf_op | source)
XLA Modules:
  0.0 70.3 jit_solution(9190884877121066625)
XLA Ops:
  0.0 3.2 %collective-permute-start.2 = (bf16[12,2,2,128,128]{4,3,2,1,0:T(8,128)(2,1)}, bf16[12,2,2,128,128]{4,3,2,1,0:T(8,128)(2,1)}, u32[]{:S(2)}, u32[]{:S(2)}) collective-permute-start(bf16[12,2,2,128,128]{4,3,2,1,0:T(8,128)(2,1)} %own_left.3), channel_id=1, source_target_pairs={{0,32},{32,0},{64,96},{96,64},{128,160},{160,128},{192,224},{224,1... | collective-permute-start | bytes 4718600 | tf_op jit(solution)/shard_map/ppermute | solution.py:339
  3.2 0.0 collective-permute-start
  3.2 0.8 %constant_dynamic-slice_fusion.2 = (bf16[2,1,64,128]{3,2,1,0:T(8,128)(2,1)S(1)}, bf16[2,1,64,128]{3,2,1,0:T(8,128)(2,1)S(1)}, bf16[2,1,64,128]{3,2,1,0:T(8,128)(2,1)S(1)}) fusion(bf16[2,32,64,128]{3,2,1,0:T(8,128)(2,1)} %param.7, s32[]{:T(128)S(6)} %select_n.36, s32[]{:T(128)S(6)} %select_n.40, s32[]{:T(128)S(6)} %select_n.38), kind=kLoop, calls=%fused_computation.17 | loop fusion | bytes 196620 | tf_op jit(solution)/shard_map/dynamic_slice | solution.py:333
  4.1 4.4 %collective-permute-start.1 = (bf16[2,3,64,128]{3,2,1,0:T(8,128)(2,1)S(1)}, bf16[2,3,64,128]{3,2,1,0:T(8,128)(2,1)S(1)}, u32[]{:S(2)}, u32[]{:S(2)}) collective-permute-start(bf16[2,3,64,128]{3,2,1,0:T(8,128)(2,1)S(1)} %pad_maximum_fusion.own_wave), channel_id=1, source_target_pairs={{0,129},{32,161},{64,193},{96,225},{128,1},{160,33},{192,65},{224,... | collective-permute-start | bytes 294920 | tf_op jit(solution)/shard_map/ppermute | solution.py:335
  8.4 2.9 %pick_right.1 = bf16[16,24,16,128]{3,2,1,0:T(8,128)(2,1)} custom-call(bf16[16,2,8,2,4,16,128]{6,5,4,3,2,1,0:T(8,128)(2,1)} %bitcast.18), custom_call_target="tpu_custom_call" | custom-call | tf_op jit(solution)/shard_map/pick_right/pallas_call | solution.py:56
  11.3 0.0 copy-start
  11.3 0.0 copy-start.5
  11.3 6.9 %all-to-all-start = ((bf16[16,24,16,128]{3,2,1,0:T(8,128)(2,1)}), bf16[16,24,16,128]{3,2,1,0:T(8,128)(2,1)S(1)}, u32[]{:S(2)}, u32[]{:S(2)}) async-start(bf16[16,24,16,128]{3,2,1,0:T(8,128)(2,1)} %pick_right.1), calls=%async_computation | async-start | bytes 3145728 | tf_op jit(solution)/shard_map/all_to_all | solution.py:342
  18.3 0.1 broadcast_in_dim.2
  18.4 0.1 reshape.129.sign
  18.5 0.0 copy-start.6
  18.5 0.0 copy-start.7
  18.5 0.0 collective-permute-done.far_table_ref
  18.5 0.0 collective-permute-done.1.far_wave
  18.5 0.0 copy-start.2
  18.5 0.0 collective-permute-done.2.far_left
  18.5 0.0 copy-done
  18.6 3.4 %make_tiles.1 = (bf16[99,16,128]{2,1,0:T(8,128)(2,1)}, bf16[99,16,128]{2,1,0:T(8,128)(2,1)}, bf16[27,16,128]{2,1,0:T(8,128)(2,1)}, bf16[27,16,128]{2,1,0:T(8,128)(2,1)}) custom-call(s32[12,32]{1,0:T(8,128)S(1)} %copy-done.5, s32[12,32]{1,0:T(8,128)S(1)} %collective-permute-done.far_table_ref, bf16[2,3,64,128]{3,2,1,0:T(8,128)(2,1)S(1)} %pad_maximum_fusion.own_wave, ...), custom_call_target="tpu_custom_call" | custom-call | flops 1000000000 | bytes 4000000 | tf_op jit(solution)/shard_map/make_tiles/pallas_call | solution.py:198
  22.0 0.8 %collective-permute-start.3 = (bf16[99,16,128]{2,1,0:T(8,128)(2,1)}, bf16[99,16,128]{2,1,0:T(8,128)(2,1)S(1)}, u32[]{:S(2)}, u32[]{:S(2)}) collective-permute-start(bf16[99,16,128]{2,1,0:T(8,128)(2,1)} %get-tuple-element.15), channel_id=1, source_target_pairs={{0,64},{32,96},{64,128},{96,160},{128,192},{160,224},{192,1},{224,... | collective-permute-start | bytes 1216520 | tf_op jit(solution)/shard_map/ppermute | solution.py:350
  22.8 2.0 %collective-permute-start.4 = (bf16[99,16,128]{2,1,0:T(8,128)(2,1)}, bf16[99,16,128]{2,1,0:T(8,128)(2,1)}, u32[]{:S(2)}, u32[]{:S(2)}) collective-permute-start(bf16[99,16,128]{2,1,0:T(8,128)(2,1)} %get-tuple-element.16), channel_id=1, source_target_pairs={{0,193},{32,225},{64,0},{96,32},{128,64},{160,96},{192,128},{224,1... | collective-permute-start | bytes 1216520 | tf_op jit(solution)/shard_map/ppermute | solution.py:351
  24.8 0.0 collective-permute-start.5
  24.8 3.6 %collective-permute-start.6 = (bf16[27,16,128]{2,1,0:T(8,128)(2,1)}, bf16[27,16,128]{2,1,0:T(8,128)(2,1)S(1)}, u32[]{:S(2)}, u32[]{:S(2)}) collective-permute-start(bf16[27,16,128]{2,1,0:T(8,128)(2,1)} %get-tuple-element.18), channel_id=1, source_target_pairs={{0,129},{32,161},{64,193},{96,225},{128,0},{160,32},{192,64},{224,... | collective-permute-start | bytes 331784 | tf_op jit(solution)/shard_map/ppermute | solution.py:353
  28.3 0.1 reshape.128
  28.5 0.1 mul.44
  28.6 0.1 stack.16
  28.7 0.1 fusion.2
  28.8 0.1 iota_add_fusion
  28.9 0.1 fusion.1
  29.0 0.1 add.143.slot_key
  29.1 0.1 add.139.real_key
  29.2 0.1 sub.29.imag_key
  29.3 0.2 make_picks.1.picks
  29.5 0.0 copy-start.1
  29.5 1.4 %copy-done.1 = bf16[12,2,2,128,128]{4,3,2,1,0:T(8,128)(2,1)S(1)} copy-done((bf16[12,2,2,128,128]{4,3,2,1,0:T(8,128)(2,1)S(1)}, bf16[12,2,2,128,128]{4,3,2,1,0:T(8,128)(2,1)}, u32[]{:S(2)}) %copy-start.1) | copy-done | bytes 1572888
  30.9 0.9 %copy-done.3 = bf16[2,3,64,128]{3,2,1,0:T(8,128)(2,1)S(1)} copy-done((bf16[2,3,64,128]{3,2,1,0:T(8,128)(2,1)S(1)}, bf16[2,3,64,128]{3,2,1,0:T(8,128)(2,1)}, u32[]{:S(2)}) %copy-start.3) | copy-done | bytes 98328
  31.8 2.6 %make_home.1.home = bf16[147,16,128]{2,1,0:T(8,128)(2,1)S(1)} custom-call(s32[12,32]{1,0:T(8,128)S(1)} %copy-done.5, s32[12,32]{1,0:T(8,128)S(1)} %collective-permute-done.far_table_ref, bf16[2,3,64,128]{3,2,1,0:T(8,128)(2,1)S(1)} %pad_maximum_fusion.own_wave, bf16[2,3,64,128]{3,2,1,0:T(8,128)(2,1)S(1)} %copy-done.3, ...), custom_call_target="tpu_custom_call" | custom-call | flops 1000000000 | bytes 4000000 | tf_op jit(solution)/shard_map/make_home/pallas_call | solution.py:198
  34.4 4.4 %all-to-all-done.right = bf16[16,24,16,128]{3,2,1,0:T(8,128)(2,1)S(1)} async-done(((bf16[16,24,16,128]{3,2,1,0:T(8,128)(2,1)}), bf16[16,24,16,128]{3,2,1,0:T(8,128)(2,1)S(1)}, u32[]{:S(2)}, u32[]{:S(2)}) %all-to-all-start) | async-done | bytes 1572896 | tf_op jit(solution)/shard_map/all_to_all | solution.py:342
  38.8 0.0 collective-permute-done.5.up2
  38.8 0.0 collective-permute-done.6.down2
  38.8 0.0 collective-permute-done.3.up1
  38.8 0.0 collective-permute-done.4.down1
  38.8 0.0 copy-done.4
  38.8 2.7 %contract.1 = f32[8,32,192]{2,1,0:T(8,128)S(1)} custom-call(bf16[147,16,128]{2,1,0:T(8,128)(2,1)S(1)} %make_home.1.home, bf16[99,16,128]{2,1,0:T(8,128)(2,1)S(1)} %collective-permute-done.3.up1, bf16[99,16,128]{2,1,0:T(8,128)(2,1)} %collective-permute-done.4.down1, bf16[27,16,128]{2,1,0:T(8,128)(2,1)S(1)} %collective-permute-done.5.up2, ...), custom_call_target="tpu_custom_call" | custom-call | tf_op jit(solution)/shard_map/contract/pallas_call | solution.py:307
  41.5 0.3 copy.17
  41.8 27.5 %all_to_all.14 = f32[256,1,192]{2,1,0:T(1,128)S(1)} all-to-all(f32[256,1,192]{2,1,0:T(1,128)S(1)} %copy.17), channel_id=1, replica_groups=mesh['row'=8,'col'=16,'wf'=2] {'row','wf','col'}, dimensions={0} | all-to-all | bytes 393216 | tf_op jit(solution)/shard_map/all_to_all | solution.py:375
  69.3 0.3 reduce_sum.9
  69.6 0.1 reshape.130
  69.7 0.6 copy.18
  (20 shorter events, 0.1 us)
Async XLA Ops:
  0.0 18.5 %collective-permute-start.2 = (bf16[12,2,2,128,128]{4,3,2,1,0:T(8,128)(2,1)}, bf16[12,2,2,128,128]{4,3,2,1,0:T(8,128)(2,1)}, u32[]{:S(2)}, u32[]{:S(2)}) collective-permute-start(bf16[12,2,2,128,128]{4,3,2,1,0:T(8,128)(2,1)} %own_left.3), channel_id=1, source_target_pairs={{0,32},{32,0},{64,96},{96,64},{128,160},{160,128},{192,224},{224,1... | collective-permute-start | bytes 4718600 | tf_op jit(solution)/shard_map/ppermute | solution.py:339
  3.2 15.3 %collective-permute-start = (s32[12,32]{1,0:T(8,128)}, s32[12,32]{1,0:T(8,128)S(1)}, u32[]{:S(2)}, u32[]{:S(2)}) collective-permute-start(s32[12,32]{1,0:T(8,128)} %own_table_ref.3), channel_id=1, source_target_pairs={{0,32},{32,0},{64,96},{96,64},{128,160},{160,128},{192,224},{224,1... | collective-permute-start | bytes 4616 | tf_op jit(solution)/shard_map/ppermute | solution.py:340
  4.1 14.4 %collective-permute-start.1 = (bf16[2,3,64,128]{3,2,1,0:T(8,128)(2,1)S(1)}, bf16[2,3,64,128]{3,2,1,0:T(8,128)(2,1)S(1)}, u32[]{:S(2)}, u32[]{:S(2)}) collective-permute-start(bf16[2,3,64,128]{3,2,1,0:T(8,128)(2,1)S(1)} %pad_maximum_fusion.own_wave), channel_id=1, source_target_pairs={{0,129},{32,161},{64,193},{96,225},{128,1},{160,33},{192,65},{224,... | collective-permute-start | bytes 294920 | tf_op jit(solution)/shard_map/ppermute | solution.py:335
  11.3 7.2 %copy-start = (bf16[12,2,2,128,128]{4,3,2,1,0:T(8,128)(2,1)S(1)}, bf16[12,2,2,128,128]{4,3,2,1,0:T(8,128)(2,1)}, u32[]{:S(2)}) copy-start(bf16[12,2,2,128,128]{4,3,2,1,0:T(8,128)(2,1)} %own_left.3) | copy-start | bytes 4718596
  11.3 7.2 %copy-start.5 = (s32[12,32]{1,0:T(8,128)S(1)}, s32[12,32]{1,0:T(8,128)}, u32[]{:S(2)}) copy-start(s32[12,32]{1,0:T(8,128)} %own_table_ref.3) | copy-start | bytes 4612
  11.3 27.4 %all-to-all-start = ((bf16[16,24,16,128]{3,2,1,0:T(8,128)(2,1)}), bf16[16,24,16,128]{3,2,1,0:T(8,128)(2,1)S(1)}, u32[]{:S(2)}, u32[]{:S(2)}) async-start(bf16[16,24,16,128]{3,2,1,0:T(8,128)(2,1)} %pick_right.1), calls=%async_computation | async-start | bytes 3145728 | tf_op jit(solution)/shard_map/all_to_all | solution.py:342
  18.5 9.9 %copy-start.6 = (s32[96]{0:T(128)S(1)}, s32[96]{0:T(128)}, u32[]{:S(2)}) copy-start(s32[96]{0:T(128)} %param.12) | copy-start | bytes 1156
  18.5 10.1 %copy-start.7 = (s32[96]{0:T(128)S(1)}, s32[96]{0:T(128)}, u32[]{:S(2)}) copy-start(s32[96]{0:T(128)} %param.13) | copy-start | bytes 1156
  18.5 3.5 %copy-start.2 = (bf16[2,3,64,128]{3,2,1,0:T(8,128)(2,1)}, bf16[2,3,64,128]{3,2,1,0:T(8,128)(2,1)S(1)}, u32[]{:S(2)}) copy-start(bf16[2,3,64,128]{3,2,1,0:T(8,128)(2,1)S(1)} %collective-permute-done.1.far_wave) | copy-start | bytes 294916
  22.0 16.8 %collective-permute-start.3 = (bf16[99,16,128]{2,1,0:T(8,128)(2,1)}, bf16[99,16,128]{2,1,0:T(8,128)(2,1)S(1)}, u32[]{:S(2)}, u32[]{:S(2)}) collective-permute-start(bf16[99,16,128]{2,1,0:T(8,128)(2,1)} %get-tuple-element.15), channel_id=1, source_target_pairs={{0,64},{32,96},{64,128},{96,160},{128,192},{160,224},{192,1},{224,... | collective-permute-start | bytes 1216520 | tf_op jit(solution)/shard_map/ppermute | solution.py:350
  22.8 16.0 %collective-permute-start.4 = (bf16[99,16,128]{2,1,0:T(8,128)(2,1)}, bf16[99,16,128]{2,1,0:T(8,128)(2,1)}, u32[]{:S(2)}, u32[]{:S(2)}) collective-permute-start(bf16[99,16,128]{2,1,0:T(8,128)(2,1)} %get-tuple-element.16), channel_id=1, source_target_pairs={{0,193},{32,225},{64,0},{96,32},{128,64},{160,96},{192,128},{224,1... | collective-permute-start | bytes 1216520 | tf_op jit(solution)/shard_map/ppermute | solution.py:351
  24.8 14.0 %collective-permute-start.5 = (bf16[27,16,128]{2,1,0:T(8,128)(2,1)}, bf16[27,16,128]{2,1,0:T(8,128)(2,1)S(1)}, u32[]{:S(2)}, u32[]{:S(2)}) collective-permute-start(bf16[27,16,128]{2,1,0:T(8,128)(2,1)} %get-tuple-element.17), channel_id=1, source_target_pairs={{0,128},{32,160},{64,192},{96,224},{128,1},{160,33},{192,65},{224,... | collective-permute-start | bytes 331784 | tf_op jit(solution)/shard_map/ppermute | solution.py:352
  24.8 14.0 %collective-permute-start.6 = (bf16[27,16,128]{2,1,0:T(8,128)(2,1)}, bf16[27,16,128]{2,1,0:T(8,128)(2,1)S(1)}, u32[]{:S(2)}, u32[]{:S(2)}) collective-permute-start(bf16[27,16,128]{2,1,0:T(8,128)(2,1)} %get-tuple-element.18), channel_id=1, source_target_pairs={{0,129},{32,161},{64,193},{96,225},{128,0},{160,32},{192,64},{224,... | collective-permute-start | bytes 331784 | tf_op jit(solution)/shard_map/ppermute | solution.py:353
  29.5 1.4 %copy-start.1 = (bf16[12,2,2,128,128]{4,3,2,1,0:T(8,128)(2,1)S(1)}, bf16[12,2,2,128,128]{4,3,2,1,0:T(8,128)(2,1)}, u32[]{:S(2)}) copy-start(bf16[12,2,2,128,128]{4,3,2,1,0:T(8,128)(2,1)} %own_left.3) | copy-start | bytes 4718596
  30.9 0.9 %copy-start.3 = (bf16[2,3,64,128]{3,2,1,0:T(8,128)(2,1)S(1)}, bf16[2,3,64,128]{3,2,1,0:T(8,128)(2,1)}, u32[]{:S(2)}) copy-start(bf16[2,3,64,128]{3,2,1,0:T(8,128)(2,1)} %copy-done.2) | copy-start | bytes 294916
  31.8 7.0 %copy-start.4 = (s32[128,32]{0,1:T(8,128)S(1)}, s32[128,32]{0,1:T(8,128)}, u32[]{:S(2)}) copy-start(s32[128,32]{0,1:T(8,128)} %param.11) | copy-start | bytes 49156

commit v8 on v7

--- a/solution.py
+++ b/solution.py
@@ -42,7 +42,13 @@
         for target in range(part * 4, part * 4 + 4):
             for second in range(2):
                 rows = jnp.concatenate(
-                    [rows_ref[second, target, j, c][None] for c in range(2) for j in range(8)],
+                    [
+                        rows_ref[second, target, 4 * w + 2 * h + t, c][None]
+                        for h in range(2)
+                        for c in range(2)
+                        for w in range(2)
+                        for t in range(2)
+                    ],
                     axis=0,
                 )
                 rows = jnp.swapaxes(rows, 0, 1)
@@ -274,7 +280,7 @@
         axis=1,
     )
     row = iota((128, 128), 0)
-    j = (row % 16) * 8 + (row // 16 % 2) * 4 + row // 32
+    j = row % 32 // 2 * 8 + row // 32 % 2 * 4 + row % 2 * 2 + row // 64
     labels = right_table[pl.ds(where()[3], 1), :].astype(F32)
     right_label = jnp.sum(jnp.where(iota((128, 128), 1) == j, labels, 0.0), axis=1, keepdims=True)
     match = right_label == slot_label
@@ -282,10 +288,10 @@
     def part(c):
         rows = [
             jnp.concatenate(
-                [paired_ref[third, pl.ds(c * 8 + w * 4 + j, 16, 16), :] for third in range(3)],
+                [paired_ref[third, pl.ds(c * 4 + w * 2 + t, 32, 8), :] for third in range(3)],
                 axis=1,
             )
-            for j in range(4)
+            for t in range(2)
             for w in range(2)
         ]
         return jnp.where(match, jnp.concatenate(rows, axis=0), 0.0)
@@ -297,9 +303,13 @@
         rest = rest - pieces[-1].astype(F32)
     total = jnp.dot(jnp.concatenate(pieces, axis=0), picks[...], preferred_element_type=F32)
     total = total[0:128] + total[128:256] + total[256:384]
-    for j in range(4):
+    total = total.astype(out.dtype)
+    out[...] = jnp.zeros(out.shape, out.dtype)
+    for t in range(2):
         for row in range(8):
-            out[row, :, j * 48 : j * 48 + 48] = total[j * 32 : j * 32 + 32, row * 48 : row * 48 + 48]
+            out[row, :, t * 48 : t * 48 + 48] = total[
+                t * 64 : t * 64 + 64, row * 48 : row * 48 + 48
+            ]
 
 
 def contract(tiles, right, right_table, picks):
@@ -308,7 +318,7 @@
         contract_kernel,
         in_specs=[whole] * 8,
         out_specs=whole,
-        out_shape=jax.ShapeDtypeStruct((8, 32, 192), F32),
+        out_shape=jax.ShapeDtypeStruct((8, 64, 128), BF),
         scratch_shapes=[pltpu.VMEM((3, 256, 128), F32)],
         compiler_params=params(16),
         name="contract",
@@ -373,9 +383,10 @@
     picks = make_picks([slot_key, real_key, imag_key, sign])
     shares = contract(tiles, right, right_table.T, picks)
     shares = lax.all_to_all(
-        shares.reshape(256, 192), ("row", "wf", "col"), 0, 0, tiled=True
-    )
-    return jnp.sum(shares, axis=0).reshape(4, 2, 2, 12).transpose(1, 2, 3, 0)
+        shares.reshape(256, 2, 128), ("row", "wf", "col"), 0, 0, tiled=True
+    )
+    total = jnp.sum(shares.astype(F32), axis=0)[:, 0:96]
+    return total.reshape(2, 2, 2, 2, 12).transpose(2, 3, 4, 0, 1).reshape(2, 2, 12, 4)
 
 
 def solution(mesh):

time: 70.6 us -> 67.5 us (0.956)
  blocking collectives: 27.5 us -> 24.7 us
    all_to_all x1, blocking collectives: 27.5 us -> 24.7 us  [local(): lax.all_to_all(shares.reshape(256, 2, 128), ('row', 'wf', 'col'), 0, 0, t...]
where the time goes in v8:
time: 67.5 us; the launch traced here: 67.1 us
  blocking collectives  24.7 us (37%)
  starting transfers between devices  20.8 us (31%)
  Pallas kernels  11.7 us (17%)
  local copies, waits for them, and re-layouts  4.62 us (7%)
  waiting for transfers between devices  4.38 us (6%)
    all_to_all x1, blocking collectives, local(): lax.all_to_all(shares.reshape(256, 2, 128), ('row', 'wf', 'col'), 0, 0, t...  24.7 us
    all_to_all x1, starting transfers between devices, local(): right = lax.all_to_all(right, 'col', 0, 0, tiled=True)  6.9 us
    pallas_call x2, Pallas kernels, make_tiles(): pl.pallas_call(functools.partial(tiles_kernel, sent), in_specs=[anywhere]...  6.03 us
    ppermute x1, starting transfers between devices, local(): lax.ppermute(own_wave, line, ring(lambda z: (z + 2) % 8 if z in (2, 3, 6,...  4.37 us
    all_to_all x1, waiting for transfers between devices, local(): right = lax.all_to_all(right, 'col', 0, 0, tiled=True)  4.36 us
    ppermute x1, starting transfers between devices, local(): lax.ppermute(down2, line, ring(lambda z: (z + 6) % 8))  3.57 us
    ppermute x1, starting transfers between devices, local(): far_left = lax.ppermute(left_operators, 'row', swap)  3.24 us
    pallas_call x1, Pallas kernels, pick_right(): pl.pallas_call(pick_right_kernel, in_specs=[pl.BlockSpec(memory_space=plt...  2.85 us
  transfers between devices with their start and end apart: 8, of which 1 were waited for; matrix products, arithmetic and copies ran while one was open for 3% of the time, Pallas kernels for 13%

profile of v8, /device:TPU:1, one launch (start us, length us, event | category | flops | bytes accessed | tf_op | source)
XLA Modules:
  0.0 67.1 jit_solution(18034769508464648814)
XLA Ops:
  0.0 3.2 %collective-permute-start.2 = (bf16[12,2,2,128,128]{4,3,2,1,0:T(8,128)(2,1)}, bf16[12,2,2,128,128]{4,3,2,1,0:T(8,128)(2,1)}, u32[]{:S(2)}, u32[]{:S(2)}) collective-permute-start(bf16[12,2,2,128,128]{4,3,2,1,0:T(8,128)(2,1)} %own_left.3), channel_id=1, source_target_pairs={{0,32},{32,0},{64,96},{96,64},{128,160},{160,128},{192,224},{224,1... | collective-permute-start | bytes 4718600 | tf_op jit(solution)/shard_map/ppermute | solution.py:349
  3.2 0.0 collective-permute-start
  3.2 0.8 %constant_dynamic-slice_fusion.2 = (bf16[2,1,64,128]{3,2,1,0:T(8,128)(2,1)S(1)}, bf16[2,1,64,128]{3,2,1,0:T(8,128)(2,1)S(1)}, bf16[2,1,64,128]{3,2,1,0:T(8,128)(2,1)S(1)}) fusion(bf16[2,32,64,128]{3,2,1,0:T(8,128)(2,1)} %param.7, s32[]{:T(128)S(6)} %select_n.36, s32[]{:T(128)S(6)} %select_n.40, s32[]{:T(128)S(6)} %select_n.38), kind=kLoop, calls=%fused_computation.18 | loop fusion | bytes 196620 | tf_op jit(solution)/shard_map/dynamic_slice | solution.py:343
  4.1 4.4 %collective-permute-start.1 = (bf16[2,3,64,128]{3,2,1,0:T(8,128)(2,1)S(1)}, bf16[2,3,64,128]{3,2,1,0:T(8,128)(2,1)S(1)}, u32[]{:S(2)}, u32[]{:S(2)}) collective-permute-start(bf16[2,3,64,128]{3,2,1,0:T(8,128)(2,1)S(1)} %pad_maximum_fusion.own_wave), channel_id=1, source_target_pairs={{0,129},{32,161},{64,193},{96,225},{128,1},{160,33},{192,65},{224,... | collective-permute-start | bytes 294920 | tf_op jit(solution)/shard_map/ppermute | solution.py:345
  8.4 2.9 %pick_right.1 = bf16[16,24,16,128]{3,2,1,0:T(8,128)(2,1)} custom-call(bf16[16,2,8,2,4,16,128]{6,5,4,3,2,1,0:T(8,128)(2,1)} %bitcast.21), custom_call_target="tpu_custom_call" | custom-call | tf_op jit(solution)/shard_map/pick_right/pallas_call | solution.py:62
  11.3 0.0 copy-start
  11.3 0.0 copy-start.5
  11.3 6.9 %all-to-all-start = ((bf16[16,24,16,128]{3,2,1,0:T(8,128)(2,1)}), bf16[16,24,16,128]{3,2,1,0:T(8,128)(2,1)S(1)}, u32[]{:S(2)}, u32[]{:S(2)}) async-start(bf16[16,24,16,128]{3,2,1,0:T(8,128)(2,1)} %pick_right.1), calls=%async_computation | async-start | bytes 3145728 | tf_op jit(solution)/shard_map/all_to_all | solution.py:352
  18.3 0.1 broadcast_in_dim.2
  18.3 0.1 reshape.131.sign
  18.5 0.0 copy-start.6
  18.5 0.0 copy-start.7
  18.5 0.0 collective-permute-done.far_table_ref
  18.5 0.0 collective-permute-done.1.far_wave
  18.5 0.0 copy-start.2
  18.5 0.0 collective-permute-done.2.far_left
  18.5 0.0 copy-done
  18.5 3.4 %make_tiles.1 = (bf16[99,16,128]{2,1,0:T(8,128)(2,1)}, bf16[99,16,128]{2,1,0:T(8,128)(2,1)}, bf16[27,16,128]{2,1,0:T(8,128)(2,1)}, bf16[27,16,128]{2,1,0:T(8,128)(2,1)}) custom-call(s32[12,32]{1,0:T(8,128)S(1)} %copy-done.5, s32[12,32]{1,0:T(8,128)S(1)} %collective-permute-done.far_table_ref, bf16[2,3,64,128]{3,2,1,0:T(8,128)(2,1)S(1)} %pad_maximum_fusion.own_wave, ...), custom_call_target="tpu_custom_call" | custom-call | flops 1000000000 | bytes 4000000 | tf_op jit(solution)/shard_map/make_tiles/pallas_call | solution.py:204
  22.0 0.0 copy-done.2
  22.0 0.8 %collective-permute-start.3 = (bf16[99,16,128]{2,1,0:T(8,128)(2,1)}, bf16[99,16,128]{2,1,0:T(8,128)(2,1)S(1)}, u32[]{:S(2)}, u32[]{:S(2)}) collective-permute-start(bf16[99,16,128]{2,1,0:T(8,128)(2,1)} %get-tuple-element.15), channel_id=1, source_target_pairs={{0,64},{32,96},{64,128},{96,160},{128,192},{160,224},{192,1},{224,... | collective-permute-start | bytes 1216520 | tf_op jit(solution)/shard_map/ppermute | solution.py:360
  22.8 1.9 %collective-permute-start.4 = (bf16[99,16,128]{2,1,0:T(8,128)(2,1)}, bf16[99,16,128]{2,1,0:T(8,128)(2,1)}, u32[]{:S(2)}, u32[]{:S(2)}) collective-permute-start(bf16[99,16,128]{2,1,0:T(8,128)(2,1)} %get-tuple-element.16), channel_id=1, source_target_pairs={{0,193},{32,225},{64,0},{96,32},{128,64},{160,96},{192,128},{224,1... | collective-permute-start | bytes 1216520 | tf_op jit(solution)/shard_map/ppermute | solution.py:361
  24.7 0.0 collective-permute-start.5
  24.7 3.6 %collective-permute-start.6 = (bf16[27,16,128]{2,1,0:T(8,128)(2,1)}, bf16[27,16,128]{2,1,0:T(8,128)(2,1)S(1)}, u32[]{:S(2)}, u32[]{:S(2)}) collective-permute-start(bf16[27,16,128]{2,1,0:T(8,128)(2,1)} %get-tuple-element.18), channel_id=1, source_target_pairs={{0,129},{32,161},{64,193},{96,225},{128,0},{160,32},{192,64},{224,... | collective-permute-start | bytes 331784 | tf_op jit(solution)/shard_map/ppermute | solution.py:363
  28.3 0.0 copy-done.6
  28.3 0.1 reshape.130
  28.5 0.1 mul.44
  28.6 0.1 stack.16
  28.7 0.1 fusion.2
  28.8 0.1 iota_add_fusion
  28.9 0.1 fusion.1
  29.0 0.1 add.143.slot_key
  29.1 0.1 add.139.real_key
  29.2 0.1 sub.29.imag_key
  29.3 0.2 make_picks.1.picks
  29.5 0.0 copy-start.1
  29.5 1.4 %copy-done.1 = bf16[12,2,2,128,128]{4,3,2,1,0:T(8,128)(2,1)S(1)} copy-done((bf16[12,2,2,128,128]{4,3,2,1,0:T(8,128)(2,1)S(1)}, bf16[12,2,2,128,128]{4,3,2,1,0:T(8,128)(2,1)}, u32[]{:S(2)}) %copy-start.1) | copy-done | bytes 1572888
  30.9 0.9 %copy-done.3 = bf16[2,3,64,128]{3,2,1,0:T(8,128)(2,1)S(1)} copy-done((bf16[2,3,64,128]{3,2,1,0:T(8,128)(2,1)S(1)}, bf16[2,3,64,128]{3,2,1,0:T(8,128)(2,1)}, u32[]{:S(2)}) %copy-start.3) | copy-done | bytes 98328
  31.8 2.6 %make_home.1.home = bf16[147,16,128]{2,1,0:T(8,128)(2,1)S(1)} custom-call(s32[12,32]{1,0:T(8,128)S(1)} %copy-done.5, s32[12,32]{1,0:T(8,128)S(1)} %collective-permute-done.far_table_ref, bf16[2,3,64,128]{3,2,1,0:T(8,128)(2,1)S(1)} %pad_maximum_fusion.own_wave, bf16[2,3,64,128]{3,2,1,0:T(8,128)(2,1)S(1)} %copy-done.3, ...), custom_call_target="tpu_custom_call" | custom-call | flops 1000000000 | bytes 4000000 | tf_op jit(solution)/shard_map/make_home/pallas_call | solution.py:204
  34.4 4.4 %all-to-all-done.right = bf16[16,24,16,128]{3,2,1,0:T(8,128)(2,1)S(1)} async-done(((bf16[16,24,16,128]{3,2,1,0:T(8,128)(2,1)}), bf16[16,24,16,128]{3,2,1,0:T(8,128)(2,1)S(1)}, u32[]{:S(2)}, u32[]{:S(2)}) %all-to-all-start) | async-done | bytes 1572896 | tf_op jit(solution)/shard_map/all_to_all | solution.py:352
  38.7 0.0 collective-permute-done.5.up2
  38.8 0.0 collective-permute-done.6.down2
  38.8 0.0 collective-permute-done.3.up1
  38.8 0.0 collective-permute-done.4.down1
  38.8 2.6 %contract.1 = bf16[8,64,128]{2,1,0:T(8,128)(2,1)S(1)} custom-call(bf16[147,16,128]{2,1,0:T(8,128)(2,1)S(1)} %make_home.1.home, bf16[99,16,128]{2,1,0:T(8,128)(2,1)S(1)} %collective-permute-done.3.up1, bf16[99,16,128]{2,1,0:T(8,128)(2,1)} %collective-permute-done.4.down1, bf16[27,16,128]{2,1,0:T(8,128)(2,1)S(1)} %collective-permute-done.5.up2, ...), custom_call_target="tpu_custom_call" | custom-call | tf_op jit(solution)/shard_map/contract/pallas_call | solution.py:317
  41.4 24.7 %all_to_all.10 = bf16[256,2,128]{2,1,0:T(2,128)(2,1)S(1)} all-to-all(bf16[256,2,128]{2,1,0:T(2,128)(2,1)S(1)} %bitcast.19), channel_id=1, replica_groups=mesh['row'=8,'col'=16,'wf'=2] {'row','wf','col'}, dimensions={0} | all-to-all | bytes 262144 | tf_op jit(solution)/shard_map/all_to_all | solution.py:385
  66.1 0.3 convert_reduce_fusion
  66.4 0.1 reshape.133
  66.5 0.6 copy.13
  (19 shorter events, 0.1 us)
Async XLA Ops:
  0.0 18.5 %collective-permute-start.2 = (bf16[12,2,2,128,128]{4,3,2,1,0:T(8,128)(2,1)}, bf16[12,2,2,128,128]{4,3,2,1,0:T(8,128)(2,1)}, u32[]{:S(2)}, u32[]{:S(2)}) collective-permute-start(bf16[12,2,2,128,128]{4,3,2,1,0:T(8,128)(2,1)} %own_left.3), channel_id=1, source_target_pairs={{0,32},{32,0},{64,96},{96,64},{128,160},{160,128},{192,224},{224,1... | collective-permute-start | bytes 4718600 | tf_op jit(solution)/shard_map/ppermute | solution.py:349
  3.2 15.2 %collective-permute-start = (s32[12,32]{1,0:T(8,128)}, s32[12,32]{1,0:T(8,128)S(1)}, u32[]{:S(2)}, u32[]{:S(2)}) collective-permute-start(s32[12,32]{1,0:T(8,128)} %own_table_ref.3), channel_id=1, source_target_pairs={{0,32},{32,0},{64,96},{96,64},{128,160},{160,128},{192,224},{224,1... | collective-permute-start | bytes 4616 | tf_op jit(solution)/shard_map/ppermute | solution.py:350
  4.1 14.4 %collective-permute-start.1 = (bf16[2,3,64,128]{3,2,1,0:T(8,128)(2,1)S(1)}, bf16[2,3,64,128]{3,2,1,0:T(8,128)(2,1)S(1)}, u32[]{:S(2)}, u32[]{:S(2)}) collective-permute-start(bf16[2,3,64,128]{3,2,1,0:T(8,128)(2,1)S(1)} %pad_maximum_fusion.own_wave), channel_id=1, source_target_pairs={{0,129},{32,161},{64,193},{96,225},{128,1},{160,33},{192,65},{224,... | collective-permute-start | bytes 294920 | tf_op jit(solution)/shard_map/ppermute | solution.py:345
  11.3 7.2 %copy-start = (bf16[12,2,2,128,128]{4,3,2,1,0:T(8,128)(2,1)S(1)}, bf16[12,2,2,128,128]{4,3,2,1,0:T(8,128)(2,1)}, u32[]{:S(2)}) copy-start(bf16[12,2,2,128,128]{4,3,2,1,0:T(8,128)(2,1)} %own_left.3) | copy-start | bytes 4718596
  11.3 7.2 %copy-start.5 = (s32[12,32]{1,0:T(8,128)S(1)}, s32[12,32]{1,0:T(8,128)}, u32[]{:S(2)}) copy-start(s32[12,32]{1,0:T(8,128)} %own_table_ref.3) | copy-start | bytes 4612
  11.3 27.4 %all-to-all-start = ((bf16[16,24,16,128]{3,2,1,0:T(8,128)(2,1)}), bf16[16,24,16,128]{3,2,1,0:T(8,128)(2,1)S(1)}, u32[]{:S(2)}, u32[]{:S(2)}) async-start(bf16[16,24,16,128]{3,2,1,0:T(8,128)(2,1)} %pick_right.1), calls=%async_computation | async-start | bytes 3145728 | tf_op jit(solution)/shard_map/all_to_all | solution.py:352
  18.5 9.9 %copy-start.6 = (s32[96]{0:T(128)S(1)}, s32[96]{0:T(128)}, u32[]{:S(2)}) copy-start(s32[96]{0:T(128)} %param.12) | copy-start | bytes 1156
  18.5 10.1 %copy-start.7 = (s32[96]{0:T(128)S(1)}, s32[96]{0:T(128)}, u32[]{:S(2)}) copy-start(s32[96]{0:T(128)} %param.13) | copy-start | bytes 1156
  18.5 3.5 %copy-start.2 = (bf16[2,3,64,128]{3,2,1,0:T(8,128)(2,1)}, bf16[2,3,64,128]{3,2,1,0:T(8,128)(2,1)S(1)}, u32[]{:S(2)}) copy-start(bf16[2,3,64,128]{3,2,1,0:T(8,128)(2,1)S(1)} %collective-permute-done.1.far_wave) | copy-start | bytes 294916
  22.0 16.8 %collective-permute-start.3 = (bf16[99,16,128]{2,1,0:T(8,128)(2,1)}, bf16[99,16,128]{2,1,0:T(8,128)(2,1)S(1)}, u32[]{:S(2)}, u32[]{:S(2)}) collective-permute-start(bf16[99,16,128]{2,1,0:T(8,128)(2,1)} %get-tuple-element.15), channel_id=1, source_target_pairs={{0,64},{32,96},{64,128},{96,160},{128,192},{160,224},{192,1},{224,... | collective-permute-start | bytes 1216520 | tf_op jit(solution)/shard_map/ppermute | solution.py:360
  22.8 16.0 %collective-permute-start.4 = (bf16[99,16,128]{2,1,0:T(8,128)(2,1)}, bf16[99,16,128]{2,1,0:T(8,128)(2,1)}, u32[]{:S(2)}, u32[]{:S(2)}) collective-permute-start(bf16[99,16,128]{2,1,0:T(8,128)(2,1)} %get-tuple-element.16), channel_id=1, source_target_pairs={{0,193},{32,225},{64,0},{96,32},{128,64},{160,96},{192,128},{224,1... | collective-permute-start | bytes 1216520 | tf_op jit(solution)/shard_map/ppermute | solution.py:361
  24.7 14.0 %collective-permute-start.5 = (bf16[27,16,128]{2,1,0:T(8,128)(2,1)}, bf16[27,16,128]{2,1,0:T(8,128)(2,1)S(1)}, u32[]{:S(2)}, u32[]{:S(2)}) collective-permute-start(bf16[27,16,128]{2,1,0:T(8,128)(2,1)} %get-tuple-element.17), channel_id=1, source_target_pairs={{0,128},{32,160},{64,192},{96,224},{128,1},{160,33},{192,65},{224,... | collective-permute-start | bytes 331784 | tf_op jit(solution)/shard_map/ppermute | solution.py:362
  24.7 14.0 %collective-permute-start.6 = (bf16[27,16,128]{2,1,0:T(8,128)(2,1)}, bf16[27,16,128]{2,1,0:T(8,128)(2,1)S(1)}, u32[]{:S(2)}, u32[]{:S(2)}) collective-permute-start(bf16[27,16,128]{2,1,0:T(8,128)(2,1)} %get-tuple-element.18), channel_id=1, source_target_pairs={{0,129},{32,161},{64,193},{96,225},{128,0},{160,32},{192,64},{224,... | collective-permute-start | bytes 331784 | tf_op jit(solution)/shard_map/ppermute | solution.py:363
  29.5 1.4 %copy-start.1 = (bf16[12,2,2,128,128]{4,3,2,1,0:T(8,128)(2,1)S(1)}, bf16[12,2,2,128,128]{4,3,2,1,0:T(8,128)(2,1)}, u32[]{:S(2)}) copy-start(bf16[12,2,2,128,128]{4,3,2,1,0:T(8,128)(2,1)} %own_left.3) | copy-start | bytes 4718596
  30.9 0.9 %copy-start.3 = (bf16[2,3,64,128]{3,2,1,0:T(8,128)(2,1)S(1)}, bf16[2,3,64,128]{3,2,1,0:T(8,128)(2,1)}, u32[]{:S(2)}) copy-start(bf16[2,3,64,128]{3,2,1,0:T(8,128)(2,1)} %copy-done.2) | copy-start | bytes 294916
  31.8 7.0 %copy-start.4 = (s32[128,32]{0,1:T(8,128)S(1)}, s32[128,32]{0,1:T(8,128)}, u32[]{:S(2)}) copy-start(s32[128,32]{0,1:T(8,128)} %param.11) | copy-start | bytes 49156

commit v9 on v8

--- a/solution.py
+++ b/solution.py
@@ -86,6 +86,7 @@
     results, outs = refs[:count], refs[count : 2 * count] if sent else refs[:count]
     sides, bras, kets, operators, own_table, far_table, sem, out_sem = refs[-8:]
     core, _, z, q = where()
+    ahead = 1 - 2 * core
     low = z < 4
     copies = [
         pltpu.make_async_copy(own_table_ref, own_table, sem.at[0]),
@@ -130,7 +131,7 @@
     leaving = []
     for half in range(2):
         if sent:
-            spots = [lax.rem(z + 1, 8), lax.rem(z + 7, 8), lax.rem(z + (6 if half else 2), 8)]
+            spots = [(z + ahead) & 7, (z - ahead) & 7, (z - 2 * ahead if half else z + 2 * ahead) & 7]
         else:
             spots = [z, z ^ 2]
         width = 16 * len(spots)
@@ -240,9 +241,9 @@
 
 
 def contract_kernel(
-    home, up1, down1, up2, down2, right, right_table, picks, out, paired_ref
+    home, ahead1, back1, ahead2, back2, right, right_table, picks, out, paired_ref
 ):
-    arrays = (home, up1, down1, up2, down2)
+    arrays = (home, ahead1, back1, ahead2, back2)
     zero = jnp.zeros((96, 128), BF)
 
     def lefts(a):
@@ -298,11 +299,11 @@
 
     rest = jnp.concatenate([part(0), part(1)], axis=1)
     pieces = []
-    for _ in range(3):
+    for _ in range(2):
         pieces.append(rest.astype(BF))
         rest = rest - pieces[-1].astype(F32)
     total = jnp.dot(jnp.concatenate(pieces, axis=0), picks[...], preferred_element_type=F32)
-    total = total[0:128] + total[128:256] + total[256:384]
+    total = total[0:128] + total[128:256]
     total = total.astype(out.dtype)
     out[...] = jnp.zeros(out.shape, out.dtype)
     for t in range(2):
@@ -330,7 +331,7 @@
     for z in range(8):
         for core in range(2):
             place = lambda z: ((z % 4) * 2 + core) * 2 + z // 4
-            pairs.append((place(z), place(step(z))))
+            pairs.append((place(z), place(step(z, core))))
     return pairs
 
 
@@ -343,24 +344,25 @@
         [lax.dynamic_slice_in_dim(wave_blocks, (q + o) % 32, 1, 1) for o in range(3)], axis=1
     )
     far_wave = lax.ppermute(
-        own_wave, line, ring(lambda z: (z + 2) % 8 if z in (2, 3, 6, 7) else (z - 2) % 8)
+        own_wave, line, ring(lambda z, core: (z + 2) % 8 if z in (2, 3, 6, 7) else (z - 2) % 8)
     )
     swap = [(i, i ^ 1) for i in range(8)]
     far_left = lax.ppermute(left_operators, "row", swap)
     far_table = lax.ppermute(left_table, "row", swap)
     right = pick_right(right_operators)
     right = lax.all_to_all(right, "col", 0, 0, tiled=True)
-    up1, down1, up2, down2 = make_tiles(
+    ahead1, back1, ahead2, back2 = make_tiles(
         True, left_table, far_table, own_wave, far_wave, left_operators, far_left
     )
-    far_wave, assignment, kramers_map, up1 = lax.optimization_barrier(
-        (far_wave, assignment, kramers_map, up1)
-    )
+    far_wave, assignment, kramers_map, ahead1 = lax.optimization_barrier(
+        (far_wave, assignment, kramers_map, ahead1)
+    )
+    ahead = lambda steps: ring(lambda z, core: (z + steps * (1 - 2 * core)) % 8)
     arrived = [
-        lax.ppermute(up1, line, ring(lambda z: (z + 1) % 8)),
-        lax.ppermute(down1, line, ring(lambda z: (z + 7) % 8)),
-        lax.ppermute(up2, line, ring(lambda z: (z + 2) % 8)),
-        lax.ppermute(down2, line, ring(lambda z: (z + 6) % 8)),
+        lax.ppermute(ahead1, line, ahead(1)),
+        lax.ppermute(back1, line, ahead(-1)),
+        lax.ppermute(ahead2, line, ahead(2)),
+        lax.ppermute(back2, line, ahead(-2)),
     ]
     (home,) = make_tiles(
         False, left_table, far_table, own_wave, far_wave, left_operators, far_left
@@ -370,7 +372,9 @@
     held = assignment.reshape(4, 2, 12)
     held = jnp.where(core == 0, held, held[:, ::-1])
     held = lax.dynamic_slice_in_dim(jnp.concatenate([held, held], axis=0), z_lo, 4, 0)
-    held = jnp.concatenate([held[0:1], held[3:4], held[1:3]], axis=0).reshape(96, 1)
+    turned = jnp.concatenate([held[0:1], held[3:4], held[1:3]], axis=0)
+    straight = jnp.concatenate([held[0:2], held[3:4], held[2:3]], axis=0)
+    held = jnp.where(core == 0, turned, straight).reshape(96, 1)
     slot_key = (held * 4 + jnp.arange(4, dtype=jnp.int32)[None, :]).reshape(384, 1)
     target = jnp.stack([jnp.arange(96, dtype=jnp.int32), kramers_map]).reshape(1, 2, 8, 12)
     target = target.transpose(2, 0, 1, 3)

time: 67.5 us -> 66.4 us (0.984)
  waiting for transfers between devices: 4.38 us -> 6.81 us
  starting transfers between devices: 20.8 us -> 18.4 us
  blocking collectives: 24.7 us -> 23.6 us
    all_to_all x1, waiting for transfers between devices: 4.36 us -> 6.79 us  [local(): right = lax.all_to_all(right, 'col', 0, 0, tiled=True)]
    ppermute x5, starting transfers between devices: 10.7 us -> 8.27 us  [the longest x1 4.37 us: local(): lax.ppermute(own_wave, line, ring(lambda z, core: (z + 2) % 8 if z in (2,...]
    all_to_all x1, blocking collectives: 24.7 us -> 23.6 us  [local(): lax.all_to_all(shares.reshape(256, 2, 128), ('row', 'wf', 'col'), 0, 0, t...]
  transfers between devices with their start and end apart: 8 -> 8, of which waited for: 1 -> 1; matrix products, arithmetic and copies ran while one was open for 3% -> 3% of each run, Pallas kernels for 13% -> 14%
where the time goes in v9:
time: 66.4 us; the launch traced here: 66 us
  blocking collectives  23.6 us (36%)
  starting transfers between devices  18.4 us (28%)
  Pallas kernels  11.6 us (17%)
  waiting for transfers between devices  6.81 us (10%)
  local copies, waits for them, and re-layouts  4.62 us (7%)
    all_to_all x1, blocking collectives, local(): lax.all_to_all(shares.reshape(256, 2, 128), ('row', 'wf', 'col'), 0, 0, t...  23.6 us
    all_to_all x1, starting transfers between devices, local(): right = lax.all_to_all(right, 'col', 0, 0, tiled=True)  6.9 us
    all_to_all x1, waiting for transfers between devices, local(): right = lax.all_to_all(right, 'col', 0, 0, tiled=True)  6.79 us
    pallas_call x2, Pallas kernels, make_tiles(): pl.pallas_call(functools.partial(tiles_kernel, sent), in_specs=[anywhere]...  6.01 us
    ppermute x1, starting transfers between devices, local(): lax.ppermute(own_wave, line, ring(lambda z, core: (z + 2) % 8 if z in (2,...  4.37 us
    ppermute x1, starting transfers between devices, local(): far_left = lax.ppermute(left_operators, 'row', swap)  3.24 us
    pallas_call x1, Pallas kernels, pick_right(): pl.pallas_call(pick_right_kernel, in_specs=[pl.BlockSpec(memory_space=plt...  2.85 us
    pallas_call x1, Pallas kernels, contract(): pl.pallas_call(contract_kernel, in_specs=[whole] * 8, out_specs=whole, ou...  2.58 us
  transfers between devices with their start and end apart: 8, of which 1 were waited for; matrix products, arithmetic and copies ran while one was open for 3% of the time, Pallas kernels for 14%

profile of v9, /device:TPU:1, one launch (start us, length us, event | category | flops | bytes accessed | tf_op | source)
XLA Modules:
  0.0 66.0 jit_solution(2584479360625669883)
XLA Ops:
  0.0 3.2 %collective-permute-start.2 = (bf16[12,2,2,128,128]{4,3,2,1,0:T(8,128)(2,1)}, bf16[12,2,2,128,128]{4,3,2,1,0:T(8,128)(2,1)}, u32[]{:S(2)}, u32[]{:S(2)}) collective-permute-start(bf16[12,2,2,128,128]{4,3,2,1,0:T(8,128)(2,1)} %own_left.3), channel_id=1, source_target_pairs={{0,32},{32,0},{64,96},{96,64},{128,160},{160,128},{192,224},{224,1... | collective-permute-start | bytes 4718600 | tf_op jit(solution)/shard_map/ppermute | solution.py:350
  3.2 0.0 collective-permute-start
  3.2 0.8 %constant_dynamic-slice_fusion.2 = (bf16[2,1,64,128]{3,2,1,0:T(8,128)(2,1)S(1)}, bf16[2,1,64,128]{3,2,1,0:T(8,128)(2,1)S(1)}, bf16[2,1,64,128]{3,2,1,0:T(8,128)(2,1)S(1)}) fusion(bf16[2,32,64,128]{3,2,1,0:T(8,128)(2,1)} %param.7, s32[]{:T(128)S(6)} %select_n.46, s32[]{:T(128)S(6)} %select_n.50, s32[]{:T(128)S(6)} %select_n.48), kind=kLoop, calls=%fused_computation.19 | loop fusion | bytes 196620 | tf_op jit(solution)/shard_map/dynamic_slice | solution.py:344
  4.1 4.4 %collective-permute-start.1 = (bf16[2,3,64,128]{3,2,1,0:T(8,128)(2,1)S(1)}, bf16[2,3,64,128]{3,2,1,0:T(8,128)(2,1)S(1)}, u32[]{:S(2)}, u32[]{:S(2)}) collective-permute-start(bf16[2,3,64,128]{3,2,1,0:T(8,128)(2,1)S(1)} %pad_maximum_fusion.own_wave), channel_id=1, source_target_pairs={{0,129},{32,161},{64,193},{96,225},{128,1},{160,33},{192,65},{224,... | collective-permute-start | bytes 294920 | tf_op jit(solution)/shard_map/ppermute | solution.py:346
  8.4 2.8 %pick_right.1 = bf16[16,24,16,128]{3,2,1,0:T(8,128)(2,1)} custom-call(bf16[16,2,8,2,4,16,128]{6,5,4,3,2,1,0:T(8,128)(2,1)} %bitcast.21), custom_call_target="tpu_custom_call" | custom-call | tf_op jit(solution)/shard_map/pick_right/pallas_call | solution.py:62
  11.3 0.0 copy-start
  11.3 0.0 copy-start.5
  11.3 6.9 %all-to-all-start = ((bf16[16,24,16,128]{3,2,1,0:T(8,128)(2,1)}), bf16[16,24,16,128]{3,2,1,0:T(8,128)(2,1)S(1)}, u32[]{:S(2)}, u32[]{:S(2)}) async-start(bf16[16,24,16,128]{3,2,1,0:T(8,128)(2,1)} %pick_right.1), calls=%async_computation | async-start | bytes 3145728 | tf_op jit(solution)/shard_map/all_to_all | solution.py:353
  18.3 0.1 broadcast_in_dim.2
  18.3 0.1 reshape.140.sign
  18.5 0.0 copy-start.6
  18.5 0.0 copy-start.7
  18.5 0.0 collective-permute-done.far_table_ref
  18.5 0.0 collective-permute-done.1.far_wave
  18.5 0.0 copy-start.2
  18.5 0.0 collective-permute-done.2.far_left
  18.5 0.0 copy-done
  18.5 0.0 copy-done.5
  18.5 3.4 %make_tiles.1 = (bf16[99,16,128]{2,1,0:T(8,128)(2,1)}, bf16[99,16,128]{2,1,0:T(8,128)(2,1)}, bf16[27,16,128]{2,1,0:T(8,128)(2,1)}, bf16[27,16,128]{2,1,0:T(8,128)(2,1)}) custom-call(s32[12,32]{1,0:T(8,128)S(1)} %copy-done.5, s32[12,32]{1,0:T(8,128)S(1)} %collective-permute-done.far_table_ref, bf16[2,3,64,128]{3,2,1,0:T(8,128)(2,1)S(1)} %pad_maximum_fusion.own_wave, ...), custom_call_target="tpu_custom_call" | custom-call | flops 1000000000 | bytes 4000000 | tf_op jit(solution)/shard_map/make_tiles/pallas_call | solution.py:205
  22.0 0.0 copy-done.2
  22.0 0.1 collective-permute-start.3
  22.1 1.5 %collective-permute-start.4 = (bf16[99,16,128]{2,1,0:T(8,128)(2,1)}, bf16[99,16,128]{2,1,0:T(8,128)(2,1)}, u32[]{:S(2)}, u32[]{:S(2)}) collective-permute-start(bf16[99,16,128]{2,1,0:T(8,128)(2,1)} %get-tuple-element.16), channel_id=1, source_target_pairs={{0,193},{32,96},{64,0},{96,160},{128,64},{160,224},{192,128},{224,... | collective-permute-start | bytes 1216520 | tf_op jit(solution)/shard_map/ppermute | solution.py:363
  23.5 0.1 collective-permute-start.5
  23.6 2.3 %collective-permute-start.6 = (bf16[27,16,128]{2,1,0:T(8,128)(2,1)}, bf16[27,16,128]{2,1,0:T(8,128)(2,1)S(1)}, u32[]{:S(2)}, u32[]{:S(2)}) collective-permute-start(bf16[27,16,128]{2,1,0:T(8,128)(2,1)} %get-tuple-element.18), channel_id=1, source_target_pairs={{0,129},{32,160},{64,193},{96,224},{128,0},{160,33},{192,64},{224,... | collective-permute-start | bytes 331784 | tf_op jit(solution)/shard_map/ppermute | solution.py:365
  25.9 0.1 reshape.139
  26.1 0.1 mul.44
  26.2 0.1 stack.16
  26.3 0.1 fusion.2
  26.4 0.1 iota_add_fusion
  26.4 0.1 fusion.1
  26.5 0.1 add.143.slot_key
  26.6 0.1 add.139.real_key
  26.8 0.1 sub.29.imag_key
  26.9 0.2 make_picks.1.picks
  27.0 0.0 copy-start.1
  27.1 1.4 %copy-done.1 = bf16[12,2,2,128,128]{4,3,2,1,0:T(8,128)(2,1)S(1)} copy-done((bf16[12,2,2,128,128]{4,3,2,1,0:T(8,128)(2,1)S(1)}, bf16[12,2,2,128,128]{4,3,2,1,0:T(8,128)(2,1)}, u32[]{:S(2)}) %copy-start.1) | copy-done | bytes 1572888
  28.5 0.9 %copy-done.3 = bf16[2,3,64,128]{3,2,1,0:T(8,128)(2,1)S(1)} copy-done((bf16[2,3,64,128]{3,2,1,0:T(8,128)(2,1)S(1)}, bf16[2,3,64,128]{3,2,1,0:T(8,128)(2,1)}, u32[]{:S(2)}) %copy-start.3) | copy-done | bytes 98328
  29.4 2.6 %make_home.1.home = bf16[147,16,128]{2,1,0:T(8,128)(2,1)S(1)} custom-call(s32[12,32]{1,0:T(8,128)S(1)} %copy-done.5, s32[12,32]{1,0:T(8,128)S(1)} %collective-permute-done.far_table_ref, bf16[2,3,64,128]{3,2,1,0:T(8,128)(2,1)S(1)} %pad_maximum_fusion.own_wave, bf16[2,3,64,128]{3,2,1,0:T(8,128)(2,1)S(1)} %copy-done.3, ...), custom_call_target="tpu_custom_call" | custom-call | flops 1000000000 | bytes 4000000 | tf_op jit(solution)/shard_map/make_home/pallas_call | solution.py:205
  32.0 6.8 %all-to-all-done.right = bf16[16,24,16,128]{3,2,1,0:T(8,128)(2,1)S(1)} async-done(((bf16[16,24,16,128]{3,2,1,0:T(8,128)(2,1)}), bf16[16,24,16,128]{3,2,1,0:T(8,128)(2,1)S(1)}, u32[]{:S(2)}, u32[]{:S(2)}) %all-to-all-start) | async-done | bytes 1572896 | tf_op jit(solution)/shard_map/all_to_all | solution.py:353
  38.7 0.0 collective-permute-done.5.ahead2
  38.7 0.0 collective-permute-done.6.back2
  38.8 0.0 collective-permute-done.3.ahead1
  38.8 0.0 collective-permute-done.4.back1
  38.8 2.6 %contract.1 = bf16[8,64,128]{2,1,0:T(8,128)(2,1)S(1)} custom-call(bf16[147,16,128]{2,1,0:T(8,128)(2,1)S(1)} %make_home.1.home, bf16[99,16,128]{2,1,0:T(8,128)(2,1)S(1)} %collective-permute-done.3.ahead1, bf16[99,16,128]{2,1,0:T(8,128)(2,1)} %collective-permute-done.4.back1, bf16[27,16,128]{2,1,0:T(8,128)(2,1)S(1)} %collective-permute-done.5.ahead2, ...), custom_call_target="tpu_custom_call" | custom-call | tf_op jit(solution)/shard_map/contract/pallas_call | solution.py:318
  41.4 23.6 %all_to_all.10 = bf16[256,2,128]{2,1,0:T(2,128)(2,1)S(1)} all-to-all(bf16[256,2,128]{2,1,0:T(2,128)(2,1)S(1)} %bitcast.19), channel_id=1, replica_groups=mesh['row'=8,'col'=16,'wf'=2] {'row','wf','col'}, dimensions={0} | all-to-all | bytes 262144 | tf_op jit(solution)/shard_map/all_to_all | solution.py:389
  65.0 0.3 convert_reduce_fusion
  65.3 0.1 reshape.142
  65.4 0.6 copy.13
  (19 shorter events, 0.2 us)
Async XLA Ops:
  0.0 18.5 %collective-permute-start.2 = (bf16[12,2,2,128,128]{4,3,2,1,0:T(8,128)(2,1)}, bf16[12,2,2,128,128]{4,3,2,1,0:T(8,128)(2,1)}, u32[]{:S(2)}, u32[]{:S(2)}) collective-permute-start(bf16[12,2,2,128,128]{4,3,2,1,0:T(8,128)(2,1)} %own_left.3), channel_id=1, source_target_pairs={{0,32},{32,0},{64,96},{96,64},{128,160},{160,128},{192,224},{224,1... | collective-permute-start | bytes 4718600 | tf_op jit(solution)/shard_map/ppermute | solution.py:350
  3.2 15.2 %collective-permute-start = (s32[12,32]{1,0:T(8,128)}, s32[12,32]{1,0:T(8,128)S(1)}, u32[]{:S(2)}, u32[]{:S(2)}) collective-permute-start(s32[12,32]{1,0:T(8,128)} %own_table_ref.3), channel_id=1, source_target_pairs={{0,32},{32,0},{64,96},{96,64},{128,160},{160,128},{192,224},{224,1... | collective-permute-start | bytes 4616 | tf_op jit(solution)/shard_map/ppermute | solution.py:351
  4.1 14.4 %collective-permute-start.1 = (bf16[2,3,64,128]{3,2,1,0:T(8,128)(2,1)S(1)}, bf16[2,3,64,128]{3,2,1,0:T(8,128)(2,1)S(1)}, u32[]{:S(2)}, u32[]{:S(2)}) collective-permute-start(bf16[2,3,64,128]{3,2,1,0:T(8,128)(2,1)S(1)} %pad_maximum_fusion.own_wave), channel_id=1, source_target_pairs={{0,129},{32,161},{64,193},{96,225},{128,1},{160,33},{192,65},{224,... | collective-permute-start | bytes 294920 | tf_op jit(solution)/shard_map/ppermute | solution.py:346
  11.3 7.2 %copy-start = (bf16[12,2,2,128,128]{4,3,2,1,0:T(8,128)(2,1)S(1)}, bf16[12,2,2,128,128]{4,3,2,1,0:T(8,128)(2,1)}, u32[]{:S(2)}) copy-start(bf16[12,2,2,128,128]{4,3,2,1,0:T(8,128)(2,1)} %own_left.3) | copy-start | bytes 4718596
  11.3 7.2 %copy-start.5 = (s32[12,32]{1,0:T(8,128)S(1)}, s32[12,32]{1,0:T(8,128)}, u32[]{:S(2)}) copy-start(s32[12,32]{1,0:T(8,128)} %own_table_ref.3) | copy-start | bytes 4612
  11.3 27.4 %all-to-all-start = ((bf16[16,24,16,128]{3,2,1,0:T(8,128)(2,1)}), bf16[16,24,16,128]{3,2,1,0:T(8,128)(2,1)S(1)}, u32[]{:S(2)}, u32[]{:S(2)}) async-start(bf16[16,24,16,128]{3,2,1,0:T(8,128)(2,1)} %pick_right.1), calls=%async_computation | async-start | bytes 3145728 | tf_op jit(solution)/shard_map/all_to_all | solution.py:353
  18.5 7.4 %copy-start.6 = (s32[96]{0:T(128)S(1)}, s32[96]{0:T(128)}, u32[]{:S(2)}) copy-start(s32[96]{0:T(128)} %param.12) | copy-start | bytes 1156
  18.5 7.7 %copy-start.7 = (s32[96]{0:T(128)S(1)}, s32[96]{0:T(128)}, u32[]{:S(2)}) copy-start(s32[96]{0:T(128)} %param.13) | copy-start | bytes 1156
  18.5 3.5 %copy-start.2 = (bf16[2,3,64,128]{3,2,1,0:T(8,128)(2,1)}, bf16[2,3,64,128]{3,2,1,0:T(8,128)(2,1)S(1)}, u32[]{:S(2)}) copy-start(bf16[2,3,64,128]{3,2,1,0:T(8,128)(2,1)S(1)} %collective-permute-done.1.far_wave) | copy-start | bytes 294916
  22.0 16.8 %collective-permute-start.3 = (bf16[99,16,128]{2,1,0:T(8,128)(2,1)}, bf16[99,16,128]{2,1,0:T(8,128)(2,1)S(1)}, u32[]{:S(2)}, u32[]{:S(2)}) collective-permute-start(bf16[99,16,128]{2,1,0:T(8,128)(2,1)} %get-tuple-element.15), channel_id=1, source_target_pairs={{0,64},{32,225},{64,128},{96,32},{128,192},{160,96},{192,1},{224,1... | collective-permute-start | bytes 1216520 | tf_op jit(solution)/shard_map/ppermute | solution.py:362
  22.1 16.7 %collective-permute-start.4 = (bf16[99,16,128]{2,1,0:T(8,128)(2,1)}, bf16[99,16,128]{2,1,0:T(8,128)(2,1)}, u32[]{:S(2)}, u32[]{:S(2)}) collective-permute-start(bf16[99,16,128]{2,1,0:T(8,128)(2,1)} %get-tuple-element.16), channel_id=1, source_target_pairs={{0,193},{32,96},{64,0},{96,160},{128,64},{160,224},{192,128},{224,... | collective-permute-start | bytes 1216520 | tf_op jit(solution)/shard_map/ppermute | solution.py:363
  23.5 15.2 %collective-permute-start.5 = (bf16[27,16,128]{2,1,0:T(8,128)(2,1)}, bf16[27,16,128]{2,1,0:T(8,128)(2,1)S(1)}, u32[]{:S(2)}, u32[]{:S(2)}) collective-permute-start(bf16[27,16,128]{2,1,0:T(8,128)(2,1)} %get-tuple-element.17), channel_id=1, source_target_pairs={{0,128},{32,161},{64,192},{96,225},{128,1},{160,32},{192,65},{224,... | collective-permute-start | bytes 331784 | tf_op jit(solution)/shard_map/ppermute | solution.py:364
  23.6 15.2 %collective-permute-start.6 = (bf16[27,16,128]{2,1,0:T(8,128)(2,1)}, bf16[27,16,128]{2,1,0:T(8,128)(2,1)S(1)}, u32[]{:S(2)}, u32[]{:S(2)}) collective-permute-start(bf16[27,16,128]{2,1,0:T(8,128)(2,1)} %get-tuple-element.18), channel_id=1, source_target_pairs={{0,129},{32,160},{64,193},{96,224},{128,0},{160,33},{192,64},{224,... | collective-permute-start | bytes 331784 | tf_op jit(solution)/shard_map/ppermute | solution.py:365
  27.0 1.4 %copy-start.1 = (bf16[12,2,2,128,128]{4,3,2,1,0:T(8,128)(2,1)S(1)}, bf16[12,2,2,128,128]{4,3,2,1,0:T(8,128)(2,1)}, u32[]{:S(2)}) copy-start(bf16[12,2,2,128,128]{4,3,2,1,0:T(8,128)(2,1)} %own_left.3) | copy-start | bytes 4718596
  28.5 0.9 %copy-start.3 = (bf16[2,3,64,128]{3,2,1,0:T(8,128)(2,1)S(1)}, bf16[2,3,64,128]{3,2,1,0:T(8,128)(2,1)}, u32[]{:S(2)}) copy-start(bf16[2,3,64,128]{3,2,1,0:T(8,128)(2,1)} %copy-done.2) | copy-start | bytes 294916
  29.3 9.4 %copy-start.4 = (s32[128,32]{0,1:T(8,128)S(1)}, s32[128,32]{0,1:T(8,128)}, u32[]{:S(2)}) copy-start(s32[128,32]{0,1:T(8,128)} %param.11) | copy-start | bytes 49156

commit v10 on v9

--- a/solution.py
+++ b/solution.py
@@ -24,8 +24,14 @@
     return pltpu.CompilerParams(vmem_limit_bytes=mebibytes * 1024 * 1024)
 
 
-def pick_right_kernel(right_ref, out_ref, rows_ref, sem):
-    core, z_lo, _, _ = where()
+def pick_kernel(right_ref, wave_ref, out_ref, wave_out, rows_ref, sem, wave_sem):
+    core, z_lo, _, q = where()
+    waves = [
+        pltpu.make_async_copy(wave_ref.at[:, (q + o) & 31], wave_out.at[:, o], wave_sem.at[o])
+        for o in range(3)
+    ]
+    for copy in waves:
+        copy.start()
     copies = []
     for part in range(4):
         for second in range(2):
@@ -56,21 +62,28 @@
                     out_ref[target, 16:24] = rows[8:16]
                 else:
                     out_ref[target, 0:16] = rows
-
-
-def pick_right(right_operators):
+    for copy in waves:
+        copy.wait()
+
+
+def pick(right_operators, wave_blocks):
+    whole = pl.BlockSpec(memory_space=pltpu.VMEM)
     return pl.pallas_call(
-        pick_right_kernel,
-        in_specs=[pl.BlockSpec(memory_space=pltpu.HBM)],
-        out_specs=pl.BlockSpec(memory_space=pltpu.VMEM),
-        out_shape=jax.ShapeDtypeStruct((16, 24, 16, 128), BF),
+        pick_kernel,
+        in_specs=[pl.BlockSpec(memory_space=pltpu.HBM)] * 2,
+        out_specs=[whole] * 2,
+        out_shape=[
+            jax.ShapeDtypeStruct((16, 24, 16, 128), BF),
+            jax.ShapeDtypeStruct((2, 3, 64, 128), BF),
+        ],
         scratch_shapes=[
             pltpu.VMEM((2, 16, 8, 2, 16, 128), BF),
             pltpu.SemaphoreType.DMA((4, 2)),
+            pltpu.SemaphoreType.DMA((3,)),
         ],
         compiler_params=params(54),
-        name="pick_right",
-    )(right_operators.reshape(16, 2, 8, 2, 4, 16, 128))
+        name="pick",
+    )(right_operators.reshape(16, 2, 8, 2, 4, 16, 128), wave_blocks)
 
 
 GROUPS = (6, 6, 6, 3, 3)
@@ -339,17 +352,14 @@
     wave_blocks, left_operators, right_operators, left_table, right_table, assignment, kramers_map
 ):
     line = ("row", "wf")
-    core, z_lo, _, q = where()
-    own_wave = jnp.concatenate(
-        [lax.dynamic_slice_in_dim(wave_blocks, (q + o) % 32, 1, 1) for o in range(3)], axis=1
-    )
+    core, z_lo, _, _ = where()
+    right, own_wave = pick(right_operators, wave_blocks)
     far_wave = lax.ppermute(
         own_wave, line, ring(lambda z, core: (z + 2) % 8 if z in (2, 3, 6, 7) else (z - 2) % 8)
     )
     swap = [(i, i ^ 1) for i in range(8)]
     far_left = lax.ppermute(left_operators, "row", swap)
     far_table = lax.ppermute(left_table, "row", swap)
-    right = pick_right(right_operators)
     right = lax.all_to_all(right, "col", 0, 0, tiled=True)
     ahead1, back1, ahead2, back2 = make_tiles(
         True, left_table, far_table, own_wave, far_wave, left_operators, far_left

time: 66.4 us -> 65.6 us (0.988)
  local copies, waits for them, and re-layouts: 4.62 us -> 3.82 us
    ppermute x1, starting transfers between devices: 0.05 us -> 1.49 us  [local(): lax.ppermute(ahead2, line, ahead(2))]
    ppermute x1, starting transfers between devices: 2.31 us -> 0.87 us  [local(): lax.ppermute(back2, line, ahead(-2))]
    dynamic_slice x1 -> x0, local copies, waits for them, and re-layouts: 0.8 us -> none  [local(): lax.dynamic_slice_in_dim(wave_blocks, (q + o) % 32, 1, 1)]
    unnamed x16 -> x18, local copies, waits for them, and re-layouts: 2.33 us -> 2.33 us
  transfers between devices with their start and end apart: 8 -> 8, of which waited for: 1 -> 2; matrix products, arithmetic and copies ran while one was open for 3% -> 2% of each run, Pallas kernels for 14% -> 14%
where the time goes in v10:
time: 65.6 us; the launch traced here: 65.3 us
  blocking collectives  23.4 us (36%)
  starting transfers between devices  18.4 us (28%)
  Pallas kernels  11.7 us (18%)
  waiting for transfers between devices  7.05 us (11%)
  local copies, waits for them, and re-layouts  3.82 us (6%)
    all_to_all x1, blocking collectives, local(): lax.all_to_all(shares.reshape(256, 2, 128), ('row', 'wf', 'col'), 0, 0, t...  23.4 us
    all_to_all x1, starting transfers between devices, local(): right = lax.all_to_all(right, 'col', 0, 0, tiled=True)  6.89 us
    all_to_all x1, waiting for transfers between devices, local(): right = lax.all_to_all(right, 'col', 0, 0, tiled=True)  6.8 us
    pallas_call x2, Pallas kernels, make_tiles(): pl.pallas_call(functools.partial(tiles_kernel, sent), in_specs=[anywhere]...  6 us
    ppermute x1, starting transfers between devices, local(): lax.ppermute(own_wave, line, ring(lambda z, core: (z + 2) % 8 if z in (2,...  4.37 us
    ppermute x1, starting transfers between devices, local(): far_left = lax.ppermute(left_operators, 'row', swap)  3.24 us
    pallas_call x1, Pallas kernels, pick(): pl.pallas_call(pick_kernel, in_specs=[pl.BlockSpec(memory_space=pltpu.HBM...  2.98 us
    pallas_call x1, Pallas kernels, contract(): pl.pallas_call(contract_kernel, in_specs=[whole] * 8, out_specs=whole, ou...  2.58 us
  transfers between devices with their start and end apart: 8, of which 2 were waited for; matrix products, arithmetic and copies ran while one was open for 2% of the time, Pallas kernels for 14%

profile of v10, /device:TPU:1, one launch (start us, length us, event | category | flops | bytes accessed | tf_op | source)
XLA Modules:
  0.0 65.3 jit_solution(2376457500442375770)
XLA Ops:
  0.0 3.2 %collective-permute-start.2 = (bf16[12,2,2,128,128]{4,3,2,1,0:T(8,128)(2,1)}, bf16[12,2,2,128,128]{4,3,2,1,0:T(8,128)(2,1)}, u32[]{:S(2)}, u32[]{:S(2)}) collective-permute-start(bf16[12,2,2,128,128]{4,3,2,1,0:T(8,128)(2,1)} %own_left.3), channel_id=1, source_target_pairs={{0,32},{32,0},{64,96},{96,64},{128,160},{160,128},{192,224},{224,1... | collective-permute-start | bytes 4718600 | tf_op jit(solution)/shard_map/ppermute | solution.py:361
  3.2 0.0 collective-permute-start
  3.2 3.0 %pick.1 = (bf16[16,24,16,128]{3,2,1,0:T(8,128)(2,1)}, bf16[2,3,64,128]{3,2,1,0:T(8,128)(2,1)}) custom-call(bf16[16,2,8,2,4,16,128]{6,5,4,3,2,1,0:T(8,128)(2,1)} %bitcast.21, bf16[2,32,64,128]{3,2,1,0:T(8,128)(2,1)} %wave_ref.1), custom_call_target="tpu_custom_call" | custom-call | tf_op jit(solution)/shard_map/pick/pallas_call | solution.py:71
  6.2 4.4 %collective-permute-start.1 = (bf16[2,3,64,128]{3,2,1,0:T(8,128)(2,1)}, bf16[2,3,64,128]{3,2,1,0:T(8,128)(2,1)S(1)}, u32[]{:S(2)}, u32[]{:S(2)}) collective-permute-start(bf16[2,3,64,128]{3,2,1,0:T(8,128)(2,1)} %get-tuple-element.15.own_wave), channel_id=1, source_target_pairs={{0,129},{32,161},{64,193},{96,225},{128,1},{160,33},{192,65},{224,... | collective-permute-start | bytes 294920 | tf_op jit(solution)/shard_map/ppermute | solution.py:357
  10.6 6.9 %all-to-all-start = ((bf16[16,24,16,128]{3,2,1,0:T(8,128)(2,1)}), bf16[16,24,16,128]{3,2,1,0:T(8,128)(2,1)S(1)}, u32[]{:S(2)}, u32[]{:S(2)}) async-start(bf16[16,24,16,128]{3,2,1,0:T(8,128)(2,1)} %get-tuple-element.22), calls=%async_computation | async-start | bytes 3145728 | tf_op jit(solution)/shard_map/all_to_all | solution.py:363
  17.5 0.1 broadcast_in_dim.2
  17.6 0.1 reshape.140.sign
  17.7 0.0 copy-start.7
  17.8 0.0 copy-start.8
  17.8 0.0 collective-permute-done.far_table_ref
  17.8 0.0 collective-permute-done.1.far_wave
  17.8 0.0 copy-start.3
  17.8 0.0 collective-permute-done.2.far_left
  17.8 0.0 copy-done
  17.8 0.0 copy-done.2
  17.8 0.0 copy-done.6
  17.8 3.4 %make_tiles.1 = (bf16[99,16,128]{2,1,0:T(8,128)(2,1)}, bf16[99,16,128]{2,1,0:T(8,128)(2,1)}, bf16[27,16,128]{2,1,0:T(8,128)(2,1)}, bf16[27,16,128]{2,1,0:T(8,128)(2,1)}) custom-call(s32[12,32]{1,0:T(8,128)S(1)} %copy-done.6, s32[12,32]{1,0:T(8,128)S(1)} %collective-permute-done.far_table_ref, bf16[2,3,64,128]{3,2,1,0:T(8,128)(2,1)S(1)} %copy-done.2, ...), custom_call_target="tpu_custom_call" | custom-call | flops 1000000000 | bytes 4000000 | tf_op jit(solution)/shard_map/make_tiles/pallas_call | solution.py:218
  21.2 0.0 copy-done.3
  21.3 0.1 collective-permute-start.3
  21.3 1.5 %collective-permute-start.4 = (bf16[99,16,128]{2,1,0:T(8,128)(2,1)}, bf16[99,16,128]{2,1,0:T(8,128)(2,1)}, u32[]{:S(2)}, u32[]{:S(2)}) collective-permute-start(bf16[99,16,128]{2,1,0:T(8,128)(2,1)} %get-tuple-element.19), channel_id=1, source_target_pairs={{0,193},{32,96},{64,0},{96,160},{128,64},{160,224},{192,128},{224,... | collective-permute-start | bytes 1216520 | tf_op jit(solution)/shard_map/ppermute | solution.py:373
  22.8 1.5 %collective-permute-start.5 = (bf16[27,16,128]{2,1,0:T(8,128)(2,1)}, bf16[27,16,128]{2,1,0:T(8,128)(2,1)S(1)}, u32[]{:S(2)}, u32[]{:S(2)}) collective-permute-start(bf16[27,16,128]{2,1,0:T(8,128)(2,1)} %get-tuple-element.20), channel_id=1, source_target_pairs={{0,128},{32,161},{64,192},{96,225},{128,1},{160,32},{192,65},{224,... | collective-permute-start | bytes 331784 | tf_op jit(solution)/shard_map/ppermute | solution.py:374
  24.3 0.9 %collective-permute-start.6 = (bf16[27,16,128]{2,1,0:T(8,128)(2,1)}, bf16[27,16,128]{2,1,0:T(8,128)(2,1)S(1)}, u32[]{:S(2)}, u32[]{:S(2)}) collective-permute-start(bf16[27,16,128]{2,1,0:T(8,128)(2,1)} %get-tuple-element.21), channel_id=1, source_target_pairs={{0,129},{32,160},{64,193},{96,224},{128,0},{160,33},{192,64},{224,... | collective-permute-start | bytes 331784 | tf_op jit(solution)/shard_map/ppermute | solution.py:375
  25.2 0.0 copy-done.7
  25.2 0.1 reshape.139
  25.4 0.1 mul.40
  25.5 0.0 copy-done.8
  25.5 0.1 stack.16
  25.5 0.1 fusion.2
  25.6 0.1 iota_add_fusion
  25.7 0.1 fusion.1
  25.8 0.1 add.106.slot_key
  25.9 0.1 add.102.real_key
  26.0 0.1 sub.29.imag_key
  26.1 0.2 make_picks.1.picks
  26.3 0.0 copy-start.1
  26.3 1.4 %copy-done.1 = bf16[12,2,2,128,128]{4,3,2,1,0:T(8,128)(2,1)S(1)} copy-done((bf16[12,2,2,128,128]{4,3,2,1,0:T(8,128)(2,1)S(1)}, bf16[12,2,2,128,128]{4,3,2,1,0:T(8,128)(2,1)}, u32[]{:S(2)}) %copy-start.1) | copy-done | bytes 1572888
  27.7 0.9 %copy-done.4 = bf16[2,3,64,128]{3,2,1,0:T(8,128)(2,1)S(1)} copy-done((bf16[2,3,64,128]{3,2,1,0:T(8,128)(2,1)S(1)}, bf16[2,3,64,128]{3,2,1,0:T(8,128)(2,1)}, u32[]{:S(2)}) %copy-start.4) | copy-done | bytes 98328
  28.6 2.6 %make_home.1.home = bf16[147,16,128]{2,1,0:T(8,128)(2,1)S(1)} custom-call(s32[12,32]{1,0:T(8,128)S(1)} %copy-done.6, s32[12,32]{1,0:T(8,128)S(1)} %collective-permute-done.far_table_ref, bf16[2,3,64,128]{3,2,1,0:T(8,128)(2,1)S(1)} %copy-done.2, bf16[2,3,64,128]{3,2,1,0:T(8,128)(2,1)S(1)} %copy-done.4, bf16[12,2,2,128,128]{4,3,2,1,0:T(8,128)(2,1)S(1)} %copy-done.1, ...), custom_call_target="tpu_custom_call" | custom-call | flops 1000000000 | bytes 4000000 | tf_op jit(solution)/shard_map/make_home/pallas_call | solution.py:218
  31.2 6.8 %all-to-all-done.right = bf16[16,24,16,128]{3,2,1,0:T(8,128)(2,1)S(1)} async-done(((bf16[16,24,16,128]{3,2,1,0:T(8,128)(2,1)}), bf16[16,24,16,128]{3,2,1,0:T(8,128)(2,1)S(1)}, u32[]{:S(2)}, u32[]{:S(2)}) %all-to-all-start) | async-done | bytes 1572896 | tf_op jit(solution)/shard_map/all_to_all | solution.py:363
  38.0 0.0 collective-permute-done.5.ahead2
  38.0 0.2 collective-permute-done.6.back2
  38.3 0.0 collective-permute-done.3.ahead1
  38.3 0.0 collective-permute-done.4.back1
  38.3 2.6 %contract.1 = bf16[8,64,128]{2,1,0:T(8,128)(2,1)S(1)} custom-call(bf16[147,16,128]{2,1,0:T(8,128)(2,1)S(1)} %make_home.1.home, bf16[99,16,128]{2,1,0:T(8,128)(2,1)S(1)} %collective-permute-done.3.ahead1, bf16[99,16,128]{2,1,0:T(8,128)(2,1)} %collective-permute-done.4.back1, bf16[27,16,128]{2,1,0:T(8,128)(2,1)S(1)} %collective-permute-done.5.ahead2, ...), custom_call_target="tpu_custom_call" | custom-call | tf_op jit(solution)/shard_map/contract/pallas_call | solution.py:331
  40.9 23.4 %all_to_all.10 = bf16[256,2,128]{2,1,0:T(2,128)(2,1)S(1)} all-to-all(bf16[256,2,128]{2,1,0:T(2,128)(2,1)S(1)} %bitcast.19), channel_id=1, replica_groups=mesh['row'=8,'col'=16,'wf'=2] {'row','wf','col'}, dimensions={0} | all-to-all | bytes 262144 | tf_op jit(solution)/shard_map/all_to_all | solution.py:399
  64.3 0.3 convert_reduce_fusion
  64.6 0.1 reshape.142
  64.6 0.6 copy.13
  (19 shorter events, 0.1 us)
Async XLA Ops:
  0.0 17.8 %collective-permute-start.2 = (bf16[12,2,2,128,128]{4,3,2,1,0:T(8,128)(2,1)}, bf16[12,2,2,128,128]{4,3,2,1,0:T(8,128)(2,1)}, u32[]{:S(2)}, u32[]{:S(2)}) collective-permute-start(bf16[12,2,2,128,128]{4,3,2,1,0:T(8,128)(2,1)} %own_left.3), channel_id=1, source_target_pairs={{0,32},{32,0},{64,96},{96,64},{128,160},{160,128},{192,224},{224,1... | collective-permute-start | bytes 4718600 | tf_op jit(solution)/shard_map/ppermute | solution.py:361
  3.2 14.5 %collective-permute-start = (s32[12,32]{1,0:T(8,128)}, s32[12,32]{1,0:T(8,128)S(1)}, u32[]{:S(2)}, u32[]{:S(2)}) collective-permute-start(s32[12,32]{1,0:T(8,128)} %own_table_ref.3), channel_id=1, source_target_pairs={{0,32},{32,0},{64,96},{96,64},{128,160},{160,128},{192,224},{224,1... | collective-permute-start | bytes 4616 | tf_op jit(solution)/shard_map/ppermute | solution.py:362
  6.2 11.5 %collective-permute-start.1 = (bf16[2,3,64,128]{3,2,1,0:T(8,128)(2,1)}, bf16[2,3,64,128]{3,2,1,0:T(8,128)(2,1)S(1)}, u32[]{:S(2)}, u32[]{:S(2)}) collective-permute-start(bf16[2,3,64,128]{3,2,1,0:T(8,128)(2,1)} %get-tuple-element.15.own_wave), channel_id=1, source_target_pairs={{0,129},{32,161},{64,193},{96,225},{128,1},{160,33},{192,65},{224,... | collective-permute-start | bytes 294920 | tf_op jit(solution)/shard_map/ppermute | solution.py:357
  10.6 7.2 %copy-start = (bf16[12,2,2,128,128]{4,3,2,1,0:T(8,128)(2,1)S(1)}, bf16[12,2,2,128,128]{4,3,2,1,0:T(8,128)(2,1)}, u32[]{:S(2)}) copy-start(bf16[12,2,2,128,128]{4,3,2,1,0:T(8,128)(2,1)} %own_left.3) | copy-start | bytes 4718596
  10.6 7.2 %copy-start.2 = (bf16[2,3,64,128]{3,2,1,0:T(8,128)(2,1)S(1)}, bf16[2,3,64,128]{3,2,1,0:T(8,128)(2,1)}, u32[]{:S(2)}) copy-start(bf16[2,3,64,128]{3,2,1,0:T(8,128)(2,1)} %get-tuple-element.15.own_wave) | copy-start | bytes 294916
  10.6 7.2 %copy-start.6 = (s32[12,32]{1,0:T(8,128)S(1)}, s32[12,32]{1,0:T(8,128)}, u32[]{:S(2)}) copy-start(s32[12,32]{1,0:T(8,128)} %own_table_ref.3) | copy-start | bytes 4612
  10.6 27.4 %all-to-all-start = ((bf16[16,24,16,128]{3,2,1,0:T(8,128)(2,1)}), bf16[16,24,16,128]{3,2,1,0:T(8,128)(2,1)S(1)}, u32[]{:S(2)}, u32[]{:S(2)}) async-start(bf16[16,24,16,128]{3,2,1,0:T(8,128)(2,1)} %get-tuple-element.22), calls=%async_computation | async-start | bytes 3145728 | tf_op jit(solution)/shard_map/all_to_all | solution.py:363
  17.7 7.4 %copy-start.7 = (s32[96]{0:T(128)S(1)}, s32[96]{0:T(128)}, u32[]{:S(2)}) copy-start(s32[96]{0:T(128)} %param.12) | copy-start | bytes 1156
  17.8 7.7 %copy-start.8 = (s32[96]{0:T(128)S(1)}, s32[96]{0:T(128)}, u32[]{:S(2)}) copy-start(s32[96]{0:T(128)} %param.13) | copy-start | bytes 1156
  17.8 3.5 %copy-start.3 = (bf16[2,3,64,128]{3,2,1,0:T(8,128)(2,1)}, bf16[2,3,64,128]{3,2,1,0:T(8,128)(2,1)S(1)}, u32[]{:S(2)}) copy-start(bf16[2,3,64,128]{3,2,1,0:T(8,128)(2,1)S(1)} %collective-permute-done.1.far_wave) | copy-start | bytes 294916
  21.3 17.0 %collective-permute-start.3 = (bf16[99,16,128]{2,1,0:T(8,128)(2,1)}, bf16[99,16,128]{2,1,0:T(8,128)(2,1)S(1)}, u32[]{:S(2)}, u32[]{:S(2)}) collective-permute-start(bf16[99,16,128]{2,1,0:T(8,128)(2,1)} %get-tuple-element.18), channel_id=1, source_target_pairs={{0,64},{32,225},{64,128},{96,32},{128,192},{160,96},{192,1},{224,1... | collective-permute-start | bytes 1216520 | tf_op jit(solution)/shard_map/ppermute | solution.py:372
  21.3 16.9 %collective-permute-start.4 = (bf16[99,16,128]{2,1,0:T(8,128)(2,1)}, bf16[99,16,128]{2,1,0:T(8,128)(2,1)}, u32[]{:S(2)}, u32[]{:S(2)}) collective-permute-start(bf16[99,16,128]{2,1,0:T(8,128)(2,1)} %get-tuple-element.19), channel_id=1, source_target_pairs={{0,193},{32,96},{64,0},{96,160},{128,64},{160,224},{192,128},{224,... | collective-permute-start | bytes 1216520 | tf_op jit(solution)/shard_map/ppermute | solution.py:373
  22.8 15.2 %collective-permute-start.5 = (bf16[27,16,128]{2,1,0:T(8,128)(2,1)}, bf16[27,16,128]{2,1,0:T(8,128)(2,1)S(1)}, u32[]{:S(2)}, u32[]{:S(2)}) collective-permute-start(bf16[27,16,128]{2,1,0:T(8,128)(2,1)} %get-tuple-element.20), channel_id=1, source_target_pairs={{0,128},{32,161},{64,192},{96,225},{128,1},{160,32},{192,65},{224,... | collective-permute-start | bytes 331784 | tf_op jit(solution)/shard_map/ppermute | solution.py:374
  24.3 14.0 %collective-permute-start.6 = (bf16[27,16,128]{2,1,0:T(8,128)(2,1)}, bf16[27,16,128]{2,1,0:T(8,128)(2,1)S(1)}, u32[]{:S(2)}, u32[]{:S(2)}) collective-permute-start(bf16[27,16,128]{2,1,0:T(8,128)(2,1)} %get-tuple-element.21), channel_id=1, source_target_pairs={{0,129},{32,160},{64,193},{96,224},{128,0},{160,33},{192,64},{224,... | collective-permute-start | bytes 331784 | tf_op jit(solution)/shard_map/ppermute | solution.py:375
  26.3 1.4 %copy-start.1 = (bf16[12,2,2,128,128]{4,3,2,1,0:T(8,128)(2,1)S(1)}, bf16[12,2,2,128,128]{4,3,2,1,0:T(8,128)(2,1)}, u32[]{:S(2)}) copy-start(bf16[12,2,2,128,128]{4,3,2,1,0:T(8,128)(2,1)} %own_left.3) | copy-start | bytes 4718596
  27.7 0.9 %copy-start.4 = (bf16[2,3,64,128]{3,2,1,0:T(8,128)(2,1)S(1)}, bf16[2,3,64,128]{3,2,1,0:T(8,128)(2,1)}, u32[]{:S(2)}) copy-start(bf16[2,3,64,128]{3,2,1,0:T(8,128)(2,1)} %copy-done.3) | copy-start | bytes 294916
  28.6 9.6 %copy-start.5 = (s32[128,32]{0,1:T(8,128)S(1)}, s32[128,32]{0,1:T(8,128)}, u32[]{:S(2)}) copy-start(s32[128,32]{0,1:T(8,128)} %param.11) | copy-start | bytes 49156

commit v11 on v10

--- a/solution.py
+++ b/solution.py
@@ -93,19 +93,17 @@
 
 
 def tiles_kernel(
-    sent, own_table_ref, far_table_ref, own_wave, far_wave, own_left, far_left, *refs
+    sent, own_table, far_table, own_wave, far_wave, own_left, far_left, *refs
 ):
     count = 4 if sent else 1
     results, outs = refs[:count], refs[count : 2 * count] if sent else refs[:count]
-    sides, bras, kets, operators, own_table, far_table, sem, out_sem = refs[-8:]
+    sides, bras, kets, operators, sem, out_sem = refs[-6:]
     core, _, z, q = where()
     ahead = 1 - 2 * core
     low = z < 4
     copies = [
-        pltpu.make_async_copy(own_table_ref, own_table, sem.at[0]),
-        pltpu.make_async_copy(far_table_ref, far_table, sem.at[1]),
-        pltpu.make_async_copy(own_left.at[:, core], operators.at[0], sem.at[2]),
-        pltpu.make_async_copy(far_left.at[:, core], operators.at[1], sem.at[3]),
+        pltpu.make_async_copy(own_left.at[:, core], operators.at[0], sem.at[0]),
+        pltpu.make_async_copy(far_left.at[:, core], operators.at[1], sem.at[1]),
     ]
     for copy in copies:
         copy.start()
@@ -126,9 +124,11 @@
             bras[0] = jnp.concatenate([re_t, im_t], axis=1)
             bras[1] = jnp.concatenate([-im_t, re_t], axis=1)
 
-    copies[0].wait()
-    copies[1].wait()
-    labels = [own_table[s, q] for s in range(12)] + [far_table[s, q] for s in range(12)]
+    columns = [
+        jnp.sum(jnp.where(iota((12, 32), 1) == q, table[...], 0), axis=1, keepdims=True)
+        for table in (own_table, far_table)
+    ]
+    labels = [column[s, 0] for column in columns for s in range(12)]
     shifts = [lax.rem(label - q + 32, 32) for label in labels]
     for out, spot in zip(outs, range(1, 5) if sent else range(1)):
         members = GROUPS[spot] * 4
@@ -142,6 +142,8 @@
             out[TILES[spot] + tile] = row.astype(BF)
 
     leaving = []
+    for copy in copies:
+        copy.wait()
     for half in range(2):
         if sent:
             spots = [(z + ahead) & 7, (z - ahead) & 7, (z - 2 * ahead if half else z + 2 * ahead) & 7]
@@ -156,7 +158,6 @@
             ],
             axis=0,
         )
-        copies[2 + half].wait()
         for s in range(12):
             operator = jnp.concatenate(
                 [operators[half, s, 0], operators[half, s, 1]], axis=1
@@ -164,7 +165,7 @@
             turned = jnp.dot(
                 operator, sides[shifts[half * 12 + s]], preferred_element_type=F32
             ).astype(BF)
-            kets[s] = jnp.concatenate(
+            kets[half * 12 + s] = jnp.concatenate(
                 [
                     jnp.concatenate([turned[:, 0:128], turned[:, 256:384]], axis=1),
                     jnp.concatenate([turned[:, 128:256], turned[:, 384:512]], axis=1),
@@ -174,7 +175,7 @@
         for group in range(3):
             whole = half * 3 + group
             brackets = [
-                jnp.dot(left, kets[group * 4 + s], preferred_element_type=F32).astype(BF)
+                jnp.dot(left, kets[whole * 4 + s], preferred_element_type=F32).astype(BF)
                 for s in range(4)
             ]
             for i in range(len(spots)):
@@ -217,18 +218,16 @@
     shapes = [(n + 3, 16, 128) for n in (TILES[1:] if sent else TILES[:1])]
     return pl.pallas_call(
         functools.partial(tiles_kernel, sent),
-        in_specs=[anywhere] * 2 + [whole] * 2 + [anywhere] * 2,
+        in_specs=[whole] * 4 + [anywhere] * 2,
         out_specs=[anywhere if sent else whole] * len(shapes),
         out_shape=[jax.ShapeDtypeStruct(shape, BF) for shape in shapes],
         scratch_shapes=[pltpu.VMEM(shape, BF) for shape in shapes if sent]
         + [
             pltpu.VMEM((3, 256, 512), BF),
             pltpu.VMEM((2, 128, 256), BF),
-            pltpu.VMEM((12, 256, 256), BF),
+            pltpu.VMEM((24, 256, 256), BF),
             pltpu.VMEM((2, 12, 2, 128, 128), BF),
-            pltpu.SMEM((12, 32), jnp.int32),
-            pltpu.SMEM((12, 32), jnp.int32),
-            pltpu.SemaphoreType.DMA((4,)),
+            pltpu.SemaphoreType.DMA((2,)),
             pltpu.SemaphoreType.DMA((2, 3)),
         ],
         cost_estimate=pl.CostEstimate(

time: 65.6 us -> 66 us (level)
  Pallas kernels: 11.7 us -> 12.5 us
    all_to_all x1, waiting for transfers between devices: 6.8 us -> 6.03 us  [local(): right = lax.all_to_all(right, 'col', 0, 0, tiled=True)]
    pallas_call x2, Pallas kernels: 6 us -> 6.76 us  [make_tiles(): pl.pallas_call(functools.partial(tiles_kernel, sent), in_specs=[whole] *...]
  transfers between devices with their start and end apart: 8 -> 8, of which waited for: 2 -> 2; matrix products, arithmetic and copies ran while one was open for 2% -> 2% of each run, Pallas kernels for 14% -> 15%
where the time goes in v11:
time: 66 us; the launch traced here: 65.6 us
  blocking collectives  23.5 us (36%)
  starting transfers between devices  18.4 us (28%)
  Pallas kernels  12.5 us (19%)
  waiting for transfers between devices  6.59 us (10%)
  local copies, waits for them, and re-layouts  3.82 us (6%)
    all_to_all x1, blocking collectives, local(): lax.all_to_all(shares.reshape(256, 2, 128), ('row', 'wf', 'col'), 0, 0, t...  23.5 us
    all_to_all x1, starting transfers between devices, local(): right = lax.all_to_all(right, 'col', 0, 0, tiled=True)  6.89 us
    pallas_call x2, Pallas kernels, make_tiles(): pl.pallas_call(functools.partial(tiles_kernel, sent), in_specs=[whole] *...  6.76 us
    all_to_all x1, waiting for transfers between devices, local(): right = lax.all_to_all(right, 'col', 0, 0, tiled=True)  6.03 us
    ppermute x1, starting transfers between devices, local(): lax.ppermute(own_wave, line, ring(lambda z, core: (z + 2) % 8 if z in (2,...  4.37 us
    ppermute x1, starting transfers between devices, local(): far_left = lax.ppermute(left_operators, 'row', swap)  3.24 us
    pallas_call x1, Pallas kernels, pick(): pl.pallas_call(pick_kernel, in_specs=[pl.BlockSpec(memory_space=pltpu.HBM...  2.98 us
    pallas_call x1, Pallas kernels, contract(): pl.pallas_call(contract_kernel, in_specs=[whole] * 8, out_specs=whole, ou...  2.58 us
  transfers between devices with their start and end apart: 8, of which 2 were waited for; matrix products, arithmetic and copies ran while one was open for 2% of the time, Pallas kernels for 15%

profile of v11, /device:TPU:1, one launch (start us, length us, event | category | flops | bytes accessed | tf_op | source)
XLA Modules:
  0.0 65.6 jit_solution(9601741136563638845)
XLA Ops:
  0.0 3.2 %collective-permute-start.2 = (bf16[12,2,2,128,128]{4,3,2,1,0:T(8,128)(2,1)}, bf16[12,2,2,128,128]{4,3,2,1,0:T(8,128)(2,1)}, u32[]{:S(2)}, u32[]{:S(2)}) collective-permute-start(bf16[12,2,2,128,128]{4,3,2,1,0:T(8,128)(2,1)} %own_left.3), channel_id=1, source_target_pairs={{0,32},{32,0},{64,96},{96,64},{128,160},{160,128},{192,224},{224,1... | collective-permute-start | bytes 4718600 | tf_op jit(solution)/shard_map/ppermute | solution.py:360
  3.2 0.0 collective-permute-start
  3.2 3.0 %pick.1 = (bf16[16,24,16,128]{3,2,1,0:T(8,128)(2,1)}, bf16[2,3,64,128]{3,2,1,0:T(8,128)(2,1)}) custom-call(bf16[16,2,8,2,4,16,128]{6,5,4,3,2,1,0:T(8,128)(2,1)} %bitcast.21, bf16[2,32,64,128]{3,2,1,0:T(8,128)(2,1)} %wave_ref.1), custom_call_target="tpu_custom_call" | custom-call | tf_op jit(solution)/shard_map/pick/pallas_call | solution.py:71
  6.2 4.4 %collective-permute-start.1 = (bf16[2,3,64,128]{3,2,1,0:T(8,128)(2,1)}, bf16[2,3,64,128]{3,2,1,0:T(8,128)(2,1)S(1)}, u32[]{:S(2)}, u32[]{:S(2)}) collective-permute-start(bf16[2,3,64,128]{3,2,1,0:T(8,128)(2,1)} %get-tuple-element.15.own_wave), channel_id=1, source_target_pairs={{0,129},{32,161},{64,193},{96,225},{128,1},{160,33},{192,65},{224,... | collective-permute-start | bytes 294920 | tf_op jit(solution)/shard_map/ppermute | solution.py:356
  10.6 6.9 %all-to-all-start = ((bf16[16,24,16,128]{3,2,1,0:T(8,128)(2,1)}), bf16[16,24,16,128]{3,2,1,0:T(8,128)(2,1)S(1)}, u32[]{:S(2)}, u32[]{:S(2)}) async-start(bf16[16,24,16,128]{3,2,1,0:T(8,128)(2,1)} %get-tuple-element.22), calls=%async_computation | async-start | bytes 3145728 | tf_op jit(solution)/shard_map/all_to_all | solution.py:362
  17.5 0.1 broadcast_in_dim.2
  17.6 0.1 reshape.140.sign
  17.7 0.0 copy-start.7
  17.8 0.0 copy-start.8
  17.8 0.0 collective-permute-done.far_table
  17.8 0.0 collective-permute-done.1.far_wave
  17.8 0.0 copy-start.3
  17.8 0.0 collective-permute-done.2.far_left
  17.8 0.0 copy-done
  17.8 0.0 copy-done.2
  17.8 0.0 copy-done.6
  17.8 3.8 %make_tiles.1 = (bf16[99,16,128]{2,1,0:T(8,128)(2,1)}, bf16[99,16,128]{2,1,0:T(8,128)(2,1)}, bf16[27,16,128]{2,1,0:T(8,128)(2,1)}, bf16[27,16,128]{2,1,0:T(8,128)(2,1)}) custom-call(s32[12,32]{1,0:T(8,128)S(1)} %copy-done.6, s32[12,32]{1,0:T(8,128)S(1)} %collective-permute-done.far_table, bf16[2,3,64,128]{3,2,1,0:T(8,128)(2,1)S(1)} %copy-done.2, ...), custom_call_target="tpu_custom_call" | custom-call | flops 1000000000 | bytes 4000000 | tf_op jit(solution)/shard_map/make_tiles/pallas_call | solution.py:219
  21.6 0.0 copy-done.3
  21.6 0.1 collective-permute-start.3
  21.7 1.5 %collective-permute-start.4 = (bf16[99,16,128]{2,1,0:T(8,128)(2,1)}, bf16[99,16,128]{2,1,0:T(8,128)(2,1)}, u32[]{:S(2)}, u32[]{:S(2)}) collective-permute-start(bf16[99,16,128]{2,1,0:T(8,128)(2,1)} %get-tuple-element.19), channel_id=1, source_target_pairs={{0,193},{32,96},{64,0},{96,160},{128,64},{160,224},{192,128},{224,... | collective-permute-start | bytes 1216520 | tf_op jit(solution)/shard_map/ppermute | solution.py:372
  23.2 1.5 %collective-permute-start.5 = (bf16[27,16,128]{2,1,0:T(8,128)(2,1)}, bf16[27,16,128]{2,1,0:T(8,128)(2,1)S(1)}, u32[]{:S(2)}, u32[]{:S(2)}) collective-permute-start(bf16[27,16,128]{2,1,0:T(8,128)(2,1)} %get-tuple-element.20), channel_id=1, source_target_pairs={{0,128},{32,161},{64,192},{96,225},{128,1},{160,32},{192,65},{224,... | collective-permute-start | bytes 331784 | tf_op jit(solution)/shard_map/ppermute | solution.py:373
  24.7 0.9 %collective-permute-start.6 = (bf16[27,16,128]{2,1,0:T(8,128)(2,1)}, bf16[27,16,128]{2,1,0:T(8,128)(2,1)S(1)}, u32[]{:S(2)}, u32[]{:S(2)}) collective-permute-start(bf16[27,16,128]{2,1,0:T(8,128)(2,1)} %get-tuple-element.21), channel_id=1, source_target_pairs={{0,129},{32,160},{64,193},{96,224},{128,0},{160,33},{192,64},{224,... | collective-permute-start | bytes 331784 | tf_op jit(solution)/shard_map/ppermute | solution.py:374
  25.5 0.0 copy-done.7
  25.5 0.1 reshape.139
  25.7 0.1 mul.40
  25.8 0.0 copy-done.8
  25.8 0.1 stack.16
  25.9 0.1 fusion.2
  26.0 0.1 iota_add_fusion
  26.1 0.1 fusion.1
  26.2 0.1 add.106.slot_key
  26.3 0.1 add.102.real_key
  26.4 0.1 sub.29.imag_key
  26.5 0.2 make_picks.1.picks
  26.7 0.0 copy-start.1
  26.7 1.4 %copy-done.1 = bf16[12,2,2,128,128]{4,3,2,1,0:T(8,128)(2,1)S(1)} copy-done((bf16[12,2,2,128,128]{4,3,2,1,0:T(8,128)(2,1)S(1)}, bf16[12,2,2,128,128]{4,3,2,1,0:T(8,128)(2,1)}, u32[]{:S(2)}) %copy-start.1) | copy-done | bytes 1572888
  28.1 0.9 %copy-done.4 = bf16[2,3,64,128]{3,2,1,0:T(8,128)(2,1)S(1)} copy-done((bf16[2,3,64,128]{3,2,1,0:T(8,128)(2,1)S(1)}, bf16[2,3,64,128]{3,2,1,0:T(8,128)(2,1)}, u32[]{:S(2)}) %copy-start.4) | copy-done | bytes 98328
  29.0 3.0 %make_home.1.home = bf16[147,16,128]{2,1,0:T(8,128)(2,1)S(1)} custom-call(s32[12,32]{1,0:T(8,128)S(1)} %copy-done.6, s32[12,32]{1,0:T(8,128)S(1)} %collective-permute-done.far_table, bf16[2,3,64,128]{3,2,1,0:T(8,128)(2,1)S(1)} %copy-done.2, bf16[2,3,64,128]{3,2,1,0:T(8,128)(2,1)S(1)} %copy-done.4, bf16[12,2,2,128,128]{4,3,2,1,0:T(8,128)(2,1)S(1)} %copy-done.1, ...), custom_call_target="tpu_custom_call" | custom-call | flops 1000000000 | bytes 4000000 | tf_op jit(solution)/shard_map/make_home/pallas_call | solution.py:219
  32.0 6.0 %all-to-all-done.right = bf16[16,24,16,128]{3,2,1,0:T(8,128)(2,1)S(1)} async-done(((bf16[16,24,16,128]{3,2,1,0:T(8,128)(2,1)}), bf16[16,24,16,128]{3,2,1,0:T(8,128)(2,1)S(1)}, u32[]{:S(2)}, u32[]{:S(2)}) %all-to-all-start) | async-done | bytes 1572896 | tf_op jit(solution)/shard_map/all_to_all | solution.py:362
  38.0 0.0 collective-permute-done.5.ahead2
  38.0 0.5 collective-permute-done.6.back2
  38.6 0.0 collective-permute-done.3.ahead1
  38.6 0.0 collective-permute-done.4.back1
  38.6 2.6 %contract.1 = bf16[8,64,128]{2,1,0:T(8,128)(2,1)S(1)} custom-call(bf16[147,16,128]{2,1,0:T(8,128)(2,1)S(1)} %make_home.1.home, bf16[99,16,128]{2,1,0:T(8,128)(2,1)S(1)} %collective-permute-done.3.ahead1, bf16[99,16,128]{2,1,0:T(8,128)(2,1)} %collective-permute-done.4.back1, bf16[27,16,128]{2,1,0:T(8,128)(2,1)S(1)} %collective-permute-done.5.ahead2, ...), custom_call_target="tpu_custom_call" | custom-call | tf_op jit(solution)/shard_map/contract/pallas_call | solution.py:330
  41.2 23.5 %all_to_all.10 = bf16[256,2,128]{2,1,0:T(2,128)(2,1)S(1)} all-to-all(bf16[256,2,128]{2,1,0:T(2,128)(2,1)S(1)} %bitcast.19), channel_id=1, replica_groups=mesh['row'=8,'col'=16,'wf'=2] {'row','wf','col'}, dimensions={0} | all-to-all | bytes 262144 | tf_op jit(solution)/shard_map/all_to_all | solution.py:398
  64.7 0.3 convert_reduce_fusion
  64.9 0.1 reshape.142
  65.0 0.6 copy.13
  (19 shorter events, 0.1 us)
Async XLA Ops:
  0.0 17.8 %collective-permute-start.2 = (bf16[12,2,2,128,128]{4,3,2,1,0:T(8,128)(2,1)}, bf16[12,2,2,128,128]{4,3,2,1,0:T(8,128)(2,1)}, u32[]{:S(2)}, u32[]{:S(2)}) collective-permute-start(bf16[12,2,2,128,128]{4,3,2,1,0:T(8,128)(2,1)} %own_left.3), channel_id=1, source_target_pairs={{0,32},{32,0},{64,96},{96,64},{128,160},{160,128},{192,224},{224,1... | collective-permute-start | bytes 4718600 | tf_op jit(solution)/shard_map/ppermute | solution.py:360
  3.2 14.5 %collective-permute-start = (s32[12,32]{1,0:T(8,128)}, s32[12,32]{1,0:T(8,128)S(1)}, u32[]{:S(2)}, u32[]{:S(2)}) collective-permute-start(s32[12,32]{1,0:T(8,128)} %own_table.3), channel_id=1, source_target_pairs={{0,32},{32,0},{64,96},{96,64},{128,160},{160,128},{192,224},{224,1... | collective-permute-start | bytes 4616 | tf_op jit(solution)/shard_map/ppermute | solution.py:361
  6.2 11.5 %collective-permute-start.1 = (bf16[2,3,64,128]{3,2,1,0:T(8,128)(2,1)}, bf16[2,3,64,128]{3,2,1,0:T(8,128)(2,1)S(1)}, u32[]{:S(2)}, u32[]{:S(2)}) collective-permute-start(bf16[2,3,64,128]{3,2,1,0:T(8,128)(2,1)} %get-tuple-element.15.own_wave), channel_id=1, source_target_pairs={{0,129},{32,161},{64,193},{96,225},{128,1},{160,33},{192,65},{224,... | collective-permute-start | bytes 294920 | tf_op jit(solution)/shard_map/ppermute | solution.py:356
  10.6 7.2 %copy-start = (bf16[12,2,2,128,128]{4,3,2,1,0:T(8,128)(2,1)S(1)}, bf16[12,2,2,128,128]{4,3,2,1,0:T(8,128)(2,1)}, u32[]{:S(2)}) copy-start(bf16[12,2,2,128,128]{4,3,2,1,0:T(8,128)(2,1)} %own_left.3) | copy-start | bytes 4718596
  10.6 7.2 %copy-start.2 = (bf16[2,3,64,128]{3,2,1,0:T(8,128)(2,1)S(1)}, bf16[2,3,64,128]{3,2,1,0:T(8,128)(2,1)}, u32[]{:S(2)}) copy-start(bf16[2,3,64,128]{3,2,1,0:T(8,128)(2,1)} %get-tuple-element.15.own_wave) | copy-start | bytes 294916
  10.6 7.2 %copy-start.6 = (s32[12,32]{1,0:T(8,128)S(1)}, s32[12,32]{1,0:T(8,128)}, u32[]{:S(2)}) copy-start(s32[12,32]{1,0:T(8,128)} %own_table.3) | copy-start | bytes 4612
  10.6 27.4 %all-to-all-start = ((bf16[16,24,16,128]{3,2,1,0:T(8,128)(2,1)}), bf16[16,24,16,128]{3,2,1,0:T(8,128)(2,1)S(1)}, u32[]{:S(2)}, u32[]{:S(2)}) async-start(bf16[16,24,16,128]{3,2,1,0:T(8,128)(2,1)} %get-tuple-element.22), calls=%async_computation | async-start | bytes 3145728 | tf_op jit(solution)/shard_map/all_to_all | solution.py:362
  17.7 7.8 %copy-start.7 = (s32[96]{0:T(128)S(1)}, s32[96]{0:T(128)}, u32[]{:S(2)}) copy-start(s32[96]{0:T(128)} %param.12) | copy-start | bytes 1156
  17.8 8.1 %copy-start.8 = (s32[96]{0:T(128)S(1)}, s32[96]{0:T(128)}, u32[]{:S(2)}) copy-start(s32[96]{0:T(128)} %param.13) | copy-start | bytes 1156
  17.8 3.8 %copy-start.3 = (bf16[2,3,64,128]{3,2,1,0:T(8,128)(2,1)}, bf16[2,3,64,128]{3,2,1,0:T(8,128)(2,1)S(1)}, u32[]{:S(2)}) copy-start(bf16[2,3,64,128]{3,2,1,0:T(8,128)(2,1)S(1)} %collective-permute-done.1.far_wave) | copy-start | bytes 294916
  21.6 16.9 %collective-permute-start.3 = (bf16[99,16,128]{2,1,0:T(8,128)(2,1)}, bf16[99,16,128]{2,1,0:T(8,128)(2,1)S(1)}, u32[]{:S(2)}, u32[]{:S(2)}) collective-permute-start(bf16[99,16,128]{2,1,0:T(8,128)(2,1)} %get-tuple-element.18), channel_id=1, source_target_pairs={{0,64},{32,225},{64,128},{96,32},{128,192},{160,96},{192,1},{224,1... | collective-permute-start | bytes 1216520 | tf_op jit(solution)/shard_map/ppermute | solution.py:371
  21.7 16.9 %collective-permute-start.4 = (bf16[99,16,128]{2,1,0:T(8,128)(2,1)}, bf16[99,16,128]{2,1,0:T(8,128)(2,1)}, u32[]{:S(2)}, u32[]{:S(2)}) collective-permute-start(bf16[99,16,128]{2,1,0:T(8,128)(2,1)} %get-tuple-element.19), channel_id=1, source_target_pairs={{0,193},{32,96},{64,0},{96,160},{128,64},{160,224},{192,128},{224,... | collective-permute-start | bytes 1216520 | tf_op jit(solution)/shard_map/ppermute | solution.py:372
  23.2 14.9 %collective-permute-start.5 = (bf16[27,16,128]{2,1,0:T(8,128)(2,1)}, bf16[27,16,128]{2,1,0:T(8,128)(2,1)S(1)}, u32[]{:S(2)}, u32[]{:S(2)}) collective-permute-start(bf16[27,16,128]{2,1,0:T(8,128)(2,1)} %get-tuple-element.20), channel_id=1, source_target_pairs={{0,128},{32,161},{64,192},{96,225},{128,1},{160,32},{192,65},{224,... | collective-permute-start | bytes 331784 | tf_op jit(solution)/shard_map/ppermute | solution.py:373
  24.7 13.9 %collective-permute-start.6 = (bf16[27,16,128]{2,1,0:T(8,128)(2,1)}, bf16[27,16,128]{2,1,0:T(8,128)(2,1)S(1)}, u32[]{:S(2)}, u32[]{:S(2)}) collective-permute-start(bf16[27,16,128]{2,1,0:T(8,128)(2,1)} %get-tuple-element.21), channel_id=1, source_target_pairs={{0,129},{32,160},{64,193},{96,224},{128,0},{160,33},{192,64},{224,... | collective-permute-start | bytes 331784 | tf_op jit(solution)/shard_map/ppermute | solution.py:374
  26.7 1.4 %copy-start.1 = (bf16[12,2,2,128,128]{4,3,2,1,0:T(8,128)(2,1)S(1)}, bf16[12,2,2,128,128]{4,3,2,1,0:T(8,128)(2,1)}, u32[]{:S(2)}) copy-start(bf16[12,2,2,128,128]{4,3,2,1,0:T(8,128)(2,1)} %own_left.3) | copy-start | bytes 4718596
  28.1 0.9 %copy-start.4 = (bf16[2,3,64,128]{3,2,1,0:T(8,128)(2,1)S(1)}, bf16[2,3,64,128]{3,2,1,0:T(8,128)(2,1)}, u32[]{:S(2)}) copy-start(bf16[2,3,64,128]{3,2,1,0:T(8,128)(2,1)} %copy-done.3) | copy-start | bytes 294916
  29.0 9.6 %copy-start.5 = (s32[128,32]{0,1:T(8,128)S(1)}, s32[128,32]{0,1:T(8,128)}, u32[]{:S(2)}) copy-start(s32[128,32]{0,1:T(8,128)} %param.11) | copy-start | bytes 49156

commit v12 on v11

--- a/solution.py
+++ b/solution.py
@@ -142,8 +142,6 @@
             out[TILES[spot] + tile] = row.astype(BF)
 
     leaving = []
-    for copy in copies:
-        copy.wait()
     for half in range(2):
         if sent:
             spots = [(z + ahead) & 7, (z - ahead) & 7, (z - 2 * ahead if half else z + 2 * ahead) & 7]
@@ -158,6 +156,7 @@
             ],
             axis=0,
         )
+        copies[half].wait()
         for s in range(12):
             operator = jnp.concatenate(
                 [operators[half, s, 0], operators[half, s, 1]], axis=1

time: 66 us -> 65.3 us (0.989)
  Pallas kernels: 12.5 us -> 11.1 us
  waiting for transfers between devices: 6.59 us -> 7.46 us
    all_to_all x1, waiting for transfers between devices: 6.03 us -> 7.44 us  [local(): right = lax.all_to_all(right, 'col', 0, 0, tiled=True)]
    pallas_call x2, Pallas kernels: 6.76 us -> 5.36 us  [make_tiles(): pl.pallas_call(functools.partial(tiles_kernel, sent), in_specs=[whole] *...]
  transfers between devices with their start and end apart: 8 -> 8, of which waited for: 2 -> 1; matrix products, arithmetic and copies ran while one was open for 2% -> 2% of each run, Pallas kernels for 15% -> 13%
where the time goes in v12:
time: 65.3 us; the launch traced here: 64.9 us
  blocking collectives  23.3 us (36%)
  starting transfers between devices  18.4 us (28%)
  Pallas kernels  11.1 us (17%)
  waiting for transfers between devices  7.46 us (11%)
  local copies, waits for them, and re-layouts  3.82 us (6%)
    all_to_all x1, blocking collectives, local(): lax.all_to_all(shares.reshape(256, 2, 128), ('row', 'wf', 'col'), 0, 0, t...  23.3 us
    all_to_all x1, waiting for transfers between devices, local(): right = lax.all_to_all(right, 'col', 0, 0, tiled=True)  7.44 us
    all_to_all x1, starting transfers between devices, local(): right = lax.all_to_all(right, 'col', 0, 0, tiled=True)  6.89 us
    pallas_call x2, Pallas kernels, make_tiles(): pl.pallas_call(functools.partial(tiles_kernel, sent), in_specs=[whole] *...  5.36 us
    ppermute x1, starting transfers between devices, local(): lax.ppermute(own_wave, line, ring(lambda z, core: (z + 2) % 8 if z in (2,...  4.37 us
    ppermute x1, starting transfers between devices, local(): far_left = lax.ppermute(left_operators, 'row', swap)  3.24 us
    pallas_call x1, Pallas kernels, pick(): pl.pallas_call(pick_kernel, in_specs=[pl.BlockSpec(memory_space=pltpu.HBM...  2.98 us
    pallas_call x1, Pallas kernels, contract(): pl.pallas_call(contract_kernel, in_specs=[whole] * 8, out_specs=whole, ou...  2.58 us
  transfers between devices with their start and end apart: 8, of which 1 were waited for; matrix products, arithmetic and copies ran while one was open for 2% of the time, Pallas kernels for 13%

profile of v12, /device:TPU:1, one launch (start us, length us, event | category | flops | bytes accessed | tf_op | source)
XLA Modules:
  0.0 64.9 jit_solution(3778092874832606951)
XLA Ops:
  0.0 3.2 %collective-permute-start.2 = (bf16[12,2,2,128,128]{4,3,2,1,0:T(8,128)(2,1)}, bf16[12,2,2,128,128]{4,3,2,1,0:T(8,128)(2,1)}, u32[]{:S(2)}, u32[]{:S(2)}) collective-permute-start(bf16[12,2,2,128,128]{4,3,2,1,0:T(8,128)(2,1)} %own_left.3), channel_id=1, source_target_pairs={{0,32},{32,0},{64,96},{96,64},{128,160},{160,128},{192,224},{224,1... | collective-permute-start | bytes 4718600 | tf_op jit(solution)/shard_map/ppermute | solution.py:359
  3.2 0.0 collective-permute-start
  3.2 3.0 %pick.1 = (bf16[16,24,16,128]{3,2,1,0:T(8,128)(2,1)}, bf16[2,3,64,128]{3,2,1,0:T(8,128)(2,1)}) custom-call(bf16[16,2,8,2,4,16,128]{6,5,4,3,2,1,0:T(8,128)(2,1)} %bitcast.21, bf16[2,32,64,128]{3,2,1,0:T(8,128)(2,1)} %wave_ref.1), custom_call_target="tpu_custom_call" | custom-call | tf_op jit(solution)/shard_map/pick/pallas_call | solution.py:71
  6.2 4.4 %collective-permute-start.1 = (bf16[2,3,64,128]{3,2,1,0:T(8,128)(2,1)}, bf16[2,3,64,128]{3,2,1,0:T(8,128)(2,1)S(1)}, u32[]{:S(2)}, u32[]{:S(2)}) collective-permute-start(bf16[2,3,64,128]{3,2,1,0:T(8,128)(2,1)} %get-tuple-element.15.own_wave), channel_id=1, source_target_pairs={{0,129},{32,161},{64,193},{96,225},{128,1},{160,33},{192,65},{224,... | collective-permute-start | bytes 294920 | tf_op jit(solution)/shard_map/ppermute | solution.py:355
  10.6 6.9 %all-to-all-start = ((bf16[16,24,16,128]{3,2,1,0:T(8,128)(2,1)}), bf16[16,24,16,128]{3,2,1,0:T(8,128)(2,1)S(1)}, u32[]{:S(2)}, u32[]{:S(2)}) async-start(bf16[16,24,16,128]{3,2,1,0:T(8,128)(2,1)} %get-tuple-element.22), calls=%async_computation | async-start | bytes 3145728 | tf_op jit(solution)/shard_map/all_to_all | solution.py:361
  17.5 0.1 broadcast_in_dim.2
  17.6 0.1 reshape.140.sign
  17.7 0.0 copy-start.7
  17.8 0.0 copy-start.8
  17.8 0.0 collective-permute-done.far_table
  17.8 0.0 collective-permute-done.1.far_wave
  17.8 0.0 copy-start.3
  17.8 0.0 collective-permute-done.2.far_left
  17.8 0.0 copy-done
  17.8 0.0 copy-done.2
  17.8 0.0 copy-done.6
  17.8 3.1 %make_tiles.1 = (bf16[99,16,128]{2,1,0:T(8,128)(2,1)}, bf16[99,16,128]{2,1,0:T(8,128)(2,1)}, bf16[27,16,128]{2,1,0:T(8,128)(2,1)}, bf16[27,16,128]{2,1,0:T(8,128)(2,1)}) custom-call(s32[12,32]{1,0:T(8,128)S(1)} %copy-done.6, s32[12,32]{1,0:T(8,128)S(1)} %collective-permute-done.far_table, bf16[2,3,64,128]{3,2,1,0:T(8,128)(2,1)S(1)} %copy-done.2, ...), custom_call_target="tpu_custom_call" | custom-call | flops 1000000000 | bytes 4000000 | tf_op jit(solution)/shard_map/make_tiles/pallas_call | solution.py:218
  20.9 0.0 copy-done.3
  20.9 0.1 collective-permute-start.3
  21.0 1.5 %collective-permute-start.4 = (bf16[99,16,128]{2,1,0:T(8,128)(2,1)}, bf16[99,16,128]{2,1,0:T(8,128)(2,1)}, u32[]{:S(2)}, u32[]{:S(2)}) collective-permute-start(bf16[99,16,128]{2,1,0:T(8,128)(2,1)} %get-tuple-element.19), channel_id=1, source_target_pairs={{0,193},{32,96},{64,0},{96,160},{128,64},{160,224},{192,128},{224,... | collective-permute-start | bytes 1216520 | tf_op jit(solution)/shard_map/ppermute | solution.py:371
  22.5 1.5 %collective-permute-start.5 = (bf16[27,16,128]{2,1,0:T(8,128)(2,1)}, bf16[27,16,128]{2,1,0:T(8,128)(2,1)S(1)}, u32[]{:S(2)}, u32[]{:S(2)}) collective-permute-start(bf16[27,16,128]{2,1,0:T(8,128)(2,1)} %get-tuple-element.20), channel_id=1, source_target_pairs={{0,128},{32,161},{64,192},{96,225},{128,1},{160,32},{192,65},{224,... | collective-permute-start | bytes 331784 | tf_op jit(solution)/shard_map/ppermute | solution.py:372
  24.0 0.9 %collective-permute-start.6 = (bf16[27,16,128]{2,1,0:T(8,128)(2,1)}, bf16[27,16,128]{2,1,0:T(8,128)(2,1)S(1)}, u32[]{:S(2)}, u32[]{:S(2)}) collective-permute-start(bf16[27,16,128]{2,1,0:T(8,128)(2,1)} %get-tuple-element.21), channel_id=1, source_target_pairs={{0,129},{32,160},{64,193},{96,224},{128,0},{160,33},{192,64},{224,... | collective-permute-start | bytes 331784 | tf_op jit(solution)/shard_map/ppermute | solution.py:373
  24.8 0.0 copy-done.7
  24.8 0.1 reshape.139
  25.0 0.1 mul.40
  25.1 0.0 copy-done.8
  25.1 0.1 stack.16
  25.2 0.1 fusion.2
  25.3 0.1 iota_add_fusion
  25.4 0.1 fusion.1
  25.5 0.1 add.106.slot_key
  25.6 0.1 add.102.real_key
  25.7 0.1 sub.29.imag_key
  25.8 0.2 make_picks.1.picks
  26.0 0.0 copy-start.1
  26.0 1.4 %copy-done.1 = bf16[12,2,2,128,128]{4,3,2,1,0:T(8,128)(2,1)S(1)} copy-done((bf16[12,2,2,128,128]{4,3,2,1,0:T(8,128)(2,1)S(1)}, bf16[12,2,2,128,128]{4,3,2,1,0:T(8,128)(2,1)}, u32[]{:S(2)}) %copy-start.1) | copy-done | bytes 1572888
  27.4 0.9 %copy-done.4 = bf16[2,3,64,128]{3,2,1,0:T(8,128)(2,1)S(1)} copy-done((bf16[2,3,64,128]{3,2,1,0:T(8,128)(2,1)S(1)}, bf16[2,3,64,128]{3,2,1,0:T(8,128)(2,1)}, u32[]{:S(2)}) %copy-start.4) | copy-done | bytes 98328
  28.3 2.3 %make_home.1.home = bf16[147,16,128]{2,1,0:T(8,128)(2,1)S(1)} custom-call(s32[12,32]{1,0:T(8,128)S(1)} %copy-done.6, s32[12,32]{1,0:T(8,128)S(1)} %collective-permute-done.far_table, bf16[2,3,64,128]{3,2,1,0:T(8,128)(2,1)S(1)} %copy-done.2, bf16[2,3,64,128]{3,2,1,0:T(8,128)(2,1)S(1)} %copy-done.4, bf16[12,2,2,128,128]{4,3,2,1,0:T(8,128)(2,1)S(1)} %copy-done.1, ...), custom_call_target="tpu_custom_call" | custom-call | flops 1000000000 | bytes 4000000 | tf_op jit(solution)/shard_map/make_home/pallas_call | solution.py:218
  30.6 7.4 %all-to-all-done.right = bf16[16,24,16,128]{3,2,1,0:T(8,128)(2,1)S(1)} async-done(((bf16[16,24,16,128]{3,2,1,0:T(8,128)(2,1)}), bf16[16,24,16,128]{3,2,1,0:T(8,128)(2,1)S(1)}, u32[]{:S(2)}, u32[]{:S(2)}) %all-to-all-start) | async-done | bytes 1572896 | tf_op jit(solution)/shard_map/all_to_all | solution.py:361
  38.0 0.0 collective-permute-done.5.ahead2
  38.0 0.0 collective-permute-done.6.back2
  38.0 0.0 collective-permute-done.3.ahead1
  38.0 0.0 collective-permute-done.4.back1
  38.1 2.6 %contract.1 = bf16[8,64,128]{2,1,0:T(8,128)(2,1)S(1)} custom-call(bf16[147,16,128]{2,1,0:T(8,128)(2,1)S(1)} %make_home.1.home, bf16[99,16,128]{2,1,0:T(8,128)(2,1)S(1)} %collective-permute-done.3.ahead1, bf16[99,16,128]{2,1,0:T(8,128)(2,1)} %collective-permute-done.4.back1, bf16[27,16,128]{2,1,0:T(8,128)(2,1)S(1)} %collective-permute-done.5.ahead2, ...), custom_call_target="tpu_custom_call" | custom-call | tf_op jit(solution)/shard_map/contract/pallas_call | solution.py:329
  40.7 23.3 %all_to_all.10 = bf16[256,2,128]{2,1,0:T(2,128)(2,1)S(1)} all-to-all(bf16[256,2,128]{2,1,0:T(2,128)(2,1)S(1)} %bitcast.19), channel_id=1, replica_groups=mesh['row'=8,'col'=16,'wf'=2] {'row','wf','col'}, dimensions={0} | all-to-all | bytes 262144 | tf_op jit(solution)/shard_map/all_to_all | solution.py:397
  64.0 0.3 convert_reduce_fusion
  64.2 0.1 reshape.142
  64.3 0.6 copy.13
  (19 shorter events, 0.1 us)
Async XLA Ops:
  0.0 17.8 %collective-permute-start.2 = (bf16[12,2,2,128,128]{4,3,2,1,0:T(8,128)(2,1)}, bf16[12,2,2,128,128]{4,3,2,1,0:T(8,128)(2,1)}, u32[]{:S(2)}, u32[]{:S(2)}) collective-permute-start(bf16[12,2,2,128,128]{4,3,2,1,0:T(8,128)(2,1)} %own_left.3), channel_id=1, source_target_pairs={{0,32},{32,0},{64,96},{96,64},{128,160},{160,128},{192,224},{224,1... | collective-permute-start | bytes 4718600 | tf_op jit(solution)/shard_map/ppermute | solution.py:359
  3.2 14.5 %collective-permute-start = (s32[12,32]{1,0:T(8,128)}, s32[12,32]{1,0:T(8,128)S(1)}, u32[]{:S(2)}, u32[]{:S(2)}) collective-permute-start(s32[12,32]{1,0:T(8,128)} %own_table.3), channel_id=1, source_target_pairs={{0,32},{32,0},{64,96},{96,64},{128,160},{160,128},{192,224},{224,1... | collective-permute-start | bytes 4616 | tf_op jit(solution)/shard_map/ppermute | solution.py:360
  6.2 11.5 %collective-permute-start.1 = (bf16[2,3,64,128]{3,2,1,0:T(8,128)(2,1)}, bf16[2,3,64,128]{3,2,1,0:T(8,128)(2,1)S(1)}, u32[]{:S(2)}, u32[]{:S(2)}) collective-permute-start(bf16[2,3,64,128]{3,2,1,0:T(8,128)(2,1)} %get-tuple-element.15.own_wave), channel_id=1, source_target_pairs={{0,129},{32,161},{64,193},{96,225},{128,1},{160,33},{192,65},{224,... | collective-permute-start | bytes 294920 | tf_op jit(solution)/shard_map/ppermute | solution.py:355
  10.6 7.2 %copy-start = (bf16[12,2,2,128,128]{4,3,2,1,0:T(8,128)(2,1)S(1)}, bf16[12,2,2,128,128]{4,3,2,1,0:T(8,128)(2,1)}, u32[]{:S(2)}) copy-start(bf16[12,2,2,128,128]{4,3,2,1,0:T(8,128)(2,1)} %own_left.3) | copy-start | bytes 4718596
  10.6 7.2 %copy-start.2 = (bf16[2,3,64,128]{3,2,1,0:T(8,128)(2,1)S(1)}, bf16[2,3,64,128]{3,2,1,0:T(8,128)(2,1)}, u32[]{:S(2)}) copy-start(bf16[2,3,64,128]{3,2,1,0:T(8,128)(2,1)} %get-tuple-element.15.own_wave) | copy-start | bytes 294916
  10.6 7.2 %copy-start.6 = (s32[12,32]{1,0:T(8,128)S(1)}, s32[12,32]{1,0:T(8,128)}, u32[]{:S(2)}) copy-start(s32[12,32]{1,0:T(8,128)} %own_table.3) | copy-start | bytes 4612
  10.6 27.4 %all-to-all-start = ((bf16[16,24,16,128]{3,2,1,0:T(8,128)(2,1)}), bf16[16,24,16,128]{3,2,1,0:T(8,128)(2,1)S(1)}, u32[]{:S(2)}, u32[]{:S(2)}) async-start(bf16[16,24,16,128]{3,2,1,0:T(8,128)(2,1)} %get-tuple-element.22), calls=%async_computation | async-start | bytes 3145728 | tf_op jit(solution)/shard_map/all_to_all | solution.py:361
  17.7 7.1 %copy-start.7 = (s32[96]{0:T(128)S(1)}, s32[96]{0:T(128)}, u32[]{:S(2)}) copy-start(s32[96]{0:T(128)} %param.12) | copy-start | bytes 1156
  17.8 7.4 %copy-start.8 = (s32[96]{0:T(128)S(1)}, s32[96]{0:T(128)}, u32[]{:S(2)}) copy-start(s32[96]{0:T(128)} %param.13) | copy-start | bytes 1156
  17.8 3.1 %copy-start.3 = (bf16[2,3,64,128]{3,2,1,0:T(8,128)(2,1)}, bf16[2,3,64,128]{3,2,1,0:T(8,128)(2,1)S(1)}, u32[]{:S(2)}) copy-start(bf16[2,3,64,128]{3,2,1,0:T(8,128)(2,1)S(1)} %collective-permute-done.1.far_wave) | copy-start | bytes 294916
  20.9 17.1 %collective-permute-start.3 = (bf16[99,16,128]{2,1,0:T(8,128)(2,1)}, bf16[99,16,128]{2,1,0:T(8,128)(2,1)S(1)}, u32[]{:S(2)}, u32[]{:S(2)}) collective-permute-start(bf16[99,16,128]{2,1,0:T(8,128)(2,1)} %get-tuple-element.18), channel_id=1, source_target_pairs={{0,64},{32,225},{64,128},{96,32},{128,192},{160,96},{192,1},{224,1... | collective-permute-start | bytes 1216520 | tf_op jit(solution)/shard_map/ppermute | solution.py:370
  21.0 17.0 %collective-permute-start.4 = (bf16[99,16,128]{2,1,0:T(8,128)(2,1)}, bf16[99,16,128]{2,1,0:T(8,128)(2,1)}, u32[]{:S(2)}, u32[]{:S(2)}) collective-permute-start(bf16[99,16,128]{2,1,0:T(8,128)(2,1)} %get-tuple-element.19), channel_id=1, source_target_pairs={{0,193},{32,96},{64,0},{96,160},{128,64},{160,224},{192,128},{224,... | collective-permute-start | bytes 1216520 | tf_op jit(solution)/shard_map/ppermute | solution.py:371
  22.5 15.6 %collective-permute-start.5 = (bf16[27,16,128]{2,1,0:T(8,128)(2,1)}, bf16[27,16,128]{2,1,0:T(8,128)(2,1)S(1)}, u32[]{:S(2)}, u32[]{:S(2)}) collective-permute-start(bf16[27,16,128]{2,1,0:T(8,128)(2,1)} %get-tuple-element.20), channel_id=1, source_target_pairs={{0,128},{32,161},{64,192},{96,225},{128,1},{160,32},{192,65},{224,... | collective-permute-start | bytes 331784 | tf_op jit(solution)/shard_map/ppermute | solution.py:372
  24.0 14.1 %collective-permute-start.6 = (bf16[27,16,128]{2,1,0:T(8,128)(2,1)}, bf16[27,16,128]{2,1,0:T(8,128)(2,1)S(1)}, u32[]{:S(2)}, u32[]{:S(2)}) collective-permute-start(bf16[27,16,128]{2,1,0:T(8,128)(2,1)} %get-tuple-element.21), channel_id=1, source_target_pairs={{0,129},{32,160},{64,193},{96,224},{128,0},{160,33},{192,64},{224,... | collective-permute-start | bytes 331784 | tf_op jit(solution)/shard_map/ppermute | solution.py:373
  26.0 1.4 %copy-start.1 = (bf16[12,2,2,128,128]{4,3,2,1,0:T(8,128)(2,1)S(1)}, bf16[12,2,2,128,128]{4,3,2,1,0:T(8,128)(2,1)}, u32[]{:S(2)}) copy-start(bf16[12,2,2,128,128]{4,3,2,1,0:T(8,128)(2,1)} %own_left.3) | copy-start | bytes 4718596
  27.4 0.9 %copy-start.4 = (bf16[2,3,64,128]{3,2,1,0:T(8,128)(2,1)S(1)}, bf16[2,3,64,128]{3,2,1,0:T(8,128)(2,1)}, u32[]{:S(2)}) copy-start(bf16[2,3,64,128]{3,2,1,0:T(8,128)(2,1)} %copy-done.3) | copy-start | bytes 294916
  28.3 9.8 %copy-start.5 = (s32[128,32]{0,1:T(8,128)S(1)}, s32[128,32]{0,1:T(8,128)}, u32[]{:S(2)}) copy-start(s32[128,32]{0,1:T(8,128)} %param.11) | copy-start | bytes 49156

commit v13 on v12

--- a/solution.py
+++ b/solution.py
@@ -22,6 +22,12 @@
 
 def params(mebibytes):
     return pltpu.CompilerParams(vmem_limit_bytes=mebibytes * 1024 * 1024)
+
+
+SPLIT = 8
+CROSS = 16 - SPLIT
+ROWS = (16 + CROSS, 16, 16, SPLIT)
+TILES = tuple(6 * rows for rows in ROWS)
 
 
 def pick_kernel(right_ref, wave_ref, out_ref, wave_out, rows_ref, sem, wave_sem):
@@ -59,7 +65,7 @@
                 )
                 rows = jnp.swapaxes(rows, 0, 1)
                 if second:
-                    out_ref[target, 16:24] = rows[8:16]
+                    out_ref[target, 16 : 16 + CROSS] = rows[SPLIT:16]
                 else:
                     out_ref[target, 0:16] = rows
     for copy in waves:
@@ -73,7 +79,7 @@
         in_specs=[pl.BlockSpec(memory_space=pltpu.HBM)] * 2,
         out_specs=[whole] * 2,
         out_shape=[
-            jax.ShapeDtypeStruct((16, 24, 16, 128), BF),
+            jax.ShapeDtypeStruct((16, 16 + CROSS, 16, 128), BF),
             jax.ShapeDtypeStruct((2, 3, 64, 128), BF),
         ],
         scratch_shapes=[
@@ -86,16 +92,10 @@
     )(right_operators.reshape(16, 2, 8, 2, 4, 16, 128), wave_blocks)
 
 
-GROUPS = (6, 6, 6, 3, 3)
-ROWS = (24, 16, 16, 8, 8)
-STARTS = (0, 96, 192, 288, 336)
-TILES = tuple(n * rows for n, rows in zip(GROUPS, ROWS))
-
-
 def tiles_kernel(
     sent, own_table, far_table, own_wave, far_wave, own_left, far_left, *refs
 ):
-    count = 4 if sent else 1
+    count = 3 if sent else 1
     results, outs = refs[:count], refs[count : 2 * count] if sent else refs[:count]
     sides, bras, kets, operators, sem, out_sem = refs[-6:]
     core, _, z, q = where()
@@ -130,21 +130,19 @@
     ]
     labels = [column[s, 0] for column in columns for s in range(12)]
     shifts = [lax.rem(label - q + 32, 32) for label in labels]
-    for out, spot in zip(outs, range(1, 5) if sent else range(1)):
-        members = GROUPS[spot] * 4
-        offset = 12 if spot == 4 else 0
+    for i, out in enumerate(outs):
+        start = 96 * (i + 1 if sent else 0)
         for tile in range(3):
-            place = (iota((16, 128), 1) + tile * 128 - STARTS[spot]) // 4
+            place = (iota((16, 128), 1) + tile * 128 - start) // 4
             row = jnp.zeros((16, 128), F32)
-            low_s, high_s = (tile * 128 - STARTS[spot]) // 4, (tile * 128 + 128 - STARTS[spot]) // 4
-            for s in range(max(0, low_s), min(members, high_s)):
-                row = jnp.where(place == s, labels[offset + s].astype(F32), row)
-            out[TILES[spot] + tile] = row.astype(BF)
+            for s in range(max(0, (tile * 128 - start) // 4), min(24, (tile * 128 + 128 - start) // 4)):
+                row = jnp.where(place == s, labels[s].astype(F32), row)
+            out[out.shape[0] - 3 + tile] = row.astype(BF)
 
     leaving = []
     for half in range(2):
         if sent:
-            spots = [(z + ahead) & 7, (z - ahead) & 7, (z - 2 * ahead if half else z + 2 * ahead) & 7]
+            spots = [(z + ahead) & 7, (z - ahead) & 7, (z + 2 * ahead) & 7]
         else:
             spots = [z, z ^ 2]
         width = 16 * len(spots)
@@ -192,19 +190,19 @@
                 )
                 rows = jnp.swapaxes(rows, 0, 1)
                 if sent and i == 2:
-                    outs[2 + half][group * 8 : group * 8 + 8] = rows[0:8]
+                    outs[2][whole * SPLIT : whole * SPLIT + SPLIT] = rows[0:SPLIT]
                 elif i == 1 and not sent:
-                    outs[0][96 + whole * 8 : 96 + whole * 8 + 8] = rows[8:16]
+                    outs[0][96 + whole * CROSS : 96 + whole * CROSS + CROSS] = rows[SPLIT:16]
                 else:
                     outs[i][whole * 16 : whole * 16 + 16] = rows
         if sent:
-            part = slice(48, TILES[1] + 3) if half else slice(0, 48)
-            for i, tiles in ((0, part), (1, part), (2 + half, slice(0, TILES[3] + 3))):
-                size = tiles.stop - tiles.start
+            for i, out in enumerate(outs):
+                middle = TILES[i + 1] // 2
+                size = middle + 3 if half else middle
                 copy = pltpu.make_async_copy(
-                    outs[i].at[pl.ds(tiles.start, size)],
-                    results[i].at[pl.ds(tiles.start, size)],
-                    out_sem.at[half, min(i, 2)],
+                    out.at[pl.ds(middle * half, size)],
+                    results[i].at[pl.ds(middle * half, size)],
+                    out_sem.at[half, i],
                 )
                 copy.start()
                 leaving.append(copy)
@@ -252,34 +250,33 @@
 
 
 def contract_kernel(
-    home, ahead1, back1, ahead2, back2, right, right_table, picks, out, paired_ref
+    home, ahead1, back1, ahead2, right, right_table, picks, out, paired_ref
 ):
-    arrays = (home, ahead1, back1, ahead2, back2)
+    arrays = (home, ahead1, back1, ahead2)
     zero = jnp.zeros((96, 128), BF)
 
     def lefts(a):
         if a >= 16:
-            return [home[96 + g * 8 + a - 16] for g in range(6)] + [zero[0:32]]
+            return [home[96 + g * CROSS + a - 16] for g in range(6)] + [zero[0:32]]
         tiles = [ref[g * 16 + a] for ref in arrays[0:3] for g in range(6)]
-        if a >= 8:
+        if a >= SPLIT:
             return tiles + [zero]
-        return tiles + [ref[g * 8 + a] for ref in arrays[3:5] for g in range(3)]
-
-    def product(start):
+        return tiles + [ahead2[g * SPLIT + a] for g in range(6)]
+
+    def product(start, stop):
         total = 0.0
-        for a in range(start, start + 8, 2):
+        for first in range(start, stop, 2):
+            pair = range(first, min(first + 2, stop))
             total += lax.dot_general(
-                jnp.concatenate([right[:, a + i].reshape(256, 128) for i in range(2)], axis=1),
-                jnp.concatenate(
-                    [jnp.concatenate(lefts(a + i), axis=0) for i in range(2)], axis=1
-                ),
+                jnp.concatenate([right[:, a].reshape(256, 128) for a in pair], axis=1),
+                jnp.concatenate([jnp.concatenate(lefts(a), axis=0) for a in pair], axis=1),
                 (((1,), (1,)), ((), ())),
                 preferred_element_type=F32,
             )
         return total
 
-    paired = product(0) + product(8)
-    cross = product(16)
+    paired = product(0, 16)
+    cross = product(16, 16 + CROSS)
     for third in range(3):
         lanes = slice(third * 128, third * 128 + 128)
         paired_ref[third] = paired[:, lanes] + cross if third == 0 else paired[:, lanes]
@@ -328,7 +325,7 @@
     whole = pl.BlockSpec(memory_space=pltpu.VMEM)
     return pl.pallas_call(
         contract_kernel,
-        in_specs=[whole] * 8,
+        in_specs=[whole] * 7,
         out_specs=whole,
         out_shape=jax.ShapeDtypeStruct((8, 64, 128), BF),
         scratch_shapes=[pltpu.VMEM((3, 256, 128), F32)],
@@ -359,7 +356,7 @@
     far_left = lax.ppermute(left_operators, "row", swap)
     far_table = lax.ppermute(left_table, "row", swap)
     right = lax.all_to_all(right, "col", 0, 0, tiled=True)
-    ahead1, back1, ahead2, back2 = make_tiles(
+    ahead1, back1, ahead2 = make_tiles(
         True, left_table, far_table, own_wave, far_wave, left_operators, far_left
     )
     far_wave, assignment, kramers_map, ahead1 = lax.optimization_barrier(
@@ -370,7 +367,6 @@
         lax.ppermute(ahead1, line, ahead(1)),
         lax.ppermute(back1, line, ahead(-1)),
         lax.ppermute(ahead2, line, ahead(2)),
-        lax.ppermute(back2, line, ahead(-2)),
     ]
     (home,) = make_tiles(
         False, left_table, far_table, own_wave, far_wave, left_operators, far_left

time: 65.3 us -> 65.4 us (level)
  starting transfers between devices: 18.4 us -> 17.5 us
  waiting for transfers between devices: 7.46 us -> 8.27 us
    ppermute x1 -> x0, starting transfers between devices: 0.87 us -> none  [local(): lax.ppermute(back2, line, ahead(-2))]
    all_to_all x1, waiting for transfers between devices: 7.44 us -> 8.26 us  [local(): right = lax.all_to_all(right, 'col', 0, 0, tiled=True)]
  transfers between devices with their start and end apart: 8 -> 7, of which waited for: 1 -> 1; matrix products, arithmetic and copies ran while one was open for 2% -> 2% of each run, Pallas kernels for 13% -> 13%
where the time goes in v13:
time: 65.4 us; the launch traced here: 65.1 us
  blocking collectives  23.4 us (36%)
  starting transfers between devices  17.5 us (27%)
  Pallas kernels  11.1 us (17%)
  waiting for transfers between devices  8.27 us (13%)
  local copies, waits for them, and re-layouts  3.82 us (6%)
    all_to_all x1, blocking collectives, local(): lax.all_to_all(shares.reshape(256, 2, 128), ('row', 'wf', 'col'), 0, 0, t...  23.4 us
    all_to_all x1, waiting for transfers between devices, local(): right = lax.all_to_all(right, 'col', 0, 0, tiled=True)  8.26 us
    all_to_all x1, starting transfers between devices, local(): right = lax.all_to_all(right, 'col', 0, 0, tiled=True)  6.89 us
    pallas_call x2, Pallas kernels, make_tiles(): pl.pallas_call(functools.partial(tiles_kernel, sent), in_specs=[whole] *...  5.4 us
    ppermute x1, starting transfers between devices, local(): lax.ppermute(own_wave, line, ring(lambda z, core: (z + 2) % 8 if z in (2,...  4.37 us
    ppermute x1, starting transfers between devices, local(): far_left = lax.ppermute(left_operators, 'row', swap)  3.24 us
    pallas_call x1, Pallas kernels, pick(): pl.pallas_call(pick_kernel, in_specs=[pl.BlockSpec(memory_space=pltpu.HBM...  2.98 us
    pallas_call x1, Pallas kernels, contract(): pl.pallas_call(contract_kernel, in_specs=[whole] * 7, out_specs=whole, ou...  2.57 us
  transfers between devices with their start and end apart: 7, of which 1 were waited for; matrix products, arithmetic and copies ran while one was open for 2% of the time, Pallas kernels for 13%

profile of v13, /device:TPU:1, one launch (start us, length us, event | category | flops | bytes accessed | tf_op | source)
XLA Modules:
  0.0 65.1 jit_solution(10638190155783138190)
XLA Ops:
  0.0 3.2 %collective-permute-start.2 = (bf16[12,2,2,128,128]{4,3,2,1,0:T(8,128)(2,1)}, bf16[12,2,2,128,128]{4,3,2,1,0:T(8,128)(2,1)}, u32[]{:S(2)}, u32[]{:S(2)}) collective-permute-start(bf16[12,2,2,128,128]{4,3,2,1,0:T(8,128)(2,1)} %own_left.3), channel_id=1, source_target_pairs={{0,32},{32,0},{64,96},{96,64},{128,160},{160,128},{192,224},{224,1... | collective-permute-start | bytes 4718600 | tf_op jit(solution)/shard_map/ppermute | solution.py:356
  3.2 0.0 collective-permute-start
  3.2 3.0 %pick.1 = (bf16[16,24,16,128]{3,2,1,0:T(8,128)(2,1)}, bf16[2,3,64,128]{3,2,1,0:T(8,128)(2,1)}) custom-call(bf16[16,2,8,2,4,16,128]{6,5,4,3,2,1,0:T(8,128)(2,1)} %bitcast.21, bf16[2,32,64,128]{3,2,1,0:T(8,128)(2,1)} %wave_ref.1), custom_call_target="tpu_custom_call" | custom-call | tf_op jit(solution)/shard_map/pick/pallas_call | solution.py:77
  6.2 4.4 %collective-permute-start.1 = (bf16[2,3,64,128]{3,2,1,0:T(8,128)(2,1)}, bf16[2,3,64,128]{3,2,1,0:T(8,128)(2,1)S(1)}, u32[]{:S(2)}, u32[]{:S(2)}) collective-permute-start(bf16[2,3,64,128]{3,2,1,0:T(8,128)(2,1)} %get-tuple-element.14.own_wave), channel_id=1, source_target_pairs={{0,129},{32,161},{64,193},{96,225},{128,1},{160,33},{192,65},{224,... | collective-permute-start | bytes 294920 | tf_op jit(solution)/shard_map/ppermute | solution.py:352
  10.6 0.0 copy-start
  10.6 6.9 %all-to-all-start = ((bf16[16,24,16,128]{3,2,1,0:T(8,128)(2,1)}), bf16[16,24,16,128]{3,2,1,0:T(8,128)(2,1)S(1)}, u32[]{:S(2)}, u32[]{:S(2)}) async-start(bf16[16,24,16,128]{3,2,1,0:T(8,128)(2,1)} %get-tuple-element.20), calls=%async_computation | async-start | bytes 3145728 | tf_op jit(solution)/shard_map/all_to_all | solution.py:358
  17.5 0.1 broadcast_in_dim.2
  17.6 0.1 reshape.140.sign
  17.7 0.0 copy-start.7
  17.8 0.0 copy-start.8
  17.8 0.0 collective-permute-done.far_table
  17.8 0.0 collective-permute-done.1.far_wave
  17.8 0.0 copy-start.3
  17.8 0.0 collective-permute-done.2.far_left
  17.8 0.0 copy-done
  17.8 0.0 copy-done.2
  17.8 0.0 copy-done.6
  17.8 3.1 %make_tiles.1 = (bf16[99,16,128]{2,1,0:T(8,128)(2,1)}, bf16[99,16,128]{2,1,0:T(8,128)(2,1)}, bf16[51,16,128]{2,1,0:T(8,128)(2,1)}) custom-call(s32[12,32]{1,0:T(8,128)S(1)} %copy-done.6, s32[12,32]{1,0:T(8,128)S(1)} %collective-permute-done.far_table, bf16[2,3,64,128]{3,2,1,0:T(8,128)(2,1)S(1)} %copy-done.2, ...), custom_call_target="tpu_custom_call" | custom-call | flops 1000000000 | bytes 4000000 | tf_op jit(solution)/shard_map/make_tiles/pallas_call | solution.py:216
  21.0 0.0 copy-done.3
  21.0 0.1 collective-permute-start.3
  21.1 1.5 %collective-permute-start.4 = (bf16[99,16,128]{2,1,0:T(8,128)(2,1)}, bf16[99,16,128]{2,1,0:T(8,128)(2,1)}, u32[]{:S(2)}, u32[]{:S(2)}) collective-permute-start(bf16[99,16,128]{2,1,0:T(8,128)(2,1)} %get-tuple-element.18), channel_id=1, source_target_pairs={{0,193},{32,96},{64,0},{96,160},{128,64},{160,224},{192,128},{224,... | collective-permute-start | bytes 1216520 | tf_op jit(solution)/shard_map/ppermute | solution.py:368
  22.5 1.5 %collective-permute-start.5 = (bf16[51,16,128]{2,1,0:T(8,128)(2,1)}, bf16[51,16,128]{2,1,0:T(8,128)(2,1)S(1)}, u32[]{:S(2)}, u32[]{:S(2)}) collective-permute-start(bf16[51,16,128]{2,1,0:T(8,128)(2,1)} %get-tuple-element.19), channel_id=1, source_target_pairs={{0,128},{32,161},{64,192},{96,225},{128,1},{160,32},{192,65},{224,... | collective-permute-start | bytes 626696 | tf_op jit(solution)/shard_map/ppermute | solution.py:369
  24.0 0.0 copy-done.7
  24.0 0.1 reshape.139
  24.2 0.1 mul.40
  24.3 0.0 copy-done.8
  24.3 0.1 stack.16
  24.4 0.1 fusion.2
  24.5 0.1 iota_add_fusion
  24.6 0.1 fusion.1
  24.6 0.1 add.106.slot_key
  24.7 0.1 add.102.real_key
  24.9 0.1 sub.29.imag_key
  25.0 0.2 make_picks.1.picks
  25.2 0.0 copy-start.1
  25.2 1.4 %copy-done.1 = bf16[12,2,2,128,128]{4,3,2,1,0:T(8,128)(2,1)S(1)} copy-done((bf16[12,2,2,128,128]{4,3,2,1,0:T(8,128)(2,1)S(1)}, bf16[12,2,2,128,128]{4,3,2,1,0:T(8,128)(2,1)}, u32[]{:S(2)}) %copy-start.1) | copy-done | bytes 1572888
  26.6 0.9 %copy-done.4 = bf16[2,3,64,128]{3,2,1,0:T(8,128)(2,1)S(1)} copy-done((bf16[2,3,64,128]{3,2,1,0:T(8,128)(2,1)S(1)}, bf16[2,3,64,128]{3,2,1,0:T(8,128)(2,1)}, u32[]{:S(2)}) %copy-start.4) | copy-done | bytes 98328
  27.5 2.3 %make_home.1.home = bf16[147,16,128]{2,1,0:T(8,128)(2,1)S(1)} custom-call(s32[12,32]{1,0:T(8,128)S(1)} %copy-done.6, s32[12,32]{1,0:T(8,128)S(1)} %collective-permute-done.far_table, bf16[2,3,64,128]{3,2,1,0:T(8,128)(2,1)S(1)} %copy-done.2, bf16[2,3,64,128]{3,2,1,0:T(8,128)(2,1)S(1)} %copy-done.4, bf16[12,2,2,128,128]{4,3,2,1,0:T(8,128)(2,1)S(1)} %copy-done.1, ...), custom_call_target="tpu_custom_call" | custom-call | flops 1000000000 | bytes 4000000 | tf_op jit(solution)/shard_map/make_home/pallas_call | solution.py:216
  29.8 8.3 %all-to-all-done.right = bf16[16,24,16,128]{3,2,1,0:T(8,128)(2,1)S(1)} async-done(((bf16[16,24,16,128]{3,2,1,0:T(8,128)(2,1)}), bf16[16,24,16,128]{3,2,1,0:T(8,128)(2,1)S(1)}, u32[]{:S(2)}, u32[]{:S(2)}) %all-to-all-start) | async-done | bytes 1572896 | tf_op jit(solution)/shard_map/all_to_all | solution.py:358
  38.0 0.0 collective-permute-done.5.ahead2
  38.0 0.0 collective-permute-done.3.ahead1
  38.0 0.0 collective-permute-done.4.back1
  38.0 0.0 copy-done.5
  38.1 2.6 %contract.1 = bf16[8,64,128]{2,1,0:T(8,128)(2,1)S(1)} custom-call(bf16[147,16,128]{2,1,0:T(8,128)(2,1)S(1)} %make_home.1.home, bf16[99,16,128]{2,1,0:T(8,128)(2,1)S(1)} %collective-permute-done.3.ahead1, bf16[99,16,128]{2,1,0:T(8,128)(2,1)} %collective-permute-done.4.back1, bf16[51,16,128]{2,1,0:T(8,128)(2,1)S(1)} %collective-permute-done.5.ahead2, ...), custom_call_target="tpu_custom_call" | custom-call | tf_op jit(solution)/shard_map/contract/pallas_call | solution.py:326
  40.6 23.4 %all_to_all.10 = bf16[256,2,128]{2,1,0:T(2,128)(2,1)S(1)} all-to-all(bf16[256,2,128]{2,1,0:T(2,128)(2,1)S(1)} %bitcast.19), channel_id=1, replica_groups=mesh['row'=8,'col'=16,'wf'=2] {'row','wf','col'}, dimensions={0} | all-to-all | bytes 262144 | tf_op jit(solution)/shard_map/all_to_all | solution.py:393
  64.1 0.3 convert_reduce_fusion
  64.4 0.1 reshape.142
  64.4 0.6 copy.13
  (17 shorter events, 0.1 us)
Async XLA Ops:
  0.0 17.8 %collective-permute-start.2 = (bf16[12,2,2,128,128]{4,3,2,1,0:T(8,128)(2,1)}, bf16[12,2,2,128,128]{4,3,2,1,0:T(8,128)(2,1)}, u32[]{:S(2)}, u32[]{:S(2)}) collective-permute-start(bf16[12,2,2,128,128]{4,3,2,1,0:T(8,128)(2,1)} %own_left.3), channel_id=1, source_target_pairs={{0,32},{32,0},{64,96},{96,64},{128,160},{160,128},{192,224},{224,1... | collective-permute-start | bytes 4718600 | tf_op jit(solution)/shard_map/ppermute | solution.py:356
  3.2 14.5 %collective-permute-start = (s32[12,32]{1,0:T(8,128)}, s32[12,32]{1,0:T(8,128)S(1)}, u32[]{:S(2)}, u32[]{:S(2)}) collective-permute-start(s32[12,32]{1,0:T(8,128)} %own_table.3), channel_id=1, source_target_pairs={{0,32},{32,0},{64,96},{96,64},{128,160},{160,128},{192,224},{224,1... | collective-permute-start | bytes 4616 | tf_op jit(solution)/shard_map/ppermute | solution.py:357
  6.2 11.5 %collective-permute-start.1 = (bf16[2,3,64,128]{3,2,1,0:T(8,128)(2,1)}, bf16[2,3,64,128]{3,2,1,0:T(8,128)(2,1)S(1)}, u32[]{:S(2)}, u32[]{:S(2)}) collective-permute-start(bf16[2,3,64,128]{3,2,1,0:T(8,128)(2,1)} %get-tuple-element.14.own_wave), channel_id=1, source_target_pairs={{0,129},{32,161},{64,193},{96,225},{128,1},{160,33},{192,65},{224,... | collective-permute-start | bytes 294920 | tf_op jit(solution)/shard_map/ppermute | solution.py:352
  10.6 7.2 %copy-start = (bf16[12,2,2,128,128]{4,3,2,1,0:T(8,128)(2,1)S(1)}, bf16[12,2,2,128,128]{4,3,2,1,0:T(8,128)(2,1)}, u32[]{:S(2)}) copy-start(bf16[12,2,2,128,128]{4,3,2,1,0:T(8,128)(2,1)} %own_left.3) | copy-start | bytes 4718596
  10.6 7.2 %copy-start.2 = (bf16[2,3,64,128]{3,2,1,0:T(8,128)(2,1)S(1)}, bf16[2,3,64,128]{3,2,1,0:T(8,128)(2,1)}, u32[]{:S(2)}) copy-start(bf16[2,3,64,128]{3,2,1,0:T(8,128)(2,1)} %get-tuple-element.14.own_wave) | copy-start | bytes 294916
  10.6 7.2 %copy-start.6 = (s32[12,32]{1,0:T(8,128)S(1)}, s32[12,32]{1,0:T(8,128)}, u32[]{:S(2)}) copy-start(s32[12,32]{1,0:T(8,128)} %own_table.3) | copy-start | bytes 4612
  10.6 27.4 %all-to-all-start = ((bf16[16,24,16,128]{3,2,1,0:T(8,128)(2,1)}), bf16[16,24,16,128]{3,2,1,0:T(8,128)(2,1)S(1)}, u32[]{:S(2)}, u32[]{:S(2)}) async-start(bf16[16,24,16,128]{3,2,1,0:T(8,128)(2,1)} %get-tuple-element.20), calls=%async_computation | async-start | bytes 3145728 | tf_op jit(solution)/shard_map/all_to_all | solution.py:358
  17.7 6.3 %copy-start.7 = (s32[96]{0:T(128)S(1)}, s32[96]{0:T(128)}, u32[]{:S(2)}) copy-start(s32[96]{0:T(128)} %param.12) | copy-start | bytes 1156
  17.8 6.6 %copy-start.8 = (s32[96]{0:T(128)S(1)}, s32[96]{0:T(128)}, u32[]{:S(2)}) copy-start(s32[96]{0:T(128)} %param.13) | copy-start | bytes 1156
  17.8 3.2 %copy-start.3 = (bf16[2,3,64,128]{3,2,1,0:T(8,128)(2,1)}, bf16[2,3,64,128]{3,2,1,0:T(8,128)(2,1)S(1)}, u32[]{:S(2)}) copy-start(bf16[2,3,64,128]{3,2,1,0:T(8,128)(2,1)S(1)} %collective-permute-done.1.far_wave) | copy-start | bytes 294916
  21.0 17.1 %collective-permute-start.3 = (bf16[99,16,128]{2,1,0:T(8,128)(2,1)}, bf16[99,16,128]{2,1,0:T(8,128)(2,1)S(1)}, u32[]{:S(2)}, u32[]{:S(2)}) collective-permute-start(bf16[99,16,128]{2,1,0:T(8,128)(2,1)} %get-tuple-element.17), channel_id=1, source_target_pairs={{0,64},{32,225},{64,128},{96,32},{128,192},{160,96},{192,1},{224,1... | collective-permute-start | bytes 1216520 | tf_op jit(solution)/shard_map/ppermute | solution.py:367
  21.1 17.0 %collective-permute-start.4 = (bf16[99,16,128]{2,1,0:T(8,128)(2,1)}, bf16[99,16,128]{2,1,0:T(8,128)(2,1)}, u32[]{:S(2)}, u32[]{:S(2)}) collective-permute-start(bf16[99,16,128]{2,1,0:T(8,128)(2,1)} %get-tuple-element.18), channel_id=1, source_target_pairs={{0,193},{32,96},{64,0},{96,160},{128,64},{160,224},{192,128},{224,... | collective-permute-start | bytes 1216520 | tf_op jit(solution)/shard_map/ppermute | solution.py:368
  22.5 15.5 %collective-permute-start.5 = (bf16[51,16,128]{2,1,0:T(8,128)(2,1)}, bf16[51,16,128]{2,1,0:T(8,128)(2,1)S(1)}, u32[]{:S(2)}, u32[]{:S(2)}) collective-permute-start(bf16[51,16,128]{2,1,0:T(8,128)(2,1)} %get-tuple-element.19), channel_id=1, source_target_pairs={{0,128},{32,161},{64,192},{96,225},{128,1},{160,32},{192,65},{224,... | collective-permute-start | bytes 626696 | tf_op jit(solution)/shard_map/ppermute | solution.py:369
  25.2 1.4 %copy-start.1 = (bf16[12,2,2,128,128]{4,3,2,1,0:T(8,128)(2,1)S(1)}, bf16[12,2,2,128,128]{4,3,2,1,0:T(8,128)(2,1)}, u32[]{:S(2)}) copy-start(bf16[12,2,2,128,128]{4,3,2,1,0:T(8,128)(2,1)} %own_left.3) | copy-start | bytes 4718596
  26.6 0.9 %copy-start.4 = (bf16[2,3,64,128]{3,2,1,0:T(8,128)(2,1)S(1)}, bf16[2,3,64,128]{3,2,1,0:T(8,128)(2,1)}, u32[]{:S(2)}) copy-start(bf16[2,3,64,128]{3,2,1,0:T(8,128)(2,1)} %copy-done.3) | copy-start | bytes 294916
  27.5 10.6 %copy-start.5 = (s32[128,32]{0,1:T(8,128)S(1)}, s32[128,32]{0,1:T(8,128)}, u32[]{:S(2)}) copy-start(s32[128,32]{0,1:T(8,128)} %param.11) | copy-start | bytes 49156

commit v14 on v13

--- a/solution.py
+++ b/solution.py
@@ -24,7 +24,7 @@
     return pltpu.CompilerParams(vmem_limit_bytes=mebibytes * 1024 * 1024)
 
 
-SPLIT = 8
+SPLIT = 7
 CROSS = 16 - SPLIT
 ROWS = (16 + CROSS, 16, 16, SPLIT)
 TILES = tuple(6 * rows for rows in ROWS)
@@ -132,12 +132,11 @@
     shifts = [lax.rem(label - q + 32, 32) for label in labels]
     for i, out in enumerate(outs):
         start = 96 * (i + 1 if sent else 0)
-        for tile in range(3):
-            place = (iota((16, 128), 1) + tile * 128 - start) // 4
-            row = jnp.zeros((16, 128), F32)
-            for s in range(max(0, (tile * 128 - start) // 4), min(24, (tile * 128 + 128 - start) // 4)):
-                row = jnp.where(place == s, labels[s].astype(F32), row)
-            out[out.shape[0] - 3 + tile] = row.astype(BF)
+        place = (iota((16, 128), 0) * 128 + iota((16, 128), 1) - start) >> 2
+        label = jnp.zeros((16, 128), F32)
+        for s in range(24):
+            label = jnp.where(place == s, labels[s].astype(F32), label)
+        out[out.shape[0] - 1] = label.astype(BF)
 
     leaving = []
     for half in range(2):
@@ -198,7 +197,7 @@
         if sent:
             for i, out in enumerate(outs):
                 middle = TILES[i + 1] // 2
-                size = middle + 3 if half else middle
+                size = middle + 1 if half else middle
                 copy = pltpu.make_async_copy(
                     out.at[pl.ds(middle * half, size)],
                     results[i].at[pl.ds(middle * half, size)],
@@ -212,7 +211,7 @@
 
 def make_tiles(sent, own_table, far_table, own_wave, far_wave, left_operators, far_left):
     anywhere, whole = pl.BlockSpec(memory_space=pl.ANY), pl.BlockSpec(memory_space=pltpu.VMEM)
-    shapes = [(n + 3, 16, 128) for n in (TILES[1:] if sent else TILES[:1])]
+    shapes = [(n + 1, 16, 128) for n in (TILES[1:] if sent else TILES[:1])]
     return pl.pallas_call(
         functools.partial(tiles_kernel, sent),
         in_specs=[whole] * 4 + [anywhere] * 2,
@@ -281,13 +280,8 @@
         lanes = slice(third * 128, third * 128 + 128)
         paired_ref[third] = paired[:, lanes] + cross if third == 0 else paired[:, lanes]
 
-    slot_label = jnp.concatenate(
-        [
-            sum(ref[n + tile].astype(F32)[0:1] for ref, n in zip(arrays, TILES))
-            for tile in range(3)
-        ],
-        axis=1,
-    )
+    slot_label = sum(ref[n].astype(F32) for ref, n in zip(arrays, TILES))
+    slot_label = jnp.concatenate([slot_label[i : i + 1] for i in range(3)], axis=1)
     row = iota((128, 128), 0)
     j = row % 32 // 2 * 8 + row // 32 % 2 * 4 + row % 2 * 2 + row // 64
     labels = right_table[pl.ds(where()[3], 1), :].astype(F32)

time: 65.4 us -> 65.4 us (level)
  local copies, waits for them, and re-layouts: 3.82 us -> 4.48 us
    all_to_all x1, blocking collectives: 23.4 us -> 22.8 us  [local(): lax.all_to_all(shares.reshape(256, 2, 128), ('row', 'wf', 'col'), 0, 0, t...]
    another operation x1, local copies, waits for them, and re-layouts: 0.08 us -> 0.74 us  [local(): jnp.stack([jnp.arange(96, dtype=jnp.int32), kramers_map])]
    unnamed x18 -> x16, local copies, waits for them, and re-layouts: 2.33 us -> 2.32 us
  transfers between devices with their start and end apart: 7 -> 7, of which waited for: 1 -> 1; matrix products, arithmetic and copies ran while one was open for 2% -> 3% of each run, Pallas kernels for 13% -> 13%
where the time goes in v14:
time: 65.4 us; the launch traced here: 65 us
  blocking collectives  22.8 us (35%)
  starting transfers between devices  17.6 us (27%)
  Pallas kernels  11.2 us (17%)
  waiting for transfers between devices  8.24 us (13%)
  local copies, waits for them, and re-layouts  4.48 us (7%)
    all_to_all x1, blocking collectives, local(): lax.all_to_all(shares.reshape(256, 2, 128), ('row', 'wf', 'col'), 0, 0, t...  22.8 us
    all_to_all x1, waiting for transfers between devices, local(): right = lax.all_to_all(right, 'col', 0, 0, tiled=True)  8.22 us
    all_to_all x1, starting transfers between devices, local(): right = lax.all_to_all(right, 'col', 0, 0, tiled=True)  6.89 us
    pallas_call x2, Pallas kernels, make_tiles(): pl.pallas_call(functools.partial(tiles_kernel, sent), in_specs=[whole] *...  5.39 us
    ppermute x1, starting transfers between devices, local(): lax.ppermute(own_wave, line, ring(lambda z, core: (z + 2) % 8 if z in (2,...  4.37 us
    ppermute x1, starting transfers between devices, local(): far_left = lax.ppermute(left_operators, 'row', swap)  3.24 us
    pallas_call x1, Pallas kernels, pick(): pl.pallas_call(pick_kernel, in_specs=[pl.BlockSpec(memory_space=pltpu.HBM...  3.02 us
    pallas_call x1, Pallas kernels, contract(): pl.pallas_call(contract_kernel, in_specs=[whole] * 7, out_specs=whole, ou...  2.59 us
  transfers between devices with their start and end apart: 7, of which 1 were waited for; matrix products, arithmetic and copies ran while one was open for 3% of the time, Pallas kernels for 13%

profile of v14, /device:TPU:1, one launch (start us, length us, event | category | flops | bytes accessed | tf_op | source)
XLA Modules:
  0.0 65.0 jit_solution(8131252713057131560)
XLA Ops:
  0.0 3.2 %collective-permute-start.2 = (bf16[12,2,2,128,128]{4,3,2,1,0:T(8,128)(2,1)}, bf16[12,2,2,128,128]{4,3,2,1,0:T(8,128)(2,1)}, u32[]{:S(2)}, u32[]{:S(2)}) collective-permute-start(bf16[12,2,2,128,128]{4,3,2,1,0:T(8,128)(2,1)} %own_left.3), channel_id=1, source_target_pairs={{0,32},{32,0},{64,96},{96,64},{128,160},{160,128},{192,224},{224,1... | collective-permute-start | bytes 4718600 | tf_op jit(solution)/shard_map/ppermute | solution.py:350
  3.2 0.0 collective-permute-start
  3.2 3.0 %pick.1 = (bf16[16,25,16,128]{3,2,1,0:T(8,128)(2,1)}, bf16[2,3,64,128]{3,2,1,0:T(8,128)(2,1)}) custom-call(bf16[16,2,8,2,4,16,128]{6,5,4,3,2,1,0:T(8,128)(2,1)} %bitcast.21, bf16[2,32,64,128]{3,2,1,0:T(8,128)(2,1)} %wave_ref.1), custom_call_target="tpu_custom_call" | custom-call | tf_op jit(solution)/shard_map/pick/pallas_call | solution.py:77
  6.3 4.4 %collective-permute-start.1 = (bf16[2,3,64,128]{3,2,1,0:T(8,128)(2,1)}, bf16[2,3,64,128]{3,2,1,0:T(8,128)(2,1)S(1)}, u32[]{:S(2)}, u32[]{:S(2)}) collective-permute-start(bf16[2,3,64,128]{3,2,1,0:T(8,128)(2,1)} %get-tuple-element.14.own_wave), channel_id=1, source_target_pairs={{0,129},{32,161},{64,193},{96,225},{128,1},{160,33},{192,65},{224,... | collective-permute-start | bytes 294920 | tf_op jit(solution)/shard_map/ppermute | solution.py:346
  10.6 0.0 copy-start
  10.7 0.0 copy-start.2
  10.7 0.0 copy-start.6
  10.7 6.9 %all-to-all-start = ((bf16[16,25,16,128]{3,2,1,0:T(8,128)(2,1)}), bf16[16,25,16,128]{3,2,1,0:T(8,128)(2,1)S(1)}, u32[]{:S(2)}, u32[]{:S(2)}) async-start(bf16[16,25,16,128]{3,2,1,0:T(8,128)(2,1)} %get-tuple-element.20), calls=%async_computation | async-start | bytes 3276800 | tf_op jit(solution)/shard_map/all_to_all | solution.py:352
  17.6 0.1 broadcast_in_dim.2
  17.7 0.1 reshape.140.sign
  17.8 0.0 copy-start.7
  17.8 0.0 collective-permute-done.far_table
  17.8 0.0 collective-permute-done.1.far_wave
  17.8 0.0 copy-start.3
  17.8 0.0 collective-permute-done.2.far_left
  17.8 0.0 copy-done
  17.8 0.0 copy-done.2
  17.9 0.0 copy-done.6
  17.9 3.1 %make_tiles.1 = (bf16[97,16,128]{2,1,0:T(8,128)(2,1)}, bf16[97,16,128]{2,1,0:T(8,128)(2,1)}, bf16[43,16,128]{2,1,0:T(8,128)(2,1)}) custom-call(s32[12,32]{1,0:T(8,128)S(1)} %copy-done.6, s32[12,32]{1,0:T(8,128)S(1)} %collective-permute-done.far_table, bf16[2,3,64,128]{3,2,1,0:T(8,128)(2,1)S(1)} %copy-done.2, ...), custom_call_target="tpu_custom_call" | custom-call | flops 1000000000 | bytes 4000000 | tf_op jit(solution)/shard_map/make_tiles/pallas_call | solution.py:215
  21.0 0.0 copy-done.3
  21.0 0.1 collective-permute-start.3
  21.1 1.5 %collective-permute-start.4 = (bf16[97,16,128]{2,1,0:T(8,128)(2,1)}, bf16[97,16,128]{2,1,0:T(8,128)(2,1)}, u32[]{:S(2)}, u32[]{:S(2)}) collective-permute-start(bf16[97,16,128]{2,1,0:T(8,128)(2,1)} %get-tuple-element.18), channel_id=1, source_target_pairs={{0,193},{32,96},{64,0},{96,160},{128,64},{160,224},{192,128},{224,... | collective-permute-start | bytes 1191944 | tf_op jit(solution)/shard_map/ppermute | solution.py:362
  22.5 1.5 %collective-permute-start.5 = (bf16[43,16,128]{2,1,0:T(8,128)(2,1)}, bf16[43,16,128]{2,1,0:T(8,128)(2,1)S(1)}, u32[]{:S(2)}, u32[]{:S(2)}) collective-permute-start(bf16[43,16,128]{2,1,0:T(8,128)(2,1)} %get-tuple-element.19), channel_id=1, source_target_pairs={{0,128},{32,161},{64,192},{96,225},{128,1},{160,32},{192,65},{224,... | collective-permute-start | bytes 528392 | tf_op jit(solution)/shard_map/ppermute | solution.py:363
  24.0 0.0 copy-done.7
  24.0 0.1 reshape.139
  24.2 0.1 mul.40
  24.3 0.7 %stack.16 = s32[1,1,8,12]{3,2,1,0:T(8,128)S(1)} reshape(s32[96]{0:T(128)} %param.13) | data formatting | bytes 768 | tf_op jit(solution)/shard_map/stack | solution.py:377
  25.1 0.1 fusion.2
  25.2 0.1 iota_add_fusion
  25.2 0.1 fusion.1
  25.3 0.1 add.106.slot_key
  25.4 0.1 add.102.real_key
  25.6 0.1 sub.29.imag_key
  25.7 0.2 make_picks.1.picks
  25.8 0.0 copy-start.1
  25.9 1.4 %copy-done.1 = bf16[12,2,2,128,128]{4,3,2,1,0:T(8,128)(2,1)S(1)} copy-done((bf16[12,2,2,128,128]{4,3,2,1,0:T(8,128)(2,1)S(1)}, bf16[12,2,2,128,128]{4,3,2,1,0:T(8,128)(2,1)}, u32[]{:S(2)}) %copy-start.1) | copy-done | bytes 1572888
  27.3 0.9 %copy-done.4 = bf16[2,3,64,128]{3,2,1,0:T(8,128)(2,1)S(1)} copy-done((bf16[2,3,64,128]{3,2,1,0:T(8,128)(2,1)S(1)}, bf16[2,3,64,128]{3,2,1,0:T(8,128)(2,1)}, u32[]{:S(2)}) %copy-start.4) | copy-done | bytes 98328
  28.2 2.3 %make_home.1.home = bf16[151,16,128]{2,1,0:T(8,128)(2,1)S(1)} custom-call(s32[12,32]{1,0:T(8,128)S(1)} %copy-done.6, s32[12,32]{1,0:T(8,128)S(1)} %collective-permute-done.far_table, bf16[2,3,64,128]{3,2,1,0:T(8,128)(2,1)S(1)} %copy-done.2, bf16[2,3,64,128]{3,2,1,0:T(8,128)(2,1)S(1)} %copy-done.4, bf16[12,2,2,128,128]{4,3,2,1,0:T(8,128)(2,1)S(1)} %copy-done.1, ...), custom_call_target="tpu_custom_call" | custom-call | flops 1000000000 | bytes 4000000 | tf_op jit(solution)/shard_map/make_home/pallas_call | solution.py:215
  30.5 8.2 %all-to-all-done.right = bf16[16,25,16,128]{3,2,1,0:T(8,128)(2,1)S(1)} async-done(((bf16[16,25,16,128]{3,2,1,0:T(8,128)(2,1)}), bf16[16,25,16,128]{3,2,1,0:T(8,128)(2,1)S(1)}, u32[]{:S(2)}, u32[]{:S(2)}) %all-to-all-start) | async-done | bytes 1638432 | tf_op jit(solution)/shard_map/all_to_all | solution.py:352
  38.7 0.0 collective-permute-done.5.ahead2
  38.7 0.0 collective-permute-done.3.ahead1
  38.7 0.0 collective-permute-done.4.back1
  38.7 0.0 copy-done.5
  38.7 2.6 %contract.1 = bf16[8,64,128]{2,1,0:T(8,128)(2,1)S(1)} custom-call(bf16[151,16,128]{2,1,0:T(8,128)(2,1)S(1)} %make_home.1.home, bf16[97,16,128]{2,1,0:T(8,128)(2,1)S(1)} %collective-permute-done.3.ahead1, bf16[97,16,128]{2,1,0:T(8,128)(2,1)} %collective-permute-done.4.back1, bf16[43,16,128]{2,1,0:T(8,128)(2,1)S(1)} %collective-permute-done.5.ahead2, ...), custom_call_target="tpu_custom_call" | custom-call | tf_op jit(solution)/shard_map/contract/pallas_call | solution.py:320
  41.3 22.8 %all_to_all.10 = bf16[256,2,128]{2,1,0:T(2,128)(2,1)S(1)} all-to-all(bf16[256,2,128]{2,1,0:T(2,128)(2,1)S(1)} %bitcast.19), channel_id=1, replica_groups=mesh['row'=8,'col'=16,'wf'=2] {'row','wf','col'}, dimensions={0} | all-to-all | bytes 262144 | tf_op jit(solution)/shard_map/all_to_all | solution.py:387
  64.0 0.3 convert_reduce_fusion
  64.3 0.1 reshape.142
  64.4 0.6 copy.13
  (15 shorter events, 0.1 us)
Async XLA Ops:
  0.0 17.8 %collective-permute-start.2 = (bf16[12,2,2,128,128]{4,3,2,1,0:T(8,128)(2,1)}, bf16[12,2,2,128,128]{4,3,2,1,0:T(8,128)(2,1)}, u32[]{:S(2)}, u32[]{:S(2)}) collective-permute-start(bf16[12,2,2,128,128]{4,3,2,1,0:T(8,128)(2,1)} %own_left.3), channel_id=1, source_target_pairs={{0,32},{32,0},{64,96},{96,64},{128,160},{160,128},{192,224},{224,1... | collective-permute-start | bytes 4718600 | tf_op jit(solution)/shard_map/ppermute | solution.py:350
  3.2 14.6 %collective-permute-start = (s32[12,32]{1,0:T(8,128)}, s32[12,32]{1,0:T(8,128)S(1)}, u32[]{:S(2)}, u32[]{:S(2)}) collective-permute-start(s32[12,32]{1,0:T(8,128)} %own_table.3), channel_id=1, source_target_pairs={{0,32},{32,0},{64,96},{96,64},{128,160},{160,128},{192,224},{224,1... | collective-permute-start | bytes 4616 | tf_op jit(solution)/shard_map/ppermute | solution.py:351
  6.3 11.5 %collective-permute-start.1 = (bf16[2,3,64,128]{3,2,1,0:T(8,128)(2,1)}, bf16[2,3,64,128]{3,2,1,0:T(8,128)(2,1)S(1)}, u32[]{:S(2)}, u32[]{:S(2)}) collective-permute-start(bf16[2,3,64,128]{3,2,1,0:T(8,128)(2,1)} %get-tuple-element.14.own_wave), channel_id=1, source_target_pairs={{0,129},{32,161},{64,193},{96,225},{128,1},{160,33},{192,65},{224,... | collective-permute-start | bytes 294920 | tf_op jit(solution)/shard_map/ppermute | solution.py:346
  10.6 7.2 %copy-start = (bf16[12,2,2,128,128]{4,3,2,1,0:T(8,128)(2,1)S(1)}, bf16[12,2,2,128,128]{4,3,2,1,0:T(8,128)(2,1)}, u32[]{:S(2)}) copy-start(bf16[12,2,2,128,128]{4,3,2,1,0:T(8,128)(2,1)} %own_left.3) | copy-start | bytes 4718596
  10.7 7.2 %copy-start.2 = (bf16[2,3,64,128]{3,2,1,0:T(8,128)(2,1)S(1)}, bf16[2,3,64,128]{3,2,1,0:T(8,128)(2,1)}, u32[]{:S(2)}) copy-start(bf16[2,3,64,128]{3,2,1,0:T(8,128)(2,1)} %get-tuple-element.14.own_wave) | copy-start | bytes 294916
  10.7 7.2 %copy-start.6 = (s32[12,32]{1,0:T(8,128)S(1)}, s32[12,32]{1,0:T(8,128)}, u32[]{:S(2)}) copy-start(s32[12,32]{1,0:T(8,128)} %own_table.3) | copy-start | bytes 4612
  10.7 28.0 %all-to-all-start = ((bf16[16,25,16,128]{3,2,1,0:T(8,128)(2,1)}), bf16[16,25,16,128]{3,2,1,0:T(8,128)(2,1)S(1)}, u32[]{:S(2)}, u32[]{:S(2)}) async-start(bf16[16,25,16,128]{3,2,1,0:T(8,128)(2,1)} %get-tuple-element.20), calls=%async_computation | async-start | bytes 3276800 | tf_op jit(solution)/shard_map/all_to_all | solution.py:352
  17.8 6.3 %copy-start.7 = (s32[96]{0:T(128)S(1)}, s32[96]{0:T(128)}, u32[]{:S(2)}) copy-start(s32[96]{0:T(128)} %param.12) | copy-start | bytes 1156
  17.8 3.2 %copy-start.3 = (bf16[2,3,64,128]{3,2,1,0:T(8,128)(2,1)}, bf16[2,3,64,128]{3,2,1,0:T(8,128)(2,1)S(1)}, u32[]{:S(2)}) copy-start(bf16[2,3,64,128]{3,2,1,0:T(8,128)(2,1)S(1)} %collective-permute-done.1.far_wave) | copy-start | bytes 294916
  21.0 17.7 %collective-permute-start.3 = (bf16[97,16,128]{2,1,0:T(8,128)(2,1)}, bf16[97,16,128]{2,1,0:T(8,128)(2,1)S(1)}, u32[]{:S(2)}, u32[]{:S(2)}) collective-permute-start(bf16[97,16,128]{2,1,0:T(8,128)(2,1)} %get-tuple-element.17), channel_id=1, source_target_pairs={{0,64},{32,225},{64,128},{96,32},{128,192},{160,96},{192,1},{224,1... | collective-permute-start | bytes 1191944 | tf_op jit(solution)/shard_map/ppermute | solution.py:361
  21.1 17.6 %collective-permute-start.4 = (bf16[97,16,128]{2,1,0:T(8,128)(2,1)}, bf16[97,16,128]{2,1,0:T(8,128)(2,1)}, u32[]{:S(2)}, u32[]{:S(2)}) collective-permute-start(bf16[97,16,128]{2,1,0:T(8,128)(2,1)} %get-tuple-element.18), channel_id=1, source_target_pairs={{0,193},{32,96},{64,0},{96,160},{128,64},{160,224},{192,128},{224,... | collective-permute-start | bytes 1191944 | tf_op jit(solution)/shard_map/ppermute | solution.py:362
  22.5 16.2 %collective-permute-start.5 = (bf16[43,16,128]{2,1,0:T(8,128)(2,1)}, bf16[43,16,128]{2,1,0:T(8,128)(2,1)S(1)}, u32[]{:S(2)}, u32[]{:S(2)}) collective-permute-start(bf16[43,16,128]{2,1,0:T(8,128)(2,1)} %get-tuple-element.19), channel_id=1, source_target_pairs={{0,128},{32,161},{64,192},{96,225},{128,1},{160,32},{192,65},{224,... | collective-permute-start | bytes 528392 | tf_op jit(solution)/shard_map/ppermute | solution.py:363
  25.8 1.4 %copy-start.1 = (bf16[12,2,2,128,128]{4,3,2,1,0:T(8,128)(2,1)S(1)}, bf16[12,2,2,128,128]{4,3,2,1,0:T(8,128)(2,1)}, u32[]{:S(2)}) copy-start(bf16[12,2,2,128,128]{4,3,2,1,0:T(8,128)(2,1)} %own_left.3) | copy-start | bytes 4718596
  27.3 0.9 %copy-start.4 = (bf16[2,3,64,128]{3,2,1,0:T(8,128)(2,1)S(1)}, bf16[2,3,64,128]{3,2,1,0:T(8,128)(2,1)}, u32[]{:S(2)}) copy-start(bf16[2,3,64,128]{3,2,1,0:T(8,128)(2,1)} %copy-done.3) | copy-start | bytes 294916
  28.2 10.5 %copy-start.5 = (s32[128,32]{0,1:T(8,128)S(1)}, s32[128,32]{0,1:T(8,128)}, u32[]{:S(2)}) copy-start(s32[128,32]{0,1:T(8,128)} %param.11) | copy-start | bytes 49156

commit v15 on v14

--- a/solution.py
+++ b/solution.py
@@ -30,7 +30,7 @@
 TILES = tuple(6 * rows for rows in ROWS)
 
 
-def pick_kernel(right_ref, wave_ref, out_ref, wave_out, rows_ref, sem, wave_sem):
+def pick_kernel(right_ref, wave_ref, result, wave_out, rows_ref, out_ref, sem, out_sem, wave_sem):
     core, z_lo, _, q = where()
     waves = [
         pltpu.make_async_copy(wave_ref.at[:, (q + o) & 31], wave_out.at[:, o], wave_sem.at[o])
@@ -39,19 +39,20 @@
     for copy in waves:
         copy.start()
     copies = []
-    for part in range(4):
+    for part in range(8):
         for second in range(2):
             copy = pltpu.make_async_copy(
-                right_ref.at[pl.ds(part * 4, 4), core, :, :, z_lo ^ (2 * second)],
-                rows_ref.at[second, pl.ds(part * 4, 4)],
+                right_ref.at[pl.ds(part * 2, 2), core, :, :, z_lo ^ (2 * second)],
+                rows_ref.at[second, pl.ds(part * 2, 2)],
                 sem.at[part, second],
             )
             copy.start()
             copies.append(copy)
-    for part in range(4):
+    leaving = []
+    for part in range(8):
         for second in range(2):
             copies[part * 2 + second].wait()
-        for target in range(part * 4, part * 4 + 4):
+        for target in range(part * 2, part * 2 + 2):
             for second in range(2):
                 rows = jnp.concatenate(
                     [
@@ -68,23 +69,29 @@
                     out_ref[target, 16 : 16 + CROSS] = rows[SPLIT:16]
                 else:
                     out_ref[target, 0:16] = rows
-    for copy in waves:
+        copy = pltpu.make_async_copy(
+            out_ref.at[pl.ds(part * 2, 2)], result.at[pl.ds(part * 2, 2)], out_sem.at[part]
+        )
+        copy.start()
+        leaving.append(copy)
+    for copy in waves + leaving:
         copy.wait()
 
 
 def pick(right_operators, wave_blocks):
-    whole = pl.BlockSpec(memory_space=pltpu.VMEM)
     return pl.pallas_call(
         pick_kernel,
         in_specs=[pl.BlockSpec(memory_space=pltpu.HBM)] * 2,
-        out_specs=[whole] * 2,
+        out_specs=[pl.BlockSpec(memory_space=pl.ANY)] * 2,
         out_shape=[
             jax.ShapeDtypeStruct((16, 16 + CROSS, 16, 128), BF),
             jax.ShapeDtypeStruct((2, 3, 64, 128), BF),
         ],
         scratch_shapes=[
             pltpu.VMEM((2, 16, 8, 2, 16, 128), BF),
-            pltpu.SemaphoreType.DMA((4, 2)),
+            pltpu.VMEM((16, 16 + CROSS, 16, 128), BF),
+            pltpu.SemaphoreType.DMA((8, 2)),
+            pltpu.SemaphoreType.DMA((8,)),
             pltpu.SemaphoreType.DMA((3,)),
         ],
         compiler_params=params(54),
@@ -249,8 +256,10 @@
 
 
 def contract_kernel(
-    home, ahead1, back1, ahead2, right, right_table, picks, out, paired_ref
+    home, ahead1, back1_ref, ahead2, right, right_table, picks, out, paired_ref, back1, sem
 ):
+    arriving = pltpu.make_async_copy(back1_ref, back1, sem.at[0])
+    arriving.start()
     arrays = (home, ahead1, back1, ahead2)
     zero = jnp.zeros((96, 128), BF)
 
@@ -274,8 +283,9 @@
             )
         return total
 
+    cross = product(16, 16 + CROSS)
+    arriving.wait()
     paired = product(0, 16)
-    cross = product(16, 16 + CROSS)
     for third in range(3):
         lanes = slice(third * 128, third * 128 + 128)
         paired_ref[third] = paired[:, lanes] + cross if third == 0 else paired[:, lanes]
@@ -319,10 +329,14 @@
     whole = pl.BlockSpec(memory_space=pltpu.VMEM)
     return pl.pallas_call(
         contract_kernel,
-        in_specs=[whole] * 7,
+        in_specs=[whole] * 2 + [pl.BlockSpec(memory_space=pl.ANY)] + [whole] * 4,
         out_specs=whole,
         out_shape=jax.ShapeDtypeStruct((8, 64, 128), BF),
-        scratch_shapes=[pltpu.VMEM((3, 256, 128), F32)],
+        scratch_shapes=[
+            pltpu.VMEM((3, 256, 128), F32),
+            pltpu.VMEM((TILES[2] + 1, 16, 128), BF),
+            pltpu.SemaphoreType.DMA((1,)),
+        ],
         compiler_params=params(16),
         name="contract",
     )(*tiles, right, right_table, picks)

time: 65.4 us -> 66.7 us (1.020)
  Pallas kernels: 11.2 us -> 12.5 us
    pallas_call x1, Pallas kernels: 3.02 us -> 4.33 us  [pick(): pl.pallas_call(pick_kernel, in_specs=[pl.BlockSpec(memory_space=pltpu.HBM...]
  transfers between devices with their start and end apart: 7 -> 7, of which waited for: 1 -> 1; matrix products, arithmetic and copies ran while one was open for 3% -> 3% of each run, Pallas kernels for 13% -> 15%
where the time goes in v15:
time: 66.7 us; the launch traced here: 66.3 us
  blocking collectives  22.8 us (34%)
  starting transfers between devices  17.5 us (26%)
  Pallas kernels  12.5 us (19%)
  waiting for transfers between devices  8.25 us (12%)
  local copies, waits for them, and re-layouts  4.48 us (7%)
    all_to_all x1, blocking collectives, local(): lax.all_to_all(shares.reshape(256, 2, 128), ('row', 'wf', 'col'), 0, 0, t...  22.8 us
    all_to_all x1, waiting for transfers between devices, local(): right = lax.all_to_all(right, 'col', 0, 0, tiled=True)  8.23 us
    all_to_all x1, starting transfers between devices, local(): right = lax.all_to_all(right, 'col', 0, 0, tiled=True)  6.89 us
    pallas_call x2, Pallas kernels, make_tiles(): pl.pallas_call(functools.partial(tiles_kernel, sent), in_specs=[whole] *...  5.38 us
    ppermute x1, starting transfers between devices, local(): lax.ppermute(own_wave, line, ring(lambda z, core: (z + 2) % 8 if z in (2,...  4.37 us
    pallas_call x1, Pallas kernels, pick(): pl.pallas_call(pick_kernel, in_specs=[pl.BlockSpec(memory_space=pltpu.HBM...  4.33 us
    ppermute x1, starting transfers between devices, local(): far_left = lax.ppermute(left_operators, 'row', swap)  3.24 us
    pallas_call x1, Pallas kernels, contract(): pl.pallas_call(contract_kernel, in_specs=[whole] * 2 + [pl.BlockSpec(memo...  2.6 us
  transfers between devices with their start and end apart: 7, of which 1 were waited for; matrix products, arithmetic and copies ran while one was open for 3% of the time, Pallas kernels for 15%

profile of v15, /device:TPU:1, one launch (start us, length us, event | category | flops | bytes accessed | tf_op | source)
XLA Modules:
  0.0 66.3 jit_solution(18332765817754926002)
XLA Ops:
  0.0 3.2 %collective-permute-start.2 = (bf16[12,2,2,128,128]{4,3,2,1,0:T(8,128)(2,1)}, bf16[12,2,2,128,128]{4,3,2,1,0:T(8,128)(2,1)}, u32[]{:S(2)}, u32[]{:S(2)}) collective-permute-start(bf16[12,2,2,128,128]{4,3,2,1,0:T(8,128)(2,1)} %own_left.3), channel_id=1, source_target_pairs={{0,32},{32,0},{64,96},{96,64},{128,160},{160,128},{192,224},{224,1... | collective-permute-start | bytes 4718600 | tf_op jit(solution)/shard_map/ppermute | solution.py:364
  3.2 0.0 collective-permute-start
  3.2 4.3 %pick.1 = (bf16[16,25,16,128]{3,2,1,0:T(8,128)(2,1)}, bf16[2,3,64,128]{3,2,1,0:T(8,128)(2,1)}) custom-call(bf16[16,2,8,2,4,16,128]{6,5,4,3,2,1,0:T(8,128)(2,1)} %bitcast.21, bf16[2,32,64,128]{3,2,1,0:T(8,128)(2,1)} %wave_ref.1), custom_call_target="tpu_custom_call" | custom-call | tf_op jit(solution)/shard_map/pick/pallas_call | solution.py:82
  7.6 4.4 %collective-permute-start.1 = (bf16[2,3,64,128]{3,2,1,0:T(8,128)(2,1)}, bf16[2,3,64,128]{3,2,1,0:T(8,128)(2,1)S(1)}, u32[]{:S(2)}, u32[]{:S(2)}) collective-permute-start(bf16[2,3,64,128]{3,2,1,0:T(8,128)(2,1)} %get-tuple-element.14.own_wave), channel_id=1, source_target_pairs={{0,129},{32,161},{64,193},{96,225},{128,1},{160,33},{192,65},{224,... | collective-permute-start | bytes 294920 | tf_op jit(solution)/shard_map/ppermute | solution.py:360
  12.0 0.0 copy-start
  12.0 0.0 copy-start.2
  12.0 0.0 copy-start.6
  12.0 6.9 %all-to-all-start = ((bf16[16,25,16,128]{3,2,1,0:T(8,128)(2,1)}), bf16[16,25,16,128]{3,2,1,0:T(8,128)(2,1)S(1)}, u32[]{:S(2)}, u32[]{:S(2)}) async-start(bf16[16,25,16,128]{3,2,1,0:T(8,128)(2,1)} %get-tuple-element.20), calls=%async_computation | async-start | bytes 3276800 | tf_op jit(solution)/shard_map/all_to_all | solution.py:366
  18.9 0.1 broadcast_in_dim.2
  19.0 0.1 reshape.140.sign
  19.1 0.0 copy-start.7
  19.1 0.0 collective-permute-done.far_table
  19.1 0.0 collective-permute-done.1.far_wave
  19.1 0.0 copy-start.3
  19.1 0.0 collective-permute-done.2.far_left
  19.1 0.0 copy-done
  19.2 0.0 copy-done.2
  19.2 0.0 copy-done.6
  19.2 3.1 %make_tiles.1 = (bf16[97,16,128]{2,1,0:T(8,128)(2,1)}, bf16[97,16,128]{2,1,0:T(8,128)(2,1)}, bf16[43,16,128]{2,1,0:T(8,128)(2,1)}) custom-call(s32[12,32]{1,0:T(8,128)S(1)} %copy-done.6, s32[12,32]{1,0:T(8,128)S(1)} %collective-permute-done.far_table, bf16[2,3,64,128]{3,2,1,0:T(8,128)(2,1)S(1)} %copy-done.2, ...), custom_call_target="tpu_custom_call" | custom-call | flops 1000000000 | bytes 4000000 | tf_op jit(solution)/shard_map/make_tiles/pallas_call | solution.py:222
  22.3 0.0 copy-done.3
  22.3 0.1 collective-permute-start.3
  22.4 1.5 %collective-permute-start.4 = (bf16[97,16,128]{2,1,0:T(8,128)(2,1)}, bf16[97,16,128]{2,1,0:T(8,128)(2,1)}, u32[]{:S(2)}, u32[]{:S(2)}) collective-permute-start(bf16[97,16,128]{2,1,0:T(8,128)(2,1)} %get-tuple-element.18), channel_id=1, source_target_pairs={{0,193},{32,96},{64,0},{96,160},{128,64},{160,224},{192,128},{224,... | collective-permute-start | bytes 1191944 | tf_op jit(solution)/shard_map/ppermute | solution.py:376
  23.8 1.5 %collective-permute-start.5 = (bf16[43,16,128]{2,1,0:T(8,128)(2,1)}, bf16[43,16,128]{2,1,0:T(8,128)(2,1)S(1)}, u32[]{:S(2)}, u32[]{:S(2)}) collective-permute-start(bf16[43,16,128]{2,1,0:T(8,128)(2,1)} %get-tuple-element.19), channel_id=1, source_target_pairs={{0,128},{32,161},{64,192},{96,225},{128,1},{160,32},{192,65},{224,... | collective-permute-start | bytes 528392 | tf_op jit(solution)/shard_map/ppermute | solution.py:377
  25.3 0.0 copy-done.7
  25.3 0.1 reshape.139
  25.5 0.1 mul.40
  25.6 0.7 %stack.16 = s32[1,1,8,12]{3,2,1,0:T(8,128)S(1)} reshape(s32[96]{0:T(128)} %param.13) | data formatting | bytes 768 | tf_op jit(solution)/shard_map/stack | solution.py:391
  26.4 0.1 fusion.2
  26.5 0.1 iota_add_fusion
  26.5 0.1 fusion.1
  26.6 0.1 add.106.slot_key
  26.7 0.1 add.102.real_key
  26.9 0.1 sub.29.imag_key
  27.0 0.2 make_picks.1.picks
  27.1 0.0 copy-start.1
  27.2 1.4 %copy-done.1 = bf16[12,2,2,128,128]{4,3,2,1,0:T(8,128)(2,1)S(1)} copy-done((bf16[12,2,2,128,128]{4,3,2,1,0:T(8,128)(2,1)S(1)}, bf16[12,2,2,128,128]{4,3,2,1,0:T(8,128)(2,1)}, u32[]{:S(2)}) %copy-start.1) | copy-done | bytes 1572888
  28.6 0.9 %copy-done.4 = bf16[2,3,64,128]{3,2,1,0:T(8,128)(2,1)S(1)} copy-done((bf16[2,3,64,128]{3,2,1,0:T(8,128)(2,1)S(1)}, bf16[2,3,64,128]{3,2,1,0:T(8,128)(2,1)}, u32[]{:S(2)}) %copy-start.4) | copy-done | bytes 98328
  29.5 2.3 %make_home.1.home = bf16[151,16,128]{2,1,0:T(8,128)(2,1)S(1)} custom-call(s32[12,32]{1,0:T(8,128)S(1)} %copy-done.6, s32[12,32]{1,0:T(8,128)S(1)} %collective-permute-done.far_table, bf16[2,3,64,128]{3,2,1,0:T(8,128)(2,1)S(1)} %copy-done.2, bf16[2,3,64,128]{3,2,1,0:T(8,128)(2,1)S(1)} %copy-done.4, bf16[12,2,2,128,128]{4,3,2,1,0:T(8,128)(2,1)S(1)} %copy-done.1, ...), custom_call_target="tpu_custom_call" | custom-call | flops 1000000000 | bytes 4000000 | tf_op jit(solution)/shard_map/make_home/pallas_call | solution.py:222
  31.8 8.2 %all-to-all-done.right = bf16[16,25,16,128]{3,2,1,0:T(8,128)(2,1)S(1)} async-done(((bf16[16,25,16,128]{3,2,1,0:T(8,128)(2,1)}), bf16[16,25,16,128]{3,2,1,0:T(8,128)(2,1)S(1)}, u32[]{:S(2)}, u32[]{:S(2)}) %all-to-all-start) | async-done | bytes 1638432 | tf_op jit(solution)/shard_map/all_to_all | solution.py:366
  40.0 0.0 collective-permute-done.5.ahead2
  40.0 0.0 collective-permute-done.3.ahead1
  40.0 0.0 collective-permute-done.4.back1_ref
  40.0 0.0 copy-done.5
  40.0 2.6 %contract.1 = bf16[8,64,128]{2,1,0:T(8,128)(2,1)S(1)} custom-call(bf16[151,16,128]{2,1,0:T(8,128)(2,1)S(1)} %make_home.1.home, bf16[97,16,128]{2,1,0:T(8,128)(2,1)S(1)} %collective-permute-done.3.ahead1, bf16[97,16,128]{2,1,0:T(8,128)(2,1)} %collective-permute-done.4.back1_ref, bf16[43,16,128]{2,1,0:T(8,128)(2,1)S(1)} %collective-permute-done.5.ahead2, ...), custom_call_target="tpu_custom_call" | custom-call | tf_op jit(solution)/shard_map/contract/pallas_call | solution.py:330
  42.6 22.8 %all_to_all.10 = bf16[256,2,128]{2,1,0:T(2,128)(2,1)S(1)} all-to-all(bf16[256,2,128]{2,1,0:T(2,128)(2,1)S(1)} %bitcast.19), channel_id=1, replica_groups=mesh['row'=8,'col'=16,'wf'=2] {'row','wf','col'}, dimensions={0} | all-to-all | bytes 262144 | tf_op jit(solution)/shard_map/all_to_all | solution.py:401
  65.4 0.3 convert_reduce_fusion
  65.7 0.1 reshape.142
  65.7 0.6 copy.13
  (15 shorter events, 0.1 us)
Async XLA Ops:
  0.0 19.1 %collective-permute-start.2 = (bf16[12,2,2,128,128]{4,3,2,1,0:T(8,128)(2,1)}, bf16[12,2,2,128,128]{4,3,2,1,0:T(8,128)(2,1)}, u32[]{:S(2)}, u32[]{:S(2)}) collective-permute-start(bf16[12,2,2,128,128]{4,3,2,1,0:T(8,128)(2,1)} %own_left.3), channel_id=1, source_target_pairs={{0,32},{32,0},{64,96},{96,64},{128,160},{160,128},{192,224},{224,1... | collective-permute-start | bytes 4718600 | tf_op jit(solution)/shard_map/ppermute | solution.py:364
  3.2 15.9 %collective-permute-start = (s32[12,32]{1,0:T(8,128)}, s32[12,32]{1,0:T(8,128)S(1)}, u32[]{:S(2)}, u32[]{:S(2)}) collective-permute-start(s32[12,32]{1,0:T(8,128)} %own_table.3), channel_id=1, source_target_pairs={{0,32},{32,0},{64,96},{96,64},{128,160},{160,128},{192,224},{224,1... | collective-permute-start | bytes 4616 | tf_op jit(solution)/shard_map/ppermute | solution.py:365
  7.6 11.5 %collective-permute-start.1 = (bf16[2,3,64,128]{3,2,1,0:T(8,128)(2,1)}, bf16[2,3,64,128]{3,2,1,0:T(8,128)(2,1)S(1)}, u32[]{:S(2)}, u32[]{:S(2)}) collective-permute-start(bf16[2,3,64,128]{3,2,1,0:T(8,128)(2,1)} %get-tuple-element.14.own_wave), channel_id=1, source_target_pairs={{0,129},{32,161},{64,193},{96,225},{128,1},{160,33},{192,65},{224,... | collective-permute-start | bytes 294920 | tf_op jit(solution)/shard_map/ppermute | solution.py:360
  12.0 7.2 %copy-start = (bf16[12,2,2,128,128]{4,3,2,1,0:T(8,128)(2,1)S(1)}, bf16[12,2,2,128,128]{4,3,2,1,0:T(8,128)(2,1)}, u32[]{:S(2)}) copy-start(bf16[12,2,2,128,128]{4,3,2,1,0:T(8,128)(2,1)} %own_left.3) | copy-start | bytes 4718596
  12.0 7.2 %copy-start.2 = (bf16[2,3,64,128]{3,2,1,0:T(8,128)(2,1)S(1)}, bf16[2,3,64,128]{3,2,1,0:T(8,128)(2,1)}, u32[]{:S(2)}) copy-start(bf16[2,3,64,128]{3,2,1,0:T(8,128)(2,1)} %get-tuple-element.14.own_wave) | copy-start | bytes 294916
  12.0 7.2 %copy-start.6 = (s32[12,32]{1,0:T(8,128)S(1)}, s32[12,32]{1,0:T(8,128)}, u32[]{:S(2)}) copy-start(s32[12,32]{1,0:T(8,128)} %own_table.3) | copy-start | bytes 4612
  12.0 28.0 %all-to-all-start = ((bf16[16,25,16,128]{3,2,1,0:T(8,128)(2,1)}), bf16[16,25,16,128]{3,2,1,0:T(8,128)(2,1)S(1)}, u32[]{:S(2)}, u32[]{:S(2)}) async-start(bf16[16,25,16,128]{3,2,1,0:T(8,128)(2,1)} %get-tuple-element.20), calls=%async_computation | async-start | bytes 3276800 | tf_op jit(solution)/shard_map/all_to_all | solution.py:366
  19.1 6.3 %copy-start.7 = (s32[96]{0:T(128)S(1)}, s32[96]{0:T(128)}, u32[]{:S(2)}) copy-start(s32[96]{0:T(128)} %param.12) | copy-start | bytes 1156
  19.1 3.2 %copy-start.3 = (bf16[2,3,64,128]{3,2,1,0:T(8,128)(2,1)}, bf16[2,3,64,128]{3,2,1,0:T(8,128)(2,1)S(1)}, u32[]{:S(2)}) copy-start(bf16[2,3,64,128]{3,2,1,0:T(8,128)(2,1)S(1)} %collective-permute-done.1.far_wave) | copy-start | bytes 294916
  22.3 17.7 %collective-permute-start.3 = (bf16[97,16,128]{2,1,0:T(8,128)(2,1)}, bf16[97,16,128]{2,1,0:T(8,128)(2,1)S(1)}, u32[]{:S(2)}, u32[]{:S(2)}) collective-permute-start(bf16[97,16,128]{2,1,0:T(8,128)(2,1)} %get-tuple-element.17), channel_id=1, source_target_pairs={{0,64},{32,225},{64,128},{96,32},{128,192},{160,96},{192,1},{224,1... | collective-permute-start | bytes 1191944 | tf_op jit(solution)/shard_map/ppermute | solution.py:375
  22.4 17.6 %collective-permute-start.4 = (bf16[97,16,128]{2,1,0:T(8,128)(2,1)}, bf16[97,16,128]{2,1,0:T(8,128)(2,1)}, u32[]{:S(2)}, u32[]{:S(2)}) collective-permute-start(bf16[97,16,128]{2,1,0:T(8,128)(2,1)} %get-tuple-element.18), channel_id=1, source_target_pairs={{0,193},{32,96},{64,0},{96,160},{128,64},{160,224},{192,128},{224,... | collective-permute-start | bytes 1191944 | tf_op jit(solution)/shard_map/ppermute | solution.py:376
  23.8 16.2 %collective-permute-start.5 = (bf16[43,16,128]{2,1,0:T(8,128)(2,1)}, bf16[43,16,128]{2,1,0:T(8,128)(2,1)S(1)}, u32[]{:S(2)}, u32[]{:S(2)}) collective-permute-start(bf16[43,16,128]{2,1,0:T(8,128)(2,1)} %get-tuple-element.19), channel_id=1, source_target_pairs={{0,128},{32,161},{64,192},{96,225},{128,1},{160,32},{192,65},{224,... | collective-permute-start | bytes 528392 | tf_op jit(solution)/shard_map/ppermute | solution.py:377
  27.1 1.4 %copy-start.1 = (bf16[12,2,2,128,128]{4,3,2,1,0:T(8,128)(2,1)S(1)}, bf16[12,2,2,128,128]{4,3,2,1,0:T(8,128)(2,1)}, u32[]{:S(2)}) copy-start(bf16[12,2,2,128,128]{4,3,2,1,0:T(8,128)(2,1)} %own_left.3) | copy-start | bytes 4718596
  28.6 0.9 %copy-start.4 = (bf16[2,3,64,128]{3,2,1,0:T(8,128)(2,1)S(1)}, bf16[2,3,64,128]{3,2,1,0:T(8,128)(2,1)}, u32[]{:S(2)}) copy-start(bf16[2,3,64,128]{3,2,1,0:T(8,128)(2,1)} %copy-done.3) | copy-start | bytes 294916
  29.5 10.5 %copy-start.5 = (s32[128,32]{0,1:T(8,128)S(1)}, s32[128,32]{0,1:T(8,128)}, u32[]{:S(2)}) copy-start(s32[128,32]{0,1:T(8,128)} %param.11) | copy-start | bytes 49156

commit v16 on v14

--- a/solution.py
+++ b/solution.py
@@ -30,7 +30,7 @@
 TILES = tuple(6 * rows for rows in ROWS)
 
 
-def pick_kernel(right_ref, wave_ref, out_ref, wave_out, rows_ref, sem, wave_sem):
+def pick_kernel(right_ref, wave_ref, result, wave_out, rows_ref, out_ref, sem, out_sem, wave_sem):
     core, z_lo, _, q = where()
     waves = [
         pltpu.make_async_copy(wave_ref.at[:, (q + o) & 31], wave_out.at[:, o], wave_sem.at[o])
@@ -48,6 +48,7 @@
             )
             copy.start()
             copies.append(copy)
+    leaving = []
     for part in range(4):
         for second in range(2):
             copies[part * 2 + second].wait()
@@ -68,7 +69,12 @@
                     out_ref[target, 16 : 16 + CROSS] = rows[SPLIT:16]
                 else:
                     out_ref[target, 0:16] = rows
-    for copy in waves:
+        copy = pltpu.make_async_copy(
+            out_ref.at[pl.ds(part * 4, 4)], result.at[pl.ds(part * 4, 4)], out_sem.at[part]
+        )
+        copy.start()
+        leaving.append(copy)
+    for copy in waves + leaving:
         copy.wait()
 
 
@@ -77,14 +83,16 @@
     return pl.pallas_call(
         pick_kernel,
         in_specs=[pl.BlockSpec(memory_space=pltpu.HBM)] * 2,
-        out_specs=[whole] * 2,
+        out_specs=[pl.BlockSpec(memory_space=pl.ANY), whole],
         out_shape=[
             jax.ShapeDtypeStruct((16, 16 + CROSS, 16, 128), BF),
             jax.ShapeDtypeStruct((2, 3, 64, 128), BF),
         ],
         scratch_shapes=[
             pltpu.VMEM((2, 16, 8, 2, 16, 128), BF),
+            pltpu.VMEM((16, 16 + CROSS, 16, 128), BF),
             pltpu.SemaphoreType.DMA((4, 2)),
+            pltpu.SemaphoreType.DMA((4,)),
             pltpu.SemaphoreType.DMA((3,)),
         ],
         compiler_params=params(54),

time: 65.4 us -> 65.6 us (level)
  no operation moved by 1% of the time
where the time goes in v16:
time: 65.6 us; the launch traced here: 65.2 us
  blocking collectives  22.8 us (35%)
  starting transfers between devices  17.5 us (27%)
  Pallas kernels  11.4 us (17%)
  waiting for transfers between devices  8.25 us (13%)
  local copies, waits for them, and re-layouts  4.48 us (7%)
    all_to_all x1, blocking collectives, local(): lax.all_to_all(shares.reshape(256, 2, 128), ('row', 'wf', 'col'), 0, 0, t...  22.8 us
    all_to_all x1, waiting for transfers between devices, local(): right = lax.all_to_all(right, 'col', 0, 0, tiled=True)  8.24 us
    all_to_all x1, starting transfers between devices, local(): right = lax.all_to_all(right, 'col', 0, 0, tiled=True)  6.89 us
    pallas_call x2, Pallas kernels, make_tiles(): pl.pallas_call(functools.partial(tiles_kernel, sent), in_specs=[whole] *...  5.39 us
    ppermute x1, starting transfers between devices, local(): lax.ppermute(own_wave, line, ring(lambda z, core: (z + 2) % 8 if z in (2,...  4.37 us
    ppermute x1, starting transfers between devices, local(): far_left = lax.ppermute(left_operators, 'row', swap)  3.24 us
    pallas_call x1, Pallas kernels, pick(): pl.pallas_call(pick_kernel, in_specs=[pl.BlockSpec(memory_space=pltpu.HBM...  3.24 us
    pallas_call x1, Pallas kernels, contract(): pl.pallas_call(contract_kernel, in_specs=[whole] * 7, out_specs=whole, ou...  2.58 us
  transfers between devices with their start and end apart: 7, of which 1 were waited for; matrix products, arithmetic and copies ran while one was open for 3% of the time, Pallas kernels for 13%

profile of v16, /device:TPU:1, one launch (start us, length us, event | category | flops | bytes accessed | tf_op | source)
XLA Modules:
  0.0 65.2 jit_solution(1735610349445730515)
XLA Ops:
  0.0 3.2 %collective-permute-start.2 = (bf16[12,2,2,128,128]{4,3,2,1,0:T(8,128)(2,1)}, bf16[12,2,2,128,128]{4,3,2,1,0:T(8,128)(2,1)}, u32[]{:S(2)}, u32[]{:S(2)}) collective-permute-start(bf16[12,2,2,128,128]{4,3,2,1,0:T(8,128)(2,1)} %own_left.3), channel_id=1, source_target_pairs={{0,32},{32,0},{64,96},{96,64},{128,160},{160,128},{192,224},{224,1... | collective-permute-start | bytes 4718600 | tf_op jit(solution)/shard_map/ppermute | solution.py:358
  3.2 0.0 collective-permute-start
  3.2 3.2 %pick.1 = (bf16[16,25,16,128]{3,2,1,0:T(8,128)(2,1)}, bf16[2,3,64,128]{3,2,1,0:T(8,128)(2,1)}) custom-call(bf16[16,2,8,2,4,16,128]{6,5,4,3,2,1,0:T(8,128)(2,1)} %bitcast.21, bf16[2,32,64,128]{3,2,1,0:T(8,128)(2,1)} %wave_ref.1), custom_call_target="tpu_custom_call" | custom-call | tf_op jit(solution)/shard_map/pick/pallas_call | solution.py:83
  6.5 4.4 %collective-permute-start.1 = (bf16[2,3,64,128]{3,2,1,0:T(8,128)(2,1)}, bf16[2,3,64,128]{3,2,1,0:T(8,128)(2,1)S(1)}, u32[]{:S(2)}, u32[]{:S(2)}) collective-permute-start(bf16[2,3,64,128]{3,2,1,0:T(8,128)(2,1)} %get-tuple-element.14.own_wave), channel_id=1, source_target_pairs={{0,129},{32,161},{64,193},{96,225},{128,1},{160,33},{192,65},{224,... | collective-permute-start | bytes 294920 | tf_op jit(solution)/shard_map/ppermute | solution.py:354
  10.9 0.0 copy-start
  10.9 0.0 copy-start.2
  10.9 0.0 copy-start.6
  10.9 6.9 %all-to-all-start = ((bf16[16,25,16,128]{3,2,1,0:T(8,128)(2,1)}), bf16[16,25,16,128]{3,2,1,0:T(8,128)(2,1)S(1)}, u32[]{:S(2)}, u32[]{:S(2)}) async-start(bf16[16,25,16,128]{3,2,1,0:T(8,128)(2,1)} %get-tuple-element.20), calls=%async_computation | async-start | bytes 3276800 | tf_op jit(solution)/shard_map/all_to_all | solution.py:360
  17.8 0.1 broadcast_in_dim.2
  17.9 0.1 reshape.140.sign
  18.0 0.0 copy-start.7
  18.0 0.0 collective-permute-done.far_table
  18.0 0.0 collective-permute-done.1.far_wave
  18.0 0.0 copy-start.3
  18.0 0.0 collective-permute-done.2.far_left
  18.0 0.0 copy-done
  18.1 0.0 copy-done.2
  18.1 0.0 copy-done.6
  18.1 3.1 %make_tiles.1 = (bf16[97,16,128]{2,1,0:T(8,128)(2,1)}, bf16[97,16,128]{2,1,0:T(8,128)(2,1)}, bf16[43,16,128]{2,1,0:T(8,128)(2,1)}) custom-call(s32[12,32]{1,0:T(8,128)S(1)} %copy-done.6, s32[12,32]{1,0:T(8,128)S(1)} %collective-permute-done.far_table, bf16[2,3,64,128]{3,2,1,0:T(8,128)(2,1)S(1)} %copy-done.2, ...), custom_call_target="tpu_custom_call" | custom-call | flops 1000000000 | bytes 4000000 | tf_op jit(solution)/shard_map/make_tiles/pallas_call | solution.py:223
  21.2 0.0 copy-done.3
  21.2 0.1 collective-permute-start.3
  21.3 1.5 %collective-permute-start.4 = (bf16[97,16,128]{2,1,0:T(8,128)(2,1)}, bf16[97,16,128]{2,1,0:T(8,128)(2,1)}, u32[]{:S(2)}, u32[]{:S(2)}) collective-permute-start(bf16[97,16,128]{2,1,0:T(8,128)(2,1)} %get-tuple-element.18), channel_id=1, source_target_pairs={{0,193},{32,96},{64,0},{96,160},{128,64},{160,224},{192,128},{224,... | collective-permute-start | bytes 1191944 | tf_op jit(solution)/shard_map/ppermute | solution.py:370
  22.7 1.5 %collective-permute-start.5 = (bf16[43,16,128]{2,1,0:T(8,128)(2,1)}, bf16[43,16,128]{2,1,0:T(8,128)(2,1)S(1)}, u32[]{:S(2)}, u32[]{:S(2)}) collective-permute-start(bf16[43,16,128]{2,1,0:T(8,128)(2,1)} %get-tuple-element.19), channel_id=1, source_target_pairs={{0,128},{32,161},{64,192},{96,225},{128,1},{160,32},{192,65},{224,... | collective-permute-start | bytes 528392 | tf_op jit(solution)/shard_map/ppermute | solution.py:371
  24.2 0.0 copy-done.7
  24.2 0.1 reshape.139
  24.4 0.1 mul.40
  24.5 0.7 %stack.16 = s32[1,1,8,12]{3,2,1,0:T(8,128)S(1)} reshape(s32[96]{0:T(128)} %param.13) | data formatting | bytes 768 | tf_op jit(solution)/shard_map/stack | solution.py:385
  25.3 0.1 fusion.2
  25.4 0.1 iota_add_fusion
  25.4 0.1 fusion.1
  25.5 0.1 add.106.slot_key
  25.6 0.1 add.102.real_key
  25.8 0.1 sub.29.imag_key
  25.9 0.2 make_picks.1.picks
  26.1 0.0 copy-start.1
  26.1 1.4 %copy-done.1 = bf16[12,2,2,128,128]{4,3,2,1,0:T(8,128)(2,1)S(1)} copy-done((bf16[12,2,2,128,128]{4,3,2,1,0:T(8,128)(2,1)S(1)}, bf16[12,2,2,128,128]{4,3,2,1,0:T(8,128)(2,1)}, u32[]{:S(2)}) %copy-start.1) | copy-done | bytes 1572888
  27.5 0.9 %copy-done.4 = bf16[2,3,64,128]{3,2,1,0:T(8,128)(2,1)S(1)} copy-done((bf16[2,3,64,128]{3,2,1,0:T(8,128)(2,1)S(1)}, bf16[2,3,64,128]{3,2,1,0:T(8,128)(2,1)}, u32[]{:S(2)}) %copy-start.4) | copy-done | bytes 98328
  28.4 2.3 %make_home.1.home = bf16[151,16,128]{2,1,0:T(8,128)(2,1)S(1)} custom-call(s32[12,32]{1,0:T(8,128)S(1)} %copy-done.6, s32[12,32]{1,0:T(8,128)S(1)} %collective-permute-done.far_table, bf16[2,3,64,128]{3,2,1,0:T(8,128)(2,1)S(1)} %copy-done.2, bf16[2,3,64,128]{3,2,1,0:T(8,128)(2,1)S(1)} %copy-done.4, bf16[12,2,2,128,128]{4,3,2,1,0:T(8,128)(2,1)S(1)} %copy-done.1, ...), custom_call_target="tpu_custom_call" | custom-call | flops 1000000000 | bytes 4000000 | tf_op jit(solution)/shard_map/make_home/pallas_call | solution.py:223
  30.7 8.2 %all-to-all-done.right = bf16[16,25,16,128]{3,2,1,0:T(8,128)(2,1)S(1)} async-done(((bf16[16,25,16,128]{3,2,1,0:T(8,128)(2,1)}), bf16[16,25,16,128]{3,2,1,0:T(8,128)(2,1)S(1)}, u32[]{:S(2)}, u32[]{:S(2)}) %all-to-all-start) | async-done | bytes 1638432 | tf_op jit(solution)/shard_map/all_to_all | solution.py:360
  38.9 0.0 collective-permute-done.5.ahead2
  38.9 0.0 collective-permute-done.3.ahead1
  38.9 0.0 collective-permute-done.4.back1
  38.9 0.0 copy-done.5
  38.9 2.6 %contract.1 = bf16[8,64,128]{2,1,0:T(8,128)(2,1)S(1)} custom-call(bf16[151,16,128]{2,1,0:T(8,128)(2,1)S(1)} %make_home.1.home, bf16[97,16,128]{2,1,0:T(8,128)(2,1)S(1)} %collective-permute-done.3.ahead1, bf16[97,16,128]{2,1,0:T(8,128)(2,1)} %collective-permute-done.4.back1, bf16[43,16,128]{2,1,0:T(8,128)(2,1)S(1)} %collective-permute-done.5.ahead2, ...), custom_call_target="tpu_custom_call" | custom-call | tf_op jit(solution)/shard_map/contract/pallas_call | solution.py:328
  41.5 22.8 %all_to_all.10 = bf16[256,2,128]{2,1,0:T(2,128)(2,1)S(1)} all-to-all(bf16[256,2,128]{2,1,0:T(2,128)(2,1)S(1)} %bitcast.19), channel_id=1, replica_groups=mesh['row'=8,'col'=16,'wf'=2] {'row','wf','col'}, dimensions={0} | all-to-all | bytes 262144 | tf_op jit(solution)/shard_map/all_to_all | solution.py:395
  64.3 0.3 convert_reduce_fusion
  64.5 0.1 reshape.142
  64.6 0.6 copy.13
  (15 shorter events, 0.1 us)
Async XLA Ops:
  0.0 18.0 %collective-permute-start.2 = (bf16[12,2,2,128,128]{4,3,2,1,0:T(8,128)(2,1)}, bf16[12,2,2,128,128]{4,3,2,1,0:T(8,128)(2,1)}, u32[]{:S(2)}, u32[]{:S(2)}) collective-permute-start(bf16[12,2,2,128,128]{4,3,2,1,0:T(8,128)(2,1)} %own_left.3), channel_id=1, source_target_pairs={{0,32},{32,0},{64,96},{96,64},{128,160},{160,128},{192,224},{224,1... | collective-permute-start | bytes 4718600 | tf_op jit(solution)/shard_map/ppermute | solution.py:358
  3.2 14.8 %collective-permute-start = (s32[12,32]{1,0:T(8,128)}, s32[12,32]{1,0:T(8,128)S(1)}, u32[]{:S(2)}, u32[]{:S(2)}) collective-permute-start(s32[12,32]{1,0:T(8,128)} %own_table.3), channel_id=1, source_target_pairs={{0,32},{32,0},{64,96},{96,64},{128,160},{160,128},{192,224},{224,1... | collective-permute-start | bytes 4616 | tf_op jit(solution)/shard_map/ppermute | solution.py:359
  6.5 11.5 %collective-permute-start.1 = (bf16[2,3,64,128]{3,2,1,0:T(8,128)(2,1)}, bf16[2,3,64,128]{3,2,1,0:T(8,128)(2,1)S(1)}, u32[]{:S(2)}, u32[]{:S(2)}) collective-permute-start(bf16[2,3,64,128]{3,2,1,0:T(8,128)(2,1)} %get-tuple-element.14.own_wave), channel_id=1, source_target_pairs={{0,129},{32,161},{64,193},{96,225},{128,1},{160,33},{192,65},{224,... | collective-permute-start | bytes 294920 | tf_op jit(solution)/shard_map/ppermute | solution.py:354
  10.9 7.2 %copy-start = (bf16[12,2,2,128,128]{4,3,2,1,0:T(8,128)(2,1)S(1)}, bf16[12,2,2,128,128]{4,3,2,1,0:T(8,128)(2,1)}, u32[]{:S(2)}) copy-start(bf16[12,2,2,128,128]{4,3,2,1,0:T(8,128)(2,1)} %own_left.3) | copy-start | bytes 4718596
  10.9 7.2 %copy-start.2 = (bf16[2,3,64,128]{3,2,1,0:T(8,128)(2,1)S(1)}, bf16[2,3,64,128]{3,2,1,0:T(8,128)(2,1)}, u32[]{:S(2)}) copy-start(bf16[2,3,64,128]{3,2,1,0:T(8,128)(2,1)} %get-tuple-element.14.own_wave) | copy-start | bytes 294916
  10.9 7.2 %copy-start.6 = (s32[12,32]{1,0:T(8,128)S(1)}, s32[12,32]{1,0:T(8,128)}, u32[]{:S(2)}) copy-start(s32[12,32]{1,0:T(8,128)} %own_table.3) | copy-start | bytes 4612
  10.9 28.0 %all-to-all-start = ((bf16[16,25,16,128]{3,2,1,0:T(8,128)(2,1)}), bf16[16,25,16,128]{3,2,1,0:T(8,128)(2,1)S(1)}, u32[]{:S(2)}, u32[]{:S(2)}) async-start(bf16[16,25,16,128]{3,2,1,0:T(8,128)(2,1)} %get-tuple-element.20), calls=%async_computation | async-start | bytes 3276800 | tf_op jit(solution)/shard_map/all_to_all | solution.py:360
  18.0 6.3 %copy-start.7 = (s32[96]{0:T(128)S(1)}, s32[96]{0:T(128)}, u32[]{:S(2)}) copy-start(s32[96]{0:T(128)} %param.12) | copy-start | bytes 1156
  18.0 3.2 %copy-start.3 = (bf16[2,3,64,128]{3,2,1,0:T(8,128)(2,1)}, bf16[2,3,64,128]{3,2,1,0:T(8,128)(2,1)S(1)}, u32[]{:S(2)}) copy-start(bf16[2,3,64,128]{3,2,1,0:T(8,128)(2,1)S(1)} %collective-permute-done.1.far_wave) | copy-start | bytes 294916
  21.2 17.7 %collective-permute-start.3 = (bf16[97,16,128]{2,1,0:T(8,128)(2,1)}, bf16[97,16,128]{2,1,0:T(8,128)(2,1)S(1)}, u32[]{:S(2)}, u32[]{:S(2)}) collective-permute-start(bf16[97,16,128]{2,1,0:T(8,128)(2,1)} %get-tuple-element.17), channel_id=1, source_target_pairs={{0,64},{32,225},{64,128},{96,32},{128,192},{160,96},{192,1},{224,1... | collective-permute-start | bytes 1191944 | tf_op jit(solution)/shard_map/ppermute | solution.py:369
  21.3 17.6 %collective-permute-start.4 = (bf16[97,16,128]{2,1,0:T(8,128)(2,1)}, bf16[97,16,128]{2,1,0:T(8,128)(2,1)}, u32[]{:S(2)}, u32[]{:S(2)}) collective-permute-start(bf16[97,16,128]{2,1,0:T(8,128)(2,1)} %get-tuple-element.18), channel_id=1, source_target_pairs={{0,193},{32,96},{64,0},{96,160},{128,64},{160,224},{192,128},{224,... | collective-permute-start | bytes 1191944 | tf_op jit(solution)/shard_map/ppermute | solution.py:370
  22.7 16.2 %collective-permute-start.5 = (bf16[43,16,128]{2,1,0:T(8,128)(2,1)}, bf16[43,16,128]{2,1,0:T(8,128)(2,1)S(1)}, u32[]{:S(2)}, u32[]{:S(2)}) collective-permute-start(bf16[43,16,128]{2,1,0:T(8,128)(2,1)} %get-tuple-element.19), channel_id=1, source_target_pairs={{0,128},{32,161},{64,192},{96,225},{128,1},{160,32},{192,65},{224,... | collective-permute-start | bytes 528392 | tf_op jit(solution)/shard_map/ppermute | solution.py:371
  26.1 1.4 %copy-start.1 = (bf16[12,2,2,128,128]{4,3,2,1,0:T(8,128)(2,1)S(1)}, bf16[12,2,2,128,128]{4,3,2,1,0:T(8,128)(2,1)}, u32[]{:S(2)}) copy-start(bf16[12,2,2,128,128]{4,3,2,1,0:T(8,128)(2,1)} %own_left.3) | copy-start | bytes 4718596
  27.5 0.9 %copy-start.4 = (bf16[2,3,64,128]{3,2,1,0:T(8,128)(2,1)S(1)}, bf16[2,3,64,128]{3,2,1,0:T(8,128)(2,1)}, u32[]{:S(2)}) copy-start(bf16[2,3,64,128]{3,2,1,0:T(8,128)(2,1)} %copy-done.3) | copy-start | bytes 294916
  28.4 10.6 %copy-start.5 = (s32[128,32]{0,1:T(8,128)S(1)}, s32[128,32]{0,1:T(8,128)}, u32[]{:S(2)}) copy-start(s32[128,32]{0,1:T(8,128)} %param.11) | copy-start | bytes 49156

commit v17 on v14

--- a/solution.py
+++ b/solution.py
@@ -234,9 +234,10 @@
     )(own_table, far_table, own_wave, far_wave, left_operators, far_left)
 
 
-def picks_kernel(slot_key, real_key, imag_key, sign, out):
+def picks_kernel(slot_key, real_key, imag_key, out):
     out[0:384] = (slot_key[...] == real_key[...]).astype(F32).astype(BF)
-    out[384:768] = jnp.where(slot_key[...] == imag_key[...], sign[...], 0.0).astype(BF)
+    sign = jnp.where(iota((384, 384), 1) % 48 < 24, -1.0, 1.0)
+    out[384:768] = jnp.where(slot_key[...] == imag_key[...], sign, 0.0).astype(BF)
 
 
 def make_picks(keys):
@@ -347,8 +348,9 @@
         own_wave, line, ring(lambda z, core: (z + 2) % 8 if z in (2, 3, 6, 7) else (z - 2) % 8)
     )
     swap = [(i, i ^ 1) for i in range(8)]
-    far_left = lax.ppermute(left_operators, "row", swap)
-    far_table = lax.ppermute(left_table, "row", swap)
+    given, given_table, _ = lax.optimization_barrier((left_operators, left_table, own_wave))
+    far_left = lax.ppermute(given, "row", swap)
+    far_table = lax.ppermute(given_table, "row", swap)
     right = lax.all_to_all(right, "col", 0, 0, tiled=True)
     ahead1, back1, ahead2 = make_tiles(
         True, left_table, far_table, own_wave, far_wave, left_operators, far_left
@@ -380,9 +382,8 @@
     part = jnp.arange(2, dtype=jnp.int32)[None, :, None, None]
     real_key = (target * 4 + kind * 2 + part).reshape(1, 384)
     imag_key = (target * 4 + kind * 2 + 1 - part).reshape(1, 384)
-    sign = jnp.broadcast_to((2 * part - 1).astype(F32), (8, 2, 2, 12)).reshape(1, 384)
-
-    picks = make_picks([slot_key, real_key, imag_key, sign])
+
+    picks = make_picks([slot_key, real_key, imag_key])
     shares = contract(tiles, right, right_table.T, picks)
     shares = lax.all_to_all(
         shares.reshape(256, 2, 128), ("row", "wf", "col"), 0, 0, tiled=True

time: 65.4 us -> 66.4 us (1.015)
  waiting for transfers between devices: 8.24 us -> 12.3 us
  blocking collectives: 22.8 us -> 20.2 us
  local copies, waits for them, and re-layouts: 4.48 us -> 3.64 us
    all_to_all x1, waiting for transfers between devices: 8.22 us -> 12.3 us  [local(): right = lax.all_to_all(right, 'col', 0, 0, tiled=True)]
    all_to_all x1, blocking collectives: 22.8 us -> 20.2 us  [local(): lax.all_to_all(shares.reshape(256, 2, 128), ('row', 'wf', 'col'), 0, 0, t...]
    unnamed x16 -> x18, local copies, waits for them, and re-layouts: 2.32 us -> 2.33 us
  transfers between devices with their start and end apart: 7 -> 7, of which waited for: 1 -> 1; matrix products, arithmetic and copies ran while one was open for 3% -> 1% of each run, Pallas kernels for 13% -> 8%
where the time goes in v17:
time: 66.4 us; the launch traced here: 66 us
  blocking collectives  20.2 us (30%)
  starting transfers between devices  17.8 us (27%)
  waiting for transfers between devices  12.3 us (19%)
  Pallas kernels  11.3 us (17%)
  local copies, waits for them, and re-layouts  3.64 us (5%)
    all_to_all x1, blocking collectives, local(): lax.all_to_all(shares.reshape(256, 2, 128), ('row', 'wf', 'col'), 0, 0, t...  20.2 us
    all_to_all x1, waiting for transfers between devices, local(): right = lax.all_to_all(right, 'col', 0, 0, tiled=True)  12.3 us
    all_to_all x1, starting transfers between devices, local(): right = lax.all_to_all(right, 'col', 0, 0, tiled=True)  6.89 us
    pallas_call x2, Pallas kernels, make_tiles(): pl.pallas_call(functools.partial(tiles_kernel, sent), in_specs=[whole] *...  5.37 us
    ppermute x1, starting transfers between devices, local(): lax.ppermute(own_wave, line, ring(lambda z, core: (z + 2) % 8 if z in (2,...  4.31 us
    ppermute x1, starting transfers between devices, local(): far_left = lax.ppermute(given, 'row', swap)  3.32 us
    pallas_call x1, Pallas kernels, pick(): pl.pallas_call(pick_kernel, in_specs=[pl.BlockSpec(memory_space=pltpu.HBM...  3.15 us
    pallas_call x1, Pallas kernels, contract(): pl.pallas_call(contract_kernel, in_specs=[whole] * 7, out_specs=whole, ou...  2.59 us
  transfers between devices with their start and end apart: 7, of which 1 were waited for; matrix products, arithmetic and copies ran while one was open for 1% of the time, Pallas kernels for 8%

profile of v17, /device:TPU:1, one launch (start us, length us, event | category | flops | bytes accessed | tf_op | source)
XLA Modules:
  0.0 66.0 jit_solution(975272090952164287)
XLA Ops:
  0.0 0.0 copy-start
  0.0 0.0 copy-start.6
  0.0 3.1 %pick.1 = (bf16[16,25,16,128]{3,2,1,0:T(8,128)(2,1)}, bf16[2,3,64,128]{3,2,1,0:T(8,128)(2,1)}) custom-call(bf16[16,2,8,2,4,16,128]{6,5,4,3,2,1,0:T(8,128)(2,1)} %bitcast.21, bf16[2,32,64,128]{3,2,1,0:T(8,128)(2,1)} %wave_ref.1), custom_call_target="tpu_custom_call" | custom-call | tf_op jit(solution)/shard_map/pick/pallas_call | solution.py:77
  3.2 0.0 copy-done
  3.2 3.3 %collective-permute-start.2 = (bf16[12,2,2,128,128]{4,3,2,1,0:T(8,128)(2,1)S(1)}, bf16[12,2,2,128,128]{4,3,2,1,0:T(8,128)(2,1)}, u32[]{:S(2)}, u32[]{:S(2)}) collective-permute-start(bf16[12,2,2,128,128]{4,3,2,1,0:T(8,128)(2,1)S(1)} %copy-done), channel_id=1, source_target_pairs={{0,32},{32,0},{64,96},{96,64},{128,160},{160,128},{192,224},{224,1... | collective-permute-start | bytes 4718600 | tf_op jit(solution)/shard_map/ppermute | solution.py:352
  6.5 4.3 %collective-permute-start.1 = (bf16[2,3,64,128]{3,2,1,0:T(8,128)(2,1)}, bf16[2,3,64,128]{3,2,1,0:T(8,128)(2,1)S(1)}, u32[]{:S(2)}, u32[]{:S(2)}) collective-permute-start(bf16[2,3,64,128]{3,2,1,0:T(8,128)(2,1)} %get-tuple-element.16.own_wave), channel_id=1, source_target_pairs={{0,129},{32,161},{64,193},{96,225},{128,1},{160,33},{192,65},{224,... | collective-permute-start | bytes 294920 | tf_op jit(solution)/shard_map/ppermute | solution.py:347
  10.8 0.0 copy-done.6
  10.8 0.4 collective-permute-start
  11.2 0.0 copy-start.2
  11.2 6.9 %all-to-all-start = ((bf16[16,25,16,128]{3,2,1,0:T(8,128)(2,1)}), bf16[16,25,16,128]{3,2,1,0:T(8,128)(2,1)S(1)}, u32[]{:S(2)}, u32[]{:S(2)}) async-start(bf16[16,25,16,128]{3,2,1,0:T(8,128)(2,1)} %get-tuple-element.24), calls=%async_computation | async-start | bytes 3276800 | tf_op jit(solution)/shard_map/all_to_all | solution.py:354
  18.1 0.0 copy-start.7
  18.1 0.0 copy-start.8
  18.1 0.0 collective-permute-done.far_table
  18.1 0.0 collective-permute-done.1.far_wave
  18.1 0.0 copy-start.3
  18.2 0.0 collective-permute-done.2.far_left
  18.2 0.0 copy-done.2
  18.2 3.1 %make_tiles.1 = (bf16[97,16,128]{2,1,0:T(8,128)(2,1)}, bf16[97,16,128]{2,1,0:T(8,128)(2,1)}, bf16[43,16,128]{2,1,0:T(8,128)(2,1)}) custom-call(s32[12,32]{1,0:T(8,128)S(1)} %copy-done.6, s32[12,32]{1,0:T(8,128)S(1)} %collective-permute-done.far_table, bf16[2,3,64,128]{3,2,1,0:T(8,128)(2,1)S(1)} %copy-done.2, ...), custom_call_target="tpu_custom_call" | custom-call | flops 1000000000 | bytes 4000000 | tf_op jit(solution)/shard_map/make_tiles/pallas_call | solution.py:215
  21.3 0.0 copy-done.3
  21.3 0.1 collective-permute-start.3
  21.4 1.5 %collective-permute-start.4 = (bf16[97,16,128]{2,1,0:T(8,128)(2,1)}, bf16[97,16,128]{2,1,0:T(8,128)(2,1)}, u32[]{:S(2)}, u32[]{:S(2)}) collective-permute-start(bf16[97,16,128]{2,1,0:T(8,128)(2,1)} %get-tuple-element.22), channel_id=1, source_target_pairs={{0,193},{32,96},{64,0},{96,160},{128,64},{160,224},{192,128},{224,... | collective-permute-start | bytes 1191944 | tf_op jit(solution)/shard_map/ppermute | solution.py:364
  22.8 1.4 %collective-permute-start.5 = (bf16[43,16,128]{2,1,0:T(8,128)(2,1)}, bf16[43,16,128]{2,1,0:T(8,128)(2,1)S(1)}, u32[]{:S(2)}, u32[]{:S(2)}) collective-permute-start(bf16[43,16,128]{2,1,0:T(8,128)(2,1)} %get-tuple-element.23), channel_id=1, source_target_pairs={{0,128},{32,161},{64,192},{96,225},{128,1},{160,32},{192,65},{224,... | collective-permute-start | bytes 528392 | tf_op jit(solution)/shard_map/ppermute | solution.py:365
  24.2 0.0 copy-done.7
  24.2 0.1 reshape.127
  24.4 0.1 mul.32
  24.5 0.0 copy-done.8
  24.5 0.1 stack.16
  24.6 0.1 fusion.2
  24.7 0.1 iota_add_fusion
  24.8 0.1 fusion.1
  24.9 0.1 add.100.slot_key
  25.0 0.1 add.96.real_key
  25.1 0.1 sub.26.imag_key
  25.2 0.2 make_picks.1.picks
  25.4 0.0 copy-start.1
  25.4 1.4 %copy-done.1 = bf16[12,2,2,128,128]{4,3,2,1,0:T(8,128)(2,1)S(1)} copy-done((bf16[12,2,2,128,128]{4,3,2,1,0:T(8,128)(2,1)S(1)}, bf16[12,2,2,128,128]{4,3,2,1,0:T(8,128)(2,1)}, u32[]{:S(2)}) %copy-start.1) | copy-done | bytes 1572888
  26.8 0.9 %copy-done.4 = bf16[2,3,64,128]{3,2,1,0:T(8,128)(2,1)S(1)} copy-done((bf16[2,3,64,128]{3,2,1,0:T(8,128)(2,1)S(1)}, bf16[2,3,64,128]{3,2,1,0:T(8,128)(2,1)}, u32[]{:S(2)}) %copy-start.4) | copy-done | bytes 98328
  27.7 2.3 %make_home.1.home = bf16[151,16,128]{2,1,0:T(8,128)(2,1)S(1)} custom-call(s32[12,32]{1,0:T(8,128)S(1)} %copy-done.6, s32[12,32]{1,0:T(8,128)S(1)} %collective-permute-done.far_table, bf16[2,3,64,128]{3,2,1,0:T(8,128)(2,1)S(1)} %copy-done.2, bf16[2,3,64,128]{3,2,1,0:T(8,128)(2,1)S(1)} %copy-done.4, bf16[12,2,2,128,128]{4,3,2,1,0:T(8,128)(2,1)S(1)} %copy-done.1, ...), custom_call_target="tpu_custom_call" | custom-call | flops 1000000000 | bytes 4000000 | tf_op jit(solution)/shard_map/make_home/pallas_call | solution.py:215
  30.0 12.3 %all-to-all-done.right = bf16[16,25,16,128]{3,2,1,0:T(8,128)(2,1)S(1)} async-done(((bf16[16,25,16,128]{3,2,1,0:T(8,128)(2,1)}), bf16[16,25,16,128]{3,2,1,0:T(8,128)(2,1)S(1)}, u32[]{:S(2)}, u32[]{:S(2)}) %all-to-all-start) | async-done | bytes 1638432 | tf_op jit(solution)/shard_map/all_to_all | solution.py:354
  42.3 0.0 collective-permute-done.5.ahead2
  42.3 0.0 collective-permute-done.3.ahead1
  42.3 0.0 collective-permute-done.4.back1
  42.3 0.0 copy-done.5
  42.3 2.6 %contract.1 = bf16[8,64,128]{2,1,0:T(8,128)(2,1)S(1)} custom-call(bf16[151,16,128]{2,1,0:T(8,128)(2,1)S(1)} %make_home.1.home, bf16[97,16,128]{2,1,0:T(8,128)(2,1)S(1)} %collective-permute-done.3.ahead1, bf16[97,16,128]{2,1,0:T(8,128)(2,1)} %collective-permute-done.4.back1, bf16[43,16,128]{2,1,0:T(8,128)(2,1)S(1)} %collective-permute-done.5.ahead2, ...), custom_call_target="tpu_custom_call" | custom-call | tf_op jit(solution)/shard_map/contract/pallas_call | solution.py:321
  44.9 20.2 %all_to_all.10 = bf16[256,2,128]{2,1,0:T(2,128)(2,1)S(1)} all-to-all(bf16[256,2,128]{2,1,0:T(2,128)(2,1)S(1)} %bitcast.19), channel_id=1, replica_groups=mesh['row'=8,'col'=16,'wf'=2] {'row','wf','col'}, dimensions={0} | all-to-all | bytes 262144 | tf_op jit(solution)/shard_map/all_to_all | solution.py:388
  65.1 0.3 convert_reduce_fusion
  65.3 0.1 reshape.129
  65.4 0.6 copy.13
  (14 shorter events, 0.1 us)
Async XLA Ops:
  0.0 3.2 %copy-start = (bf16[12,2,2,128,128]{4,3,2,1,0:T(8,128)(2,1)S(1)}, bf16[12,2,2,128,128]{4,3,2,1,0:T(8,128)(2,1)}, u32[]{:S(2)}) copy-start(bf16[12,2,2,128,128]{4,3,2,1,0:T(8,128)(2,1)} %own_left.3) | copy-start | bytes 4718596
  0.0 10.8 %copy-start.6 = (s32[12,32]{1,0:T(8,128)S(1)}, s32[12,32]{1,0:T(8,128)}, u32[]{:S(2)}) copy-start(s32[12,32]{1,0:T(8,128)} %own_table.3) | copy-start | bytes 4612
  3.2 15.0 %collective-permute-start.2 = (bf16[12,2,2,128,128]{4,3,2,1,0:T(8,128)(2,1)S(1)}, bf16[12,2,2,128,128]{4,3,2,1,0:T(8,128)(2,1)}, u32[]{:S(2)}, u32[]{:S(2)}) collective-permute-start(bf16[12,2,2,128,128]{4,3,2,1,0:T(8,128)(2,1)S(1)} %copy-done), channel_id=1, source_target_pairs={{0,32},{32,0},{64,96},{96,64},{128,160},{160,128},{192,224},{224,1... | collective-permute-start | bytes 4718600 | tf_op jit(solution)/shard_map/ppermute | solution.py:352
  6.5 11.6 %collective-permute-start.1 = (bf16[2,3,64,128]{3,2,1,0:T(8,128)(2,1)}, bf16[2,3,64,128]{3,2,1,0:T(8,128)(2,1)S(1)}, u32[]{:S(2)}, u32[]{:S(2)}) collective-permute-start(bf16[2,3,64,128]{3,2,1,0:T(8,128)(2,1)} %get-tuple-element.16.own_wave), channel_id=1, source_target_pairs={{0,129},{32,161},{64,193},{96,225},{128,1},{160,33},{192,65},{224,... | collective-permute-start | bytes 294920 | tf_op jit(solution)/shard_map/ppermute | solution.py:347
  10.8 7.3 %collective-permute-start = (s32[12,32]{1,0:T(8,128)S(1)}, s32[12,32]{1,0:T(8,128)S(1)}, u32[]{:S(2)}, u32[]{:S(2)}) collective-permute-start(s32[12,32]{1,0:T(8,128)S(1)} %copy-done.6), channel_id=1, source_target_pairs={{0,32},{32,0},{64,96},{96,64},{128,160},{160,128},{192,224},{224,1... | collective-permute-start | bytes 4616 | tf_op jit(solution)/shard_map/ppermute | solution.py:353
  11.2 7.0 %copy-start.2 = (bf16[2,3,64,128]{3,2,1,0:T(8,128)(2,1)S(1)}, bf16[2,3,64,128]{3,2,1,0:T(8,128)(2,1)}, u32[]{:S(2)}) copy-start(bf16[2,3,64,128]{3,2,1,0:T(8,128)(2,1)} %get-tuple-element.16.own_wave) | copy-start | bytes 294916
  11.2 31.1 %all-to-all-start = ((bf16[16,25,16,128]{3,2,1,0:T(8,128)(2,1)}), bf16[16,25,16,128]{3,2,1,0:T(8,128)(2,1)S(1)}, u32[]{:S(2)}, u32[]{:S(2)}) async-start(bf16[16,25,16,128]{3,2,1,0:T(8,128)(2,1)} %get-tuple-element.24), calls=%async_computation | async-start | bytes 3276800 | tf_op jit(solution)/shard_map/all_to_all | solution.py:354
  18.1 6.2 %copy-start.7 = (s32[96]{0:T(128)S(1)}, s32[96]{0:T(128)}, u32[]{:S(2)}) copy-start(s32[96]{0:T(128)} %param.12) | copy-start | bytes 1156
  18.1 6.4 %copy-start.8 = (s32[96]{0:T(128)S(1)}, s32[96]{0:T(128)}, u32[]{:S(2)}) copy-start(s32[96]{0:T(128)} %param.13) | copy-start | bytes 1156
  18.1 3.1 %copy-start.3 = (bf16[2,3,64,128]{3,2,1,0:T(8,128)(2,1)}, bf16[2,3,64,128]{3,2,1,0:T(8,128)(2,1)S(1)}, u32[]{:S(2)}) copy-start(bf16[2,3,64,128]{3,2,1,0:T(8,128)(2,1)S(1)} %collective-permute-done.1.far_wave) | copy-start | bytes 294916
  21.3 21.0 %collective-permute-start.3 = (bf16[97,16,128]{2,1,0:T(8,128)(2,1)}, bf16[97,16,128]{2,1,0:T(8,128)(2,1)S(1)}, u32[]{:S(2)}, u32[]{:S(2)}) collective-permute-start(bf16[97,16,128]{2,1,0:T(8,128)(2,1)} %get-tuple-element.21), channel_id=1, source_target_pairs={{0,64},{32,225},{64,128},{96,32},{128,192},{160,96},{192,1},{224,1... | collective-permute-start | bytes 1191944 | tf_op jit(solution)/shard_map/ppermute | solution.py:363
  21.4 20.9 %collective-permute-start.4 = (bf16[97,16,128]{2,1,0:T(8,128)(2,1)}, bf16[97,16,128]{2,1,0:T(8,128)(2,1)}, u32[]{:S(2)}, u32[]{:S(2)}) collective-permute-start(bf16[97,16,128]{2,1,0:T(8,128)(2,1)} %get-tuple-element.22), channel_id=1, source_target_pairs={{0,193},{32,96},{64,0},{96,160},{128,64},{160,224},{192,128},{224,... | collective-permute-start | bytes 1191944 | tf_op jit(solution)/shard_map/ppermute | solution.py:364
  22.8 19.5 %collective-permute-start.5 = (bf16[43,16,128]{2,1,0:T(8,128)(2,1)}, bf16[43,16,128]{2,1,0:T(8,128)(2,1)S(1)}, u32[]{:S(2)}, u32[]{:S(2)}) collective-permute-start(bf16[43,16,128]{2,1,0:T(8,128)(2,1)} %get-tuple-element.23), channel_id=1, source_target_pairs={{0,128},{32,161},{64,192},{96,225},{128,1},{160,32},{192,65},{224,... | collective-permute-start | bytes 528392 | tf_op jit(solution)/shard_map/ppermute | solution.py:365
  25.4 1.4 %copy-start.1 = (bf16[12,2,2,128,128]{4,3,2,1,0:T(8,128)(2,1)S(1)}, bf16[12,2,2,128,128]{4,3,2,1,0:T(8,128)(2,1)}, u32[]{:S(2)}) copy-start(bf16[12,2,2,128,128]{4,3,2,1,0:T(8,128)(2,1)} %own_left.3) | copy-start | bytes 4718596
  26.8 0.9 %copy-start.4 = (bf16[2,3,64,128]{3,2,1,0:T(8,128)(2,1)S(1)}, bf16[2,3,64,128]{3,2,1,0:T(8,128)(2,1)}, u32[]{:S(2)}) copy-start(bf16[2,3,64,128]{3,2,1,0:T(8,128)(2,1)} %copy-done.3) | copy-start | bytes 294916
  27.7 14.6 %copy-start.5 = (s32[128,32]{0,1:T(8,128)S(1)}, s32[128,32]{0,1:T(8,128)}, u32[]{:S(2)}) copy-start(s32[128,32]{0,1:T(8,128)} %param.11) | copy-start | bytes 49156

commit v18 on v17

--- a/solution.py
+++ b/solution.py
@@ -24,7 +24,7 @@
     return pltpu.CompilerParams(vmem_limit_bytes=mebibytes * 1024 * 1024)
 
 
-SPLIT = 7
+SPLIT = 8
 CROSS = 16 - SPLIT
 ROWS = (16 + CROSS, 16, 16, SPLIT)
 TILES = tuple(6 * rows for rows in ROWS)
@@ -348,9 +348,8 @@
         own_wave, line, ring(lambda z, core: (z + 2) % 8 if z in (2, 3, 6, 7) else (z - 2) % 8)
     )
     swap = [(i, i ^ 1) for i in range(8)]
-    given, given_table, _ = lax.optimization_barrier((left_operators, left_table, own_wave))
-    far_left = lax.ppermute(given, "row", swap)
-    far_table = lax.ppermute(given_table, "row", swap)
+    far_left = lax.ppermute(left_operators, "row", swap)
+    far_table = lax.ppermute(left_table, "row", swap)
     right = lax.all_to_all(right, "col", 0, 0, tiled=True)
     ahead1, back1, ahead2 = make_tiles(
         True, left_table, far_table, own_wave, far_wave, left_operators, far_left

time: 66.4 us -> 65.8 us (level)
  waiting for transfers between devices: 12.3 us -> 6 us
  local copies, waits for them, and re-layouts: 3.64 us -> 6.64 us
  blocking collectives: 20.2 us -> 23 us
    all_to_all x1, waiting for transfers between devices: 12.3 us -> 5.99 us  [local(): right = lax.all_to_all(right, 'col', 0, 0, tiled=True)]
    unnamed x18 -> x26, local copies, waits for them, and re-layouts: 2.33 us -> 5.33 us
    all_to_all x1, blocking collectives: 20.2 us -> 23 us  [local(): lax.all_to_all(shares.reshape(256, 2, 128), ('row', 'wf', 'col'), 0, 0, t...]
  transfers between devices with their start and end apart: 7 -> 7, of which waited for: 1 -> 1; matrix products, arithmetic and copies ran while one was open for 1% -> 1% of each run, Pallas kernels for 8% -> 13%
where the time goes in v18:
time: 65.8 us; the launch traced here: 65.3 us
  blocking collectives  23 us (35%)
  starting transfers between devices  17.7 us (27%)
  Pallas kernels  11 us (17%)
  local copies, waits for them, and re-layouts  6.64 us (10%)
  waiting for transfers between devices  6 us (9%)
    all_to_all x1, blocking collectives, local(): lax.all_to_all(shares.reshape(256, 2, 128), ('row', 'wf', 'col'), 0, 0, t...  23 us
    all_to_all x1, starting transfers between devices, local(): right = lax.all_to_all(right, 'col', 0, 0, tiled=True)  6.89 us
    all_to_all x1, waiting for transfers between devices, local(): right = lax.all_to_all(right, 'col', 0, 0, tiled=True)  5.99 us
    pallas_call x2, Pallas kernels, make_tiles(): pl.pallas_call(functools.partial(tiles_kernel, sent), in_specs=[whole] *...  5.39 us
    unnamed x26, local copies, waits for them, and re-layouts  5.33 us
    ppermute x1, starting transfers between devices, local(): lax.ppermute(own_wave, line, ring(lambda z, core: (z + 2) % 8 if z in (2,...  4.37 us
    ppermute x1, starting transfers between devices, local(): far_left = lax.ppermute(left_operators, 'row', swap)  3.24 us
    pallas_call x1, Pallas kernels, pick(): pl.pallas_call(pick_kernel, in_specs=[pl.BlockSpec(memory_space=pltpu.HBM...  2.99 us
  transfers between devices with their start and end apart: 7, of which 1 were waited for; matrix products, arithmetic and copies ran while one was open for 1% of the time, Pallas kernels for 13%

profile of v18, /device:TPU:1, one launch (start us, length us, event | category | flops | bytes accessed | tf_op | source)
XLA Modules:
  0.0 65.3 jit_solution(8372021713212360792)
XLA Ops:
  0.0 3.2 %collective-permute-start.2 = (bf16[12,2,2,128,128]{4,3,2,1,0:T(8,128)(2,1)}, bf16[12,2,2,128,128]{4,3,2,1,0:T(8,128)(2,1)}, u32[]{:S(2)}, u32[]{:S(2)}) collective-permute-start(bf16[12,2,2,128,128]{4,3,2,1,0:T(8,128)(2,1)} %own_left.3), channel_id=1, source_target_pairs={{0,32},{32,0},{64,96},{96,64},{128,160},{160,128},{192,224},{224,1... | collective-permute-start | bytes 4718600 | tf_op jit(solution)/shard_map/ppermute | solution.py:351
  3.2 0.0 collective-permute-start
  3.2 3.0 %pick.1 = (bf16[16,24,16,128]{3,2,1,0:T(8,128)(2,1)}, bf16[2,3,64,128]{3,2,1,0:T(8,128)(2,1)}) custom-call(bf16[16,2,8,2,4,16,128]{6,5,4,3,2,1,0:T(8,128)(2,1)} %bitcast.21, bf16[2,32,64,128]{3,2,1,0:T(8,128)(2,1)} %wave_ref.1), custom_call_target="tpu_custom_call" | custom-call | tf_op jit(solution)/shard_map/pick/pallas_call | solution.py:77
  6.2 4.4 %collective-permute-start.1 = (bf16[2,3,64,128]{3,2,1,0:T(8,128)(2,1)}, bf16[2,3,64,128]{3,2,1,0:T(8,128)(2,1)S(1)}, u32[]{:S(2)}, u32[]{:S(2)}) collective-permute-start(bf16[2,3,64,128]{3,2,1,0:T(8,128)(2,1)} %get-tuple-element.14.own_wave), channel_id=1, source_target_pairs={{0,129},{32,161},{64,193},{96,225},{128,1},{160,33},{192,65},{224,... | collective-permute-start | bytes 294920 | tf_op jit(solution)/shard_map/ppermute | solution.py:347
  10.6 6.9 %all-to-all-start = ((bf16[16,24,16,128]{3,2,1,0:T(8,128)(2,1)}), bf16[16,24,16,128]{3,2,1,0:T(8,128)(2,1)S(1)}, u32[]{:S(2)}, u32[]{:S(2)}) async-start(bf16[16,24,16,128]{3,2,1,0:T(8,128)(2,1)} %get-tuple-element.20), calls=%async_computation | async-start | bytes 3145728 | tf_op jit(solution)/shard_map/all_to_all | solution.py:353
  17.5 0.0 copy-start.11
  17.6 0.0 copy-start.12
  17.6 0.0 collective-permute-done.far_table
  17.6 0.0 copy-start.9
  17.6 0.0 collective-permute-done.1.far_wave
  17.6 0.0 copy-start.4
  17.6 0.0 collective-permute-done.2.far_left
  17.6 0.0 copy-done
  17.6 0.0 copy-done.2
  17.6 0.0 copy-done.7
  17.6 3.1 %make_tiles.1 = (bf16[97,16,128]{2,1,0:T(8,128)(2,1)}, bf16[97,16,128]{2,1,0:T(8,128)(2,1)}, bf16[49,16,128]{2,1,0:T(8,128)(2,1)}) custom-call(s32[12,32]{1,0:T(8,128)S(1)} %copy-done.7, s32[12,32]{1,0:T(8,128)S(1)} %collective-permute-done.far_table, bf16[2,3,64,128]{3,2,1,0:T(8,128)(2,1)S(1)} %copy-done.2, ...), custom_call_target="tpu_custom_call" | custom-call | flops 1000000000 | bytes 4000000 | tf_op jit(solution)/shard_map/make_tiles/pallas_call | solution.py:215
  20.8 0.0 copy-done.9
  20.8 0.1 collective-permute-start.3
  20.9 1.5 %collective-permute-start.4 = (bf16[97,16,128]{2,1,0:T(8,128)(2,1)}, bf16[97,16,128]{2,1,0:T(8,128)(2,1)S(1)}, u32[]{:S(2)}, u32[]{:S(2)}) collective-permute-start(bf16[97,16,128]{2,1,0:T(8,128)(2,1)} %get-tuple-element.18), channel_id=1, source_target_pairs={{0,193},{32,96},{64,0},{96,160},{128,64},{160,224},{192,128},{224,... | collective-permute-start | bytes 1191944 | tf_op jit(solution)/shard_map/ppermute | solution.py:363
  22.3 1.7 %collective-permute-start.5 = (bf16[49,16,128]{2,1,0:T(8,128)(2,1)}, bf16[49,16,128]{2,1,0:T(8,128)(2,1)}, u32[]{:S(2)}, u32[]{:S(2)}) collective-permute-start(bf16[49,16,128]{2,1,0:T(8,128)(2,1)} %get-tuple-element.19), channel_id=1, source_target_pairs={{0,128},{32,161},{64,192},{96,225},{128,1},{160,32},{192,65},{224,... | collective-permute-start | bytes 602120 | tf_op jit(solution)/shard_map/ppermute | solution.py:364
  24.0 0.1 reshape.127
  24.2 0.1 mul.32
  24.3 0.1 stack.16
  24.4 0.1 fusion.2
  24.5 0.1 iota_add_fusion
  24.5 0.1 fusion.1
  24.6 0.1 add.100.slot_key
  24.8 0.1 add.96.real_key
  24.9 0.1 sub.26.imag_key
  25.0 0.2 make_picks.1.picks
  25.2 0.0 copy-start.1
  25.2 1.4 %copy-done.1 = bf16[12,2,2,128,128]{4,3,2,1,0:T(8,128)(2,1)S(1)} copy-done((bf16[12,2,2,128,128]{4,3,2,1,0:T(8,128)(2,1)S(1)}, bf16[12,2,2,128,128]{4,3,2,1,0:T(8,128)(2,1)}, u32[]{:S(2)}) %copy-start.1) | copy-done | bytes 1572888
  26.6 0.9 %copy-done.3 = bf16[2,3,64,128]{3,2,1,0:T(8,128)(2,1)S(1)} copy-done((bf16[2,3,64,128]{3,2,1,0:T(8,128)(2,1)S(1)}, bf16[2,3,64,128]{3,2,1,0:T(8,128)(2,1)}, u32[]{:S(2)}) %copy-start.3) | copy-done | bytes 98328
  27.5 0.9 %copy-done.5 = bf16[2,3,64,128]{3,2,1,0:T(8,128)(2,1)S(1)} copy-done((bf16[2,3,64,128]{3,2,1,0:T(8,128)(2,1)S(1)}, bf16[2,3,64,128]{3,2,1,0:T(8,128)(2,1)}, u32[]{:S(2)}) %copy-start.5) | copy-done | bytes 98328
  28.4 0.7 %copy-done.8 = s32[12,32]{1,0:T(8,128)S(1)} copy-done((s32[12,32]{1,0:T(8,128)S(1)}, s32[12,32]{1,0:T(8,128)}, u32[]{:S(2)}) %copy-start.8) | copy-done | bytes 1560
  29.1 0.7 %copy-done.10 = s32[12,32]{1,0:T(8,128)S(1)} copy-done((s32[12,32]{1,0:T(8,128)S(1)}, s32[12,32]{1,0:T(8,128)}, u32[]{:S(2)}) %copy-start.10) | copy-done | bytes 1560
  29.8 2.3 %make_home.1.home = bf16[145,16,128]{2,1,0:T(8,128)(2,1)S(1)} custom-call(s32[12,32]{1,0:T(8,128)S(1)} %copy-done.8, s32[12,32]{1,0:T(8,128)S(1)} %copy-done.10, bf16[2,3,64,128]{3,2,1,0:T(8,128)(2,1)S(1)} %copy-done.3, bf16[2,3,64,128]{3,2,1,0:T(8,128)(2,1)S(1)} %copy-done.5, bf16[12,2,2,128,128]{4,3,2,1,0:T(8,128)(2,1)S(1)} %copy-done.1, ...), custom_call_target="tpu_custom_call" | custom-call | flops 1000000000 | bytes 4000000 | tf_op jit(solution)/shard_map/make_home/pallas_call | solution.py:215
  32.1 6.0 %all-to-all-done.right = bf16[16,24,16,128]{3,2,1,0:T(8,128)(2,1)S(1)} async-done(((bf16[16,24,16,128]{3,2,1,0:T(8,128)(2,1)}), bf16[16,24,16,128]{3,2,1,0:T(8,128)(2,1)S(1)}, u32[]{:S(2)}, u32[]{:S(2)}) %all-to-all-start) | async-done | bytes 1572896 | tf_op jit(solution)/shard_map/all_to_all | solution.py:353
  38.0 0.0 collective-permute-done.5.ahead2
  38.0 0.0 collective-permute-done.3.ahead1
  38.0 0.0 collective-permute-done.4.back1
  38.0 0.0 copy-start.6
  38.1 0.7 %copy-done.6 = s32[128,32]{0,1:T(8,128)S(1)} copy-done((s32[128,32]{0,1:T(8,128)S(1)}, s32[128,32]{0,1:T(8,128)}, u32[]{:S(2)}) %copy-start.6) | copy-done | bytes 16408
  38.8 2.5 %contract.1 = bf16[8,64,128]{2,1,0:T(8,128)(2,1)S(1)} custom-call(bf16[145,16,128]{2,1,0:T(8,128)(2,1)S(1)} %make_home.1.home, bf16[97,16,128]{2,1,0:T(8,128)(2,1)S(1)} %collective-permute-done.3.ahead1, bf16[97,16,128]{2,1,0:T(8,128)(2,1)S(1)} %collective-permute-done.4.back1, bf16[49,16,128]{2,1,0:T(8,128)(2,1)} %collective-permute-done.5.ahead2, ...), custom_call_target="tpu_custom_call" | custom-call | tf_op jit(solution)/shard_map/contract/pallas_call | solution.py:321
  41.3 23.0 %all_to_all.10 = bf16[256,2,128]{2,1,0:T(2,128)(2,1)S(1)} all-to-all(bf16[256,2,128]{2,1,0:T(2,128)(2,1)S(1)} %bitcast.19), channel_id=1, replica_groups=mesh['row'=8,'col'=16,'wf'=2] {'row','wf','col'}, dimensions={0} | all-to-all | bytes 262144 | tf_op jit(solution)/shard_map/all_to_all | solution.py:387
  64.3 0.3 convert_reduce_fusion
  64.6 0.1 reshape.129
  64.7 0.6 copy.13
  (22 shorter events, 0.1 us)
Async XLA Ops:
  0.0 17.6 %collective-permute-start.2 = (bf16[12,2,2,128,128]{4,3,2,1,0:T(8,128)(2,1)}, bf16[12,2,2,128,128]{4,3,2,1,0:T(8,128)(2,1)}, u32[]{:S(2)}, u32[]{:S(2)}) collective-permute-start(bf16[12,2,2,128,128]{4,3,2,1,0:T(8,128)(2,1)} %own_left.3), channel_id=1, source_target_pairs={{0,32},{32,0},{64,96},{96,64},{128,160},{160,128},{192,224},{224,1... | collective-permute-start | bytes 4718600 | tf_op jit(solution)/shard_map/ppermute | solution.py:351
  3.2 14.3 %collective-permute-start = (s32[12,32]{1,0:T(8,128)}, s32[12,32]{1,0:T(8,128)S(1)}, u32[]{:S(2)}, u32[]{:S(2)}) collective-permute-start(s32[12,32]{1,0:T(8,128)} %own_table.3), channel_id=1, source_target_pairs={{0,32},{32,0},{64,96},{96,64},{128,160},{160,128},{192,224},{224,1... | collective-permute-start | bytes 4616 | tf_op jit(solution)/shard_map/ppermute | solution.py:352
  6.2 11.4 %collective-permute-start.1 = (bf16[2,3,64,128]{3,2,1,0:T(8,128)(2,1)}, bf16[2,3,64,128]{3,2,1,0:T(8,128)(2,1)S(1)}, u32[]{:S(2)}, u32[]{:S(2)}) collective-permute-start(bf16[2,3,64,128]{3,2,1,0:T(8,128)(2,1)} %get-tuple-element.14.own_wave), channel_id=1, source_target_pairs={{0,129},{32,161},{64,193},{96,225},{128,1},{160,33},{192,65},{224,... | collective-permute-start | bytes 294920 | tf_op jit(solution)/shard_map/ppermute | solution.py:347
  10.6 7.0 %copy-start = (bf16[12,2,2,128,128]{4,3,2,1,0:T(8,128)(2,1)S(1)}, bf16[12,2,2,128,128]{4,3,2,1,0:T(8,128)(2,1)}, u32[]{:S(2)}) copy-start(bf16[12,2,2,128,128]{4,3,2,1,0:T(8,128)(2,1)} %own_left.3) | copy-start | bytes 4718596
  10.6 7.0 %copy-start.2 = (bf16[2,3,64,128]{3,2,1,0:T(8,128)(2,1)S(1)}, bf16[2,3,64,128]{3,2,1,0:T(8,128)(2,1)}, u32[]{:S(2)}) copy-start(bf16[2,3,64,128]{3,2,1,0:T(8,128)(2,1)} %get-tuple-element.14.own_wave) | copy-start | bytes 294916
  10.6 7.0 %copy-start.7 = (s32[12,32]{1,0:T(8,128)S(1)}, s32[12,32]{1,0:T(8,128)}, u32[]{:S(2)}) copy-start(s32[12,32]{1,0:T(8,128)} %own_table.3) | copy-start | bytes 4612
  10.6 27.4 %all-to-all-start = ((bf16[16,24,16,128]{3,2,1,0:T(8,128)(2,1)}), bf16[16,24,16,128]{3,2,1,0:T(8,128)(2,1)S(1)}, u32[]{:S(2)}, u32[]{:S(2)}) async-start(bf16[16,24,16,128]{3,2,1,0:T(8,128)(2,1)} %get-tuple-element.20), calls=%async_computation | async-start | bytes 3145728 | tf_op jit(solution)/shard_map/all_to_all | solution.py:353
  17.5 6.5 %copy-start.11 = (s32[96]{0:T(128)S(1)}, s32[96]{0:T(128)}, u32[]{:S(2)}) copy-start(s32[96]{0:T(128)} %param.12) | copy-start | bytes 1156
  17.6 6.7 %copy-start.12 = (s32[96]{0:T(128)S(1)}, s32[96]{0:T(128)}, u32[]{:S(2)}) copy-start(s32[96]{0:T(128)} %param.13) | copy-start | bytes 1156
  17.6 3.2 %copy-start.9 = (s32[12,32]{1,0:T(8,128)}, s32[12,32]{1,0:T(8,128)S(1)}, u32[]{:S(2)}) copy-start(s32[12,32]{1,0:T(8,128)S(1)} %collective-permute-done.far_table) | copy-start | bytes 4612
  17.6 3.2 %copy-start.4 = (bf16[2,3,64,128]{3,2,1,0:T(8,128)(2,1)}, bf16[2,3,64,128]{3,2,1,0:T(8,128)(2,1)S(1)}, u32[]{:S(2)}) copy-start(bf16[2,3,64,128]{3,2,1,0:T(8,128)(2,1)S(1)} %collective-permute-done.1.far_wave) | copy-start | bytes 294916
  20.8 17.3 %collective-permute-start.3 = (bf16[97,16,128]{2,1,0:T(8,128)(2,1)}, bf16[97,16,128]{2,1,0:T(8,128)(2,1)S(1)}, u32[]{:S(2)}, u32[]{:S(2)}) collective-permute-start(bf16[97,16,128]{2,1,0:T(8,128)(2,1)} %get-tuple-element.17), channel_id=1, source_target_pairs={{0,64},{32,225},{64,128},{96,32},{128,192},{160,96},{192,1},{224,1... | collective-permute-start | bytes 1191944 | tf_op jit(solution)/shard_map/ppermute | solution.py:362
  20.9 17.2 %collective-permute-start.4 = (bf16[97,16,128]{2,1,0:T(8,128)(2,1)}, bf16[97,16,128]{2,1,0:T(8,128)(2,1)S(1)}, u32[]{:S(2)}, u32[]{:S(2)}) collective-permute-start(bf16[97,16,128]{2,1,0:T(8,128)(2,1)} %get-tuple-element.18), channel_id=1, source_target_pairs={{0,193},{32,96},{64,0},{96,160},{128,64},{160,224},{192,128},{224,... | collective-permute-start | bytes 1191944 | tf_op jit(solution)/shard_map/ppermute | solution.py:363
  22.3 15.7 %collective-permute-start.5 = (bf16[49,16,128]{2,1,0:T(8,128)(2,1)}, bf16[49,16,128]{2,1,0:T(8,128)(2,1)}, u32[]{:S(2)}, u32[]{:S(2)}) collective-permute-start(bf16[49,16,128]{2,1,0:T(8,128)(2,1)} %get-tuple-element.19), channel_id=1, source_target_pairs={{0,128},{32,161},{64,192},{96,225},{128,1},{160,32},{192,65},{224,... | collective-permute-start | bytes 602120 | tf_op jit(solution)/shard_map/ppermute | solution.py:364
  25.2 1.4 %copy-start.1 = (bf16[12,2,2,128,128]{4,3,2,1,0:T(8,128)(2,1)S(1)}, bf16[12,2,2,128,128]{4,3,2,1,0:T(8,128)(2,1)}, u32[]{:S(2)}) copy-start(bf16[12,2,2,128,128]{4,3,2,1,0:T(8,128)(2,1)} %own_left.3) | copy-start | bytes 4718596
  26.6 0.9 %copy-start.3 = (bf16[2,3,64,128]{3,2,1,0:T(8,128)(2,1)S(1)}, bf16[2,3,64,128]{3,2,1,0:T(8,128)(2,1)}, u32[]{:S(2)}) copy-start(bf16[2,3,64,128]{3,2,1,0:T(8,128)(2,1)} %get-tuple-element.14.own_wave) | copy-start | bytes 294916
  27.5 0.9 %copy-start.5 = (bf16[2,3,64,128]{3,2,1,0:T(8,128)(2,1)S(1)}, bf16[2,3,64,128]{3,2,1,0:T(8,128)(2,1)}, u32[]{:S(2)}) copy-start(bf16[2,3,64,128]{3,2,1,0:T(8,128)(2,1)} %copy-done.4) | copy-start | bytes 294916
  28.4 0.7 %copy-start.8 = (s32[12,32]{1,0:T(8,128)S(1)}, s32[12,32]{1,0:T(8,128)}, u32[]{:S(2)}) copy-start(s32[12,32]{1,0:T(8,128)} %own_table.3) | copy-start | bytes 4612
  29.1 0.7 %copy-start.10 = (s32[12,32]{1,0:T(8,128)S(1)}, s32[12,32]{1,0:T(8,128)}, u32[]{:S(2)}) copy-start(s32[12,32]{1,0:T(8,128)} %copy-done.9) | copy-start | bytes 4612
  38.0 0.7 %copy-start.6 = (s32[128,32]{0,1:T(8,128)S(1)}, s32[128,32]{0,1:T(8,128)}, u32[]{:S(2)}) copy-start(s32[128,32]{0,1:T(8,128)} %param.11) | copy-start | bytes 49156

commit v19 on v14

--- a/solution.py
+++ b/solution.py
@@ -24,7 +24,7 @@
     return pltpu.CompilerParams(vmem_limit_bytes=mebibytes * 1024 * 1024)
 
 
-SPLIT = 7
+SPLIT = 8
 CROSS = 16 - SPLIT
 ROWS = (16 + CROSS, 16, 16, SPLIT)
 TILES = tuple(6 * rows for rows in ROWS)

time: 65.4 us -> 66 us (level)
  local copies, waits for them, and re-layouts: 4.48 us -> 8.12 us
  waiting for transfers between devices: 8.24 us -> 4.71 us
    all_to_all x1, waiting for transfers between devices: 8.22 us -> 4.7 us  [local(): right = lax.all_to_all(right, 'col', 0, 0, tiled=True)]
    unnamed x16 -> x22, local copies, waits for them, and re-layouts: 2.32 us -> 5.31 us
  transfers between devices with their start and end apart: 7 -> 7, of which waited for: 1 -> 1; matrix products, arithmetic and copies ran while one was open for 3% -> 4% of each run, Pallas kernels for 13% -> 13%
where the time goes in v19:
time: 66 us; the launch traced here: 65.4 us
  blocking collectives  23.2 us (35%)
  starting transfers between devices  17.5 us (27%)
  Pallas kernels  11.1 us (17%)
  local copies, waits for them, and re-layouts  8.12 us (12%)
  waiting for transfers between devices  4.71 us (7%)
    all_to_all x1, blocking collectives, local(): lax.all_to_all(shares.reshape(256, 2, 128), ('row', 'wf', 'col'), 0, 0, t...  23.2 us
    all_to_all x1, starting transfers between devices, local(): right = lax.all_to_all(right, 'col', 0, 0, tiled=True)  6.89 us
    pallas_call x2, Pallas kernels, make_tiles(): pl.pallas_call(functools.partial(tiles_kernel, sent), in_specs=[whole] *...  5.38 us
    unnamed x22, local copies, waits for them, and re-layouts  5.31 us
    all_to_all x1, waiting for transfers between devices, local(): right = lax.all_to_all(right, 'col', 0, 0, tiled=True)  4.7 us
    ppermute x1, starting transfers between devices, local(): lax.ppermute(own_wave, line, ring(lambda z, core: (z + 2) % 8 if z in (2,...  4.37 us
    ppermute x1, starting transfers between devices, local(): far_left = lax.ppermute(left_operators, 'row', swap)  3.24 us
    pallas_call x1, Pallas kernels, pick(): pl.pallas_call(pick_kernel, in_specs=[pl.BlockSpec(memory_space=pltpu.HBM...  3 us
  transfers between devices with their start and end apart: 7, of which 1 were waited for; matrix products, arithmetic and copies ran while one was open for 4% of the time, Pallas kernels for 13%

profile of v19, /device:TPU:1, one launch (start us, length us, event | category | flops | bytes accessed | tf_op | source)
XLA Modules:
  0.0 65.4 jit_solution(10044052978604283402)
XLA Ops:
  0.0 3.2 %collective-permute-start.2 = (bf16[12,2,2,128,128]{4,3,2,1,0:T(8,128)(2,1)}, bf16[12,2,2,128,128]{4,3,2,1,0:T(8,128)(2,1)}, u32[]{:S(2)}, u32[]{:S(2)}) collective-permute-start(bf16[12,2,2,128,128]{4,3,2,1,0:T(8,128)(2,1)} %own_left.3), channel_id=1, source_target_pairs={{0,32},{32,0},{64,96},{96,64},{128,160},{160,128},{192,224},{224,1... | collective-permute-start | bytes 4718600 | tf_op jit(solution)/shard_map/ppermute | solution.py:350
  3.2 0.0 collective-permute-start
  3.2 3.0 %pick.1 = (bf16[16,24,16,128]{3,2,1,0:T(8,128)(2,1)}, bf16[2,3,64,128]{3,2,1,0:T(8,128)(2,1)}) custom-call(bf16[16,2,8,2,4,16,128]{6,5,4,3,2,1,0:T(8,128)(2,1)} %bitcast.21, bf16[2,32,64,128]{3,2,1,0:T(8,128)(2,1)} %wave_ref.1), custom_call_target="tpu_custom_call" | custom-call | tf_op jit(solution)/shard_map/pick/pallas_call | solution.py:77
  6.2 4.4 %collective-permute-start.1 = (bf16[2,3,64,128]{3,2,1,0:T(8,128)(2,1)}, bf16[2,3,64,128]{3,2,1,0:T(8,128)(2,1)S(1)}, u32[]{:S(2)}, u32[]{:S(2)}) collective-permute-start(bf16[2,3,64,128]{3,2,1,0:T(8,128)(2,1)} %get-tuple-element.14.own_wave), channel_id=1, source_target_pairs={{0,129},{32,161},{64,193},{96,225},{128,1},{160,33},{192,65},{224,... | collective-permute-start | bytes 294920 | tf_op jit(solution)/shard_map/ppermute | solution.py:346
  10.6 6.9 %all-to-all-start = ((bf16[16,24,16,128]{3,2,1,0:T(8,128)(2,1)}), bf16[16,24,16,128]{3,2,1,0:T(8,128)(2,1)S(1)}, u32[]{:S(2)}, u32[]{:S(2)}) async-start(bf16[16,24,16,128]{3,2,1,0:T(8,128)(2,1)} %get-tuple-element.20), calls=%async_computation | async-start | bytes 3145728 | tf_op jit(solution)/shard_map/all_to_all | solution.py:352
  17.6 0.1 broadcast_in_dim.2
  17.6 0.1 reshape.140.sign
  17.8 0.0 collective-permute-done.far_table
  17.8 0.0 copy-start.9
  17.8 0.0 collective-permute-done.1.far_wave
  17.8 0.0 copy-start.4
  17.8 0.0 collective-permute-done.2.far_left
  17.8 0.0 copy-done
  17.8 0.0 copy-done.2
  17.8 3.1 %make_tiles.1 = (bf16[97,16,128]{2,1,0:T(8,128)(2,1)}, bf16[97,16,128]{2,1,0:T(8,128)(2,1)}, bf16[49,16,128]{2,1,0:T(8,128)(2,1)}) custom-call(s32[12,32]{1,0:T(8,128)S(1)} %copy-done.7, s32[12,32]{1,0:T(8,128)S(1)} %collective-permute-done.far_table, bf16[2,3,64,128]{3,2,1,0:T(8,128)(2,1)S(1)} %copy-done.2, ...), custom_call_target="tpu_custom_call" | custom-call | flops 1000000000 | bytes 4000000 | tf_op jit(solution)/shard_map/make_tiles/pallas_call | solution.py:215
  20.9 0.0 copy-done.9
  21.0 0.0 copy-done.4
  21.0 0.1 collective-permute-start.3
  21.1 1.5 %collective-permute-start.4 = (bf16[97,16,128]{2,1,0:T(8,128)(2,1)}, bf16[97,16,128]{2,1,0:T(8,128)(2,1)S(1)}, u32[]{:S(2)}, u32[]{:S(2)}) collective-permute-start(bf16[97,16,128]{2,1,0:T(8,128)(2,1)} %get-tuple-element.18), channel_id=1, source_target_pairs={{0,193},{32,96},{64,0},{96,160},{128,64},{160,224},{192,128},{224,... | collective-permute-start | bytes 1191944 | tf_op jit(solution)/shard_map/ppermute | solution.py:362
  22.5 1.5 %collective-permute-start.5 = (bf16[49,16,128]{2,1,0:T(8,128)(2,1)}, bf16[49,16,128]{2,1,0:T(8,128)(2,1)}, u32[]{:S(2)}, u32[]{:S(2)}) collective-permute-start(bf16[49,16,128]{2,1,0:T(8,128)(2,1)} %get-tuple-element.19), channel_id=1, source_target_pairs={{0,128},{32,161},{64,192},{96,225},{128,1},{160,32},{192,65},{224,... | collective-permute-start | bytes 602120 | tf_op jit(solution)/shard_map/ppermute | solution.py:363
  24.0 0.7 %reshape.139 = s32[4,2,12]{2,1,0:T(2,128)S(1)} reshape(s32[96]{0:T(128)} %param.12) | data formatting | bytes 768 | tf_op jit(solution)/shard_map/reshape | solution.py:370
  24.9 0.1 mul.40
  24.9 0.7 %stack.16 = s32[1,1,8,12]{3,2,1,0:T(8,128)S(1)} reshape(s32[96]{0:T(128)} %param.13) | data formatting | bytes 768 | tf_op jit(solution)/shard_map/stack | solution.py:377
  25.7 0.1 fusion.2
  25.8 0.1 iota_add_fusion
  25.9 0.1 fusion.1
  26.0 0.1 add.106.slot_key
  26.1 0.1 add.102.real_key
  26.2 0.1 sub.29.imag_key
  26.3 0.2 make_picks.1.picks
  26.5 0.0 copy-start.1
  26.5 1.4 %copy-done.1 = bf16[12,2,2,128,128]{4,3,2,1,0:T(8,128)(2,1)S(1)} copy-done((bf16[12,2,2,128,128]{4,3,2,1,0:T(8,128)(2,1)S(1)}, bf16[12,2,2,128,128]{4,3,2,1,0:T(8,128)(2,1)}, u32[]{:S(2)}) %copy-start.1) | copy-done | bytes 1572888
  27.9 0.9 %copy-done.3 = bf16[2,3,64,128]{3,2,1,0:T(8,128)(2,1)S(1)} copy-done((bf16[2,3,64,128]{3,2,1,0:T(8,128)(2,1)S(1)}, bf16[2,3,64,128]{3,2,1,0:T(8,128)(2,1)}, u32[]{:S(2)}) %copy-start.3) | copy-done | bytes 98328
  28.8 0.9 %copy-done.5 = bf16[2,3,64,128]{3,2,1,0:T(8,128)(2,1)S(1)} copy-done((bf16[2,3,64,128]{3,2,1,0:T(8,128)(2,1)S(1)}, bf16[2,3,64,128]{3,2,1,0:T(8,128)(2,1)}, u32[]{:S(2)}) %copy-start.5) | copy-done | bytes 98328
  29.7 0.7 %copy-done.8 = s32[12,32]{1,0:T(8,128)S(1)} copy-done((s32[12,32]{1,0:T(8,128)S(1)}, s32[12,32]{1,0:T(8,128)}, u32[]{:S(2)}) %copy-start.8) | copy-done | bytes 1560
  30.4 0.7 %copy-done.10 = s32[12,32]{1,0:T(8,128)S(1)} copy-done((s32[12,32]{1,0:T(8,128)S(1)}, s32[12,32]{1,0:T(8,128)}, u32[]{:S(2)}) %copy-start.10) | copy-done | bytes 1560
  31.1 2.3 %make_home.1.home = bf16[145,16,128]{2,1,0:T(8,128)(2,1)S(1)} custom-call(s32[12,32]{1,0:T(8,128)S(1)} %copy-done.8, s32[12,32]{1,0:T(8,128)S(1)} %copy-done.10, bf16[2,3,64,128]{3,2,1,0:T(8,128)(2,1)S(1)} %copy-done.3, bf16[2,3,64,128]{3,2,1,0:T(8,128)(2,1)S(1)} %copy-done.5, bf16[12,2,2,128,128]{4,3,2,1,0:T(8,128)(2,1)S(1)} %copy-done.1, ...), custom_call_target="tpu_custom_call" | custom-call | flops 1000000000 | bytes 4000000 | tf_op jit(solution)/shard_map/make_home/pallas_call | solution.py:215
  33.4 4.7 %all-to-all-done.right = bf16[16,24,16,128]{3,2,1,0:T(8,128)(2,1)S(1)} async-done(((bf16[16,24,16,128]{3,2,1,0:T(8,128)(2,1)}), bf16[16,24,16,128]{3,2,1,0:T(8,128)(2,1)S(1)}, u32[]{:S(2)}, u32[]{:S(2)}) %all-to-all-start) | async-done | bytes 1572896 | tf_op jit(solution)/shard_map/all_to_all | solution.py:352
  38.0 0.0 collective-permute-done.5.ahead2
  38.0 0.0 collective-permute-done.3.ahead1
  38.1 0.0 collective-permute-done.4.back1
  38.1 0.0 copy-start.6
  38.1 0.7 %copy-done.6 = s32[128,32]{0,1:T(8,128)S(1)} copy-done((s32[128,32]{0,1:T(8,128)S(1)}, s32[128,32]{0,1:T(8,128)}, u32[]{:S(2)}) %copy-start.6) | copy-done | bytes 16408
  38.8 2.5 %contract.1 = bf16[8,64,128]{2,1,0:T(8,128)(2,1)S(1)} custom-call(bf16[145,16,128]{2,1,0:T(8,128)(2,1)S(1)} %make_home.1.home, bf16[97,16,128]{2,1,0:T(8,128)(2,1)S(1)} %collective-permute-done.3.ahead1, bf16[97,16,128]{2,1,0:T(8,128)(2,1)S(1)} %collective-permute-done.4.back1, bf16[49,16,128]{2,1,0:T(8,128)(2,1)} %collective-permute-done.5.ahead2, ...), custom_call_target="tpu_custom_call" | custom-call | tf_op jit(solution)/shard_map/contract/pallas_call | solution.py:320
  41.3 23.2 %all_to_all.10 = bf16[256,2,128]{2,1,0:T(2,128)(2,1)S(1)} all-to-all(bf16[256,2,128]{2,1,0:T(2,128)(2,1)S(1)} %bitcast.19), channel_id=1, replica_groups=mesh['row'=8,'col'=16,'wf'=2] {'row','wf','col'}, dimensions={0} | all-to-all | bytes 262144 | tf_op jit(solution)/shard_map/all_to_all | solution.py:387
  64.5 0.3 convert_reduce_fusion
  64.7 0.1 reshape.142
  64.8 0.6 copy.13
  (21 shorter events, 0.1 us)
Async XLA Ops:
  0.0 17.8 %collective-permute-start.2 = (bf16[12,2,2,128,128]{4,3,2,1,0:T(8,128)(2,1)}, bf16[12,2,2,128,128]{4,3,2,1,0:T(8,128)(2,1)}, u32[]{:S(2)}, u32[]{:S(2)}) collective-permute-start(bf16[12,2,2,128,128]{4,3,2,1,0:T(8,128)(2,1)} %own_left.3), channel_id=1, source_target_pairs={{0,32},{32,0},{64,96},{96,64},{128,160},{160,128},{192,224},{224,1... | collective-permute-start | bytes 4718600 | tf_op jit(solution)/shard_map/ppermute | solution.py:350
  3.2 14.5 %collective-permute-start = (s32[12,32]{1,0:T(8,128)}, s32[12,32]{1,0:T(8,128)S(1)}, u32[]{:S(2)}, u32[]{:S(2)}) collective-permute-start(s32[12,32]{1,0:T(8,128)} %own_table.3), channel_id=1, source_target_pairs={{0,32},{32,0},{64,96},{96,64},{128,160},{160,128},{192,224},{224,1... | collective-permute-start | bytes 4616 | tf_op jit(solution)/shard_map/ppermute | solution.py:351
  6.2 11.5 %collective-permute-start.1 = (bf16[2,3,64,128]{3,2,1,0:T(8,128)(2,1)}, bf16[2,3,64,128]{3,2,1,0:T(8,128)(2,1)S(1)}, u32[]{:S(2)}, u32[]{:S(2)}) collective-permute-start(bf16[2,3,64,128]{3,2,1,0:T(8,128)(2,1)} %get-tuple-element.14.own_wave), channel_id=1, source_target_pairs={{0,129},{32,161},{64,193},{96,225},{128,1},{160,33},{192,65},{224,... | collective-permute-start | bytes 294920 | tf_op jit(solution)/shard_map/ppermute | solution.py:346
  10.6 7.2 %copy-start = (bf16[12,2,2,128,128]{4,3,2,1,0:T(8,128)(2,1)S(1)}, bf16[12,2,2,128,128]{4,3,2,1,0:T(8,128)(2,1)}, u32[]{:S(2)}) copy-start(bf16[12,2,2,128,128]{4,3,2,1,0:T(8,128)(2,1)} %own_left.3) | copy-start | bytes 4718596
  10.6 7.2 %copy-start.2 = (bf16[2,3,64,128]{3,2,1,0:T(8,128)(2,1)S(1)}, bf16[2,3,64,128]{3,2,1,0:T(8,128)(2,1)}, u32[]{:S(2)}) copy-start(bf16[2,3,64,128]{3,2,1,0:T(8,128)(2,1)} %get-tuple-element.14.own_wave) | copy-start | bytes 294916
  10.6 7.2 %copy-start.7 = (s32[12,32]{1,0:T(8,128)S(1)}, s32[12,32]{1,0:T(8,128)}, u32[]{:S(2)}) copy-start(s32[12,32]{1,0:T(8,128)} %own_table.3) | copy-start | bytes 4612
  10.6 27.4 %all-to-all-start = ((bf16[16,24,16,128]{3,2,1,0:T(8,128)(2,1)}), bf16[16,24,16,128]{3,2,1,0:T(8,128)(2,1)S(1)}, u32[]{:S(2)}, u32[]{:S(2)}) async-start(bf16[16,24,16,128]{3,2,1,0:T(8,128)(2,1)} %get-tuple-element.20), calls=%async_computation | async-start | bytes 3145728 | tf_op jit(solution)/shard_map/all_to_all | solution.py:352
  17.8 3.2 %copy-start.9 = (s32[12,32]{1,0:T(8,128)}, s32[12,32]{1,0:T(8,128)S(1)}, u32[]{:S(2)}) copy-start(s32[12,32]{1,0:T(8,128)S(1)} %collective-permute-done.far_table) | copy-start | bytes 4612
  17.8 3.2 %copy-start.4 = (bf16[2,3,64,128]{3,2,1,0:T(8,128)(2,1)}, bf16[2,3,64,128]{3,2,1,0:T(8,128)(2,1)S(1)}, u32[]{:S(2)}) copy-start(bf16[2,3,64,128]{3,2,1,0:T(8,128)(2,1)S(1)} %collective-permute-done.1.far_wave) | copy-start | bytes 294916
  21.0 17.1 %collective-permute-start.3 = (bf16[97,16,128]{2,1,0:T(8,128)(2,1)}, bf16[97,16,128]{2,1,0:T(8,128)(2,1)S(1)}, u32[]{:S(2)}, u32[]{:S(2)}) collective-permute-start(bf16[97,16,128]{2,1,0:T(8,128)(2,1)} %get-tuple-element.17), channel_id=1, source_target_pairs={{0,64},{32,225},{64,128},{96,32},{128,192},{160,96},{192,1},{224,1... | collective-permute-start | bytes 1191944 | tf_op jit(solution)/shard_map/ppermute | solution.py:361
  21.1 17.0 %collective-permute-start.4 = (bf16[97,16,128]{2,1,0:T(8,128)(2,1)}, bf16[97,16,128]{2,1,0:T(8,128)(2,1)S(1)}, u32[]{:S(2)}, u32[]{:S(2)}) collective-permute-start(bf16[97,16,128]{2,1,0:T(8,128)(2,1)} %get-tuple-element.18), channel_id=1, source_target_pairs={{0,193},{32,96},{64,0},{96,160},{128,64},{160,224},{192,128},{224,... | collective-permute-start | bytes 1191944 | tf_op jit(solution)/shard_map/ppermute | solution.py:362
  22.5 15.5 %collective-permute-start.5 = (bf16[49,16,128]{2,1,0:T(8,128)(2,1)}, bf16[49,16,128]{2,1,0:T(8,128)(2,1)}, u32[]{:S(2)}, u32[]{:S(2)}) collective-permute-start(bf16[49,16,128]{2,1,0:T(8,128)(2,1)} %get-tuple-element.19), channel_id=1, source_target_pairs={{0,128},{32,161},{64,192},{96,225},{128,1},{160,32},{192,65},{224,... | collective-permute-start | bytes 602120 | tf_op jit(solution)/shard_map/ppermute | solution.py:363
  26.5 1.4 %copy-start.1 = (bf16[12,2,2,128,128]{4,3,2,1,0:T(8,128)(2,1)S(1)}, bf16[12,2,2,128,128]{4,3,2,1,0:T(8,128)(2,1)}, u32[]{:S(2)}) copy-start(bf16[12,2,2,128,128]{4,3,2,1,0:T(8,128)(2,1)} %own_left.3) | copy-start | bytes 4718596
  27.9 0.9 %copy-start.3 = (bf16[2,3,64,128]{3,2,1,0:T(8,128)(2,1)S(1)}, bf16[2,3,64,128]{3,2,1,0:T(8,128)(2,1)}, u32[]{:S(2)}) copy-start(bf16[2,3,64,128]{3,2,1,0:T(8,128)(2,1)} %get-tuple-element.14.own_wave) | copy-start | bytes 294916
  28.8 0.9 %copy-start.5 = (bf16[2,3,64,128]{3,2,1,0:T(8,128)(2,1)S(1)}, bf16[2,3,64,128]{3,2,1,0:T(8,128)(2,1)}, u32[]{:S(2)}) copy-start(bf16[2,3,64,128]{3,2,1,0:T(8,128)(2,1)} %copy-done.4) | copy-start | bytes 294916
  29.7 0.7 %copy-start.8 = (s32[12,32]{1,0:T(8,128)S(1)}, s32[12,32]{1,0:T(8,128)}, u32[]{:S(2)}) copy-start(s32[12,32]{1,0:T(8,128)} %own_table.3) | copy-start | bytes 4612
  30.4 0.7 %copy-start.10 = (s32[12,32]{1,0:T(8,128)S(1)}, s32[12,32]{1,0:T(8,128)}, u32[]{:S(2)}) copy-start(s32[12,32]{1,0:T(8,128)} %copy-done.9) | copy-start | bytes 4612
  38.1 0.7 %copy-start.6 = (s32[128,32]{0,1:T(8,128)S(1)}, s32[128,32]{0,1:T(8,128)}, u32[]{:S(2)}) copy-start(s32[128,32]{0,1:T(8,128)} %param.11) | copy-start | bytes 49156
